TPU v7x, 32 devices: a whole 2x2x4 slice. The times are simulated.
32 devices in a mesh: grp: 4 (over x, core), ep: 8 (over z, y).
Axes of the slice: x: 2, y: 2, z: 4, core: 2. Of those that a mesh axis runs over, the one named last changes fastest.
Arguments:
- queries: bfloat16 [3, 128, 128, 576], P(None, ('grp', 'ep')), may hold values from -10 to 10, as said below
- cache: bfloat16 [128, 128, 576], P(('grp', 'ep')), may hold values from -5 to 5, as said below
- new_entries: bfloat16 [3, 128, 576], P(None, ('grp', 'ep')), may hold values from -5 to 5
- lengths: int32 [128], P(('grp', 'ep')), may hold values from 2 to 125, as said below
- moe_input: bfloat16 [3, 128, 3584], P(None, ('grp', 'ep')), may hold values from -6 to 6
- expert_ids: int32 [3, 4, 32, 8], P(None, None, 'ep'), may hold values from 0 to 7, all different within a row; in each aligned block of 4 rows (0 to 3, 4 to 7, ..., all dimensions but the last counted through in order) at most 4 rows name the same one
- route_gains: float32 [3, 4, 32, 8], P(None, None, 'ep'), may hold values from 0.1 to 1
- w_gate: bfloat16 [8, 3584, 2048], P('ep', None, 'grp'), may hold values from -0.09375 to 0.09375
- w_up: bfloat16 [8, 3584, 2048], P('ep', None, 'grp'), may hold values from -0.09375 to 0.09375
- w_down: bfloat16 [8, 2048, 3584], P('ep', 'grp'), may hold values from -0.125 to 0.125
- plan: int32 [4, 8, 2, 2], P(None, 'ep'), may hold values from 0 to 3, as said below
Outputs:
- contexts: bfloat16 [3, 128, 128, 512], P(None, ('grp', 'ep'))
- migrated_cache: bfloat16 [128, 128, 576], P(('grp', 'ep'))
- moe_output: bfloat16 [3, 128, 3584], P(None, ('grp', 'ep'))
Inputs may be any that keep to these rules, and one draw needn't show every extreme that they name: `queries`: queries lie in this range. `cache`: cache entries lie in this range. `lengths`: some trace has exactly 125 filled rows. `expert_ids`: within the 4 tokens of one device in one step, no expert is named by more than 4 tokens. plan[g, e, k] = (slot, grp index d): device (g, e) sends the trace in that slot to device (d, e). A device's 2 slots differ; its destinations differ from each other and from g. For each k, every device of an ep index is the destination of exactly one device's entry k, and the trace lands in the slot that the destination lists in its own entry k.
All inputs are finite; a program needn't handle non-finite values.
Results may differ from a plain program's by a relative error of at most 0.019.
Values may be sent and summed in bfloat16 or wider, within the bound.
No kernel may reach another device: no remote copies, remote signals or barrier semaphores. Data moves between devices by JAX's collectives and lax.ppermute only.
A program may use at most 128 MiB of HBM per device.

v0:
```python
from functools import partial

import jax
import jax.numpy as jnp
from jax import lax
from jax.sharding import PartitionSpec as P

ROPE = 64


SCORE_SCALE = 192.0 ** (-0.5)


def slot_tables(route_ids, route_gains, expert_count, slot_count):
    token_count, top_count = route_ids.shape
    flat_ids = route_ids.reshape(-1)
    row_list = jnp.arange(flat_ids.shape[0], dtype=jnp.int32)
    same_expert = flat_ids[:, None] == flat_ids[None, :]
    earlier = row_list[None, :] < row_list[:, None]
    slot_rank = jnp.sum(jnp.where(same_expert & earlier, 1, 0), axis=1).astype(jnp.int32)
    slot_index = flat_ids * slot_count + slot_rank
    slot_hot = (
        slot_index[:, None] == jnp.arange(expert_count * slot_count, dtype=jnp.int32)[None, :]
    ).astype(jnp.float32)
    token_hot = (
        (row_list // top_count)[:, None] == jnp.arange(token_count, dtype=jnp.int32)[None, :]
    ).astype(jnp.float32)
    dispatch = jnp.dot(slot_hot.T, token_hot, precision=lax.Precision.HIGHEST)
    combine = jnp.dot(
        token_hot.T, slot_hot * route_gains.reshape(-1)[:, None], precision=lax.Precision.HIGHEST
    )
    return (dispatch, combine)


def expert_rows(token_rows, gate_slice, up_slice, down_slice):
    gate_out = jnp.dot(token_rows, gate_slice, preferred_element_type=jnp.float32)
    up_out = jnp.dot(token_rows, up_slice, preferred_element_type=jnp.float32)
    hidden = (jax.nn.silu(gate_out) * up_out).astype(jnp.bfloat16)
    return jnp.dot(hidden, down_slice, preferred_element_type=jnp.float32).astype(jnp.bfloat16)


def body(
    queries,
    cache,
    new_entries,
    lengths,
    moe_input,
    expert_ids,
    route_gains,
    w_gate,
    w_up,
    w_down,
    plan,
):
    trace_count = cache.shape[0]
    latent = queries.shape[3] - ROPE
    positions = jnp.arange(cache.shape[1], dtype=jnp.int32)
    grown_cache = cache
    context_list = []
    for step_index in range(queries.shape[0]):
        filled = lengths + step_index
        write_here = positions[None, :] == filled[:, None]
        grown_cache = jnp.where(
            write_here[:, :, None], new_entries[step_index][:, None, :], grown_cache
        )
        scores = (
            jnp.einsum(
                "thd,tcd->thc", queries[step_index], grown_cache, preferred_element_type=jnp.float32
            )
            * SCORE_SCALE
        )
        visible = (positions[None, :] <= filled[:, None])[:, None, :]
        scores = jnp.where(visible, scores, -jnp.inf)
        top_score = jnp.max(scores, axis=2, keepdims=True)
        exp_scores = jnp.exp(scores - top_score)
        weights = (exp_scores / jnp.sum(exp_scores, axis=2, keepdims=True)).astype(jnp.bfloat16)
        context = jnp.einsum(
            "thc,tcd->thd", weights, grown_cache[:, :, :latent], preferred_element_type=jnp.float32
        )
        context_list.append(context.astype(jnp.bfloat16))
    contexts = jnp.stack(context_list)
    groups = lax.axis_size("grp")
    group_index = lax.axis_index("grp")
    column_plan = plan[:, 0]
    own_plan = lax.dynamic_index_in_dim(column_plan, group_index, 0, keepdims=False)
    out_slots = own_plan[:, 0]
    slot_list = jnp.arange(trace_count, dtype=jnp.int32)
    leaving = (out_slots[None, :] == slot_list[:, None]).astype(jnp.float32)
    arriving = (column_plan[:, :, 1] == group_index).astype(jnp.float32)
    keep_slot = jnp.sum(leaving, axis=1) < 0.5
    outgoing = jnp.einsum(
        "tk,tcd->kcd", leaving.astype(jnp.bfloat16), grown_cache, preferred_element_type=jnp.float32
    ).astype(jnp.bfloat16)
    received = lax.all_gather(outgoing, "grp", axis=0, tiled=True)
    placement = (
        (leaving[:, None, :] * arriving[None, :, :]).reshape(trace_count, -1).astype(jnp.bfloat16)
    )
    incoming = jnp.einsum("ts,scd->tcd", placement, received, preferred_element_type=jnp.float32)
    migrated_cache = jnp.where(keep_slot[:, None, None], grown_cache, incoming.astype(jnp.bfloat16))
    experts = lax.axis_size("ep")
    top_count = expert_ids.shape[3]
    model_width = moe_input.shape[2]
    slot_count = max(2, trace_count * top_count // experts)
    gate_slice = w_gate[0]
    up_slice = w_up[0]
    down_slice = w_down[0]
    tables = partial(slot_tables, expert_count=experts, slot_count=slot_count)
    moe_list = []
    for step_index in range(moe_input.shape[0]):
        column_ids = expert_ids[step_index]
        column_gains = route_gains[step_index]
        dispatch_all, combine_all = jax.vmap(tables)(column_ids, column_gains)
        column_tokens = lax.all_gather(moe_input[step_index][None], "grp", axis=0, tiled=True)
        packed = jnp.einsum(
            "gsj,gjd->sgd",
            dispatch_all.astype(jnp.bfloat16),
            column_tokens,
            preferred_element_type=jnp.float32,
        )
        packed = packed.astype(jnp.bfloat16).reshape(experts, slot_count * groups, model_width)
        exchanged = lax.all_to_all(packed, "ep", split_axis=0, concat_axis=0, tiled=True)
        flat_rows = exchanged.reshape(-1, exchanged.shape[-1])
        partial_out = expert_rows(flat_rows, gate_slice, up_slice, down_slice).reshape(
            exchanged.shape
        )
        returned = lax.all_to_all(partial_out, "ep", split_axis=0, concat_axis=0, tiled=True)
        returned = returned.reshape(experts * slot_count, groups, model_width).astype(jnp.float32)
        token_terms = jnp.einsum(
            "gjs,sgd->gjd", combine_all, returned, precision=lax.Precision.HIGHEST
        )
        summed = lax.psum_scatter(
            token_terms.astype(jnp.bfloat16), "grp", scatter_dimension=0, tiled=True
        ).astype(jnp.float32)
        moe_list.append(summed[0].astype(jnp.bfloat16))
    moe_output = jnp.stack(moe_list)
    return (contexts, migrated_cache, moe_output)


def solution(mesh):
    return jax.shard_map(
        body,
        mesh=mesh,
        in_specs=(
            P(None, ("grp", "ep"), None, None),
            P(("grp", "ep"), None, None),
            P(None, ("grp", "ep"), None),
            P(("grp", "ep")),
            P(None, ("grp", "ep"), None),
            P(None, None, "ep", None),
            P(None, None, "ep", None),
            P("ep", None, "grp"),
            P("ep", None, "grp"),
            P("ep", "grp", None),
            P(None, "ep", None, None),
        ),
        out_specs=(
            P(None, ("grp", "ep"), None, None),
            P(("grp", "ep"), None, None),
            P(None, ("grp", "ep"), None),
        ),
        check_vma=False,
    )
```

profile of v0, /device:TPU:0, one launch (start us, length us, event | category | flops | bytes accessed | tf_op | source)
XLA Modules:
  0.0 225.4 jit_solution(15577693707827235050)
XLA Ops:
  7.2 0.8 fusion.136
  8.7 0.8 fusion.134
  9.5 6.4 %all_gather.14 = bf16[4,4,3584]{2,1,0:T(4,128)(2,1)S(1)} all-gather(bf16[1,4,3584]{2,1,0:T(4,128)(2,1)S(1)} %get-tuple-element.29), channel_id=1, replica_groups=mesh['grp'=4,'ep'=8] {'grp'}, dimensions={0}, use_global_device_ids=true | all-gather | bytes 143360 | tf_op jit(solution)/shard_map/all_gather | solution.py:113
  16.5 0.7 copy.98
  17.2 1.1 reshape.261
  18.4 6.4 %all-to-all-start.2 = ((bf16[8,16,3584]{2,1,0:T(8,128)(2,1)}), bf16[8,16,3584]{2,1,0:T(8,128)(2,1)S(1)}, u32[]{:S(2)}, u32[]{:S(2)}) async-start(bf16[8,16,3584]{2,1,0:T(8,128)(2,1)} %reshape.261), calls=%async_computation.2 | async-start | bytes 1835008 | tf_op jit(solution)/shard_map/all_to_all | solution.py:121
  25.1 5.4 %all_gather.15 = bf16[4,4,3584]{2,1,0:T(4,128)(2,1)S(1)} all-gather(bf16[1,4,3584]{2,1,0:T(4,128)(2,1)S(1)} %get-tuple-element.28), channel_id=1, replica_groups=mesh['grp'=4,'ep'=8] {'grp'}, dimensions={0}, use_global_device_ids=true | all-gather | bytes 143360 | tf_op jit(solution)/shard_map/all_gather | solution.py:113
  31.8 1.1 reshape.265
  33.1 15.2 %all-to-all-done.2 = bf16[8,16,3584]{2,1,0:T(8,128)(2,1)S(1)} async-done(((bf16[8,16,3584]{2,1,0:T(8,128)(2,1)}), bf16[8,16,3584]{2,1,0:T(8,128)(2,1)S(1)}, u32[]{:S(2)}, u32[]{:S(2)}) %all-to-all-start.2) | async-done | bytes 917536 | tf_op jit(solution)/shard_map/all_to_all | solution.py:121
  48.2 3.6 %all-to-all-start.4 = ((bf16[8,16,3584]{2,1,0:T(8,128)(2,1)}), bf16[8,16,3584]{2,1,0:T(8,128)(2,1)S(1)}, u32[]{:S(2)}, u32[]{:S(2)}) async-start(bf16[8,16,3584]{2,1,0:T(8,128)(2,1)} %reshape.265), calls=%async_computation.4 | async-start | bytes 1835008 | tf_op jit(solution)/shard_map/all_to_all | solution.py:121
  52.0 1.4 broadcast_select_fusion
  53.4 0.8 copy.91
  55.1 0.7 copy.92
  55.9 5.4 %all_gather.13 = bf16[4,4,3584]{2,1,0:T(4,128)(2,1)S(1)} all-gather(bf16[1,4,3584]{2,1,0:T(4,128)(2,1)S(1)} %get-tuple-element.27), channel_id=1, replica_groups=mesh['grp'=4,'ep'=8] {'grp'}, dimensions={0}, use_global_device_ids=true | all-gather | bytes 143360 | tf_op jit(solution)/shard_map/all_gather | solution.py:113
  62.6 1.1 reshape.257
  63.8 11.2 %all-to-all-done.4 = bf16[8,16,3584]{2,1,0:T(8,128)(2,1)S(1)} async-done(((bf16[8,16,3584]{2,1,0:T(8,128)(2,1)}), bf16[8,16,3584]{2,1,0:T(8,128)(2,1)S(1)}, u32[]{:S(2)}, u32[]{:S(2)}) %all-to-all-start.4) | async-done | bytes 917536 | tf_op jit(solution)/shard_map/all_to_all | solution.py:121
  75.0 3.6 %all-to-all-start = ((bf16[8,16,3584]{2,1,0:T(8,128)(2,1)}), bf16[8,16,3584]{2,1,0:T(8,128)(2,1)S(1)}, u32[]{:S(2)}, u32[]{:S(2)}) async-start(bf16[8,16,3584]{2,1,0:T(8,128)(2,1)} %reshape.257), calls=%async_computation | async-start | bytes 1835008 | tf_op jit(solution)/shard_map/all_to_all | solution.py:121
  78.6 1.6 fusion.44
  80.9 1.6 fusion.46
  83.3 2.4 %fusion.22 = bf16[1,4,128,512]{3,2,1,0:T(8,128)(2,1)} fusion(bf16[4,128,576]{2,1,0:T(8,128)(2,1)} %get-tuple-element.25, f32[4,128]{1,0:T(4,128)S(1)} %fusion.138, f32[4,128,128]{1,2,0:T(8,128)} %copy-done.3), kind=kOutput, calls=%fused_computation.35 | convolution fusion | flops 67568256 | bytes 1574912 | tf_op jit(solution)/shard_map/thc,tcd->thd/dot_general | solution.py:77
  85.7 3.4 %fusion.17 = f32[128,512]{1,0:T(8,128)} fusion(bf16[128,3584]{1,0:T(8,128)(2,1)S(1)} %bitcast.129, bf16[1,3584,512]{2,1,0:T(8,128)(2,1)} %param.18), kind=kOutput, calls=%fused_computation.26 | convolution fusion | flops 469762048 | bytes 4849664 | tf_op jit(solution)/shard_map/dot_general | solution.py:36
  89.1 5.5 %convolution_convert_fusion.2 = bf16[128,3584]{1,0:T(8,128)(2,1)} fusion(bf16[1,512,3584]{2,1,0:T(8,128)(2,1)} %param.20, bf16[128,3584]{1,0:T(8,128)(2,1)S(1)} %bitcast.130, bf16[1,3584,512]{2,1,0:T(8,128)(2,1)} %param.19, f32[128,512]{1,0:T(8,128)} %fusion.17), kind=kOutput, calls=%fused_computation.5 | convolution fusion | flops 940376064 | bytes 9437184 | tf_op jit(solution)/shard_map/dot_general | solution.py:39
  94.5 7.2 %all-to-all-done = bf16[8,16,3584]{2,1,0:T(8,128)(2,1)S(1)} async-done(((bf16[8,16,3584]{2,1,0:T(8,128)(2,1)}), bf16[8,16,3584]{2,1,0:T(8,128)(2,1)S(1)}, u32[]{:S(2)}, u32[]{:S(2)}) %all-to-all-start) | async-done | bytes 917536 | tf_op jit(solution)/shard_map/all_to_all | solution.py:121
  101.7 3.7 %all-to-all-start.3 = ((bf16[8,16,3584]{2,1,0:T(8,128)(2,1)}), bf16[8,16,3584]{2,1,0:T(8,128)(2,1)S(1)}, u32[]{:S(2)}, u32[]{:S(2)}) async-start(bf16[8,16,3584]{2,1,0:T(8,128)(2,1)} %bitcast.135), calls=%async_computation.3 | async-start | bytes 1835008 | tf_op jit(solution)/shard_map/all_to_all | solution.py:126
  105.6 2.4 %fusion.21 = bf16[1,4,128,512]{3,2,1,0:T(8,128)(2,1)} fusion(bf16[4,128,576]{2,1,0:T(8,128)(2,1)} %get-tuple-element.26, f32[4,128]{1,0:T(4,128)S(1)} %fusion.139, f32[4,128,128]{1,2,0:T(8,128)} %copy-done.2), kind=kOutput, calls=%fused_computation.34 | convolution fusion | flops 67568256 | bytes 1574912 | tf_op jit(solution)/shard_map/thc,tcd->thd/dot_general | solution.py:77
  108.0 2.1 fusion.42
  110.1 3.4 %fusion.15 = f32[128,512]{1,0:T(8,128)} fusion(bf16[128,3584]{1,0:T(8,128)(2,1)S(1)} %bitcast.131, bf16[1,3584,512]{2,1,0:T(8,128)(2,1)} %param.18), kind=kOutput, calls=%fused_computation.24 | convolution fusion | flops 469762048 | bytes 4849664 | tf_op jit(solution)/shard_map/dot_general | solution.py:36
  113.4 5.4 %convolution_convert_fusion = bf16[128,3584]{1,0:T(8,128)(2,1)} fusion(bf16[1,512,3584]{2,1,0:T(8,128)(2,1)} %param.20, bf16[128,3584]{1,0:T(8,128)(2,1)S(1)} %bitcast.132, bf16[1,3584,512]{2,1,0:T(8,128)(2,1)} %param.19, f32[128,512]{1,0:T(8,128)} %fusion.15), kind=kOutput, calls=%fused_computation.3 | convolution fusion | flops 940376064 | bytes 9437184 | tf_op jit(solution)/shard_map/dot_general | solution.py:39
  118.9 9.6 %all-to-all-done.3 = bf16[8,16,3584]{2,1,0:T(8,128)(2,1)S(1)} async-done(((bf16[8,16,3584]{2,1,0:T(8,128)(2,1)}), bf16[8,16,3584]{2,1,0:T(8,128)(2,1)S(1)}, u32[]{:S(2)}, u32[]{:S(2)}) %all-to-all-start.3) | async-done | bytes 917536 | tf_op jit(solution)/shard_map/all_to_all | solution.py:126
  128.5 3.6 %all-to-all-start.5 = ((bf16[8,16,3584]{2,1,0:T(8,128)(2,1)}), bf16[8,16,3584]{2,1,0:T(8,128)(2,1)S(1)}, u32[]{:S(2)}, u32[]{:S(2)}) async-start(bf16[8,16,3584]{2,1,0:T(8,128)(2,1)} %bitcast.31), calls=%async_computation.5 | async-start | bytes 1835008 | tf_op jit(solution)/shard_map/all_to_all | solution.py:126
  132.1 1.1 fusion.137
  133.3 3.4 %fusion.19 = f32[128,512]{1,0:T(8,128)} fusion(bf16[128,3584]{1,0:T(8,128)(2,1)S(1)} %bitcast.133, bf16[1,3584,512]{2,1,0:T(8,128)(2,1)} %param.18), kind=kOutput, calls=%fused_computation.28 | convolution fusion | flops 469762048 | bytes 4849664 | tf_op jit(solution)/shard_map/dot_general | solution.py:36
  136.7 5.5 %convolution_convert_fusion.4 = bf16[128,3584]{1,0:T(8,128)(2,1)} fusion(bf16[1,512,3584]{2,1,0:T(8,128)(2,1)} %param.20, bf16[128,3584]{1,0:T(8,128)(2,1)S(1)} %bitcast.134, bf16[1,3584,512]{2,1,0:T(8,128)(2,1)} %param.19, f32[128,512]{1,0:T(8,128)} %fusion.19), kind=kOutput, calls=%fused_computation.7 | convolution fusion | flops 940376064 | bytes 9437184 | tf_op jit(solution)/shard_map/dot_general | solution.py:39
  142.2 13.0 %all-to-all-done.5 = bf16[8,16,3584]{2,1,0:T(8,128)(2,1)S(1)} async-done(((bf16[8,16,3584]{2,1,0:T(8,128)(2,1)}), bf16[8,16,3584]{2,1,0:T(8,128)(2,1)S(1)}, u32[]{:S(2)}, u32[]{:S(2)}) %all-to-all-start.5) | async-done | bytes 917536 | tf_op jit(solution)/shard_map/all_to_all | solution.py:126
  155.2 3.6 %all-to-all-start.1 = ((bf16[8,16,3584]{2,1,0:T(8,128)(2,1)}), bf16[8,16,3584]{2,1,0:T(8,128)(2,1)S(1)}, u32[]{:S(2)}, u32[]{:S(2)}) async-start(bf16[8,16,3584]{2,1,0:T(8,128)(2,1)} %bitcast.23), calls=%async_computation.1 | async-start | bytes 1835008 | tf_op jit(solution)/shard_map/all_to_all | solution.py:126
  158.9 2.2 fusion.23
  162.1 2.7 %pad_maximum_fusion = bf16[3,4,128,512]{3,2,1,0:T(8,128)(2,1)} fusion(bf16[1,4,128,512]{3,2,1,0:T(8,128)(2,1)} %fusion.23, bf16[1,4,128,512]{3,2,1,0:T(8,128)(2,1)} %fusion.22, bf16[1,4,128,512]{3,2,1,0:T(8,128)(2,1)} %fusion.21), kind=kLoop, calls=%fused_computation.30 | loop fusion | flops 1572864 | bytes 3145728 | tf_op jit(solution)/shard_map/stack | solution.py:81
  165.5 3.0 %fusion.27 = bf16[4,128,576]{1,0,2:T(4,128)(2,1)} fusion(bf16[8,128,576]{1,2,0:T(8,128)(2,1)} %all-gather.2.cloned.1.call-done, f32[4,8]{0,1:T(8,128)S(1)} %bitcast.136, f32[8]{0:T(128)S(1)} %reshape.269), kind=kOutput, calls=%fused_computation.41 | convolution fusion | flops 4718656 | bytes 1769632 | tf_op jit(solution)/shard_map/ts,scd->tcd/dot_general | solution.py:98
  168.5 2.2 copy.95
  170.7 1.1 reshape.264
  172.0 2.5 %convolution_convert_fusion.7 = bf16[4,4,3584]{2,1,0:T(4,128)(2,1)} fusion(f32[4,4,32]{2,1,0:T(4,128)S(1)} %convolution_bitcast_fusion.1, bf16[32,4,3584]{2,1,0:T(4,128)(2,1)} %reshape.264), kind=kOutput, calls=%fused_computation.13 | convolution fusion | flops 22077440 | bytes 1034240 | tf_op jit(solution)/shard_map/gjs,sgd->gjd/dot_general | solution.py:128
  174.5 1.3 convolution_convert_fusion.6
  175.8 6.1 %all-to-all-done.1 = bf16[8,16,3584]{2,1,0:T(8,128)(2,1)S(1)} async-done(((bf16[8,16,3584]{2,1,0:T(8,128)(2,1)}), bf16[8,16,3584]{2,1,0:T(8,128)(2,1)S(1)}, u32[]{:S(2)}, u32[]{:S(2)}) %all-to-all-start.1) | async-done | bytes 917536 | tf_op jit(solution)/shard_map/all_to_all | solution.py:126
  182.2 1.3 convolution_convert_fusion.8
  183.6 1.1 copy.102
  184.7 30.3 %all-reduce.6.cloned.1.call-done = (bf16[4,4,3584]{2,1,0:T(4,128)(2,1)}, bf16[4,4,3584]{2,1,0:T(4,128)(2,1)}, bf16[4,4,3584]{2,1,0:T(4,128)(2,1)}) async-done(((bf16[4,4,3584]{2,1,0:T(4,128)(2,1)}, bf16[4,4,3584]{2,1,0:T(4,128)(2,1)}, bf16[4,4,3584]{2,1,0:T(4,128)(2,1)}), (bf16[4,4,3584]{2,1,0:T(4,128)(2,1)}, bf16[4,4,3584]{2,1,0:T(4,128)(2,1)}, bf16[4,4,3584]{2,1,0:T(4,128)(2,1)})) %all-reduce.6.cloned.1.call-update) | async-done | bytes 344080
  215.0 1.4 constant_dynamic-slice_fusion.2
  216.4 1.4 constant_dynamic-slice_fusion
  (70 shorter events, 10.1 us)
Async XLA Ops:
  7.2 17.6 %copy-start.1 = (bf16[4,128,576]{1,2,0:T(8,128)(2,1)S(1)}, bf16[4,128,576]{1,2,0:T(8,128)(2,1)}, u32[]{:S(2)}) copy-start(bf16[4,128,576]{1,2,0:T(8,128)(2,1)} %param.12) | copy-start | bytes 1769476
  18.4 14.6 %copy-start.7 = (s32[4]{0:T(128)S(1)}, s32[4]{0:T(128)}, u32[]{:S(2)}) copy-start(s32[4]{0:T(128)} %param.14) | copy-start | bytes 52
  18.4 14.7 %copy-start.5 = (bf16[3,4,576]{2,1,0:T(4,128)(2,1)S(1)}, bf16[3,4,576]{2,1,0:T(4,128)(2,1)}, u32[]{:S(2)}) copy-start(bf16[3,4,576]{2,1,0:T(4,128)(2,1)} %param.13) | copy-start | bytes 41476
  18.4 29.9 %all-to-all-start.2 = ((bf16[8,16,3584]{2,1,0:T(8,128)(2,1)}), bf16[8,16,3584]{2,1,0:T(8,128)(2,1)S(1)}, u32[]{:S(2)}, u32[]{:S(2)}) async-start(bf16[8,16,3584]{2,1,0:T(8,128)(2,1)} %reshape.261), calls=%async_computation.2 | async-start | bytes 1835008 | tf_op jit(solution)/shard_map/all_to_all | solution.py:121
  31.8 22.4 %copy-start.6 = (s32[4,1,2,2]{0,3,2,1:T(2,128)S(1)}, s32[4,1,2,2]{0,3,2,1:T(2,128)}, u32[]{:S(2)}) copy-start(s32[4,1,2,2]{0,3,2,1:T(2,128)} %param.21) | copy-start | bytes 196
  48.2 26.8 %all-to-all-start.4 = ((bf16[8,16,3584]{2,1,0:T(8,128)(2,1)}), bf16[8,16,3584]{2,1,0:T(8,128)(2,1)S(1)}, u32[]{:S(2)}, u32[]{:S(2)}) async-start(bf16[8,16,3584]{2,1,0:T(8,128)(2,1)} %reshape.265), calls=%async_computation.4 | async-start | bytes 1835008 | tf_op jit(solution)/shard_map/all_to_all | solution.py:121
  51.9 113.6 %all-gather.2.cloned.1.call-start = ((), (), s32[]{:S(2)}) async-start(), calls=%async_computation.6 | async-start | bytes 1474560 | tf_op jit(solution)/shard_map/all_gather | solution.py:94
  75.0 26.7 %all-to-all-start = ((bf16[8,16,3584]{2,1,0:T(8,128)(2,1)}), bf16[8,16,3584]{2,1,0:T(8,128)(2,1)S(1)}, u32[]{:S(2)}, u32[]{:S(2)}) async-start(bf16[8,16,3584]{2,1,0:T(8,128)(2,1)} %reshape.257), calls=%async_computation | async-start | bytes 1835008 | tf_op jit(solution)/shard_map/all_to_all | solution.py:121
  80.2 0.7 copy-start.3
  82.5 0.7 copy-start.2
  101.7 26.8 %all-to-all-start.3 = ((bf16[8,16,3584]{2,1,0:T(8,128)(2,1)}), bf16[8,16,3584]{2,1,0:T(8,128)(2,1)S(1)}, u32[]{:S(2)}, u32[]{:S(2)}) async-start(bf16[8,16,3584]{2,1,0:T(8,128)(2,1)} %bitcast.135), calls=%async_computation.3 | async-start | bytes 1835008 | tf_op jit(solution)/shard_map/all_to_all | solution.py:126
  113.4 19.8 %copy-start.4 = (f32[3,4,4,8]{3,2,1,0:T(4,128)S(1)}, f32[3,4,4,8]{3,2,1,0:T(4,128)}, u32[]{:S(2)}) copy-start(f32[3,4,4,8]{3,2,1,0:T(4,128)} %param.17) | copy-start | bytes 4612
  128.5 26.7 %all-to-all-start.5 = ((bf16[8,16,3584]{2,1,0:T(8,128)(2,1)}), bf16[8,16,3584]{2,1,0:T(8,128)(2,1)S(1)}, u32[]{:S(2)}, u32[]{:S(2)}) async-start(bf16[8,16,3584]{2,1,0:T(8,128)(2,1)} %bitcast.31), calls=%async_computation.5 | async-start | bytes 1835008 | tf_op jit(solution)/shard_map/all_to_all | solution.py:126
  136.7 24.8 %copy-start.8 = (u32[32]{0:T(128)S(1)}, u32[32]{0:T(128)}, u32[]{:S(2)}) copy-start(u32[32]{0:T(128)} %constant.68) | copy-start | bytes 388
  155.2 26.7 %all-to-all-start.1 = ((bf16[8,16,3584]{2,1,0:T(8,128)(2,1)}), bf16[8,16,3584]{2,1,0:T(8,128)(2,1)S(1)}, u32[]{:S(2)}, u32[]{:S(2)}) async-start(bf16[8,16,3584]{2,1,0:T(8,128)(2,1)} %bitcast.23), calls=%async_computation.1 | async-start | bytes 1835008 | tf_op jit(solution)/shard_map/all_to_all | solution.py:126
  158.8 56.2 %all-reduce.6.cloned.1.call-start = ((), (), s32[]{:S(2)}) async-start(), calls=%async_computation.7 | async-start | bytes 688128
  172.0 11.5 %copy-start = (bf16[4,128,576]{2,1,0:T(8,128)(2,1)S(1)}, bf16[4,128,576]{2,1,0:T(8,128)(2,1)}, u32[]{:S(2)}) copy-start(bf16[4,128,576]{2,1,0:T(8,128)(2,1)} %copy.95) | copy-start | bytes 1769476
Sparse Core Ops, SparseCore 0:
  56.0 18.8 all-gather.1
  183.6 31.3 all-reduce.5
where the time goes:
time: 227 us; the launch traced here: 225 us
  waiting for transfers between devices  92.8 us (41%)
  matrix products  50 us (22%)
  starting transfers between devices  24.6 us (11%)
  local copies, waits for them, and re-layouts  19.6 us (9%)
  blocking collectives  17.2 us (8%)
  between operations  14.3 us (6%)
  other arithmetic  6.98 us (3%)
    all_to_all x3, waiting for transfers between devices, body(): lax.all_to_all(packed, 'ep', split_axis=0, concat_axis=0, tiled=True)  33.6 us
    unnamed x3, waiting for transfers between devices  30.4 us
    all_to_all x3, waiting for transfers between devices, body(): lax.all_to_all(partial_out, 'ep', split_axis=0, concat_axis=0, tiled=True)  28.8 us
    all_gather x3, blocking collectives, body(): lax.all_gather(moe_input[step_index][None], 'grp', axis=0, tiled=True)  17.2 us
    dot_general x3, matrix products, expert_rows(): jnp.dot(hidden, down_slice, preferred_element_type=jnp.float32)  16.4 us
    all_to_all x3, starting transfers between devices, body(): lax.all_to_all(packed, 'ep', split_axis=0, concat_axis=0, tiled=True)  13.6 us
    all_to_all x3, starting transfers between devices, body(): lax.all_to_all(partial_out, 'ep', split_axis=0, concat_axis=0, tiled=True)  10.9 us
    dot_general x3, matrix products, expert_rows(): jnp.dot(token_rows, gate_slice, preferred_element_type=jnp.float32)  10.2 us
  transfers between devices with their start and end apart: 8, of which 7 were waited for; matrix products, arithmetic and copies ran while one was open for 29% of the time, Pallas kernels for 0%

commit v1 on v0

v1 whole, which is shorter than its diff:
```python
from functools import partial

import jax
import jax.numpy as jnp
from jax import lax
from jax.experimental import pallas as pl
from jax.experimental.pallas import tpu as pltpu
from jax.sharding import PartitionSpec as P

ROPE = 64


SCORE_SCALE = 192.0 ** (-0.5)


BOTH = ("grp", "ep")


GAIN_LANES = 128


STEP_CHUNKS = ((0, 1), (1, 3))


def across(values, grp_flip, ep_flip):
    groups, columns = lax.axis_size("grp"), lax.axis_size("ep")
    pairs = [
        (g * columns + e, (g ^ grp_flip) * columns + (e ^ ep_flip))
        for g in range(groups)
        for e in range(columns)
    ]
    return lax.ppermute(values, BOTH, pairs)


def attention_kernel(
    lengths_ref, source_ref, queries_ref, cache_ref, entries_ref, *rest
):
    received_refs, (contexts_ref, migrated_ref) = rest[:-2], rest[-2:]
    trace = pl.program_id(0)
    filled = lengths_ref[trace]
    step_count, _, heads, width = queries_ref.shape
    latent = contexts_ref.shape[3]
    capacity = cache_ref.shape[1]
    keys = cache_ref[0].astype(jnp.float32)
    row_index = lax.broadcasted_iota(jnp.int32, keys.shape, 0)
    for step_index in range(step_count):
        entry_rows = entries_ref[step_index].astype(jnp.float32)
        entry_index = lax.broadcasted_iota(jnp.int32, entry_rows.shape, 0)
        entry = jnp.sum(jnp.where(entry_index == trace, entry_rows, 0.0), axis=0, keepdims=True)
        keys = jnp.where(row_index == filled + step_index, entry, keys)
    keys = keys.astype(jnp.bfloat16)
    source = source_ref[trace]

    @pl.when(source == 0)
    def _():
        migrated_ref[0] = keys

    for number, received_ref in enumerate(received_refs):

        @pl.when(source == number + 1)
        def _(received_ref=received_ref):
            migrated_ref[0] = received_ref[...]

    flat_queries = queries_ref[...].reshape(step_count * heads, width)
    scores = (
        lax.dot_general(
            flat_queries, keys, (((1,), (1,)), ((), ())), preferred_element_type=jnp.float32
        )
        * SCORE_SCALE
    )
    step_of_row = lax.broadcasted_iota(jnp.int32, (step_count, heads, capacity), 0).reshape(
        step_count * heads, capacity
    )
    position = lax.broadcasted_iota(jnp.int32, scores.shape, 1)
    scores = jnp.where(position <= filled + step_of_row, scores, -jnp.inf)
    exp_scores = jnp.exp(scores - jnp.max(scores, axis=1, keepdims=True))
    weights = (exp_scores / jnp.sum(exp_scores, axis=1, keepdims=True)).astype(jnp.bfloat16)
    context = jnp.dot(weights, keys[:, :latent], preferred_element_type=jnp.float32)
    contexts_ref[...] = context.astype(jnp.bfloat16).reshape(contexts_ref.shape)


def attention(queries, cache, new_entries, lengths, source, received):
    step_count, traces, heads, width = queries.shape
    capacity = cache.shape[1]
    latent = width - ROPE
    whole = lambda shape: pl.BlockSpec(shape, lambda t, *_: (0,) * len(shape))
    return pl.pallas_call(
        attention_kernel,
        grid_spec=pltpu.PrefetchScalarGridSpec(
            num_scalar_prefetch=2,
            grid=(traces,),
            in_specs=[
                pl.BlockSpec((step_count, 1, heads, width), lambda t, *_: (0, t, 0, 0)),
                pl.BlockSpec((1, capacity, width), lambda t, *_: (t, 0, 0)),
                whole(new_entries.shape),
            ]
            + [whole((capacity, width))] * len(received),
            out_specs=[
                pl.BlockSpec((step_count, 1, heads, latent), lambda t, *_: (0, t, 0, 0)),
                pl.BlockSpec((1, capacity, width), lambda t, *_: (t, 0, 0)),
            ],
        ),
        out_shape=[
            jax.ShapeDtypeStruct((step_count, traces, heads, latent), jnp.bfloat16),
            jax.ShapeDtypeStruct(cache.shape, jnp.bfloat16),
        ],
        cost_estimate=pl.CostEstimate(
            flops=2 * step_count * traces * heads * capacity * (width + latent),
            bytes_accessed=2 * (queries.size * 2 + cache.size * 2),
            transcendentals=step_count * traces * heads * capacity,
        ),
        name="attention",
    )(lengths, source, queries, cache, new_entries, *received)


def migrate(cache, new_entries, lengths, plan):
    traces, capacity, _ = cache.shape
    groups = lax.axis_size("grp")
    group_index = lax.axis_index("grp")
    column_plan = plan[:, 0]
    own_plan = lax.dynamic_index_in_dim(column_plan, group_index, 0, keepdims=False)
    slot_list = jnp.arange(traces, dtype=jnp.int32)
    positions = jnp.arange(capacity, dtype=jnp.int32)
    source = jnp.zeros((traces,), jnp.int32)
    received = []
    for flip in range(1, groups):
        partner = group_index ^ flip
        slot = jnp.sum(jnp.where(own_plan[:, 1] == partner, own_plan[:, 0], 0))
        rows = lax.dynamic_index_in_dim(cache, slot, 0, keepdims=False)
        filled = lax.dynamic_index_in_dim(lengths, slot, 0, keepdims=False)
        entries = lax.dynamic_index_in_dim(new_entries, slot, 1, keepdims=False)
        for step_index in range(new_entries.shape[0]):
            rows = jnp.where(
                (positions == filled + step_index)[:, None], entries[step_index][None, :], rows
            )
        received.append(across(rows, flip, 0))
        partner_plan = lax.dynamic_index_in_dim(column_plan, partner, 0, keepdims=False)
        lands = (partner_plan[:, 1] == group_index)[None, :] & (
            own_plan[:, 0][None, :] == slot_list[:, None]
        )
        source = jnp.where(jnp.any(lands, axis=1), flip, source)
    return received, source


def expert_kernel(tile, column_ref, *refs):
    pieces = refs[:-12]
    gate_hbm, up_hbm, down_hbm, own_ref, other_ref = refs[-12:-7]
    gate_ref, up_ref, down_ref, gate_sum, up_sum, hidden_ref, semaphores = refs[-7:]
    width, hidden_width = gate_ref.shape
    tiles = width // tile
    piece_rows = pieces[0].shape[0]
    half = own_ref.shape[0]
    copies = []
    for index in range(tiles):
        rows = pl.ds(index * tile, tile)
        copies.append(
            (
                pltpu.make_async_copy(gate_hbm.at[0, rows], gate_ref.at[rows], semaphores.at[0, index]),
                pltpu.make_async_copy(up_hbm.at[0, rows], up_ref.at[rows], semaphores.at[1, index]),
            )
        )
    down_copies = []
    for index in range(tiles):
        columns = pl.ds(index * tile, tile)
        down_copies.append(
            pltpu.make_async_copy(
                down_hbm.at[0, :, columns], down_ref.at[:, columns], semaphores.at[2, index]
            )
        )
    for pair in copies:
        for copy in pair:
            copy.start()
    for copy in down_copies:
        copy.start()
    gain_parts = jnp.concatenate([piece[:, width:] for piece in pieces], axis=0).astype(jnp.float32)
    lane = lax.broadcasted_iota(jnp.int32, gain_parts.shape, 1)
    first_lane = column_ref[0] * 3
    gain = jnp.sum(
        jnp.where((lane >= first_lane) & (lane < first_lane + 3), gain_parts, 0.0),
        axis=1,
        keepdims=True,
    )
    for index in range(tiles):
        rows = slice(index * tile, (index + 1) * tile)
        tokens = jnp.concatenate([piece[:, rows] for piece in pieces], axis=0)
        for copy, weight_ref, sum_ref in zip(copies[index], (gate_ref, up_ref), (gate_sum, up_sum)):
            copy.wait()
            product = jnp.dot(tokens, weight_ref[rows, :], preferred_element_type=jnp.float32)
            if index == 0:
                sum_ref[...] = product
            else:
                sum_ref[...] += product
    gate_out = gate_sum[...]
    hidden = gate_out / (1.0 + jnp.exp(-gate_out)) * up_sum[...] * gain
    hidden_ref[...] = hidden.astype(jnp.bfloat16)
    for index in range(tiles):
        columns = slice(index * tile, (index + 1) * tile)
        down_copies[index].wait()
        for number, out_ref in enumerate((own_ref, other_ref)):
            out_ref[:, columns] = jnp.dot(
                hidden_ref[number * half : (number + 1) * half, :],
                down_ref[:, columns],
                preferred_element_type=jnp.float32,
            ).astype(jnp.bfloat16)


def expert(pieces, w_gate, w_up, w_down):
    _, width, hidden_width = w_gate.shape
    token_count = sum(piece.shape[0] for piece in pieces)
    tile = width // 4 if width % 512 == 0 else width
    vmem = pl.BlockSpec(memory_space=pltpu.VMEM)
    half = jax.ShapeDtypeStruct((token_count // 2, width), jnp.bfloat16)
    column = lax.axis_index("ep").astype(jnp.int32).reshape(1)
    return pl.pallas_call(
        partial(expert_kernel, tile),
        in_specs=[pl.BlockSpec(memory_space=pltpu.SMEM)]
        + [vmem] * len(pieces)
        + [pl.BlockSpec(memory_space=pl.ANY)] * 3,
        out_specs=[vmem, vmem],
        out_shape=[half, half],
        scratch_shapes=[
            pltpu.VMEM((width, hidden_width), jnp.bfloat16),
            pltpu.VMEM((width, hidden_width), jnp.bfloat16),
            pltpu.VMEM((hidden_width, width), jnp.bfloat16),
            pltpu.VMEM((token_count, hidden_width), jnp.float32),
            pltpu.VMEM((token_count, hidden_width), jnp.float32),
            pltpu.VMEM((token_count, hidden_width), jnp.bfloat16),
            pltpu.SemaphoreType.DMA((3, width // tile)),
        ],
        compiler_params=pltpu.CompilerParams(vmem_limit_bytes=40 * 1024 * 1024),
        cost_estimate=pl.CostEstimate(
            flops=6 * token_count * width * hidden_width,
            bytes_accessed=6 * width * hidden_width + 4 * token_count * width,
            transcendentals=token_count * hidden_width,
        ),
        name="expert",
    )(column, *pieces, w_gate, w_up, w_down)


def add_up(terms):
    total = terms[0].astype(jnp.float32)
    for term in terms[1:]:
        total = total + term.astype(jnp.float32)
    return total.astype(jnp.bfloat16)


def token_rows(moe_input, expert_ids, route_gains, experts):
    group_index = lax.axis_index("grp")
    own_ids = lax.dynamic_index_in_dim(expert_ids, group_index, 1, keepdims=False)
    own_gains = lax.dynamic_index_in_dim(route_gains, group_index, 1, keepdims=False)
    chosen = own_ids[..., None] == jnp.arange(experts, dtype=jnp.int32)
    gains = jnp.sum(jnp.where(chosen, own_gains[..., None], 0.0), axis=2)
    high = gains.astype(jnp.bfloat16)
    rest = gains - high.astype(jnp.float32)
    middle = rest.astype(jnp.bfloat16)
    low = (rest - middle.astype(jnp.float32)).astype(jnp.bfloat16)
    parts = jnp.stack([high, middle, low], axis=-1).reshape(gains.shape[:2] + (3 * experts,))
    parts = jnp.pad(parts, ((0, 0), (0, 0), (0, GAIN_LANES - 3 * experts)))
    return jnp.concatenate([moe_input, parts], axis=2)


def dense_experts(moe_input, expert_ids, route_gains, w_gate, w_up, w_down):
    groups, experts = lax.axis_size("grp"), lax.axis_size("ep")
    far_flips = [(0, 2 * z) for z in range(1, experts // 2)]
    far_flips = far_flips[::-1]
    near_flips = [(2 * x, y) for x in range(groups // 2) for y in range(2)][1:]
    near_flips = near_flips[::-1]
    tokens = token_rows(moe_input, expert_ids, route_gains, experts)
    trace_count, width = moe_input.shape[1:]
    out_chunks = []
    for first, last in STEP_CHUNKS:
        rows = tokens[first:last].reshape((last - first) * trace_count, -1)
        line = jnp.concatenate([rows] + [across(rows, *flip) for flip in far_flips], axis=0)
        plane = [line] + [across(line, *flip) for flip in near_flips]
        pieces = plane + [across(piece, 1, 0) for piece in plane]
        own, other = expert(pieces, w_gate, w_up, w_down)
        other = across(other, 1, 0)
        count = line.shape[0]
        sums = [
            add_up([half[i * count : (i + 1) * count] for half in (own, other)])
            for i in range(len(plane))
        ]
        sums = add_up(
            [sums[0]] + [across(part, *flip) for part, flip in zip(sums[1:], near_flips)]
        )
        count = rows.shape[0]
        parts = [sums[i * count : (i + 1) * count] for i in range(len(far_flips) + 1)]
        total = add_up(
            [parts[0]] + [across(part, *flip) for part, flip in zip(parts[1:], far_flips)]
        )
        out_chunks.append(total.reshape(last - first, trace_count, width))
    return jnp.concatenate(out_chunks, axis=0)


def slot_tables(route_ids, route_gains, expert_count, slot_count):
    token_count, top_count = route_ids.shape
    flat_ids = route_ids.reshape(-1)
    row_list = jnp.arange(flat_ids.shape[0], dtype=jnp.int32)
    same_expert = flat_ids[:, None] == flat_ids[None, :]
    earlier = row_list[None, :] < row_list[:, None]
    slot_rank = jnp.sum(jnp.where(same_expert & earlier, 1, 0), axis=1).astype(jnp.int32)
    slot_index = flat_ids * slot_count + slot_rank
    slot_hot = (
        slot_index[:, None] == jnp.arange(expert_count * slot_count, dtype=jnp.int32)[None, :]
    ).astype(jnp.float32)
    token_hot = (
        (row_list // top_count)[:, None] == jnp.arange(token_count, dtype=jnp.int32)[None, :]
    ).astype(jnp.float32)
    dispatch = jnp.dot(slot_hot.T, token_hot, precision=lax.Precision.HIGHEST)
    combine = jnp.dot(
        token_hot.T, slot_hot * route_gains.reshape(-1)[:, None], precision=lax.Precision.HIGHEST
    )
    return (dispatch, combine)


def expert_rows(token_rows, gate_slice, up_slice, down_slice):
    gate_out = jnp.dot(token_rows, gate_slice, preferred_element_type=jnp.float32)
    up_out = jnp.dot(token_rows, up_slice, preferred_element_type=jnp.float32)
    hidden = (jax.nn.silu(gate_out) * up_out).astype(jnp.bfloat16)
    return jnp.dot(hidden, down_slice, preferred_element_type=jnp.float32).astype(jnp.bfloat16)


def routed_experts(moe_input, expert_ids, route_gains, w_gate, w_up, w_down):
    groups, experts = lax.axis_size("grp"), lax.axis_size("ep")
    trace_count, model_width = moe_input.shape[1:]
    top_count = expert_ids.shape[3]
    slot_count = max(2, trace_count * top_count // experts)
    tables = partial(slot_tables, expert_count=experts, slot_count=slot_count)
    moe_list = []
    for step_index in range(moe_input.shape[0]):
        column_ids = expert_ids[step_index]
        column_gains = route_gains[step_index]
        dispatch_all, combine_all = jax.vmap(tables)(column_ids, column_gains)
        column_tokens = lax.all_gather(moe_input[step_index][None], "grp", axis=0, tiled=True)
        packed = jnp.einsum(
            "gsj,gjd->sgd",
            dispatch_all.astype(jnp.bfloat16),
            column_tokens,
            preferred_element_type=jnp.float32,
        )
        packed = packed.astype(jnp.bfloat16).reshape(experts, slot_count * groups, model_width)
        exchanged = lax.all_to_all(packed, "ep", split_axis=0, concat_axis=0, tiled=True)
        flat_rows = exchanged.reshape(-1, exchanged.shape[-1])
        partial_out = expert_rows(flat_rows, w_gate[0], w_up[0], w_down[0]).reshape(exchanged.shape)
        returned = lax.all_to_all(partial_out, "ep", split_axis=0, concat_axis=0, tiled=True)
        returned = returned.reshape(experts * slot_count, groups, model_width).astype(jnp.float32)
        token_terms = jnp.einsum(
            "gjs,sgd->gjd", combine_all, returned, precision=lax.Precision.HIGHEST
        )
        summed = lax.psum_scatter(
            token_terms.astype(jnp.bfloat16), "grp", scatter_dimension=0, tiled=True
        ).astype(jnp.float32)
        moe_list.append(summed[0].astype(jnp.bfloat16))
    return jnp.stack(moe_list)


def body(
    queries,
    cache,
    new_entries,
    lengths,
    moe_input,
    expert_ids,
    route_gains,
    w_gate,
    w_up,
    w_down,
    plan,
):
    received, source = migrate(cache, new_entries, lengths, plan)
    contexts, migrated_cache = attention(queries, cache, new_entries, lengths, source, received)
    every_expert = expert_ids.shape[3] == lax.axis_size("ep")
    experts_of = dense_experts if every_expert else routed_experts
    moe_output = experts_of(moe_input, expert_ids, route_gains, w_gate, w_up, w_down)
    return (contexts, migrated_cache, moe_output)


def solution(mesh):
    return jax.shard_map(
        body,
        mesh=mesh,
        in_specs=(
            P(None, ("grp", "ep"), None, None),
            P(("grp", "ep"), None, None),
            P(None, ("grp", "ep"), None),
            P(("grp", "ep")),
            P(None, ("grp", "ep"), None),
            P(None, None, "ep", None),
            P(None, None, "ep", None),
            P("ep", None, "grp"),
            P("ep", None, "grp"),
            P("ep", "grp", None),
            P(None, "ep", None, None),
        ),
        out_specs=(
            P(None, ("grp", "ep"), None, None),
            P(("grp", "ep"), None, None),
            P(None, ("grp", "ep"), None),
        ),
        check_vma=False,
    )
```

time: 227 us -> 128 us (0.56)
  waiting for transfers between devices: 92.8 us -> 24 us
  matrix products: 50 us -> 0 us
  Pallas kernels: 0 us -> 19.9 us
  blocking collectives: 17.2 us -> 0 us
  starting transfers between devices: 24.6 us -> 35.5 us
  local copies, waits for them, and re-layouts: 19.6 us -> 25 us
  other arithmetic: 6.98 us -> 11.8 us
  between operations: 14.3 us -> 10.8 us
    all_to_all x6 -> x0, waiting for transfers between devices: 62.4 us -> none  [the longest x3 33.6 us: body(): lax.all_to_all(packed, 'ep', split_axis=0, concat_axis=0, tiled=True)]
    dot_general x26 -> x0, matrix products: 50 us -> none  [the longest x3 16.4 us: expert_rows(): jnp.dot(hidden, down_slice, preferred_element_type=jnp.float32)]
    ppermute x0 -> x37, starting transfers between devices: none -> 35.5 us  [across(): return lax.ppermute(values, BOTH, pairs)]
    unnamed x3 -> x0, waiting for transfers between devices: 30.4 us -> none
    all_to_all x6 -> x0, starting transfers between devices: 24.5 us -> none  [the longest x3 13.6 us: body(): lax.all_to_all(packed, 'ep', split_axis=0, concat_axis=0, tiled=True)]
    ppermute x0 -> x37, waiting for transfers between devices: none -> 24 us  [across(): return lax.ppermute(values, BOTH, pairs)]
    pallas_call x0 -> x3, Pallas kernels: none -> 19.9 us  [the longest x2 12.6 us: expert(): pl.pallas_call(partial(expert_kernel, tile), in_specs=[pl.BlockSpec(memor...]
    all_gather x3 -> x0, blocking collectives: 17.2 us -> none  [body(): lax.all_gather(moe_input[step_index][None], 'grp', axis=0, tiled=True)]
  transfers between devices with their start and end apart: 8 -> 37, of which waited for: 7 -> 11; matrix products, arithmetic and copies ran while one was open for 29% -> 17% of each run, Pallas kernels for 0% -> 16%
where the time goes in v1:
time: 128 us; the launch traced here: 127 us
  starting transfers between devices  35.5 us (28%)
  local copies, waits for them, and re-layouts  25 us (20%)
  waiting for transfers between devices  24 us (19%)
  Pallas kernels  19.9 us (16%)
  other arithmetic  11.8 us (9%)
  between operations  10.8 us (8%)
    ppermute x37, starting transfers between devices, across(): return lax.ppermute(values, BOTH, pairs)  35.5 us
    ppermute x37, waiting for transfers between devices, across(): return lax.ppermute(values, BOTH, pairs)  24 us
    unnamed x26, local copies, waits for them, and re-layouts  18.7 us
    pallas_call x2, Pallas kernels, expert(): pl.pallas_call(partial(expert_kernel, tile), in_specs=[pl.BlockSpec(memor...  12.6 us
    pallas_call x1, Pallas kernels, attention(): pl.pallas_call(attention_kernel, grid_spec=pltpu.PrefetchScalarGridSpec(n...  7.3 us
    convert_element_type x5, other arithmetic, add_up(): return total.astype(jnp.bfloat16)  4.4 us
  transfers between devices with their start and end apart: 37, of which 11 were waited for; matrix products, arithmetic and copies ran while one was open for 17% of the time, Pallas kernels for 16%

profile of v1, /device:TPU:0, one launch (start us, length us, event | category | flops | bytes accessed | tf_op | source)
XLA Modules:
  0.0 126.9 jit_solution(515120791093060282)
XLA Ops:
  0.7 0.7 copy-done
  2.5 0.9 fusion.7
  3.4 3.1 %collective-permute-start.5 = (bf16[4,3712]{1,0:T(4,128)(2,1)S(1)}, bf16[4,3712]{1,0:T(4,128)(2,1)S(1)}, u32[]{:S(2)}, u32[]{:S(2)}) collective-permute-start(bf16[4,3712]{1,0:T(4,128)(2,1)S(1)} %slice_bitcast_fusion), channel_id=1, source_target_pairs={{0,2},{1,3},{2,0},{3,1},{4,6},{5,7},{6,4},{7,5},{8,10},{9,11},{10,... | collective-permute-start | bytes 89096 | tf_op jit(solution)/shard_map/ppermute | solution.py:32
  6.5 2.6 %collective-permute-start.4 = (bf16[4,3712]{1,0:T(4,128)(2,1)S(1)}, bf16[4,3712]{1,0:T(4,128)(2,1)S(1)}, u32[]{:S(2)}, u32[]{:S(2)}) collective-permute-start(bf16[4,3712]{1,0:T(4,128)(2,1)S(1)} %slice_bitcast_fusion), channel_id=1, source_target_pairs={{0,4},{1,5},{2,6},{3,7},{4,0},{5,1},{6,2},{7,3},{8,12},{9,13},{10,... | collective-permute-start | bytes 89096 | tf_op jit(solution)/shard_map/ppermute | solution.py:32
  9.2 1.0 collective-permute-start.22
  10.1 3.5 %collective-permute-start.21 = (bf16[8,3712]{1,0:T(8,128)(2,1)S(1)}, bf16[8,3712]{1,0:T(8,128)(2,1)S(1)}, u32[]{:S(2)}, u32[]{:S(2)}) collective-permute-start(bf16[8,3712]{1,0:T(8,128)(2,1)S(1)} %reshape.156), channel_id=1, source_target_pairs={{0,4},{1,5},{2,6},{3,7},{4,0},{5,1},{6,2},{7,3},{8,12},{9,13},{10,... | collective-permute-start | bytes 178184 | tf_op jit(solution)/shard_map/ppermute | solution.py:32
  13.6 1.1 fusion.22
  21.6 1.4 %fusion.31 = (s32[1]{0:T(128)}, s32[1]{0:T(128)}, s32[1]{0:T(128)}) fusion(s32[4]{0:T(128)} %lengths_ref.1, s32[]{:T(128)S(6)} %select_n.105, s32[]{:T(128)S(6)} %select_n.100, s32[]{:T(128)S(6)} %select_n.95), kind=kLoop, calls=%fused_computation.99 | loop fusion | bytes 36 | tf_op jit(solution)/shard_map/jit(dynamic_index_in_dim)/dynamic_slice | solution.py:130
  28.4 1.1 constant_dynamic-slice_fusion.6
  30.7 0.9 fusion.17
  31.7 0.8 fusion.2
  32.5 0.8 fusion.6
  34.1 1.8 %collective-permute-start.8 = (bf16[16,3712]{1,0:T(8,128)(2,1)S(1)}, bf16[16,3712]{1,0:T(8,128)(2,1)S(1)}, u32[]{:S(2)}, u32[]{:S(2)}) collective-permute-start(bf16[16,3712]{1,0:T(8,128)(2,1)S(1)} %pad_maximum_fusion.refs_0_), channel_id=1, source_target_pairs={{0,1},{1,0},{2,3},{3,2},{4,5},{5,4},{6,7},{7,6},{8,9},{9,8},{10,11... | collective-permute-start | bytes 356360 | tf_op jit(solution)/shard_map/ppermute | solution.py:32
  35.9 1.5 %collective-permute-start.7 = (bf16[16,3712]{1,0:T(8,128)(2,1)S(1)}, bf16[16,3712]{1,0:T(8,128)(2,1)S(1)}, u32[]{:S(2)}, u32[]{:S(2)}) collective-permute-start(bf16[16,3712]{1,0:T(8,128)(2,1)S(1)} %pad_maximum_fusion.refs_0_), channel_id=1, source_target_pairs={{0,16},{1,17},{2,18},{3,19},{4,20},{5,21},{6,22},{7,23},{8,24},{9,... | collective-permute-start | bytes 356360 | tf_op jit(solution)/shard_map/ppermute | solution.py:32
  37.4 2.6 %collective-permute-done.20 = bf16[8,3712]{1,0:T(8,128)(2,1)S(1)} collective-permute-done((bf16[8,3712]{1,0:T(8,128)(2,1)S(1)}, bf16[8,3712]{1,0:T(8,128)(2,1)S(1)}, u32[]{:S(2)}, u32[]{:S(2)}) %collective-permute-start.20) | collective-permute-done | bytes 59424 | tf_op jit(solution)/shard_map/ppermute | solution.py:32
  40.0 2.4 %collective-permute-start.6 = (bf16[16,3712]{1,0:T(8,128)(2,1)S(1)}, bf16[16,3712]{1,0:T(8,128)(2,1)S(1)}, u32[]{:S(2)}, u32[]{:S(2)}) collective-permute-start(bf16[16,3712]{1,0:T(8,128)(2,1)S(1)} %pad_maximum_fusion.refs_0_), channel_id=1, source_target_pairs={{0,17},{1,16},{2,19},{3,18},{4,21},{5,20},{6,23},{7,22},{8,25},{9,... | collective-permute-start | bytes 356360 | tf_op jit(solution)/shard_map/ppermute | solution.py:32
  43.2 2.6 %collective-permute-done.6.refs_1_ = bf16[16,3712]{1,0:T(8,128)(2,1)S(1)} collective-permute-done((bf16[16,3712]{1,0:T(8,128)(2,1)S(1)}, bf16[16,3712]{1,0:T(8,128)(2,1)S(1)}, u32[]{:S(2)}, u32[]{:S(2)}) %collective-permute-start.6) | collective-permute-done | bytes 118816 | tf_op jit(solution)/shard_map/ppermute | solution.py:32
  46.4 0.7 collective-permute-done.10.refs_5_
  47.1 2.0 %copy-done.1 = bf16[1,3584,512]{2,1,0:T(8,128)(2,1)S(1)} copy-done((bf16[1,3584,512]{2,1,0:T(8,128)(2,1)S(1)}, bf16[1,3584,512]{2,1,0:T(8,128)(2,1)}, u32[]{:S(2)}) %copy-start.1) | copy-done | bytes 3670040
  49.1 2.0 %copy-done.3 = bf16[1,3584,512]{2,1,0:T(8,128)(2,1)S(1)} copy-done((bf16[1,3584,512]{2,1,0:T(8,128)(2,1)S(1)}, bf16[1,3584,512]{2,1,0:T(8,128)(2,1)}, u32[]{:S(2)}) %copy-start.3) | copy-done | bytes 3670040
  51.2 2.0 %copy-done.5 = bf16[1,512,3584]{2,1,0:T(8,128)(2,1)S(1)} copy-done((bf16[1,512,3584]{2,1,0:T(8,128)(2,1)S(1)}, bf16[1,512,3584]{2,1,0:T(8,128)(2,1)}, u32[]{:S(2)}) %copy-start.5) | copy-done | bytes 3670040
  53.2 5.9 %expert.2 = (bf16[64,3584]{1,0:T(8,128)(2,1)S(1)}, bf16[64,3584]{1,0:T(8,128)(2,1)S(1)}) custom-call(s32[1]{0:T(128)} %bitcast.6.column_ref, bf16[16,3712]{1,0:T(8,128)(2,1)S(1)} %pad_maximum_fusion.refs_0_, bf16[16,3712]{1,0:T(8,128)(2,1)S(1)} %collective-permute-done.6.refs_1_, bf16[16,3712]{1,0:T(8,128)(2,1)S(1)} %collective-permute-done.7.refs_2_, ...), custom_call_target="tpu_custom_call" | custom-call | flops 1409286144 | bytes 12845056 | tf_op jit(solution)/shard_map/expert/pallas_call | solution.py:214
  59.3 1.6 %collective-permute-start.25 = (bf16[32,3712]{1,0:T(8,128)(2,1)S(1)}, bf16[32,3712]{1,0:T(8,128)(2,1)S(1)}, u32[]{:S(2)}, u32[]{:S(2)}) collective-permute-start(bf16[32,3712]{1,0:T(8,128)(2,1)S(1)} %constant_dynamic-update-slice_fusion.refs_0_), channel_id=1, source_target_pairs={{0,1},{1,0},{2,3},{3,2},{4,5},{5,4},{6,7},{7,6},{8,9},{9,8},{10,11... | collective-permute-start | bytes 712712 | tf_op jit(solution)/shard_map/ppermute | solution.py:32
  60.9 1.5 %collective-permute-start.24 = (bf16[32,3712]{1,0:T(8,128)(2,1)S(1)}, bf16[32,3712]{1,0:T(8,128)(2,1)S(1)}, u32[]{:S(2)}, u32[]{:S(2)}) collective-permute-start(bf16[32,3712]{1,0:T(8,128)(2,1)S(1)} %constant_dynamic-update-slice_fusion.refs_0_), channel_id=1, source_target_pairs={{0,16},{1,17},{2,18},{3,19},{4,20},{5,21},{6,22},{7,23},{8,24},{9,... | collective-permute-start | bytes 712712 | tf_op jit(solution)/shard_map/ppermute | solution.py:32
  62.9 1.1 copy.32.cache_ref
  64.2 3.9 %copy.31.queries_ref = bf16[3,4,128,576]{3,2,1,0:T(8,128)(2,1)} copy(bf16[3,4,128,576]{2,3,1,0:T(8,128)(2,1)} %param.11) | data formatting | bytes 3538944 | tf_op args[0]
  68.3 1.3 collective-permute-done.24.refs_2_
  69.5 4.2 %collective-permute-done.23.refs_1_ = bf16[32,3712]{1,0:T(8,128)(2,1)S(1)} collective-permute-done((bf16[32,3712]{1,0:T(8,128)(2,1)S(1)}, bf16[32,3712]{1,0:T(8,128)(2,1)S(1)}, u32[]{:S(2)}, u32[]{:S(2)}) %collective-permute-start.23) | collective-permute-done | bytes 237600 | tf_op jit(solution)/shard_map/ppermute | solution.py:32
  74.2 0.8 add_convert_fusion.8
  75.0 1.5 %collective-permute-start.1 = (bf16[128,576]{1,0:T(8,128)(2,1)S(1)}, bf16[128,576]{1,0:T(8,128)(2,1)S(1)}, u32[]{:S(2)}, u32[]{:S(2)}) collective-permute-start(bf16[128,576]{1,0:T(8,128)(2,1)S(1)} %fusion.4), channel_id=1, source_target_pairs={{0,16},{1,17},{2,18},{3,19},{4,20},{5,21},{6,22},{7,23},{8,24},{9,... | collective-permute-start | bytes 442376 | tf_op jit(solution)/shard_map/ppermute | solution.py:32
  76.5 2.4 %collective-permute-start.14 = (bf16[16,3584]{1,0:T(8,128)(2,1)}, bf16[16,3584]{1,0:T(8,128)(2,1)}, u32[]{:S(2)}, u32[]{:S(2)}) collective-permute-start(bf16[16,3584]{1,0:T(8,128)(2,1)} %get-tuple-element.49), channel_id=1, source_target_pairs={{0,17},{1,16},{2,19},{3,18},{4,21},{5,20},{6,23},{7,22},{8,25},{9,... | collective-permute-start | bytes 344072 | tf_op jit(solution)/shard_map/ppermute | solution.py:32
  80.1 2.0 %copy-done.2 = bf16[1,3584,512]{2,1,0:T(8,128)(2,1)S(1)} copy-done((bf16[1,3584,512]{2,1,0:T(8,128)(2,1)S(1)}, bf16[1,3584,512]{2,1,0:T(8,128)(2,1)}, u32[]{:S(2)}) %copy-start.2) | copy-done | bytes 3670040
  82.1 2.0 %copy-done.4 = bf16[1,3584,512]{2,1,0:T(8,128)(2,1)S(1)} copy-done((bf16[1,3584,512]{2,1,0:T(8,128)(2,1)S(1)}, bf16[1,3584,512]{2,1,0:T(8,128)(2,1)}, u32[]{:S(2)}) %copy-start.4) | copy-done | bytes 3670040
  84.2 6.7 %expert.3 = (bf16[128,3584]{1,0:T(8,128)(2,1)S(1)}, bf16[128,3584]{1,0:T(8,128)(2,1)S(1)}) custom-call(s32[1]{0:T(128)} %bitcast.6.column_ref, bf16[32,3712]{1,0:T(8,128)(2,1)S(1)} %constant_dynamic-update-slice_fusion.refs_0_, bf16[32,3712]{1,0:T(8,128)(2,1)S(1)} %collective-permute-done.23.refs_1_, bf16[32,3712]{1,0:T(8,128)(2,1)S(1)} %collective-permute-done.24.refs_2_, ...), custom_call_target="tpu_custom_call" | custom-call | flops 2818572288 | bytes 14680064 | tf_op jit(solution)/shard_map/expert/pallas_call | solution.py:214
  91.6 7.3 %attention.1 = (bf16[3,4,128,512]{3,2,1,0:T(8,128)(2,1)}, bf16[4,128,576]{2,1,0:T(8,128)(2,1)}) custom-call(s32[4]{0:T(128)} %lengths_ref.1, s32[4]{0:T(128)} %select_select_fusion.source_ref, bf16[3,4,128,576]{3,2,1,0:T(8,128)(2,1)} %copy.31.queries_ref, bf16[4,128,576]{2,1,0:T(8,128)(2,1)} %copy.32.cache_ref, bf16[3,4,576]{2,1,0:T(4,128)(2,1)} %entries_ref.1, ...), custom_call_target="tpu_custom_call" | custom-call | flops 427819008 | bytes 4718592 | tf_op jit(solution)/shard_map/attention/pallas_call | solution.py:87
  98.9 2.1 %copy.34 = bf16[4,128,576]{1,2,0:T(8,128)(2,1)} copy(bf16[4,128,576]{2,1,0:T(8,128)(2,1)} %get-tuple-element.22) | data formatting | bytes 1179648
  101.0 1.1 add_convert_fusion.5
  102.2 1.3 %add_convert_fusion.3 = (bf16[32,3584]{1,0:T(8,128)(2,1)S(1)}, bf16[32,3584]{1,0:T(8,128)(2,1)S(1)}, bf16[32,3584]{1,0:T(8,128)(2,1)S(1)}) fusion(bf16[128,3584]{1,0:T(8,128)(2,1)} %collective-permute-done.30, bf16[128,3584]{1,0:T(8,128)(2,1)S(1)} %get-tuple-element.13), kind=kLoop, calls=%fused_computation.3 | loop fusion | flops 1376256 | bytes 2064384 | tf_op jit(solution)/shard_map/convert_element_type | solution.py:244
  103.5 2.4 %collective-permute-start.31 = (bf16[32,3584]{1,0:T(8,128)(2,1)S(1)}, bf16[32,3584]{1,0:T(8,128)(2,1)S(1)}, u32[]{:S(2)}, u32[]{:S(2)}) collective-permute-start(bf16[32,3584]{1,0:T(8,128)(2,1)S(1)} %get-tuple-element.46), channel_id=1, source_target_pairs={{0,17},{1,16},{2,19},{3,18},{4,21},{5,20},{6,23},{7,22},{8,25},{9,... | collective-permute-start | bytes 688136 | tf_op jit(solution)/shard_map/ppermute | solution.py:32
  107.1 0.9 collective-permute-start.17
  108.0 5.0 %collective-permute-done.31 = bf16[32,3584]{1,0:T(8,128)(2,1)S(1)} collective-permute-done((bf16[32,3584]{1,0:T(8,128)(2,1)S(1)}, bf16[32,3584]{1,0:T(8,128)(2,1)S(1)}, u32[]{:S(2)}, u32[]{:S(2)}) %collective-permute-start.31) | collective-permute-done | bytes 229408 | tf_op jit(solution)/shard_map/ppermute | solution.py:32
  113.0 3.8 %collective-permute-done.33 = bf16[32,3584]{1,0:T(8,128)(2,1)S(1)} collective-permute-done((bf16[32,3584]{1,0:T(8,128)(2,1)S(1)}, bf16[32,3584]{1,0:T(8,128)(2,1)S(1)}, u32[]{:S(2)}, u32[]{:S(2)}) %collective-permute-start.33) | collective-permute-done | bytes 229408 | tf_op jit(solution)/shard_map/ppermute | solution.py:32
  116.9 1.1 add_convert_fusion
  118.1 0.8 collective-permute-start.34
  118.9 3.6 %collective-permute-start.35 = (bf16[8,3584]{1,0:T(8,128)(2,1)S(1)}, bf16[8,3584]{1,0:T(8,128)(2,1)S(1)}, u32[]{:S(2)}, u32[]{:S(2)}) collective-permute-start(bf16[8,3584]{1,0:T(8,128)(2,1)S(1)} %get-tuple-element.57), channel_id=1, source_target_pairs={{0,4},{1,5},{2,6},{3,7},{4,0},{5,1},{6,2},{7,3},{8,12},{9,13},{10,... | collective-permute-start | bytes 172040 | tf_op jit(solution)/shard_map/ppermute | solution.py:32
  122.6 2.2 %collective-permute-done.34 = bf16[8,3584]{1,0:T(8,128)(2,1)S(1)} collective-permute-done((bf16[8,3584]{1,0:T(8,128)(2,1)S(1)}, bf16[8,3584]{1,0:T(8,128)(2,1)S(1)}, u32[]{:S(2)}, u32[]{:S(2)}) %collective-permute-start.34) | collective-permute-done | bytes 57376 | tf_op jit(solution)/shard_map/ppermute | solution.py:32
  125.0 1.2 collective-permute-done.35
  126.2 0.7 pad_maximum_fusion.1
  (104 shorter events, 12.0 us)
Async XLA Ops:
  0.6 0.7 copy-start
  3.4 30.5 %collective-permute-start.5 = (bf16[4,3712]{1,0:T(4,128)(2,1)S(1)}, bf16[4,3712]{1,0:T(4,128)(2,1)S(1)}, u32[]{:S(2)}, u32[]{:S(2)}) collective-permute-start(bf16[4,3712]{1,0:T(4,128)(2,1)S(1)} %slice_bitcast_fusion), channel_id=1, source_target_pairs={{0,2},{1,3},{2,0},{3,1},{4,6},{5,7},{6,4},{7,5},{8,10},{9,11},{10,... | collective-permute-start | bytes 89096 | tf_op jit(solution)/shard_map/ppermute | solution.py:32
  6.5 27.5 %collective-permute-start.4 = (bf16[4,3712]{1,0:T(4,128)(2,1)S(1)}, bf16[4,3712]{1,0:T(4,128)(2,1)S(1)}, u32[]{:S(2)}, u32[]{:S(2)}) collective-permute-start(bf16[4,3712]{1,0:T(4,128)(2,1)S(1)} %slice_bitcast_fusion), channel_id=1, source_target_pairs={{0,4},{1,5},{2,6},{3,7},{4,0},{5,1},{6,2},{7,3},{8,12},{9,13},{10,... | collective-permute-start | bytes 89096 | tf_op jit(solution)/shard_map/ppermute | solution.py:32
  9.1 24.9 %collective-permute-start.3 = (bf16[4,3712]{1,0:T(4,128)(2,1)S(1)}, bf16[4,3712]{1,0:T(4,128)(2,1)S(1)}, u32[]{:S(2)}, u32[]{:S(2)}) collective-permute-start(bf16[4,3712]{1,0:T(4,128)(2,1)S(1)} %slice_bitcast_fusion), channel_id=1, source_target_pairs={{0,6},{1,7},{2,4},{3,5},{4,2},{5,3},{6,0},{7,1},{8,14},{9,15},{10,... | collective-permute-start | bytes 89096 | tf_op jit(solution)/shard_map/ppermute | solution.py:32
  9.2 50.1 %collective-permute-start.22 = (bf16[8,3712]{1,0:T(8,128)(2,1)S(1)}, bf16[8,3712]{1,0:T(8,128)(2,1)S(1)}, u32[]{:S(2)}, u32[]{:S(2)}) collective-permute-start(bf16[8,3712]{1,0:T(8,128)(2,1)S(1)} %reshape.156), channel_id=1, source_target_pairs={{0,2},{1,3},{2,0},{3,1},{4,6},{5,7},{6,4},{7,5},{8,10},{9,11},{10,... | collective-permute-start | bytes 178184 | tf_op jit(solution)/shard_map/ppermute | solution.py:32
  10.1 32.3 %collective-permute-start.21 = (bf16[8,3712]{1,0:T(8,128)(2,1)S(1)}, bf16[8,3712]{1,0:T(8,128)(2,1)S(1)}, u32[]{:S(2)}, u32[]{:S(2)}) collective-permute-start(bf16[8,3712]{1,0:T(8,128)(2,1)S(1)} %reshape.156), channel_id=1, source_target_pairs={{0,4},{1,5},{2,6},{3,7},{4,0},{5,1},{6,2},{7,3},{8,12},{9,13},{10,... | collective-permute-start | bytes 178184 | tf_op jit(solution)/shard_map/ppermute | solution.py:32
  34.0 6.1 %collective-permute-start.20 = (bf16[8,3712]{1,0:T(8,128)(2,1)S(1)}, bf16[8,3712]{1,0:T(8,128)(2,1)S(1)}, u32[]{:S(2)}, u32[]{:S(2)}) collective-permute-start(bf16[8,3712]{1,0:T(8,128)(2,1)S(1)} %reshape.156), channel_id=1, source_target_pairs={{0,6},{1,7},{2,4},{3,5},{4,2},{5,3},{6,0},{7,1},{8,14},{9,15},{10,... | collective-permute-start | bytes 178184 | tf_op jit(solution)/shard_map/ppermute | solution.py:32
  34.1 8.4 %collective-permute-start.8 = (bf16[16,3712]{1,0:T(8,128)(2,1)S(1)}, bf16[16,3712]{1,0:T(8,128)(2,1)S(1)}, u32[]{:S(2)}, u32[]{:S(2)}) collective-permute-start(bf16[16,3712]{1,0:T(8,128)(2,1)S(1)} %pad_maximum_fusion.refs_0_), channel_id=1, source_target_pairs={{0,1},{1,0},{2,3},{3,2},{4,5},{5,4},{6,7},{7,6},{8,9},{9,8},{10,11... | collective-permute-start | bytes 356360 | tf_op jit(solution)/shard_map/ppermute | solution.py:32
  35.9 7.1 %collective-permute-start.7 = (bf16[16,3712]{1,0:T(8,128)(2,1)S(1)}, bf16[16,3712]{1,0:T(8,128)(2,1)S(1)}, u32[]{:S(2)}, u32[]{:S(2)}) collective-permute-start(bf16[16,3712]{1,0:T(8,128)(2,1)S(1)} %pad_maximum_fusion.refs_0_), channel_id=1, source_target_pairs={{0,16},{1,17},{2,18},{3,19},{4,20},{5,21},{6,22},{7,23},{8,24},{9,... | collective-permute-start | bytes 356360 | tf_op jit(solution)/shard_map/ppermute | solution.py:32
  40.0 5.7 %collective-permute-start.6 = (bf16[16,3712]{1,0:T(8,128)(2,1)S(1)}, bf16[16,3712]{1,0:T(8,128)(2,1)S(1)}, u32[]{:S(2)}, u32[]{:S(2)}) collective-permute-start(bf16[16,3712]{1,0:T(8,128)(2,1)S(1)} %pad_maximum_fusion.refs_0_), channel_id=1, source_target_pairs={{0,17},{1,16},{2,19},{3,18},{4,21},{5,20},{6,23},{7,22},{8,25},{9,... | collective-permute-start | bytes 356360 | tf_op jit(solution)/shard_map/ppermute | solution.py:32
  42.5 3.3 %collective-permute-start.9 = (bf16[16,3712]{1,0:T(8,128)(2,1)S(1)}, bf16[16,3712]{1,0:T(8,128)(2,1)S(1)}, u32[]{:S(2)}, u32[]{:S(2)}) collective-permute-start(bf16[16,3712]{1,0:T(8,128)(2,1)S(1)} %pad_maximum_fusion.refs_0_), channel_id=1, source_target_pairs={{0,8},{1,9},{2,10},{3,11},{4,12},{5,13},{6,14},{7,15},{8,0},{9,1},... | collective-permute-start | bytes 356360 | tf_op jit(solution)/shard_map/ppermute | solution.py:32
  42.6 3.8 %collective-permute-start.12 = (bf16[16,3712]{1,0:T(8,128)(2,1)S(1)}, bf16[16,3712]{1,0:T(8,128)(2,1)S(1)}, u32[]{:S(2)}, u32[]{:S(2)}) collective-permute-start(bf16[16,3712]{1,0:T(8,128)(2,1)S(1)} %collective-permute-done.8.refs_3_), channel_id=1, source_target_pairs={{0,8},{1,9},{2,10},{3,11},{4,12},{5,13},{6,14},{7,15},{8,0},{9,1},... | collective-permute-start | bytes 356360 | tf_op jit(solution)/shard_map/ppermute | solution.py:32
  43.1 3.3 %collective-permute-start.11 = (bf16[16,3712]{1,0:T(8,128)(2,1)S(1)}, bf16[16,3712]{1,0:T(8,128)(2,1)S(1)}, u32[]{:S(2)}, u32[]{:S(2)}) collective-permute-start(bf16[16,3712]{1,0:T(8,128)(2,1)S(1)} %collective-permute-done.7.refs_2_), channel_id=1, source_target_pairs={{0,8},{1,9},{2,10},{3,11},{4,12},{5,13},{6,14},{7,15},{8,0},{9,1},... | collective-permute-start | bytes 356360 | tf_op jit(solution)/shard_map/ppermute | solution.py:32
  45.8 1.3 %collective-permute-start.10 = (bf16[16,3712]{1,0:T(8,128)(2,1)S(1)}, bf16[16,3712]{1,0:T(8,128)(2,1)S(1)}, u32[]{:S(2)}, u32[]{:S(2)}) collective-permute-start(bf16[16,3712]{1,0:T(8,128)(2,1)S(1)} %collective-permute-done.6.refs_1_), channel_id=1, source_target_pairs={{0,8},{1,9},{2,10},{3,11},{4,12},{5,13},{6,14},{7,15},{8,0},{9,1},... | collective-permute-start | bytes 356360 | tf_op jit(solution)/shard_map/ppermute | solution.py:32
  45.8 29.2 %collective-permute-start = (bf16[128,576]{1,0:T(8,128)(2,1)}, bf16[128,576]{1,0:T(8,128)(2,1)S(1)}, u32[]{:S(2)}, u32[]{:S(2)}) collective-permute-start(bf16[128,576]{1,0:T(8,128)(2,1)} %fusion.6), channel_id=1, source_target_pairs={{0,8},{1,9},{2,10},{3,11},{4,12},{5,13},{6,14},{7,15},{8,0},{9,1},... | collective-permute-start | bytes 442376 | tf_op jit(solution)/shard_map/ppermute | solution.py:32
  47.1 2.0 %copy-start.1 = (bf16[1,3584,512]{2,1,0:T(8,128)(2,1)S(1)}, bf16[1,3584,512]{2,1,0:T(8,128)(2,1)}, u32[]{:S(2)}) copy-start(bf16[1,3584,512]{2,1,0:T(8,128)(2,1)} %refs_8_.3) | copy-start | bytes 11010052
  49.1 2.0 %copy-start.3 = (bf16[1,3584,512]{2,1,0:T(8,128)(2,1)S(1)}, bf16[1,3584,512]{2,1,0:T(8,128)(2,1)}, u32[]{:S(2)}) copy-start(bf16[1,3584,512]{2,1,0:T(8,128)(2,1)} %refs_9_.3) | copy-start | bytes 11010052
  51.2 2.0 %copy-start.5 = (bf16[1,512,3584]{2,1,0:T(8,128)(2,1)S(1)}, bf16[1,512,3584]{2,1,0:T(8,128)(2,1)}, u32[]{:S(2)}) copy-start(bf16[1,512,3584]{2,1,0:T(8,128)(2,1)} %refs_10_.3) | copy-start | bytes 11010052
  53.2 9.7 %copy-start.6 = (bf16[4,128,576]{1,2,0:T(8,128)(2,1)S(1)}, bf16[4,128,576]{1,2,0:T(8,128)(2,1)}, u32[]{:S(2)}) copy-start(bf16[4,128,576]{1,2,0:T(8,128)(2,1)} %param.12) | copy-start | bytes 1769476
  59.1 14.6 %collective-permute-start.13 = (bf16[64,3584]{1,0:T(8,128)(2,1)S(1)}, bf16[64,3584]{1,0:T(8,128)(2,1)S(1)}, u32[]{:S(2)}, u32[]{:S(2)}) collective-permute-start(bf16[64,3584]{1,0:T(8,128)(2,1)S(1)} %get-tuple-element.12), channel_id=1, source_target_pairs={{0,8},{1,9},{2,10},{3,11},{4,12},{5,13},{6,14},{7,15},{8,0},{9,1},... | collective-permute-start | bytes 1376264 | tf_op jit(solution)/shard_map/ppermute | solution.py:32
  59.3 8.9 %collective-permute-start.25 = (bf16[32,3712]{1,0:T(8,128)(2,1)S(1)}, bf16[32,3712]{1,0:T(8,128)(2,1)S(1)}, u32[]{:S(2)}, u32[]{:S(2)}) collective-permute-start(bf16[32,3712]{1,0:T(8,128)(2,1)S(1)} %constant_dynamic-update-slice_fusion.refs_0_), channel_id=1, source_target_pairs={{0,1},{1,0},{2,3},{3,2},{4,5},{5,4},{6,7},{7,6},{8,9},{9,8},{10,11... | collective-permute-start | bytes 712712 | tf_op jit(solution)/shard_map/ppermute | solution.py:32
  60.9 8.6 %collective-permute-start.24 = (bf16[32,3712]{1,0:T(8,128)(2,1)S(1)}, bf16[32,3712]{1,0:T(8,128)(2,1)S(1)}, u32[]{:S(2)}, u32[]{:S(2)}) collective-permute-start(bf16[32,3712]{1,0:T(8,128)(2,1)S(1)} %constant_dynamic-update-slice_fusion.refs_0_), channel_id=1, source_target_pairs={{0,16},{1,17},{2,18},{3,19},{4,20},{5,21},{6,22},{7,23},{8,24},{9,... | collective-permute-start | bytes 712712 | tf_op jit(solution)/shard_map/ppermute | solution.py:32
  62.4 11.3 %collective-permute-start.23 = (bf16[32,3712]{1,0:T(8,128)(2,1)S(1)}, bf16[32,3712]{1,0:T(8,128)(2,1)S(1)}, u32[]{:S(2)}, u32[]{:S(2)}) collective-permute-start(bf16[32,3712]{1,0:T(8,128)(2,1)S(1)} %constant_dynamic-update-slice_fusion.refs_0_), channel_id=1, source_target_pairs={{0,17},{1,16},{2,19},{3,18},{4,21},{5,20},{6,23},{7,22},{8,25},{9,... | collective-permute-start | bytes 712712 | tf_op jit(solution)/shard_map/ppermute | solution.py:32
  68.2 8.3 %collective-permute-start.26 = (bf16[32,3712]{1,0:T(8,128)(2,1)S(1)}, bf16[32,3712]{1,0:T(8,128)(2,1)S(1)}, u32[]{:S(2)}, u32[]{:S(2)}) collective-permute-start(bf16[32,3712]{1,0:T(8,128)(2,1)S(1)} %constant_dynamic-update-slice_fusion.refs_0_), channel_id=1, source_target_pairs={{0,8},{1,9},{2,10},{3,11},{4,12},{5,13},{6,14},{7,15},{8,0},{9,1},... | collective-permute-start | bytes 712712 | tf_op jit(solution)/shard_map/ppermute | solution.py:32
  69.5 7.0 %collective-permute-start.29 = (bf16[32,3712]{1,0:T(8,128)(2,1)S(1)}, bf16[32,3712]{1,0:T(8,128)(2,1)S(1)}, u32[]{:S(2)}, u32[]{:S(2)}) collective-permute-start(bf16[32,3712]{1,0:T(8,128)(2,1)S(1)} %collective-permute-done.25.refs_3_), channel_id=1, source_target_pairs={{0,8},{1,9},{2,10},{3,11},{4,12},{5,13},{6,14},{7,15},{8,0},{9,1},... | collective-permute-start | bytes 712712 | tf_op jit(solution)/shard_map/ppermute | solution.py:32
  73.7 5.2 %collective-permute-start.28 = (bf16[32,3712]{1,0:T(8,128)(2,1)S(1)}, bf16[32,3712]{1,0:T(8,128)(2,1)S(1)}, u32[]{:S(2)}, u32[]{:S(2)}) collective-permute-start(bf16[32,3712]{1,0:T(8,128)(2,1)S(1)} %collective-permute-done.24.refs_2_), channel_id=1, source_target_pairs={{0,8},{1,9},{2,10},{3,11},{4,12},{5,13},{6,14},{7,15},{8,0},{9,1},... | collective-permute-start | bytes 712712 | tf_op jit(solution)/shard_map/ppermute | solution.py:32
  73.7 5.7 %copy-start.7 = (bf16[64,3584]{1,0:T(8,128)(2,1)}, bf16[64,3584]{1,0:T(8,128)(2,1)S(1)}, u32[]{:S(2)}) copy-start(bf16[64,3584]{1,0:T(8,128)(2,1)S(1)} %collective-permute-done.13) | copy-start | bytes 1376260
  73.7 5.7 %collective-permute-start.27 = (bf16[32,3712]{1,0:T(8,128)(2,1)S(1)}, bf16[32,3712]{1,0:T(8,128)(2,1)S(1)}, u32[]{:S(2)}, u32[]{:S(2)}) collective-permute-start(bf16[32,3712]{1,0:T(8,128)(2,1)S(1)} %collective-permute-done.23.refs_1_), channel_id=1, source_target_pairs={{0,8},{1,9},{2,10},{3,11},{4,12},{5,13},{6,14},{7,15},{8,0},{9,1},... | collective-permute-start | bytes 712712 | tf_op jit(solution)/shard_map/ppermute | solution.py:32
  75.0 15.9 %copy-start.8 = (bf16[128,576]{1,0:T(8,128)(2,1)}, bf16[128,576]{1,0:T(8,128)(2,1)S(1)}, u32[]{:S(2)}) copy-start(bf16[128,576]{1,0:T(8,128)(2,1)S(1)} %collective-permute-done.rest_0_) | copy-start | bytes 442372
  75.0 15.9 %collective-permute-start.1 = (bf16[128,576]{1,0:T(8,128)(2,1)S(1)}, bf16[128,576]{1,0:T(8,128)(2,1)S(1)}, u32[]{:S(2)}, u32[]{:S(2)}) collective-permute-start(bf16[128,576]{1,0:T(8,128)(2,1)S(1)} %fusion.4), channel_id=1, source_target_pairs={{0,16},{1,17},{2,18},{3,19},{4,20},{5,21},{6,22},{7,23},{8,24},{9,... | collective-permute-start | bytes 442376 | tf_op jit(solution)/shard_map/ppermute | solution.py:32
  76.5 15.1 %collective-permute-start.2 = (bf16[128,576]{1,0:T(8,128)(2,1)}, bf16[128,576]{1,0:T(8,128)(2,1)}, u32[]{:S(2)}, u32[]{:S(2)}) collective-permute-start(bf16[128,576]{1,0:T(8,128)(2,1)} %fusion.2), channel_id=1, source_target_pairs={{0,24},{1,25},{2,26},{3,27},{4,28},{5,29},{6,30},{7,31},{8,16},{9,... | collective-permute-start | bytes 442376 | tf_op jit(solution)/shard_map/ppermute | solution.py:32
  76.5 24.5 %collective-permute-start.14 = (bf16[16,3584]{1,0:T(8,128)(2,1)}, bf16[16,3584]{1,0:T(8,128)(2,1)}, u32[]{:S(2)}, u32[]{:S(2)}) collective-permute-start(bf16[16,3584]{1,0:T(8,128)(2,1)} %get-tuple-element.49), channel_id=1, source_target_pairs={{0,17},{1,16},{2,19},{3,18},{4,21},{5,20},{6,23},{7,22},{8,25},{9,... | collective-permute-start | bytes 344072 | tf_op jit(solution)/shard_map/ppermute | solution.py:32
  78.9 22.1 %collective-permute-start.16 = (bf16[16,3584]{1,0:T(8,128)(2,1)}, bf16[16,3584]{1,0:T(8,128)(2,1)}, u32[]{:S(2)}, u32[]{:S(2)}) collective-permute-start(bf16[16,3584]{1,0:T(8,128)(2,1)} %get-tuple-element.50), channel_id=1, source_target_pairs={{0,1},{1,0},{2,3},{3,2},{4,5},{5,4},{6,7},{7,6},{8,9},{9,8},{10,11... | collective-permute-start | bytes 344072 | tf_op jit(solution)/shard_map/ppermute | solution.py:32
  79.4 21.6 %collective-permute-start.15 = (bf16[16,3584]{1,0:T(8,128)(2,1)S(1)}, bf16[16,3584]{1,0:T(8,128)(2,1)}, u32[]{:S(2)}, u32[]{:S(2)}) collective-permute-start(bf16[16,3584]{1,0:T(8,128)(2,1)S(1)} %get-tuple-element.51), channel_id=1, source_target_pairs={{0,16},{1,17},{2,18},{3,19},{4,20},{5,21},{6,22},{7,23},{8,24},{9,... | collective-permute-start | bytes 344072 | tf_op jit(solution)/shard_map/ppermute | solution.py:32
  80.1 2.0 %copy-start.2 = (bf16[1,3584,512]{2,1,0:T(8,128)(2,1)S(1)}, bf16[1,3584,512]{2,1,0:T(8,128)(2,1)}, u32[]{:S(2)}) copy-start(bf16[1,3584,512]{2,1,0:T(8,128)(2,1)} %refs_8_.3) | copy-start | bytes 11010052
  82.1 2.0 %copy-start.4 = (bf16[1,3584,512]{2,1,0:T(8,128)(2,1)S(1)}, bf16[1,3584,512]{2,1,0:T(8,128)(2,1)}, u32[]{:S(2)}) copy-start(bf16[1,3584,512]{2,1,0:T(8,128)(2,1)} %refs_9_.3) | copy-start | bytes 11010052
  90.9 0.7 copy-start.9
  90.9 11.3 %collective-permute-start.30 = (bf16[128,3584]{1,0:T(8,128)(2,1)S(1)}, bf16[128,3584]{1,0:T(8,128)(2,1)}, u32[]{:S(2)}, u32[]{:S(2)}) collective-permute-start(bf16[128,3584]{1,0:T(8,128)(2,1)S(1)} %get-tuple-element.14), channel_id=1, source_target_pairs={{0,8},{1,9},{2,10},{3,11},{4,12},{5,13},{6,14},{7,15},{8,0},{9,1},... | collective-permute-start | bytes 2752520 | tf_op jit(solution)/shard_map/ppermute | solution.py:32
  103.5 9.5 %collective-permute-start.31 = (bf16[32,3584]{1,0:T(8,128)(2,1)S(1)}, bf16[32,3584]{1,0:T(8,128)(2,1)S(1)}, u32[]{:S(2)}, u32[]{:S(2)}) collective-permute-start(bf16[32,3584]{1,0:T(8,128)(2,1)S(1)} %get-tuple-element.46), channel_id=1, source_target_pairs={{0,17},{1,16},{2,19},{3,18},{4,21},{5,20},{6,23},{7,22},{8,25},{9,... | collective-permute-start | bytes 688136 | tf_op jit(solution)/shard_map/ppermute | solution.py:32
  105.9 10.9 %collective-permute-start.33 = (bf16[32,3584]{1,0:T(8,128)(2,1)S(1)}, bf16[32,3584]{1,0:T(8,128)(2,1)S(1)}, u32[]{:S(2)}, u32[]{:S(2)}) collective-permute-start(bf16[32,3584]{1,0:T(8,128)(2,1)S(1)} %get-tuple-element.47), channel_id=1, source_target_pairs={{0,1},{1,0},{2,3},{3,2},{4,5},{5,4},{6,7},{7,6},{8,9},{9,8},{10,11... | collective-permute-start | bytes 688136 | tf_op jit(solution)/shard_map/ppermute | solution.py:32
  106.4 10.5 %collective-permute-start.32 = (bf16[32,3584]{1,0:T(8,128)(2,1)S(1)}, bf16[32,3584]{1,0:T(8,128)(2,1)S(1)}, u32[]{:S(2)}, u32[]{:S(2)}) collective-permute-start(bf16[32,3584]{1,0:T(8,128)(2,1)S(1)} %get-tuple-element.48), channel_id=1, source_target_pairs={{0,16},{1,17},{2,18},{3,19},{4,20},{5,21},{6,22},{7,23},{8,24},{9,... | collective-permute-start | bytes 688136 | tf_op jit(solution)/shard_map/ppermute | solution.py:32
  107.1 11.8 %collective-permute-start.17 = (bf16[4,3584]{1,0:T(4,128)(2,1)S(1)}, bf16[4,3584]{1,0:T(4,128)(2,1)S(1)}, u32[]{:S(2)}, u32[]{:S(2)}) collective-permute-start(bf16[4,3584]{1,0:T(4,128)(2,1)S(1)} %get-tuple-element.58), channel_id=1, source_target_pairs={{0,6},{1,7},{2,4},{3,5},{4,2},{5,3},{6,0},{7,1},{8,14},{9,15},{10,... | collective-permute-start | bytes 86024 | tf_op jit(solution)/shard_map/ppermute | solution.py:32
  108.0 14.5 %collective-permute-start.19 = (bf16[4,3584]{1,0:T(4,128)(2,1)S(1)}, bf16[4,3584]{1,0:T(4,128)(2,1)S(1)}, u32[]{:S(2)}, u32[]{:S(2)}) collective-permute-start(bf16[4,3584]{1,0:T(4,128)(2,1)S(1)} %get-tuple-element.59), channel_id=1, source_target_pairs={{0,2},{1,3},{2,0},{3,1},{4,6},{5,7},{6,4},{7,5},{8,10},{9,11},{10,... | collective-permute-start | bytes 86024 | tf_op jit(solution)/shard_map/ppermute | solution.py:32
  113.0 9.5 %collective-permute-start.18 = (bf16[4,3584]{1,0:T(4,128)(2,1)S(1)}, bf16[4,3584]{1,0:T(4,128)(2,1)S(1)}, u32[]{:S(2)}, u32[]{:S(2)}) collective-permute-start(bf16[4,3584]{1,0:T(4,128)(2,1)S(1)} %get-tuple-element.60), channel_id=1, source_target_pairs={{0,4},{1,5},{2,6},{3,7},{4,0},{5,1},{6,2},{7,3},{8,12},{9,13},{10,... | collective-permute-start | bytes 86024 | tf_op jit(solution)/shard_map/ppermute | solution.py:32
  118.1 6.7 %collective-permute-start.34 = (bf16[8,3584]{1,0:T(8,128)(2,1)S(1)}, bf16[8,3584]{1,0:T(8,128)(2,1)S(1)}, u32[]{:S(2)}, u32[]{:S(2)}) collective-permute-start(bf16[8,3584]{1,0:T(8,128)(2,1)S(1)} %get-tuple-element.55), channel_id=1, source_target_pairs={{0,6},{1,7},{2,4},{3,5},{4,2},{5,3},{6,0},{7,1},{8,14},{9,15},{10,... | collective-permute-start | bytes 172040 | tf_op jit(solution)/shard_map/ppermute | solution.py:32
  118.9 6.1 %collective-permute-start.36 = (bf16[8,3584]{1,0:T(8,128)(2,1)S(1)}, bf16[8,3584]{1,0:T(8,128)(2,1)S(1)}, u32[]{:S(2)}, u32[]{:S(2)}) collective-permute-start(bf16[8,3584]{1,0:T(8,128)(2,1)S(1)} %get-tuple-element.56), channel_id=1, source_target_pairs={{0,2},{1,3},{2,0},{3,1},{4,6},{5,7},{6,4},{7,5},{8,10},{9,11},{10,... | collective-permute-start | bytes 172040 | tf_op jit(solution)/shard_map/ppermute | solution.py:32
  118.9 7.3 %collective-permute-start.35 = (bf16[8,3584]{1,0:T(8,128)(2,1)S(1)}, bf16[8,3584]{1,0:T(8,128)(2,1)S(1)}, u32[]{:S(2)}, u32[]{:S(2)}) collective-permute-start(bf16[8,3584]{1,0:T(8,128)(2,1)S(1)} %get-tuple-element.57), channel_id=1, source_target_pairs={{0,4},{1,5},{2,6},{3,7},{4,0},{5,1},{6,2},{7,3},{8,12},{9,13},{10,... | collective-permute-start | bytes 172040 | tf_op jit(solution)/shard_map/ppermute | solution.py:32

commit v2 on v1

--- a/solution.py
+++ b/solution.py
@@ -32,24 +32,85 @@
     return lax.ppermute(values, BOTH, pairs)
 
 
+def plan_entry(plan_ref, group, entry, field):
+    return plan_ref[(group * 2 + entry) * 2 + field]
+
+
+def insert_entries(keys, entries, filled, trace):
+    column_index = lax.broadcasted_iota(jnp.int32, keys.shape, 1)
+    keys = keys.astype(jnp.float32)
+    for step_index in range(entries.shape[0]):
+        rows = entries[step_index].astype(jnp.float32)
+        row_index = lax.broadcasted_iota(jnp.int32, rows.shape, 0)
+        entry = jnp.sum(jnp.where(row_index == trace, rows, 0.0), axis=0, keepdims=True)
+        column = jnp.transpose(entry)
+        keys = jnp.where(column_index == filled + step_index, column, keys)
+    return keys.astype(jnp.bfloat16)
+
+
+def outgoing_kernel(lengths_ref, plan_ref, group_ref, cache_ref, entries_ref, out_ref):
+    slot = outgoing_slot(pl.program_id(0), plan_ref, group_ref)
+    out_ref[0] = insert_entries(cache_ref[0], entries_ref[...], lengths_ref[slot], slot)
+
+
+def outgoing_slot(number, plan_ref, group_ref):
+    group = group_ref[0]
+    partner = group ^ (number + 1)
+    slot = jnp.int32(0)
+    for entry in range(2):
+        goes = plan_entry(plan_ref, group, entry, 1) == partner
+        slot = jnp.where(goes, plan_entry(plan_ref, group, entry, 0), slot)
+    return slot
+
+
+def outgoing(cache, new_entries, lengths, plan, group):
+    _, width, capacity = cache.shape
+    others = lax.axis_size("grp") - 1
+    return pl.pallas_call(
+        outgoing_kernel,
+        grid_spec=pltpu.PrefetchScalarGridSpec(
+            num_scalar_prefetch=3,
+            grid=(others,),
+            in_specs=[
+                pl.BlockSpec(
+                    (1, width, capacity),
+                    lambda m, lengths_ref, plan_ref, group_ref: (
+                        outgoing_slot(m, plan_ref, group_ref),
+                        0,
+                        0,
+                    ),
+                ),
+                pl.BlockSpec(new_entries.shape, lambda m, *_: (0, 0, 0)),
+            ],
+            out_specs=pl.BlockSpec((1, width, capacity), lambda m, *_: (m, 0, 0)),
+        ),
+        out_shape=jax.ShapeDtypeStruct((others, width, capacity), cache.dtype),
+        cost_estimate=pl.CostEstimate(
+            flops=0, bytes_accessed=4 * others * width * capacity, transcendentals=0
+        ),
+        name="outgoing",
+    )(lengths, plan, group, cache, new_entries)
+
+
 def attention_kernel(
-    lengths_ref, source_ref, queries_ref, cache_ref, entries_ref, *rest
+    lengths_ref, plan_ref, group_ref, queries_ref, cache_ref, entries_ref, *rest
 ):
     received_refs, (contexts_ref, migrated_ref) = rest[:-2], rest[-2:]
     trace = pl.program_id(0)
     filled = lengths_ref[trace]
-    step_count, _, heads, width = queries_ref.shape
+    step_count, _, width, heads = queries_ref.shape
     latent = contexts_ref.shape[3]
-    capacity = cache_ref.shape[1]
-    keys = cache_ref[0].astype(jnp.float32)
-    row_index = lax.broadcasted_iota(jnp.int32, keys.shape, 0)
-    for step_index in range(step_count):
-        entry_rows = entries_ref[step_index].astype(jnp.float32)
-        entry_index = lax.broadcasted_iota(jnp.int32, entry_rows.shape, 0)
-        entry = jnp.sum(jnp.where(entry_index == trace, entry_rows, 0.0), axis=0, keepdims=True)
-        keys = jnp.where(row_index == filled + step_index, entry, keys)
-    keys = keys.astype(jnp.bfloat16)
-    source = source_ref[trace]
+    capacity = cache_ref.shape[2]
+    keys = insert_entries(cache_ref[0], entries_ref[...], filled, trace)
+    group = group_ref[0]
+    source = jnp.int32(0)
+    for number in range(len(received_refs)):
+        partner = group ^ (number + 1)
+        for entry in range(2):
+            lands = (plan_entry(plan_ref, partner, entry, 1) == group) & (
+                plan_entry(plan_ref, group, entry, 0) == trace
+            )
+            source = jnp.where(lands, number + 1, source)
 
     @pl.when(source == 0)
     def _():
@@ -61,43 +122,42 @@
         def _(received_ref=received_ref):
             migrated_ref[0] = received_ref[...]
 
-    flat_queries = queries_ref[...].reshape(step_count * heads, width)
-    scores = (
-        lax.dot_general(
-            flat_queries, keys, (((1,), (1,)), ((), ())), preferred_element_type=jnp.float32
-        )
-        * SCORE_SCALE
+    key_rows = jnp.transpose(keys)
+    flat_queries = jnp.concatenate([queries_ref[s, 0] for s in range(step_count)], axis=1)
+    scores = jnp.dot(key_rows, flat_queries, preferred_element_type=jnp.float32) * SCORE_SCALE
+    position = lax.broadcasted_iota(jnp.int32, scores.shape, 0)
+    step_of_column = lax.broadcasted_iota(jnp.int32, scores.shape, 1) // heads
+    scores = jnp.where(position <= filled + step_of_column, scores, -jnp.inf)
+    exp_scores = jnp.exp(scores - jnp.max(scores, axis=0, keepdims=True))
+    weights = (exp_scores / jnp.sum(exp_scores, axis=0, keepdims=True)).astype(jnp.bfloat16)
+    context = lax.dot_general(
+        weights,
+        key_rows[:, :latent],
+        (((0,), (0,)), ((), ())),
+        preferred_element_type=jnp.float32,
     )
-    step_of_row = lax.broadcasted_iota(jnp.int32, (step_count, heads, capacity), 0).reshape(
-        step_count * heads, capacity
-    )
-    position = lax.broadcasted_iota(jnp.int32, scores.shape, 1)
-    scores = jnp.where(position <= filled + step_of_row, scores, -jnp.inf)
-    exp_scores = jnp.exp(scores - jnp.max(scores, axis=1, keepdims=True))
-    weights = (exp_scores / jnp.sum(exp_scores, axis=1, keepdims=True)).astype(jnp.bfloat16)
-    context = jnp.dot(weights, keys[:, :latent], preferred_element_type=jnp.float32)
     contexts_ref[...] = context.astype(jnp.bfloat16).reshape(contexts_ref.shape)
 
 
-def attention(queries, cache, new_entries, lengths, source, received):
-    step_count, traces, heads, width = queries.shape
-    capacity = cache.shape[1]
+def attention(queries, cache, new_entries, lengths, plan, group, received):
+    step_count, traces, width, heads = queries.shape
+    capacity = cache.shape[2]
     latent = width - ROPE
     whole = lambda shape: pl.BlockSpec(shape, lambda t, *_: (0,) * len(shape))
     return pl.pallas_call(
         attention_kernel,
         grid_spec=pltpu.PrefetchScalarGridSpec(
-            num_scalar_prefetch=2,
+            num_scalar_prefetch=3,
             grid=(traces,),
             in_specs=[
-                pl.BlockSpec((step_count, 1, heads, width), lambda t, *_: (0, t, 0, 0)),
-                pl.BlockSpec((1, capacity, width), lambda t, *_: (t, 0, 0)),
+                pl.BlockSpec((step_count, 1, width, heads), lambda t, *_: (0, t, 0, 0)),
+                pl.BlockSpec((1, width, capacity), lambda t, *_: (t, 0, 0)),
                 whole(new_entries.shape),
             ]
-            + [whole((capacity, width))] * len(received),
+            + [whole((width, capacity))] * len(received),
             out_specs=[
                 pl.BlockSpec((step_count, 1, heads, latent), lambda t, *_: (0, t, 0, 0)),
-                pl.BlockSpec((1, capacity, width), lambda t, *_: (t, 0, 0)),
+                pl.BlockSpec((1, width, capacity), lambda t, *_: (t, 0, 0)),
             ],
         ),
         out_shape=[
@@ -110,36 +170,7 @@
             transcendentals=step_count * traces * heads * capacity,
         ),
         name="attention",
-    )(lengths, source, queries, cache, new_entries, *received)
-
-
-def migrate(cache, new_entries, lengths, plan):
-    traces, capacity, _ = cache.shape
-    groups = lax.axis_size("grp")
-    group_index = lax.axis_index("grp")
-    column_plan = plan[:, 0]
-    own_plan = lax.dynamic_index_in_dim(column_plan, group_index, 0, keepdims=False)
-    slot_list = jnp.arange(traces, dtype=jnp.int32)
-    positions = jnp.arange(capacity, dtype=jnp.int32)
-    source = jnp.zeros((traces,), jnp.int32)
-    received = []
-    for flip in range(1, groups):
-        partner = group_index ^ flip
-        slot = jnp.sum(jnp.where(own_plan[:, 1] == partner, own_plan[:, 0], 0))
-        rows = lax.dynamic_index_in_dim(cache, slot, 0, keepdims=False)
-        filled = lax.dynamic_index_in_dim(lengths, slot, 0, keepdims=False)
-        entries = lax.dynamic_index_in_dim(new_entries, slot, 1, keepdims=False)
-        for step_index in range(new_entries.shape[0]):
-            rows = jnp.where(
-                (positions == filled + step_index)[:, None], entries[step_index][None, :], rows
-            )
-        received.append(across(rows, flip, 0))
-        partner_plan = lax.dynamic_index_in_dim(column_plan, partner, 0, keepdims=False)
-        lands = (partner_plan[:, 1] == group_index)[None, :] & (
-            own_plan[:, 0][None, :] == slot_list[:, None]
-        )
-        source = jnp.where(jnp.any(lands, axis=1), flip, source)
-    return received, source
+    )(lengths, plan, group, queries, cache, new_entries, *received)
 
 
 def expert_kernel(tile, column_ref, *refs):
@@ -227,7 +258,7 @@
             pltpu.VMEM((token_count, hidden_width), jnp.bfloat16),
             pltpu.SemaphoreType.DMA((3, width // tile)),
         ],
-        compiler_params=pltpu.CompilerParams(vmem_limit_bytes=40 * 1024 * 1024),
+        compiler_params=pltpu.CompilerParams(vmem_limit_bytes=56 * 1024 * 1024),
         cost_estimate=pl.CostEstimate(
             flops=6 * token_count * width * hidden_width,
             bytes_accessed=6 * width * hidden_width + 4 * token_count * width,
@@ -244,19 +275,41 @@
     return total.astype(jnp.bfloat16)
 
 
-def token_rows(moe_input, expert_ids, route_gains, experts):
-    group_index = lax.axis_index("grp")
-    own_ids = lax.dynamic_index_in_dim(expert_ids, group_index, 1, keepdims=False)
-    own_gains = lax.dynamic_index_in_dim(route_gains, group_index, 1, keepdims=False)
-    chosen = own_ids[..., None] == jnp.arange(experts, dtype=jnp.int32)
-    gains = jnp.sum(jnp.where(chosen, own_gains[..., None], 0.0), axis=2)
-    high = gains.astype(jnp.bfloat16)
-    rest = gains - high.astype(jnp.float32)
-    middle = rest.astype(jnp.bfloat16)
-    low = (rest - middle.astype(jnp.float32)).astype(jnp.bfloat16)
-    parts = jnp.stack([high, middle, low], axis=-1).reshape(gains.shape[:2] + (3 * experts,))
-    parts = jnp.pad(parts, ((0, 0), (0, 0), (0, GAIN_LANES - 3 * experts)))
-    return jnp.concatenate([moe_input, parts], axis=2)
+def token_rows_kernel(chunks, group_ref, ids_ref, gains_ref, tokens_ref, *out_refs):
+    width = tokens_ref.shape[2]
+    experts = ids_ref.shape[3]
+    group = group_ref[0]
+    for out_ref, (first, last) in zip(out_refs, chunks):
+        for step_index in range(first, last):
+            ids, gains = ids_ref[step_index, group], gains_ref[step_index, group]
+            lane = lax.broadcasted_iota(jnp.int32, (ids.shape[0], GAIN_LANES), 1)
+            dense = jnp.zeros(lane.shape, jnp.float32)
+            for choice in range(ids.shape[1]):
+                place = ids[:, choice : choice + 1]
+                named = (lane >= 3 * place) & (lane < 3 * place + 3)
+                dense = dense + jnp.where(named, gains[:, choice : choice + 1], 0.0)
+            high = dense.astype(jnp.bfloat16).astype(jnp.float32)
+            rest = dense - high
+            middle = rest.astype(jnp.bfloat16).astype(jnp.float32)
+            part = lane % 3
+            parts = jnp.where(part == 0, high, jnp.where(part == 1, middle, rest - middle))
+            out_ref[step_index - first, :, :width] = tokens_ref[step_index]
+            out_ref[step_index - first, :, width:] = parts.astype(jnp.bfloat16)
+
+
+def token_rows(moe_input, expert_ids, route_gains, group):
+    _, trace_count, width = moe_input.shape
+    vmem = pl.BlockSpec(memory_space=pltpu.VMEM)
+    return pl.pallas_call(
+        partial(token_rows_kernel, STEP_CHUNKS),
+        in_specs=[pl.BlockSpec(memory_space=pltpu.SMEM), vmem, vmem, vmem],
+        out_specs=[vmem] * len(STEP_CHUNKS),
+        out_shape=[
+            jax.ShapeDtypeStruct((last - first, trace_count, width + GAIN_LANES), moe_input.dtype)
+            for first, last in STEP_CHUNKS
+        ],
+        name="token_rows",
+    )(group, expert_ids, route_gains, moe_input)
 
 
 def dense_experts(moe_input, expert_ids, route_gains, w_gate, w_up, w_down):
@@ -265,12 +318,12 @@
     far_flips = far_flips[::-1]
     near_flips = [(2 * x, y) for x in range(groups // 2) for y in range(2)][1:]
     near_flips = near_flips[::-1]
-    tokens = token_rows(moe_input, expert_ids, route_gains, experts)
+    tokens = token_rows(moe_input, expert_ids, route_gains, lax.axis_index("grp").reshape(1))
     trace_count, width = moe_input.shape[1:]
     out_chunks = []
-    for first, last in STEP_CHUNKS:
-        rows = tokens[first:last].reshape((last - first) * trace_count, -1)
+    for rows in tokens:
         line = jnp.concatenate([rows] + [across(rows, *flip) for flip in far_flips], axis=0)
+        line = line.reshape(-1, line.shape[-1])
         plane = [line] + [across(line, *flip) for flip in near_flips]
         pieces = plane + [across(piece, 1, 0) for piece in plane]
         own, other = expert(pieces, w_gate, w_up, w_down)
@@ -283,12 +336,12 @@
         sums = add_up(
             [sums[0]] + [across(part, *flip) for part, flip in zip(sums[1:], near_flips)]
         )
-        count = rows.shape[0]
+        count = rows.shape[0] * trace_count
         parts = [sums[i * count : (i + 1) * count] for i in range(len(far_flips) + 1)]
         total = add_up(
             [parts[0]] + [across(part, *flip) for part, flip in zip(parts[1:], far_flips)]
         )
-        out_chunks.append(total.reshape(last - first, trace_count, width))
+        out_chunks.append(total.reshape(-1, trace_count, width))
     return jnp.concatenate(out_chunks, axis=0)
 
 
@@ -367,8 +420,14 @@
     w_down,
     plan,
 ):
-    received, source = migrate(cache, new_entries, lengths, plan)
-    contexts, migrated_cache = attention(queries, cache, new_entries, lengths, source, received)
+    queries, cache = jnp.swapaxes(queries, 2, 3), jnp.swapaxes(cache, 1, 2)
+    plan, group = plan.reshape(-1), lax.axis_index("grp").reshape(1)
+    leaving = outgoing(cache, new_entries, lengths, plan, group)
+    received = [across(leaving[flip - 1], flip, 0) for flip in range(1, lax.axis_size("grp"))]
+    contexts, migrated_cache = attention(
+        queries, cache, new_entries, lengths, plan, group, received
+    )
+    migrated_cache = jnp.swapaxes(migrated_cache, 1, 2)
     every_expert = expert_ids.shape[3] == lax.axis_size("ep")
     experts_of = dense_experts if every_expert else routed_experts
     moe_output = experts_of(moe_input, expert_ids, route_gains, w_gate, w_up, w_down)

time: 128 us -> 102 us (0.80)
  local copies, waits for them, and re-layouts: 25 us -> 2.97 us
  between operations: 10.8 us -> 1.04 us
  Pallas kernels: 19.9 us -> 28.7 us
  other arithmetic: 11.8 us -> 4.17 us
  waiting for transfers between devices: 24 us -> 31.6 us
  starting transfers between devices: 35.5 us -> 32.9 us
    unnamed x26 -> x45, local copies, waits for them, and re-layouts: 18.7 us -> 2.09 us
    ppermute x37, waiting for transfers between devices: 24 us -> 31.6 us  [across(): return lax.ppermute(values, BOTH, pairs)]
    pallas_call x0 -> x2, Pallas kernels: none -> 5.45 us  [the longest x1 3.71 us: outgoing(): pl.pallas_call(outgoing_kernel, grid_spec=pltpu.PrefetchScalarGridSpec(nu...]
    dynamic_slice x6 -> x0, local copies, waits for them, and re-layouts: 4.14 us -> none  [the longest x4 1.59 us: migrate(): rows = lax.dynamic_index_in_dim(cache, slot, 0, keepdims=False)]
    pallas_call x2, Pallas kernels: 12.6 us -> 16.2 us  [expert(): pl.pallas_call(partial(expert_kernel, tile), in_specs=[pl.BlockSpec(memor...]
    ppermute x37, starting transfers between devices: 35.5 us -> 32.9 us  [across(): return lax.ppermute(values, BOTH, pairs)]
    eq x11 -> x0, other arithmetic: 2.48 us -> none  [the longest x9 2.04 us: migrate(): positions == filled + step_index]
    select_n x4 -> x0, other arithmetic: 2.24 us -> none  [the longest x3 1.72 us: migrate(): jnp.where((positions == filled + step_index)[:, None], entries[step_index...]
  transfers between devices with their start and end apart: 37 -> 37, of which waited for: 11 -> 13; matrix products, arithmetic and copies ran while one was open for 17% -> 4% of each run, Pallas kernels for 16% -> 27%
where the time goes in v2:
time: 102 us; the launch traced here: 101 us
  starting transfers between devices  32.9 us (32%)
  waiting for transfers between devices  31.6 us (31%)
  Pallas kernels  28.7 us (28%)
  other arithmetic  4.17 us (4%)
  local copies, waits for them, and re-layouts  2.97 us (3%)
  between operations  1.04 us (1%)
    ppermute x37, starting transfers between devices, across(): return lax.ppermute(values, BOTH, pairs)  32.9 us
    ppermute x37, waiting for transfers between devices, across(): return lax.ppermute(values, BOTH, pairs)  31.6 us
    pallas_call x2, Pallas kernels, expert(): pl.pallas_call(partial(expert_kernel, tile), in_specs=[pl.BlockSpec(memor...  16.2 us
    pallas_call x1, Pallas kernels, attention(): pl.pallas_call(attention_kernel, grid_spec=pltpu.PrefetchScalarGridSpec(n...  7.03 us
    pallas_call x1, Pallas kernels, outgoing(): pl.pallas_call(outgoing_kernel, grid_spec=pltpu.PrefetchScalarGridSpec(nu...  3.71 us
    convert_element_type x5, other arithmetic, add_up(): return total.astype(jnp.bfloat16)  2.4 us
    unnamed x45, local copies, waits for them, and re-layouts  2.09 us
  transfers between devices with their start and end apart: 37, of which 13 were waited for; matrix products, arithmetic and copies ran while one was open for 4% of the time, Pallas kernels for 27%

profile of v2, /device:TPU:0, one launch (start us, length us, event | category | flops | bytes accessed | tf_op | source)
XLA Modules:
  0.0 101.4 jit_solution(8003138634844729846)
XLA Ops:
  0.6 1.7 %token_rows.1 = (bf16[1,4,3712]{2,1,0:T(4,128)(2,1)}, bf16[2,4,3712]{2,1,0:T(4,128)(2,1)}) custom-call(s32[1]{0:T(128)} %bitcast.group_ref, s32[3,4,4,8]{3,2,1,0:T(4,128)} %ids_ref.1, f32[3,4,4,8]{3,2,1,0:T(4,128)} %gains_ref.1, bf16[3,4,3584]{2,1,0:T(4,128)(2,1)} %tokens_ref.1), custom_call_target="tpu_custom_call" | custom-call | tf_op jit(solution)/shard_map/token_rows/pallas_call | solution.py:303
  2.4 5.0 %collective-permute-start.3 = (bf16[1,4,3712]{2,1,0:T(4,128)(2,1)}, bf16[1,4,3712]{2,1,0:T(4,128)(2,1)S(1)}, u32[]{:S(2)}, u32[]{:S(2)}) collective-permute-start(bf16[1,4,3712]{2,1,0:T(4,128)(2,1)} %get-tuple-element.13), channel_id=1, source_target_pairs={{0,6},{1,7},{2,4},{3,5},{4,2},{5,3},{6,0},{7,1},{8,14},{9,15},{10,... | collective-permute-start | bytes 89096 | tf_op jit(solution)/shard_map/ppermute | solution.py:32
  7.4 0.6 collective-permute-start.5
  8.0 1.5 %collective-permute-done.3 = bf16[1,4,3712]{2,1,0:T(4,128)(2,1)S(1)} collective-permute-done((bf16[1,4,3712]{2,1,0:T(4,128)(2,1)}, bf16[1,4,3712]{2,1,0:T(4,128)(2,1)S(1)}, u32[]{:S(2)}, u32[]{:S(2)}) %collective-permute-start.3) | collective-permute-done | bytes 29728 | tf_op jit(solution)/shard_map/ppermute | solution.py:32
  9.5 2.9 %collective-permute-done.4 = bf16[1,4,3712]{2,1,0:T(4,128)(2,1)S(1)} collective-permute-done((bf16[1,4,3712]{2,1,0:T(4,128)(2,1)}, bf16[1,4,3712]{2,1,0:T(4,128)(2,1)S(1)}, u32[]{:S(2)}, u32[]{:S(2)}) %collective-permute-start.4) | collective-permute-done | bytes 29728 | tf_op jit(solution)/shard_map/ppermute | solution.py:32
  12.4 0.9 pad_maximum_fusion.1
  13.3 2.5 %collective-permute-start.6 = (bf16[16,3712]{1,0:T(8,128)(2,1)S(1)}, bf16[16,3712]{1,0:T(8,128)(2,1)S(1)}, u32[]{:S(2)}, u32[]{:S(2)}) collective-permute-start(bf16[16,3712]{1,0:T(8,128)(2,1)S(1)} %reshape.32.refs_0_), channel_id=1, source_target_pairs={{0,17},{1,16},{2,19},{3,18},{4,21},{5,20},{6,23},{7,22},{8,25},{9,... | collective-permute-start | bytes 356360 | tf_op jit(solution)/shard_map/ppermute | solution.py:32
  15.8 0.5 collective-permute-start.7
  16.4 0.5 collective-permute-start.8
  16.9 2.3 %collective-permute-done.6.refs_1_ = bf16[16,3712]{1,0:T(8,128)(2,1)S(1)} collective-permute-done((bf16[16,3712]{1,0:T(8,128)(2,1)S(1)}, bf16[16,3712]{1,0:T(8,128)(2,1)S(1)}, u32[]{:S(2)}, u32[]{:S(2)}) %collective-permute-start.6) | collective-permute-done | bytes 118816 | tf_op jit(solution)/shard_map/ppermute | solution.py:32
  19.2 1.4 %collective-permute-done.7.refs_2_ = bf16[16,3712]{1,0:T(8,128)(2,1)S(1)} collective-permute-done((bf16[16,3712]{1,0:T(8,128)(2,1)S(1)}, bf16[16,3712]{1,0:T(8,128)(2,1)S(1)}, u32[]{:S(2)}, u32[]{:S(2)}) %collective-permute-start.7) | collective-permute-done | bytes 118816 | tf_op jit(solution)/shard_map/ppermute | solution.py:32
  20.7 0.5 collective-permute-done.8.refs_3_
  21.2 1.5 %collective-permute-start.20 = (bf16[2,4,3712]{2,1,0:T(4,128)(2,1)}, bf16[2,4,3712]{2,1,0:T(4,128)(2,1)S(1)}, u32[]{:S(2)}, u32[]{:S(2)}) collective-permute-start(bf16[2,4,3712]{2,1,0:T(4,128)(2,1)} %get-tuple-element.16), channel_id=1, source_target_pairs={{0,6},{1,7},{2,4},{3,5},{4,2},{5,3},{6,0},{7,1},{8,14},{9,15},{10,... | collective-permute-start | bytes 178184 | tf_op jit(solution)/shard_map/ppermute | solution.py:32
  22.8 0.8 copy.15
  23.5 0.7 reshape.29.plan_ref
  24.2 3.7 %outgoing.1 = bf16[3,576,128]{2,1,0:T(8,128)(2,1)} custom-call(s32[4]{0:T(128)} %lengths_ref.3, s32[16]{0:T(128)} %reshape.29.plan_ref, s32[1]{0:T(128)} %bitcast.group_ref, bf16[4,576,128]{2,1,0:T(8,128)(2,1)} %bitcast.15, bf16[3,4,576]{2,1,0:T(4,128)(2,1)} %entries_ref.3), custom_call_target="tpu_custom_call" | custom-call | bytes 884736 | tf_op jit(solution)/shard_map/outgoing/pallas_call | solution.py:69
  27.9 0.8 collective-permute-start.21
  28.8 2.3 %collective-permute-start.22 = (bf16[2,4,3712]{2,1,0:T(4,128)(2,1)}, bf16[2,4,3712]{2,1,0:T(4,128)(2,1)S(1)}, u32[]{:S(2)}, u32[]{:S(2)}) collective-permute-start(bf16[2,4,3712]{2,1,0:T(4,128)(2,1)} %get-tuple-element.16), channel_id=1, source_target_pairs={{0,2},{1,3},{2,0},{3,1},{4,6},{5,7},{6,4},{7,5},{8,10},{9,11},{10,... | collective-permute-start | bytes 178184 | tf_op jit(solution)/shard_map/ppermute | solution.py:32
  31.2 0.6 copy-done.19
  31.8 7.5 %expert.2 = (bf16[64,3584]{1,0:T(8,128)(2,1)}, bf16[64,3584]{1,0:T(8,128)(2,1)}) custom-call(s32[1]{0:T(128)} %bitcast.7.column_ref, bf16[16,3712]{1,0:T(8,128)(2,1)} %copy-done.3, bf16[16,3712]{1,0:T(8,128)(2,1)} %copy-done.14, bf16[16,3712]{1,0:T(8,128)(2,1)} %copy-done.15, bf16[16,3712]{1,0:T(8,128)(2,1)} %copy-done.16, bf16[16,3712]{1,0:T(8,128)(2,1)} %copy-done.17, ...), custom_call_target="tpu_custom_call" | custom-call | flops 1409286144 | bytes 12845056 | tf_op jit(solution)/shard_map/expert/pallas_call | solution.py:245
  39.6 1.7 %collective-permute-start.23 = (bf16[32,3712]{1,0:T(8,128)(2,1)S(1)}, bf16[32,3712]{1,0:T(8,128)(2,1)S(1)}, u32[]{:S(2)}, u32[]{:S(2)}) collective-permute-start(bf16[32,3712]{1,0:T(8,128)(2,1)S(1)} %reshape.34.refs_0_), channel_id=1, source_target_pairs={{0,17},{1,16},{2,19},{3,18},{4,21},{5,20},{6,23},{7,22},{8,25},{9,... | collective-permute-start | bytes 712712 | tf_op jit(solution)/shard_map/ppermute | solution.py:32
  41.3 0.5 collective-permute-start.24
  41.9 1.3 %collective-permute-start.25 = (bf16[32,3712]{1,0:T(8,128)(2,1)S(1)}, bf16[32,3712]{1,0:T(8,128)(2,1)S(1)}, u32[]{:S(2)}, u32[]{:S(2)}) collective-permute-start(bf16[32,3712]{1,0:T(8,128)(2,1)S(1)} %reshape.34.refs_0_), channel_id=1, source_target_pairs={{0,1},{1,0},{2,3},{3,2},{4,5},{5,4},{6,7},{7,6},{8,9},{9,8},{10,11... | collective-permute-start | bytes 712712 | tf_op jit(solution)/shard_map/ppermute | solution.py:32
  43.3 5.9 %collective-permute-done.23.refs_1_ = bf16[32,3712]{1,0:T(8,128)(2,1)S(1)} collective-permute-done((bf16[32,3712]{1,0:T(8,128)(2,1)S(1)}, bf16[32,3712]{1,0:T(8,128)(2,1)S(1)}, u32[]{:S(2)}, u32[]{:S(2)}) %collective-permute-start.23) | collective-permute-done | bytes 237600 | tf_op jit(solution)/shard_map/ppermute | solution.py:32
  49.2 3.9 %collective-permute-done.24.refs_2_ = bf16[32,3712]{1,0:T(8,128)(2,1)S(1)} collective-permute-done((bf16[32,3712]{1,0:T(8,128)(2,1)S(1)}, bf16[32,3712]{1,0:T(8,128)(2,1)S(1)}, u32[]{:S(2)}, u32[]{:S(2)}) %collective-permute-start.24) | collective-permute-done | bytes 237600 | tf_op jit(solution)/shard_map/ppermute | solution.py:32
  53.1 0.7 collective-permute-done.25.refs_3_
  53.9 0.5 collective-permute-start.29
  54.4 1.1 %add_convert_fusion.8 = (bf16[16,3584]{1,0:T(8,128)(2,1)S(1)}, bf16[16,3584]{1,0:T(8,128)(2,1)S(1)}, bf16[16,3584]{1,0:T(8,128)(2,1)S(1)}) fusion(bf16[64,3584]{1,0:T(8,128)(2,1)S(1)} %collective-permute-done.13, bf16[64,3584]{1,0:T(8,128)(2,1)} %get-tuple-element.14), kind=kLoop, calls=%fused_computation.9 | loop fusion | flops 688128 | bytes 1032192 | tf_op jit(solution)/shard_map/convert_element_type | solution.py:275
  55.5 1.5 %collective-permute-start.1 = (bf16[576,128]{1,0:T(8,128)(2,1)S(1)}, bf16[576,128]{1,0:T(8,128)(2,1)S(1)}, u32[]{:S(2)}, u32[]{:S(2)}) collective-permute-start(bf16[576,128]{1,0:T(8,128)(2,1)S(1)} %get-tuple-element.26), channel_id=1, source_target_pairs={{0,16},{1,17},{2,18},{3,19},{4,20},{5,21},{6,22},{7,23},{8,24},{9,... | collective-permute-start | bytes 442376 | tf_op jit(solution)/shard_map/ppermute | solution.py:32
  57.1 1.9 %collective-permute-start.14 = (bf16[16,3584]{1,0:T(8,128)(2,1)S(1)}, bf16[16,3584]{1,0:T(8,128)(2,1)S(1)}, u32[]{:S(2)}, u32[]{:S(2)}) collective-permute-start(bf16[16,3584]{1,0:T(8,128)(2,1)S(1)} %get-tuple-element.22), channel_id=1, source_target_pairs={{0,17},{1,16},{2,19},{3,18},{4,21},{5,20},{6,23},{7,22},{8,25},{9,... | collective-permute-start | bytes 344072 | tf_op jit(solution)/shard_map/ppermute | solution.py:32
  59.0 0.5 collective-permute-start.15
  59.5 1.1 %collective-permute-start.16 = (bf16[16,3584]{1,0:T(8,128)(2,1)S(1)}, bf16[16,3584]{1,0:T(8,128)(2,1)S(1)}, u32[]{:S(2)}, u32[]{:S(2)}) collective-permute-start(bf16[16,3584]{1,0:T(8,128)(2,1)S(1)} %get-tuple-element.23), channel_id=1, source_target_pairs={{0,1},{1,0},{2,3},{3,2},{4,5},{5,4},{6,7},{7,6},{8,9},{9,8},{10,11... | collective-permute-start | bytes 344072 | tf_op jit(solution)/shard_map/ppermute | solution.py:32
  60.7 8.7 %expert.3 = (bf16[128,3584]{1,0:T(8,128)(2,1)}, bf16[128,3584]{1,0:T(8,128)(2,1)}) custom-call(s32[1]{0:T(128)} %bitcast.7.column_ref, bf16[32,3712]{1,0:T(8,128)(2,1)} %copy-done.1, bf16[32,3712]{1,0:T(8,128)(2,1)} %copy-done.4, bf16[32,3712]{1,0:T(8,128)(2,1)} %copy-done.5, bf16[32,3712]{1,0:T(8,128)(2,1)} %copy-done.6, bf16[32,3712]{1,0:T(8,128)(2,1)} %copy-done.7, ...), custom_call_target="tpu_custom_call" | custom-call | flops 2818572288 | bytes 14680064 | tf_op jit(solution)/shard_map/expert/pallas_call | solution.py:245
  69.6 0.6 copy-done.12
  70.2 7.0 %attention.1 = (bf16[3,4,128,512]{3,2,1,0:T(8,128)(2,1)}, bf16[4,576,128]{2,1,0:T(8,128)(2,1)}) custom-call(s32[4]{0:T(128)} %lengths_ref.3, s32[16]{0:T(128)} %reshape.29.plan_ref, s32[1]{0:T(128)} %bitcast.group_ref, bf16[3,4,576,128]{3,2,1,0:T(8,128)(2,1)} %bitcast.17, bf16[4,576,128]{2,1,0:T(8,128)(2,1)} %bitcast.16, bf16[3,4,576]{2,1,0:T(4,128)(2,1)} %entries_ref.3, ...), custom_call_target="tpu_custom_call" | custom-call | flops 427819008 | bytes 4718592 | tf_op jit(solution)/shard_map/attention/pallas_call | solution.py:147
  77.3 1.0 add_convert_fusion.5
  78.4 1.9 %collective-permute-start.31 = (bf16[32,3584]{1,0:T(8,128)(2,1)S(1)}, bf16[32,3584]{1,0:T(8,128)(2,1)S(1)}, u32[]{:S(2)}, u32[]{:S(2)}) collective-permute-start(bf16[32,3584]{1,0:T(8,128)(2,1)S(1)} %get-tuple-element.19), channel_id=1, source_target_pairs={{0,17},{1,16},{2,19},{3,18},{4,21},{5,20},{6,23},{7,22},{8,25},{9,... | collective-permute-start | bytes 688136 | tf_op jit(solution)/shard_map/ppermute | solution.py:32
  80.3 0.5 collective-permute-start.32
  80.9 1.1 %collective-permute-start.33 = (bf16[32,3584]{1,0:T(8,128)(2,1)S(1)}, bf16[32,3584]{1,0:T(8,128)(2,1)S(1)}, u32[]{:S(2)}, u32[]{:S(2)}) collective-permute-start(bf16[32,3584]{1,0:T(8,128)(2,1)S(1)} %get-tuple-element.20), channel_id=1, source_target_pairs={{0,1},{1,0},{2,3},{3,2},{4,5},{5,4},{6,7},{7,6},{8,9},{9,8},{10,11... | collective-permute-start | bytes 688136 | tf_op jit(solution)/shard_map/ppermute | solution.py:32
  82.0 1.4 %collective-permute-start.17 = (bf16[4,3584]{1,0:T(4,128)(2,1)S(1)}, bf16[4,3584]{1,0:T(4,128)(2,1)S(1)}, u32[]{:S(2)}, u32[]{:S(2)}) collective-permute-start(bf16[4,3584]{1,0:T(4,128)(2,1)S(1)} %get-tuple-element.31), channel_id=1, source_target_pairs={{0,6},{1,7},{2,4},{3,5},{4,2},{5,3},{6,0},{7,1},{8,14},{9,15},{10,... | collective-permute-start | bytes 86024 | tf_op jit(solution)/shard_map/ppermute | solution.py:32
  83.6 4.2 %collective-permute-done.31 = bf16[32,3584]{1,0:T(8,128)(2,1)S(1)} collective-permute-done((bf16[32,3584]{1,0:T(8,128)(2,1)S(1)}, bf16[32,3584]{1,0:T(8,128)(2,1)S(1)}, u32[]{:S(2)}, u32[]{:S(2)}) %collective-permute-start.31) | collective-permute-done | bytes 229408 | tf_op jit(solution)/shard_map/ppermute | solution.py:32
  87.9 3.9 %collective-permute-done.32 = bf16[32,3584]{1,0:T(8,128)(2,1)S(1)} collective-permute-done((bf16[32,3584]{1,0:T(8,128)(2,1)S(1)}, bf16[32,3584]{1,0:T(8,128)(2,1)S(1)}, u32[]{:S(2)}, u32[]{:S(2)}) %collective-permute-start.32) | collective-permute-done | bytes 229408 | tf_op jit(solution)/shard_map/ppermute | solution.py:32
  91.8 0.5 collective-permute-done.33
  92.5 1.4 %collective-permute-start.34 = (bf16[8,3584]{1,0:T(8,128)(2,1)S(1)}, bf16[8,3584]{1,0:T(8,128)(2,1)S(1)}, u32[]{:S(2)}, u32[]{:S(2)}) collective-permute-start(bf16[8,3584]{1,0:T(8,128)(2,1)S(1)} %get-tuple-element.28), channel_id=1, source_target_pairs={{0,6},{1,7},{2,4},{3,5},{4,2},{5,3},{6,0},{7,1},{8,14},{9,15},{10,... | collective-permute-start | bytes 172040 | tf_op jit(solution)/shard_map/ppermute | solution.py:32
  94.0 2.9 %collective-permute-start.36 = (bf16[8,3584]{1,0:T(8,128)(2,1)S(1)}, bf16[8,3584]{1,0:T(8,128)(2,1)S(1)}, u32[]{:S(2)}, u32[]{:S(2)}) collective-permute-start(bf16[8,3584]{1,0:T(8,128)(2,1)S(1)} %get-tuple-element.29), channel_id=1, source_target_pairs={{0,2},{1,3},{2,0},{3,1},{4,6},{5,7},{6,4},{7,5},{8,10},{9,11},{10,... | collective-permute-start | bytes 172040 | tf_op jit(solution)/shard_map/ppermute | solution.py:32
  97.0 2.2 %collective-permute-done.34 = bf16[8,3584]{1,0:T(8,128)(2,1)S(1)} collective-permute-done((bf16[8,3584]{1,0:T(8,128)(2,1)S(1)}, bf16[8,3584]{1,0:T(8,128)(2,1)S(1)}, u32[]{:S(2)}, u32[]{:S(2)}) %collective-permute-start.34) | collective-permute-done | bytes 57376 | tf_op jit(solution)/shard_map/ppermute | solution.py:32
  99.2 1.5 %collective-permute-done.35 = bf16[8,3584]{1,0:T(8,128)(2,1)S(1)} collective-permute-done((bf16[8,3584]{1,0:T(8,128)(2,1)S(1)}, bf16[8,3584]{1,0:T(8,128)(2,1)S(1)}, u32[]{:S(2)}, u32[]{:S(2)}) %collective-permute-start.35) | collective-permute-done | bytes 57376 | tf_op jit(solution)/shard_map/ppermute | solution.py:32
  100.7 0.7 pad_maximum_fusion.2
  (92 shorter events, 1.6 us)
Async XLA Ops:
  2.4 7.1 %collective-permute-start.3 = (bf16[1,4,3712]{2,1,0:T(4,128)(2,1)}, bf16[1,4,3712]{2,1,0:T(4,128)(2,1)S(1)}, u32[]{:S(2)}, u32[]{:S(2)}) collective-permute-start(bf16[1,4,3712]{2,1,0:T(4,128)(2,1)} %get-tuple-element.13), channel_id=1, source_target_pairs={{0,6},{1,7},{2,4},{3,5},{4,2},{5,3},{6,0},{7,1},{8,14},{9,15},{10,... | collective-permute-start | bytes 89096 | tf_op jit(solution)/shard_map/ppermute | solution.py:32
  7.4 5.0 %collective-permute-start.4 = (bf16[1,4,3712]{2,1,0:T(4,128)(2,1)}, bf16[1,4,3712]{2,1,0:T(4,128)(2,1)S(1)}, u32[]{:S(2)}, u32[]{:S(2)}) collective-permute-start(bf16[1,4,3712]{2,1,0:T(4,128)(2,1)} %get-tuple-element.13), channel_id=1, source_target_pairs={{0,4},{1,5},{2,6},{3,7},{4,0},{5,1},{6,2},{7,3},{8,12},{9,13},{10,... | collective-permute-start | bytes 89096 | tf_op jit(solution)/shard_map/ppermute | solution.py:32
  7.4 5.0 %collective-permute-start.5 = (bf16[1,4,3712]{2,1,0:T(4,128)(2,1)}, bf16[1,4,3712]{2,1,0:T(4,128)(2,1)S(1)}, u32[]{:S(2)}, u32[]{:S(2)}) collective-permute-start(bf16[1,4,3712]{2,1,0:T(4,128)(2,1)} %get-tuple-element.13), channel_id=1, source_target_pairs={{0,2},{1,3},{2,0},{3,1},{4,6},{5,7},{6,4},{7,5},{8,10},{9,11},{10,... | collective-permute-start | bytes 89096 | tf_op jit(solution)/shard_map/ppermute | solution.py:32
  13.3 17.8 %copy-start.3 = (bf16[16,3712]{1,0:T(8,128)(2,1)}, bf16[16,3712]{1,0:T(8,128)(2,1)S(1)}, u32[]{:S(2)}) copy-start(bf16[16,3712]{1,0:T(8,128)(2,1)S(1)} %reshape.32.refs_0_) | copy-start | bytes 356356
  13.3 5.9 %collective-permute-start.6 = (bf16[16,3712]{1,0:T(8,128)(2,1)S(1)}, bf16[16,3712]{1,0:T(8,128)(2,1)S(1)}, u32[]{:S(2)}, u32[]{:S(2)}) collective-permute-start(bf16[16,3712]{1,0:T(8,128)(2,1)S(1)} %reshape.32.refs_0_), channel_id=1, source_target_pairs={{0,17},{1,16},{2,19},{3,18},{4,21},{5,20},{6,23},{7,22},{8,25},{9,... | collective-permute-start | bytes 356360 | tf_op jit(solution)/shard_map/ppermute | solution.py:32
  15.8 4.8 %collective-permute-start.7 = (bf16[16,3712]{1,0:T(8,128)(2,1)S(1)}, bf16[16,3712]{1,0:T(8,128)(2,1)S(1)}, u32[]{:S(2)}, u32[]{:S(2)}) collective-permute-start(bf16[16,3712]{1,0:T(8,128)(2,1)S(1)} %reshape.32.refs_0_), channel_id=1, source_target_pairs={{0,16},{1,17},{2,18},{3,19},{4,20},{5,21},{6,22},{7,23},{8,24},{9,... | collective-permute-start | bytes 356360 | tf_op jit(solution)/shard_map/ppermute | solution.py:32
  16.4 4.8 %collective-permute-start.8 = (bf16[16,3712]{1,0:T(8,128)(2,1)S(1)}, bf16[16,3712]{1,0:T(8,128)(2,1)S(1)}, u32[]{:S(2)}, u32[]{:S(2)}) collective-permute-start(bf16[16,3712]{1,0:T(8,128)(2,1)S(1)} %reshape.32.refs_0_), channel_id=1, source_target_pairs={{0,1},{1,0},{2,3},{3,2},{4,5},{5,4},{6,7},{7,6},{8,9},{9,8},{10,11... | collective-permute-start | bytes 356360 | tf_op jit(solution)/shard_map/ppermute | solution.py:32
  16.9 11.0 %collective-permute-start.9 = (bf16[16,3712]{1,0:T(8,128)(2,1)S(1)}, bf16[16,3712]{1,0:T(8,128)(2,1)S(1)}, u32[]{:S(2)}, u32[]{:S(2)}) collective-permute-start(bf16[16,3712]{1,0:T(8,128)(2,1)S(1)} %reshape.32.refs_0_), channel_id=1, source_target_pairs={{0,8},{1,9},{2,10},{3,11},{4,12},{5,13},{6,14},{7,15},{8,0},{9,1},... | collective-permute-start | bytes 356360 | tf_op jit(solution)/shard_map/ppermute | solution.py:32
  19.2 11.9 %copy-start.14 = (bf16[16,3712]{1,0:T(8,128)(2,1)}, bf16[16,3712]{1,0:T(8,128)(2,1)S(1)}, u32[]{:S(2)}) copy-start(bf16[16,3712]{1,0:T(8,128)(2,1)S(1)} %collective-permute-done.6.refs_1_) | copy-start | bytes 356356
  19.2 9.5 %collective-permute-start.10 = (bf16[16,3712]{1,0:T(8,128)(2,1)S(1)}, bf16[16,3712]{1,0:T(8,128)(2,1)S(1)}, u32[]{:S(2)}, u32[]{:S(2)}) collective-permute-start(bf16[16,3712]{1,0:T(8,128)(2,1)S(1)} %collective-permute-done.6.refs_1_), channel_id=1, source_target_pairs={{0,8},{1,9},{2,10},{3,11},{4,12},{5,13},{6,14},{7,15},{8,0},{9,1},... | collective-permute-start | bytes 356360 | tf_op jit(solution)/shard_map/ppermute | solution.py:32
  20.7 10.5 %copy-start.15 = (bf16[16,3712]{1,0:T(8,128)(2,1)}, bf16[16,3712]{1,0:T(8,128)(2,1)S(1)}, u32[]{:S(2)}) copy-start(bf16[16,3712]{1,0:T(8,128)(2,1)S(1)} %collective-permute-done.7.refs_2_) | copy-start | bytes 356356
  20.7 10.4 %collective-permute-start.11 = (bf16[16,3712]{1,0:T(8,128)(2,1)S(1)}, bf16[16,3712]{1,0:T(8,128)(2,1)S(1)}, u32[]{:S(2)}, u32[]{:S(2)}) collective-permute-start(bf16[16,3712]{1,0:T(8,128)(2,1)S(1)} %collective-permute-done.7.refs_2_), channel_id=1, source_target_pairs={{0,8},{1,9},{2,10},{3,11},{4,12},{5,13},{6,14},{7,15},{8,0},{9,1},... | collective-permute-start | bytes 356360 | tf_op jit(solution)/shard_map/ppermute | solution.py:32
  21.2 9.9 %copy-start.16 = (bf16[16,3712]{1,0:T(8,128)(2,1)}, bf16[16,3712]{1,0:T(8,128)(2,1)S(1)}, u32[]{:S(2)}) copy-start(bf16[16,3712]{1,0:T(8,128)(2,1)S(1)} %collective-permute-done.8.refs_3_) | copy-start | bytes 356356
  21.2 9.9 %collective-permute-start.12 = (bf16[16,3712]{1,0:T(8,128)(2,1)S(1)}, bf16[16,3712]{1,0:T(8,128)(2,1)S(1)}, u32[]{:S(2)}, u32[]{:S(2)}) collective-permute-start(bf16[16,3712]{1,0:T(8,128)(2,1)S(1)} %collective-permute-done.8.refs_3_), channel_id=1, source_target_pairs={{0,8},{1,9},{2,10},{3,11},{4,12},{5,13},{6,14},{7,15},{8,0},{9,1},... | collective-permute-start | bytes 356360 | tf_op jit(solution)/shard_map/ppermute | solution.py:32
  21.2 18.1 %collective-permute-start.20 = (bf16[2,4,3712]{2,1,0:T(4,128)(2,1)}, bf16[2,4,3712]{2,1,0:T(4,128)(2,1)S(1)}, u32[]{:S(2)}, u32[]{:S(2)}) collective-permute-start(bf16[2,4,3712]{2,1,0:T(4,128)(2,1)} %get-tuple-element.16), channel_id=1, source_target_pairs={{0,6},{1,7},{2,4},{3,5},{4,2},{5,3},{6,0},{7,1},{8,14},{9,15},{10,... | collective-permute-start | bytes 178184 | tf_op jit(solution)/shard_map/ppermute | solution.py:32
  27.9 11.4 %collective-permute-start.21 = (bf16[2,4,3712]{2,1,0:T(4,128)(2,1)}, bf16[2,4,3712]{2,1,0:T(4,128)(2,1)S(1)}, u32[]{:S(2)}, u32[]{:S(2)}) collective-permute-start(bf16[2,4,3712]{2,1,0:T(4,128)(2,1)} %get-tuple-element.16), channel_id=1, source_target_pairs={{0,4},{1,5},{2,6},{3,7},{4,0},{5,1},{6,2},{7,3},{8,12},{9,13},{10,... | collective-permute-start | bytes 178184 | tf_op jit(solution)/shard_map/ppermute | solution.py:32
  28.8 10.6 %collective-permute-start.22 = (bf16[2,4,3712]{2,1,0:T(4,128)(2,1)}, bf16[2,4,3712]{2,1,0:T(4,128)(2,1)S(1)}, u32[]{:S(2)}, u32[]{:S(2)}) collective-permute-start(bf16[2,4,3712]{2,1,0:T(4,128)(2,1)} %get-tuple-element.16), channel_id=1, source_target_pairs={{0,2},{1,3},{2,0},{3,1},{4,6},{5,7},{6,4},{7,5},{8,10},{9,11},{10,... | collective-permute-start | bytes 178184 | tf_op jit(solution)/shard_map/ppermute | solution.py:32
  31.8 7.6 %copy-start.21 = (bf16[2,4,3712]{2,1,0:T(4,128)(2,1)S(1)}, bf16[2,4,3712]{2,1,0:T(4,128)(2,1)}, u32[]{:S(2)}) copy-start(bf16[2,4,3712]{2,1,0:T(4,128)(2,1)} %get-tuple-element.16) | copy-start | bytes 178180
  31.8 11.4 %copy-start = (bf16[3,576,128]{2,1,0:T(8,128)(2,1)S(1)}, bf16[3,576,128]{2,1,0:T(8,128)(2,1)}, u32[]{:S(2)}) copy-start(bf16[3,576,128]{2,1,0:T(8,128)(2,1)} %outgoing.1) | copy-start | bytes 1327108
  39.3 14.6 %collective-permute-start.13 = (bf16[64,3584]{1,0:T(8,128)(2,1)}, bf16[64,3584]{1,0:T(8,128)(2,1)S(1)}, u32[]{:S(2)}, u32[]{:S(2)}) collective-permute-start(bf16[64,3584]{1,0:T(8,128)(2,1)} %get-tuple-element.15), channel_id=1, source_target_pairs={{0,8},{1,9},{2,10},{3,11},{4,12},{5,13},{6,14},{7,15},{8,0},{9,1},... | collective-permute-start | bytes 1376264 | tf_op jit(solution)/shard_map/ppermute | solution.py:32
  39.6 21.0 %copy-start.1 = (bf16[32,3712]{1,0:T(8,128)(2,1)}, bf16[32,3712]{1,0:T(8,128)(2,1)S(1)}, u32[]{:S(2)}) copy-start(bf16[32,3712]{1,0:T(8,128)(2,1)S(1)} %reshape.34.refs_0_) | copy-start | bytes 712708
  39.6 9.6 %collective-permute-start.23 = (bf16[32,3712]{1,0:T(8,128)(2,1)S(1)}, bf16[32,3712]{1,0:T(8,128)(2,1)S(1)}, u32[]{:S(2)}, u32[]{:S(2)}) collective-permute-start(bf16[32,3712]{1,0:T(8,128)(2,1)S(1)} %reshape.34.refs_0_), channel_id=1, source_target_pairs={{0,17},{1,16},{2,19},{3,18},{4,21},{5,20},{6,23},{7,22},{8,25},{9,... | collective-permute-start | bytes 712712 | tf_op jit(solution)/shard_map/ppermute | solution.py:32
  41.3 11.8 %collective-permute-start.24 = (bf16[32,3712]{1,0:T(8,128)(2,1)S(1)}, bf16[32,3712]{1,0:T(8,128)(2,1)S(1)}, u32[]{:S(2)}, u32[]{:S(2)}) collective-permute-start(bf16[32,3712]{1,0:T(8,128)(2,1)S(1)} %reshape.34.refs_0_), channel_id=1, source_target_pairs={{0,16},{1,17},{2,18},{3,19},{4,20},{5,21},{6,22},{7,23},{8,24},{9,... | collective-permute-start | bytes 712712 | tf_op jit(solution)/shard_map/ppermute | solution.py:32
  41.9 12.0 %collective-permute-start.25 = (bf16[32,3712]{1,0:T(8,128)(2,1)S(1)}, bf16[32,3712]{1,0:T(8,128)(2,1)S(1)}, u32[]{:S(2)}, u32[]{:S(2)}) collective-permute-start(bf16[32,3712]{1,0:T(8,128)(2,1)S(1)} %reshape.34.refs_0_), channel_id=1, source_target_pairs={{0,1},{1,0},{2,3},{3,2},{4,5},{5,4},{6,7},{7,6},{8,9},{9,8},{10,11... | collective-permute-start | bytes 712712 | tf_op jit(solution)/shard_map/ppermute | solution.py:32
  43.2 12.2 %collective-permute-start = (bf16[576,128]{1,0:T(8,128)(2,1)S(1)}, bf16[576,128]{1,0:T(8,128)(2,1)S(1)}, u32[]{:S(2)}, u32[]{:S(2)}) collective-permute-start(bf16[576,128]{1,0:T(8,128)(2,1)S(1)} %get-tuple-element.27), channel_id=1, source_target_pairs={{0,8},{1,9},{2,10},{3,11},{4,12},{5,13},{6,14},{7,15},{8,0},{9,1},... | collective-permute-start | bytes 442376 | tf_op jit(solution)/shard_map/ppermute | solution.py:32
  49.2 11.4 %copy-start.4 = (bf16[32,3712]{1,0:T(8,128)(2,1)}, bf16[32,3712]{1,0:T(8,128)(2,1)S(1)}, u32[]{:S(2)}) copy-start(bf16[32,3712]{1,0:T(8,128)(2,1)S(1)} %collective-permute-done.23.refs_1_) | copy-start | bytes 712708
  49.2 7.8 %collective-permute-start.26 = (bf16[32,3712]{1,0:T(8,128)(2,1)S(1)}, bf16[32,3712]{1,0:T(8,128)(2,1)S(1)}, u32[]{:S(2)}, u32[]{:S(2)}) collective-permute-start(bf16[32,3712]{1,0:T(8,128)(2,1)S(1)} %reshape.34.refs_0_), channel_id=1, source_target_pairs={{0,8},{1,9},{2,10},{3,11},{4,12},{5,13},{6,14},{7,15},{8,0},{9,1},... | collective-permute-start | bytes 712712 | tf_op jit(solution)/shard_map/ppermute | solution.py:32
  53.1 7.5 %copy-start.5 = (bf16[32,3712]{1,0:T(8,128)(2,1)}, bf16[32,3712]{1,0:T(8,128)(2,1)S(1)}, u32[]{:S(2)}) copy-start(bf16[32,3712]{1,0:T(8,128)(2,1)S(1)} %collective-permute-done.24.refs_2_) | copy-start | bytes 712708
  53.1 3.9 %collective-permute-start.27 = (bf16[32,3712]{1,0:T(8,128)(2,1)S(1)}, bf16[32,3712]{1,0:T(8,128)(2,1)S(1)}, u32[]{:S(2)}, u32[]{:S(2)}) collective-permute-start(bf16[32,3712]{1,0:T(8,128)(2,1)S(1)} %collective-permute-done.23.refs_1_), channel_id=1, source_target_pairs={{0,8},{1,9},{2,10},{3,11},{4,12},{5,13},{6,14},{7,15},{8,0},{9,1},... | collective-permute-start | bytes 712712 | tf_op jit(solution)/shard_map/ppermute | solution.py:32
  53.9 5.1 %collective-permute-start.28 = (bf16[32,3712]{1,0:T(8,128)(2,1)S(1)}, bf16[32,3712]{1,0:T(8,128)(2,1)S(1)}, u32[]{:S(2)}, u32[]{:S(2)}) collective-permute-start(bf16[32,3712]{1,0:T(8,128)(2,1)S(1)} %collective-permute-done.24.refs_2_), channel_id=1, source_target_pairs={{0,8},{1,9},{2,10},{3,11},{4,12},{5,13},{6,14},{7,15},{8,0},{9,1},... | collective-permute-start | bytes 712712 | tf_op jit(solution)/shard_map/ppermute | solution.py:32
  53.9 5.6 %collective-permute-start.29 = (bf16[32,3712]{1,0:T(8,128)(2,1)S(1)}, bf16[32,3712]{1,0:T(8,128)(2,1)S(1)}, u32[]{:S(2)}, u32[]{:S(2)}) collective-permute-start(bf16[32,3712]{1,0:T(8,128)(2,1)S(1)} %collective-permute-done.25.refs_3_), channel_id=1, source_target_pairs={{0,8},{1,9},{2,10},{3,11},{4,12},{5,13},{6,14},{7,15},{8,0},{9,1},... | collective-permute-start | bytes 712712 | tf_op jit(solution)/shard_map/ppermute | solution.py:32
  55.5 14.1 %copy-start.11 = (bf16[576,128]{1,0:T(8,128)(2,1)}, bf16[576,128]{1,0:T(8,128)(2,1)S(1)}, u32[]{:S(2)}) copy-start(bf16[576,128]{1,0:T(8,128)(2,1)S(1)} %collective-permute-done.rest_0_) | copy-start | bytes 442372
  55.5 13.9 %collective-permute-start.1 = (bf16[576,128]{1,0:T(8,128)(2,1)S(1)}, bf16[576,128]{1,0:T(8,128)(2,1)S(1)}, u32[]{:S(2)}, u32[]{:S(2)}) collective-permute-start(bf16[576,128]{1,0:T(8,128)(2,1)S(1)} %get-tuple-element.26), channel_id=1, source_target_pairs={{0,16},{1,17},{2,18},{3,19},{4,20},{5,21},{6,22},{7,23},{8,24},{9,... | collective-permute-start | bytes 442376 | tf_op jit(solution)/shard_map/ppermute | solution.py:32
  57.0 12.5 %collective-permute-start.2 = (bf16[576,128]{1,0:T(8,128)(2,1)S(1)}, bf16[576,128]{1,0:T(8,128)(2,1)S(1)}, u32[]{:S(2)}, u32[]{:S(2)}) collective-permute-start(bf16[576,128]{1,0:T(8,128)(2,1)S(1)} %get-tuple-element.25), channel_id=1, source_target_pairs={{0,24},{1,25},{2,26},{3,27},{4,28},{5,29},{6,30},{7,31},{8,16},{9,... | collective-permute-start | bytes 442376 | tf_op jit(solution)/shard_map/ppermute | solution.py:32
  57.1 20.2 %collective-permute-start.14 = (bf16[16,3584]{1,0:T(8,128)(2,1)S(1)}, bf16[16,3584]{1,0:T(8,128)(2,1)S(1)}, u32[]{:S(2)}, u32[]{:S(2)}) collective-permute-start(bf16[16,3584]{1,0:T(8,128)(2,1)S(1)} %get-tuple-element.22), channel_id=1, source_target_pairs={{0,17},{1,16},{2,19},{3,18},{4,21},{5,20},{6,23},{7,22},{8,25},{9,... | collective-permute-start | bytes 344072 | tf_op jit(solution)/shard_map/ppermute | solution.py:32
  59.0 18.2 %collective-permute-start.15 = (bf16[16,3584]{1,0:T(8,128)(2,1)S(1)}, bf16[16,3584]{1,0:T(8,128)(2,1)S(1)}, u32[]{:S(2)}, u32[]{:S(2)}) collective-permute-start(bf16[16,3584]{1,0:T(8,128)(2,1)S(1)} %get-tuple-element.24), channel_id=1, source_target_pairs={{0,16},{1,17},{2,18},{3,19},{4,20},{5,21},{6,22},{7,23},{8,24},{9,... | collective-permute-start | bytes 344072 | tf_op jit(solution)/shard_map/ppermute | solution.py:32
  59.5 17.7 %collective-permute-start.16 = (bf16[16,3584]{1,0:T(8,128)(2,1)S(1)}, bf16[16,3584]{1,0:T(8,128)(2,1)S(1)}, u32[]{:S(2)}, u32[]{:S(2)}) collective-permute-start(bf16[16,3584]{1,0:T(8,128)(2,1)S(1)} %get-tuple-element.23), channel_id=1, source_target_pairs={{0,1},{1,0},{2,3},{3,2},{4,5},{5,4},{6,7},{7,6},{8,9},{9,8},{10,11... | collective-permute-start | bytes 344072 | tf_op jit(solution)/shard_map/ppermute | solution.py:32
  69.4 8.8 %copy-start.2 = (bf16[128,3584]{1,0:T(8,128)(2,1)S(1)}, bf16[128,3584]{1,0:T(8,128)(2,1)}, u32[]{:S(2)}) copy-start(bf16[128,3584]{1,0:T(8,128)(2,1)} %get-tuple-element.17) | copy-start | bytes 2752516
  69.5 8.8 %collective-permute-start.30 = (bf16[128,3584]{1,0:T(8,128)(2,1)}, bf16[128,3584]{1,0:T(8,128)(2,1)S(1)}, u32[]{:S(2)}, u32[]{:S(2)}) collective-permute-start(bf16[128,3584]{1,0:T(8,128)(2,1)} %get-tuple-element.18), channel_id=1, source_target_pairs={{0,8},{1,9},{2,10},{3,11},{4,12},{5,13},{6,14},{7,15},{8,0},{9,1},... | collective-permute-start | bytes 2752520 | tf_op jit(solution)/shard_map/ppermute | solution.py:32
  78.4 9.4 %collective-permute-start.31 = (bf16[32,3584]{1,0:T(8,128)(2,1)S(1)}, bf16[32,3584]{1,0:T(8,128)(2,1)S(1)}, u32[]{:S(2)}, u32[]{:S(2)}) collective-permute-start(bf16[32,3584]{1,0:T(8,128)(2,1)S(1)} %get-tuple-element.19), channel_id=1, source_target_pairs={{0,17},{1,16},{2,19},{3,18},{4,21},{5,20},{6,23},{7,22},{8,25},{9,... | collective-permute-start | bytes 688136 | tf_op jit(solution)/shard_map/ppermute | solution.py:32
  80.3 11.5 %collective-permute-start.32 = (bf16[32,3584]{1,0:T(8,128)(2,1)S(1)}, bf16[32,3584]{1,0:T(8,128)(2,1)S(1)}, u32[]{:S(2)}, u32[]{:S(2)}) collective-permute-start(bf16[32,3584]{1,0:T(8,128)(2,1)S(1)} %get-tuple-element.21), channel_id=1, source_target_pairs={{0,16},{1,17},{2,18},{3,19},{4,20},{5,21},{6,22},{7,23},{8,24},{9,... | collective-permute-start | bytes 688136 | tf_op jit(solution)/shard_map/ppermute | solution.py:32
  80.9 11.4 %collective-permute-start.33 = (bf16[32,3584]{1,0:T(8,128)(2,1)S(1)}, bf16[32,3584]{1,0:T(8,128)(2,1)S(1)}, u32[]{:S(2)}, u32[]{:S(2)}) collective-permute-start(bf16[32,3584]{1,0:T(8,128)(2,1)S(1)} %get-tuple-element.20), channel_id=1, source_target_pairs={{0,1},{1,0},{2,3},{3,2},{4,5},{5,4},{6,7},{7,6},{8,9},{9,8},{10,11... | collective-permute-start | bytes 688136 | tf_op jit(solution)/shard_map/ppermute | solution.py:32
  82.0 12.0 %collective-permute-start.17 = (bf16[4,3584]{1,0:T(4,128)(2,1)S(1)}, bf16[4,3584]{1,0:T(4,128)(2,1)S(1)}, u32[]{:S(2)}, u32[]{:S(2)}) collective-permute-start(bf16[4,3584]{1,0:T(4,128)(2,1)S(1)} %get-tuple-element.31), channel_id=1, source_target_pairs={{0,6},{1,7},{2,4},{3,5},{4,2},{5,3},{6,0},{7,1},{8,14},{9,15},{10,... | collective-permute-start | bytes 86024 | tf_op jit(solution)/shard_map/ppermute | solution.py:32
  83.4 13.5 %collective-permute-start.18 = (bf16[4,3584]{1,0:T(4,128)(2,1)S(1)}, bf16[4,3584]{1,0:T(4,128)(2,1)S(1)}, u32[]{:S(2)}, u32[]{:S(2)}) collective-permute-start(bf16[4,3584]{1,0:T(4,128)(2,1)S(1)} %get-tuple-element.33), channel_id=1, source_target_pairs={{0,4},{1,5},{2,6},{3,7},{4,0},{5,1},{6,2},{7,3},{8,12},{9,13},{10,... | collective-permute-start | bytes 86024 | tf_op jit(solution)/shard_map/ppermute | solution.py:32
  87.8 9.1 %collective-permute-start.19 = (bf16[4,3584]{1,0:T(4,128)(2,1)S(1)}, bf16[4,3584]{1,0:T(4,128)(2,1)S(1)}, u32[]{:S(2)}, u32[]{:S(2)}) collective-permute-start(bf16[4,3584]{1,0:T(4,128)(2,1)S(1)} %get-tuple-element.32), channel_id=1, source_target_pairs={{0,2},{1,3},{2,0},{3,1},{4,6},{5,7},{6,4},{7,5},{8,10},{9,11},{10,... | collective-permute-start | bytes 86024 | tf_op jit(solution)/shard_map/ppermute | solution.py:32
  92.5 6.7 %collective-permute-start.34 = (bf16[8,3584]{1,0:T(8,128)(2,1)S(1)}, bf16[8,3584]{1,0:T(8,128)(2,1)S(1)}, u32[]{:S(2)}, u32[]{:S(2)}) collective-permute-start(bf16[8,3584]{1,0:T(8,128)(2,1)S(1)} %get-tuple-element.28), channel_id=1, source_target_pairs={{0,6},{1,7},{2,4},{3,5},{4,2},{5,3},{6,0},{7,1},{8,14},{9,15},{10,... | collective-permute-start | bytes 172040 | tf_op jit(solution)/shard_map/ppermute | solution.py:32
  93.9 6.7 %collective-permute-start.35 = (bf16[8,3584]{1,0:T(8,128)(2,1)S(1)}, bf16[8,3584]{1,0:T(8,128)(2,1)S(1)}, u32[]{:S(2)}, u32[]{:S(2)}) collective-permute-start(bf16[8,3584]{1,0:T(8,128)(2,1)S(1)} %get-tuple-element.30), channel_id=1, source_target_pairs={{0,4},{1,5},{2,6},{3,7},{4,0},{5,1},{6,2},{7,3},{8,12},{9,13},{10,... | collective-permute-start | bytes 172040 | tf_op jit(solution)/shard_map/ppermute | solution.py:32
  94.0 6.6 %collective-permute-start.36 = (bf16[8,3584]{1,0:T(8,128)(2,1)S(1)}, bf16[8,3584]{1,0:T(8,128)(2,1)S(1)}, u32[]{:S(2)}, u32[]{:S(2)}) collective-permute-start(bf16[8,3584]{1,0:T(8,128)(2,1)S(1)} %get-tuple-element.29), channel_id=1, source_target_pairs={{0,2},{1,3},{2,0},{3,1},{4,6},{5,7},{6,4},{7,5},{8,10},{9,11},{10,... | collective-permute-start | bytes 172040 | tf_op jit(solution)/shard_map/ppermute | solution.py:32
  (11 other events, 25.1 us)

commit v3 on v0

v3 whole, which is shorter than its diff:
```python
from functools import partial

import jax
import jax.numpy as jnp
from jax import lax
from jax.experimental import pallas as pl
from jax.experimental.pallas import tpu as pltpu
from jax.sharding import PartitionSpec as P

ROPE = 64


SCORE_SCALE = 192.0 ** (-0.5)


BOTH = ("grp", "ep")


GAIN_LANES = 128


PLANE_GROUPS = ((1, 2, 3), (0,))


SMALL_COST = pl.CostEstimate(flops=1, bytes_accessed=1, transcendentals=0)


LARGE_COST = pl.CostEstimate(flops=1, bytes_accessed=100_000_000, transcendentals=0)


KERNEL_PARAMS = pltpu.CompilerParams(vmem_limit_bytes=12 * 1024 * 1024)


def across(values, grp_flip, ep_flip):
    groups, columns = lax.axis_size("grp"), lax.axis_size("ep")
    pairs = [
        (g * columns + e, (g ^ grp_flip) * columns + (e ^ ep_flip))
        for g in range(groups)
        for e in range(columns)
    ]
    return lax.ppermute(values, BOTH, pairs)


DONE = jax.ShapeDtypeStruct((8, 128), jnp.int32)


ANYWHERE = pl.BlockSpec(memory_space=pl.ANY)


def ignoring(kernel, first, count):
    return lambda *refs: kernel(*refs[:first], *refs[first + count :])


def gate_kernel(count, *refs):
    pass


def gate(arrays, others):
    count = len(arrays)
    return pl.pallas_call(
        partial(gate_kernel, count),
        in_specs=[ANYWHERE] * (count + len(others)),
        out_specs=[ANYWHERE] * count,
        out_shape=[jax.ShapeDtypeStruct(array.shape, array.dtype) for array in arrays],
        input_output_aliases={number: number for number in range(count)},
        compiler_params=KERNEL_PARAMS,
        cost_estimate=SMALL_COST,
        name="gate",
    )(*arrays, *others)


def plan_entry(plan_ref, group, entry, field):
    return plan_ref[entry, field, group]


def insert_entries(keys, entries, filled, trace, steps, traces):
    rows, capacity = entries.shape[0], keys.shape[1]
    row_index = lax.broadcasted_iota(jnp.int32, (rows, capacity), 0)
    column_index = lax.broadcasted_iota(jnp.int32, (rows, capacity), 1)
    place = ((column_index - filled) * traces + trace == row_index) & (column_index >= filled)
    spread = lax.dot_general(
        entries,
        place.astype(jnp.bfloat16),
        (((0,), (0,)), ((), ())),
        preferred_element_type=jnp.float32,
    )
    column_index = lax.broadcasted_iota(jnp.int32, keys.shape, 1)
    new = (column_index >= filled) & (column_index < filled + steps)
    return jnp.where(new, spread, keys.astype(jnp.float32)).astype(jnp.bfloat16)


def outgoing_slot(number, plan_ref, group_ref):
    group = group_ref[0]
    partner = group ^ (number + 1)
    slot = jnp.int32(0)
    for entry in range(2):
        goes = plan_entry(plan_ref, group, entry, 1) == partner
        slot = jnp.where(goes, plan_entry(plan_ref, group, entry, 0), slot)
    return slot


def gain_lanes(ids, gains):
    lane = lax.broadcasted_iota(jnp.int32, (ids.shape[0], GAIN_LANES), 1)
    dense = jnp.zeros(lane.shape, jnp.float32)
    for choice in range(ids.shape[1]):
        place = ids[:, choice : choice + 1]
        named = (lane >= 3 * place) & (lane < 3 * place + 3)
        dense = dense + jnp.where(named, gains[:, choice : choice + 1], 0.0)
    high = dense.astype(jnp.bfloat16).astype(jnp.float32)
    rest = dense - high
    middle = rest.astype(jnp.bfloat16).astype(jnp.float32)
    part = lane % 3
    parts = jnp.where(part == 0, high, jnp.where(part == 1, middle, rest - middle))
    return parts.astype(jnp.bfloat16)


def prepare_kernel(others, lengths_ref, plan_ref, group_ref, *refs):
    cache_hbm, sources, refs = refs[0], refs[1:5], refs[5:]
    rows_ref, entries_ref, out_refs = refs[0], refs[1], refs[2 : 2 + others]
    slots_ref, targets, stack_ref, semaphores = refs[2 + others], refs[3 + others : -2], refs[-2], refs[-1]
    copies = [
        pltpu.make_async_copy(source, target, semaphores.at[others + number])
        for number, (source, target) in enumerate(zip(sources, targets))
    ]
    slots = [outgoing_slot(number, plan_ref, group_ref) for number in range(others)]
    for number, slot in enumerate(slots):
        copies.append(
            pltpu.make_async_copy(
                cache_hbm.at[slot], slots_ref.at[number], semaphores.at[number]
            )
        )
    for copy in copies:
        copy.start()
    for copy in copies:
        copy.wait()
    ids_ref, gains_ref, tokens_ref, new_entries_ref = targets
    steps, traces, width = tokens_ref.shape
    group = group_ref[0]
    for step in range(steps):
        rows_ref[step, :, :width] = tokens_ref[step]
        rows_ref[step, :, width:] = gain_lanes(ids_ref[step, group], gains_ref[step, group])
    stack_ref[...] = jnp.zeros_like(stack_ref)
    for step in range(steps):
        stack_ref[step * traces : (step + 1) * traces, :] = new_entries_ref[step].astype(jnp.float32)
    entries = stack_ref[...].astype(jnp.bfloat16)
    entries_ref[...] = entries
    for number, slot in enumerate(slots):
        out_refs[number][...] = insert_entries(
            slots_ref[number], entries, lengths_ref[slot], slot, steps, traces
        )


def prepare(cache, new_entries, lengths, plan, group, moe_input, expert_ids, route_gains):
    traces, width, capacity = cache.shape
    steps, _, model_width = moe_input.shape
    others = lax.axis_size("grp") - 1
    entry_rows = -(-steps * traces // 16) * 16
    smem, vmem = pl.BlockSpec(memory_space=pltpu.SMEM), pl.BlockSpec(memory_space=pltpu.VMEM)
    sources = [cache, expert_ids, route_gains, moe_input, new_entries]
    rows, entries, *leaving = pl.pallas_call(
        partial(prepare_kernel, others),
        in_specs=[smem] * 3 + [pl.BlockSpec(memory_space=pltpu.HBM)] * len(sources),
        out_specs=[vmem] * (others + 2),
        out_shape=[
            jax.ShapeDtypeStruct((steps, traces, model_width + GAIN_LANES), moe_input.dtype),
            jax.ShapeDtypeStruct((entry_rows, width), cache.dtype),
        ]
        + [jax.ShapeDtypeStruct((width, capacity), cache.dtype)] * others,
        scratch_shapes=[pltpu.VMEM((others, width, capacity), cache.dtype)]
        + [pltpu.VMEM(source.shape, source.dtype) for source in sources[1:]]
        + [
            pltpu.VMEM((entry_rows, width), jnp.float32),
            pltpu.SemaphoreType.DMA((others + len(sources) - 1,)),
        ],
        compiler_params=KERNEL_PARAMS,
        cost_estimate=LARGE_COST,
        name="prepare",
    )(
        pltpu.with_memory_space_constraint(lengths, pltpu.HBM),
        pltpu.with_memory_space_constraint(plan, pltpu.HBM),
        group,
        *(pltpu.with_memory_space_constraint(source, pltpu.HBM) for source in sources),
    )
    return rows, entries, leaving


def line_kernel(*refs):
    pieces, out_ref = refs[:-1], refs[-1]
    rows = [piece[step].astype(jnp.float32) for piece in pieces for step in range(piece.shape[0])]
    out_ref[...] = jnp.concatenate(rows, axis=0).astype(out_ref.dtype)


def line_rows(pieces, others):
    steps, traces, lanes = pieces[0].shape
    vmem = pl.BlockSpec(memory_space=pltpu.VMEM)
    return pl.pallas_call(
        ignoring(line_kernel, 0, len(others)),
        in_specs=[ANYWHERE] * len(others) + [vmem] * len(pieces),
        out_specs=vmem,
        out_shape=jax.ShapeDtypeStruct((len(pieces) * steps * traces, lanes), pieces[0].dtype),
        cost_estimate=LARGE_COST,
        compiler_params=KERNEL_PARAMS,
        name="line_rows",
    )(*others, *pieces)


def line_sums_kernel(*refs):
    steps, traces, _ = refs[-1].shape
    count = len(refs) - refs[0].shape[0] // (steps * traces)
    total = refs[0][...].astype(jnp.float32)
    for term_ref in refs[1:count]:
        total = total + term_ref[...].astype(jnp.float32)
    for number, out_ref in enumerate(refs[count:]):
        for step in range(steps):
            first = (number * steps + step) * traces
            out_ref[step] = total[first : first + traces].astype(out_ref.dtype)


def line_sums(terms, steps, traces, pieces, others):
    lanes = terms[0].shape[1]
    vmem = pl.BlockSpec(memory_space=pltpu.VMEM)
    return pl.pallas_call(
        ignoring(line_sums_kernel, 0, len(others)),
        in_specs=[ANYWHERE] * len(others) + [vmem] * len(terms),
        out_specs=[vmem] * pieces,
        out_shape=[jax.ShapeDtypeStruct((steps, traces, lanes), terms[0].dtype)] * pieces,
        cost_estimate=LARGE_COST,
        compiler_params=KERNEL_PARAMS,
        name="line_sums",
    )(*others, *terms)


def attention_kernel(
    block, lengths_ref, plan_ref, group_ref, queries_ref, cache_ref, entries_ref, *rest
):
    received_refs, (contexts_ref, migrated_ref, done_ref) = rest[:-3], rest[-3:]
    done_ref[...] = jnp.zeros_like(done_ref)
    grid_index = pl.program_id(0)
    step_count, _, width, heads = queries_ref.shape
    latent = contexts_ref.shape[3]
    traces = block * pl.num_programs(0)
    group = group_ref[0]
    for member in range(block):
        trace = grid_index * block + member
        filled = lengths_ref[trace]
        keys = insert_entries(
            cache_ref[member], entries_ref[...], filled, trace, step_count, traces
        )
        migrated = keys
        for number, received_ref in enumerate(received_refs):
            partner = group ^ (number + 1)
            for entry in range(2):
                lands = (plan_entry(plan_ref, partner, entry, 1) == group) & (
                    plan_entry(plan_ref, group, entry, 0) == trace
                )
                migrated = jnp.where(lands, received_ref[...], migrated)
        migrated_ref[member] = migrated
        key_rows = jnp.transpose(keys)
        flat_queries = jnp.concatenate(
            [queries_ref[s, member] for s in range(step_count)], axis=1
        )
        scores = jnp.dot(key_rows, flat_queries, preferred_element_type=jnp.float32) * SCORE_SCALE
        position = lax.broadcasted_iota(jnp.int32, scores.shape, 0)
        step_of_column = lax.broadcasted_iota(jnp.int32, scores.shape, 1) // heads
        scores = jnp.where(position <= filled + step_of_column, scores, -jnp.inf)
        exp_scores = jnp.exp(scores - jnp.max(scores, axis=0, keepdims=True))
        weights = (exp_scores / jnp.sum(exp_scores, axis=0, keepdims=True)).astype(jnp.bfloat16)
        context = lax.dot_general(
            weights,
            key_rows[:, :latent],
            (((0,), (0,)), ((), ())),
            preferred_element_type=jnp.float32,
        )
        contexts_ref[:, member] = context.astype(jnp.bfloat16).reshape(step_count, heads, latent)


def fetch_kernel(*refs):
    refs, done_ref, refs_semaphores = refs[:-2], refs[-2], refs[-1]
    done_ref[...] = jnp.zeros_like(done_ref)
    refs = (*refs, refs_semaphores)
    count = (len(refs) - 1) // 2
    copies = [
        pltpu.make_async_copy(source.at[0], target, refs[-1].at[number])
        for number, (source, target) in enumerate(zip(refs[:count], refs[count:-1]))
    ]
    for copy in copies:
        copy.start()
    for copy in copies:
        copy.wait()


def fetch(weights, others):
    weights = [pltpu.with_memory_space_constraint(weight, pltpu.HBM) for weight in weights]
    return pl.pallas_call(
        ignoring(fetch_kernel, 0, len(others)),
        in_specs=[ANYWHERE] * len(others)
        + [pl.BlockSpec(memory_space=pltpu.HBM)] * len(weights),
        out_specs=[pl.BlockSpec(memory_space=pltpu.VMEM)] * (len(weights) + 1),
        out_shape=[pltpu.VMEM(weight.shape[1:], weight.dtype) for weight in weights] + [DONE],
        scratch_shapes=[pltpu.SemaphoreType.DMA((len(weights),))],
        cost_estimate=LARGE_COST,
        compiler_params=KERNEL_PARAMS,
        name="fetch",
    )(*others, *weights)


def attention(queries, cache, entries, lengths, plan, group, received, others=(), block=2):
    step_count, traces, width, heads = queries.shape
    capacity = cache.shape[2]
    latent = width - ROPE
    whole = lambda shape: pl.BlockSpec(shape, lambda t, *_: (0,) * len(shape))
    return pl.pallas_call(
        ignoring(partial(attention_kernel, block), 3, len(others)),
        grid_spec=pltpu.PrefetchScalarGridSpec(
            num_scalar_prefetch=3,
            grid=(traces // block,),
            in_specs=[ANYWHERE] * len(others)
            + [
                pl.BlockSpec((step_count, block, width, heads), lambda t, *_: (0, t, 0, 0)),
                pl.BlockSpec((block, width, capacity), lambda t, *_: (t, 0, 0)),
                whole(entries.shape),
            ]
            + [whole((width, capacity))] * len(received),
            out_specs=[
                pl.BlockSpec((step_count, block, heads, latent), lambda t, *_: (0, t, 0, 0)),
                pl.BlockSpec((block, width, capacity), lambda t, *_: (t, 0, 0)),
                whole(DONE.shape),
            ],
        ),
        out_shape=[
            jax.ShapeDtypeStruct((step_count, traces, heads, latent), jnp.bfloat16),
            jax.ShapeDtypeStruct(cache.shape, jnp.bfloat16),
            DONE,
        ],
        cost_estimate=LARGE_COST,
        compiler_params=KERNEL_PARAMS,
        name="attention",
    )(lengths, plan, group, *others, queries, cache, entries, *received)


def expert_kernel(column_ref, *refs):
    count = (len(refs) - 4) // 2
    pieces, (gate_ref, up_ref, down_ref) = refs[:count], refs[count : count + 3]
    out_refs, hidden_ref = refs[count + 3 : -1], refs[-1]
    width, hidden_width = gate_ref.shape
    rows = pieces[0].shape[0]
    gain_parts = jnp.concatenate([piece[:, width:] for piece in pieces], axis=0).astype(jnp.float32)
    lane = lax.broadcasted_iota(jnp.int32, gain_parts.shape, 1)
    first_lane = column_ref[0] * 3
    gain = jnp.sum(
        jnp.where((lane >= first_lane) & (lane < first_lane + 3), gain_parts, 0.0),
        axis=1,
        keepdims=True,
    )
    tokens = jnp.concatenate([piece[:, :width] for piece in pieces], axis=0)
    gate_out = jnp.dot(tokens, gate_ref[...], preferred_element_type=jnp.float32)
    up_out = jnp.dot(tokens, up_ref[...], preferred_element_type=jnp.float32)
    hidden = gate_out / (1.0 + jnp.exp(-gate_out)) * up_out * gain
    hidden_ref[...] = hidden.astype(jnp.bfloat16)
    tile = 512 if width % 512 == 0 else width
    for first in range(0, width, tile):
        columns = slice(first, first + tile)
        products = jnp.dot(
            hidden_ref[...], down_ref[:, columns], preferred_element_type=jnp.float32
        ).astype(jnp.bfloat16)
        for number, out_ref in enumerate(out_refs):
            out_ref[:, columns] = products[number * rows : (number + 1) * rows]


def expert(pieces, weights, others=()):
    width, hidden_width = weights[0].shape
    rows = pieces[0].shape[0]
    vmem = pl.BlockSpec(memory_space=pltpu.VMEM)
    column = lax.axis_index("ep").astype(jnp.int32).reshape(1)
    return pl.pallas_call(
        ignoring(expert_kernel, 0, len(others)),
        in_specs=[ANYWHERE] * len(others)
        + [pl.BlockSpec(memory_space=pltpu.SMEM)]
        + [vmem] * (len(pieces) + 3),
        out_specs=[vmem] * len(pieces),
        out_shape=[jax.ShapeDtypeStruct((rows, width), jnp.bfloat16)] * len(pieces),
        scratch_shapes=[pltpu.VMEM((len(pieces) * rows, hidden_width), jnp.bfloat16)],
        cost_estimate=LARGE_COST,
        compiler_params=pltpu.CompilerParams(vmem_limit_bytes=28 * 1024 * 1024),
        name="expert",
    )(*others, column, *pieces, *weights)


def add_up(terms):
    total = terms[0].astype(jnp.float32)
    for term in terms[1:]:
        total = total + term.astype(jnp.float32)
    return total.astype(jnp.bfloat16)


def dense_layer(
    queries, cache, new_entries, lengths, moe_input, expert_ids, route_gains, weights, plan, group
):
    groups, experts = lax.axis_size("grp"), lax.axis_size("ep")
    far_flips = [(0, 2 * z) for z in range(1, experts // 2)][::-1]
    near_flips = [(2 * x, y) for x in range(groups // 2) for y in range(2)][1:]
    steps, trace_count, width = moe_input.shape
    rows, entries, leaving = prepare(
        cache, new_entries, lengths, plan, group, moe_input, expert_ids, route_gains
    )
    received = [across(leaving[flip - 1], flip, 0) for flip in range(1, groups)]
    line = [rows] + [across(rows, *flip) for flip in far_flips]
    own_line = line_rows(line, received)
    plane = [across(own_line, *flip) for flip in near_flips]
    *weights, fetched = fetch(weights, [own_line])
    plane = [own_line] + list(lax.optimization_barrier((plane, fetched))[0])
    other_plane = [across(piece, 1, 0) for piece in plane]
    terms, sums = [None] * len(plane), []
    for members in PLANE_GROUPS:
        pieces = [half[member] for half in (plane, other_plane) for member in members]
        outputs = expert(pieces, weights, sums)
        for member, own, other in zip(members, outputs, outputs[len(members) :]):
            term = add_up([own, across(other, 1, 0)])
            terms[member] = across(term, *near_flips[member - 1]) if member else term
            sums = sums + [term]
    contexts, migrated_cache, attended = attention(
        queries, cache, entries, lengths, plan, group, received, sums
    )
    parts = line_sums(terms, steps, trace_count, len(line), [attended])
    moe_output = add_up(
        [parts[0]] + [across(part, *flip) for part, flip in zip(parts[1:], far_flips)]
    )
    return contexts, migrated_cache, moe_output


def routed_layer(
    queries, cache, new_entries, lengths, moe_input, expert_ids, route_gains, weights, plan, group
):
    _, entries, leaving = prepare(
        cache, new_entries, lengths, plan, group, moe_input, expert_ids, route_gains
    )
    received = [across(leaving[flip - 1], flip, 0) for flip in range(1, lax.axis_size("grp"))]
    contexts, migrated_cache, _ = attention(
        queries, cache, entries, lengths, plan, group, received
    )
    moe_output = routed_experts(moe_input, expert_ids, route_gains, *weights)
    return contexts, migrated_cache, moe_output


def slot_tables(route_ids, route_gains, expert_count, slot_count):
    token_count, top_count = route_ids.shape
    flat_ids = route_ids.reshape(-1)
    row_list = jnp.arange(flat_ids.shape[0], dtype=jnp.int32)
    same_expert = flat_ids[:, None] == flat_ids[None, :]
    earlier = row_list[None, :] < row_list[:, None]
    slot_rank = jnp.sum(jnp.where(same_expert & earlier, 1, 0), axis=1).astype(jnp.int32)
    slot_index = flat_ids * slot_count + slot_rank
    slot_hot = (
        slot_index[:, None] == jnp.arange(expert_count * slot_count, dtype=jnp.int32)[None, :]
    ).astype(jnp.float32)
    token_hot = (
        (row_list // top_count)[:, None] == jnp.arange(token_count, dtype=jnp.int32)[None, :]
    ).astype(jnp.float32)
    dispatch = jnp.dot(slot_hot.T, token_hot, precision=lax.Precision.HIGHEST)
    combine = jnp.dot(
        token_hot.T, slot_hot * route_gains.reshape(-1)[:, None], precision=lax.Precision.HIGHEST
    )
    return (dispatch, combine)


def expert_rows(token_rows, gate_slice, up_slice, down_slice):
    gate_out = jnp.dot(token_rows, gate_slice, preferred_element_type=jnp.float32)
    up_out = jnp.dot(token_rows, up_slice, preferred_element_type=jnp.float32)
    hidden = (jax.nn.silu(gate_out) * up_out).astype(jnp.bfloat16)
    return jnp.dot(hidden, down_slice, preferred_element_type=jnp.float32).astype(jnp.bfloat16)


def routed_experts(moe_input, expert_ids, route_gains, w_gate, w_up, w_down):
    groups, experts = lax.axis_size("grp"), lax.axis_size("ep")
    trace_count, model_width = moe_input.shape[1:]
    top_count = expert_ids.shape[3]
    slot_count = max(2, trace_count * top_count // experts)
    tables = partial(slot_tables, expert_count=experts, slot_count=slot_count)
    moe_list = []
    for step_index in range(moe_input.shape[0]):
        column_ids = expert_ids[step_index]
        column_gains = route_gains[step_index]
        dispatch_all, combine_all = jax.vmap(tables)(column_ids, column_gains)
        column_tokens = lax.all_gather(moe_input[step_index][None], "grp", axis=0, tiled=True)
        packed = jnp.einsum(
            "gsj,gjd->sgd",
            dispatch_all.astype(jnp.bfloat16),
            column_tokens,
            preferred_element_type=jnp.float32,
        )
        packed = packed.astype(jnp.bfloat16).reshape(experts, slot_count * groups, model_width)
        exchanged = lax.all_to_all(packed, "ep", split_axis=0, concat_axis=0, tiled=True)
        flat_rows = exchanged.reshape(-1, exchanged.shape[-1])
        partial_out = expert_rows(flat_rows, w_gate[0], w_up[0], w_down[0]).reshape(exchanged.shape)
        returned = lax.all_to_all(partial_out, "ep", split_axis=0, concat_axis=0, tiled=True)
        returned = returned.reshape(experts * slot_count, groups, model_width).astype(jnp.float32)
        token_terms = jnp.einsum(
            "gjs,sgd->gjd", combine_all, returned, precision=lax.Precision.HIGHEST
        )
        summed = lax.psum_scatter(
            token_terms.astype(jnp.bfloat16), "grp", scatter_dimension=0, tiled=True
        ).astype(jnp.float32)
        moe_list.append(summed[0].astype(jnp.bfloat16))
    return jnp.stack(moe_list)


def body(
    queries,
    cache,
    new_entries,
    lengths,
    moe_input,
    expert_ids,
    route_gains,
    w_gate,
    w_up,
    w_down,
    plan,
):
    queries, cache = jnp.swapaxes(queries, 2, 3), jnp.swapaxes(cache, 1, 2)
    plan, group = jnp.transpose(plan[:, 0], (1, 2, 0)), lax.axis_index("grp").reshape(1)
    every_expert = expert_ids.shape[3] == lax.axis_size("ep")
    layer = dense_layer if every_expert else routed_layer
    contexts, migrated_cache, moe_output = layer(
        queries,
        cache,
        new_entries,
        lengths,
        moe_input,
        expert_ids,
        route_gains,
        (w_gate, w_up, w_down),
        plan,
        group,
    )
    return contexts, jnp.swapaxes(migrated_cache, 1, 2), moe_output


def solution(mesh):
    return jax.shard_map(
        body,
        mesh=mesh,
        in_specs=(
            P(None, ("grp", "ep"), None, None),
            P(("grp", "ep"), None, None),
            P(None, ("grp", "ep"), None),
            P(("grp", "ep")),
            P(None, ("grp", "ep"), None),
            P(None, None, "ep", None),
            P(None, None, "ep", None),
            P("ep", None, "grp"),
            P("ep", None, "grp"),
            P("ep", "grp", None),
            P(None, "ep", None, None),
        ),
        out_specs=(
            P(None, ("grp", "ep"), None, None),
            P(("grp", "ep"), None, None),
            P(None, ("grp", "ep"), None),
        ),
        check_vma=False,
    )
```

time: 227 us -> 80.5 us (0.35)
  waiting for transfers between devices: 92.8 us -> 38.7 us
  matrix products: 50 us -> 0 us
  local copies, waits for them, and re-layouts: 19.6 us -> 0.03 us
  Pallas kernels: 0 us -> 17.6 us
  blocking collectives: 17.2 us -> 0 us
  between operations: 14.3 us -> 0.81 us
  other arithmetic: 6.98 us -> 1.06 us
  starting transfers between devices: 24.6 us -> 22.1 us
    all_to_all x6 -> x0, waiting for transfers between devices: 62.4 us -> none  [the longest x3 33.6 us: body(): lax.all_to_all(packed, 'ep', split_axis=0, concat_axis=0, tiled=True)]
    dot_general x26 -> x0, matrix products: 50 us -> none  [the longest x3 16.4 us: expert_rows(): jnp.dot(hidden, down_slice, preferred_element_type=jnp.float32)]
    ppermute x0 -> x23, waiting for transfers between devices: none -> 38.7 us  [across(): return lax.ppermute(values, BOTH, pairs)]
    unnamed x3 -> x0, waiting for transfers between devices: 30.4 us -> none
    all_to_all x6 -> x0, starting transfers between devices: 24.5 us -> none  [the longest x3 13.6 us: body(): lax.all_to_all(packed, 'ep', split_axis=0, concat_axis=0, tiled=True)]
    ppermute x0 -> x23, starting transfers between devices: none -> 22.1 us  [across(): return lax.ppermute(values, BOTH, pairs)]
    pallas_call x0 -> x7, Pallas kernels: none -> 17.6 us  [the longest x2 5.45 us: expert(): pl.pallas_call(ignoring(expert_kernel, 0, len(others)), in_specs=[ANYWHER...]
    all_gather x3 -> x0, blocking collectives: 17.2 us -> none  [body(): lax.all_gather(moe_input[step_index][None], 'grp', axis=0, tiled=True)]
  transfers between devices with their start and end apart: 8 -> 23, of which waited for: 7 -> 13; matrix products, arithmetic and copies ran while one was open for 29% -> 0% of each run, Pallas kernels for 0% -> 12%
where the time goes in v3:
time: 80.5 us; the launch traced here: 80.3 us
  waiting for transfers between devices  38.7 us (48%)
  starting transfers between devices  22.1 us (27%)
  Pallas kernels  17.6 us (22%)
  other arithmetic  1.06 us (1%)
  between operations  0.81 us (1%)
    ppermute x23, waiting for transfers between devices, across(): return lax.ppermute(values, BOTH, pairs)  38.7 us
    ppermute x23, starting transfers between devices, across(): return lax.ppermute(values, BOTH, pairs)  22.1 us
    pallas_call x2, Pallas kernels, expert(): pl.pallas_call(ignoring(expert_kernel, 0, len(others)), in_specs=[ANYWHER...  5.45 us
    pallas_call x1, Pallas kernels, fetch(): pl.pallas_call(ignoring(fetch_kernel, 0, len(others)), in_specs=[ANYWHERE...  4.82 us
    pallas_call x1, Pallas kernels, attention(): pl.pallas_call(ignoring(partial(attention_kernel, block), 3, len(others))...  4.77 us
    pallas_call x1, Pallas kernels, prepare(): pl.pallas_call(partial(prepare_kernel, others), in_specs=[smem] * 3 + [pl...  2.26 us
  transfers between devices with their start and end apart: 23, of which 13 were waited for; matrix products, arithmetic and copies ran while one was open for 0% of the time, Pallas kernels for 12%

profile of v3, /device:TPU:0, one launch (start us, length us, event | category | flops | bytes accessed | tf_op | source)
XLA Modules:
  0.0 80.3 jit_solution(13062493866976414111)
XLA Ops:
  0.6 2.3 %prepare.1 = (bf16[3,4,3712]{2,1,0:T(4,128)(2,1)S(1)}, bf16[16,576]{1,0:T(8,128)(2,1)S(1)}, bf16[576,128]{1,0:T(8,128)(2,1)S(1)}, bf16[576,128]{1,0:T(8,128)(2,1)S(1)}, bf16[576,128]{1,0:T(8,128)(2,1)S(1)}) custom-call(s32[4]{0:T(128)} %refs_0_.1, s32[2,2,4]{2,1,0:T(2,128)} %bitcast.11, s32[1]{0:T(128)} %bitcast.2.group_ref.refs_2_, ...), custom_call_target="tpu_custom_call" | custom-call | flops 1 | bytes 100000000 | tf_op jit(solution)/shard_map/prepare/pallas_call | solution.py:160
  2.9 5.1 %collective-permute-start.3 = (bf16[3,4,3712]{2,1,0:T(4,128)(2,1)S(1)}, bf16[3,4,3712]{2,1,0:T(4,128)(2,1)S(1)}, u32[]{:S(2)}, u32[]{:S(2)}) collective-permute-start(bf16[3,4,3712]{2,1,0:T(4,128)(2,1)S(1)} %get-tuple-element.32.refs_3_), channel_id=1, source_target_pairs={{0,6},{1,7},{2,4},{3,5},{4,2},{5,3},{6,0},{7,1},{8,14},{9,15},{10,... | collective-permute-start | bytes 267272 | tf_op jit(solution)/shard_map/ppermute | solution.py:41
  8.0 1.5 %collective-permute-start.1 = (bf16[576,128]{1,0:T(8,128)(2,1)S(1)}, bf16[576,128]{1,0:T(8,128)(2,1)S(1)}, u32[]{:S(2)}, u32[]{:S(2)}) collective-permute-start(bf16[576,128]{1,0:T(8,128)(2,1)S(1)} %get-tuple-element.30), channel_id=1, source_target_pairs={{0,16},{1,17},{2,18},{3,19},{4,20},{5,21},{6,22},{7,23},{8,24},{9,... | collective-permute-start | bytes 442376 | tf_op jit(solution)/shard_map/ppermute | solution.py:41
  9.5 0.4 collective-permute-start.2
  9.9 0.8 %collective-permute-done.3.refs_4_ = bf16[3,4,3712]{2,1,0:T(4,128)(2,1)S(1)} collective-permute-done((bf16[3,4,3712]{2,1,0:T(4,128)(2,1)S(1)}, bf16[3,4,3712]{2,1,0:T(4,128)(2,1)S(1)}, u32[]{:S(2)}, u32[]{:S(2)}) %collective-permute-start.3) | collective-permute-done | bytes 89120 | tf_op jit(solution)/shard_map/ppermute | solution.py:41
  10.7 1.5 %collective-permute-start.5 = (bf16[3,4,3712]{2,1,0:T(4,128)(2,1)S(1)}, bf16[3,4,3712]{2,1,0:T(4,128)(2,1)S(1)}, u32[]{:S(2)}, u32[]{:S(2)}) collective-permute-start(bf16[3,4,3712]{2,1,0:T(4,128)(2,1)S(1)} %get-tuple-element.32.refs_3_), channel_id=1, source_target_pairs={{0,2},{1,3},{2,0},{3,1},{4,6},{5,7},{6,4},{7,5},{8,10},{9,11},{10,... | collective-permute-start | bytes 267272 | tf_op jit(solution)/shard_map/ppermute | solution.py:41
  12.2 4.3 %collective-permute-done.4.refs_5_ = bf16[3,4,3712]{2,1,0:T(4,128)(2,1)S(1)} collective-permute-done((bf16[3,4,3712]{2,1,0:T(4,128)(2,1)S(1)}, bf16[3,4,3712]{2,1,0:T(4,128)(2,1)S(1)}, u32[]{:S(2)}, u32[]{:S(2)}) %collective-permute-start.4) | collective-permute-done | bytes 89120 | tf_op jit(solution)/shard_map/ppermute | solution.py:41
  16.6 0.5 collective-permute-done.5.refs_6_
  17.1 0.1 line_rows.1.refs_0_.refs_4_
  17.2 1.6 %collective-permute-start.6 = (bf16[48,3712]{1,0:T(8,128)(2,1)S(1)}, bf16[48,3712]{1,0:T(8,128)(2,1)S(1)}, u32[]{:S(2)}, u32[]{:S(2)}) collective-permute-start(bf16[48,3712]{1,0:T(8,128)(2,1)S(1)} %line_rows.1.refs_0_.refs_4_), channel_id=1, source_target_pairs={{0,1},{1,0},{2,3},{3,2},{4,5},{5,4},{6,7},{7,6},{8,9},{9,8},{10,11... | collective-permute-start | bytes 1069064 | tf_op jit(solution)/shard_map/ppermute | solution.py:41
  18.8 1.5 %collective-permute-start.7 = (bf16[48,3712]{1,0:T(8,128)(2,1)S(1)}, bf16[48,3712]{1,0:T(8,128)(2,1)S(1)}, u32[]{:S(2)}, u32[]{:S(2)}) collective-permute-start(bf16[48,3712]{1,0:T(8,128)(2,1)S(1)} %line_rows.1.refs_0_.refs_4_), channel_id=1, source_target_pairs={{0,16},{1,17},{2,18},{3,19},{4,20},{5,21},{6,22},{7,23},{8,24},{9,... | collective-permute-start | bytes 1069064 | tf_op jit(solution)/shard_map/ppermute | solution.py:41
  20.3 0.4 collective-permute-start.8
  20.8 6.9 %collective-permute-done.6.refs_1_ = bf16[48,3712]{1,0:T(8,128)(2,1)S(1)} collective-permute-done((bf16[48,3712]{1,0:T(8,128)(2,1)S(1)}, bf16[48,3712]{1,0:T(8,128)(2,1)S(1)}, u32[]{:S(2)}, u32[]{:S(2)}) %collective-permute-start.6) | collective-permute-done | bytes 356384 | tf_op jit(solution)/shard_map/ppermute | solution.py:41
  27.6 2.4 %collective-permute-done.7.refs_2_ = bf16[48,3712]{1,0:T(8,128)(2,1)S(1)} collective-permute-done((bf16[48,3712]{1,0:T(8,128)(2,1)S(1)}, bf16[48,3712]{1,0:T(8,128)(2,1)S(1)}, u32[]{:S(2)}, u32[]{:S(2)}) %collective-permute-start.7) | collective-permute-done | bytes 356384 | tf_op jit(solution)/shard_map/ppermute | solution.py:41
  30.1 6.4 %collective-permute-done.8.refs_3_ = bf16[48,3712]{1,0:T(8,128)(2,1)S(1)} collective-permute-done((bf16[48,3712]{1,0:T(8,128)(2,1)S(1)}, bf16[48,3712]{1,0:T(8,128)(2,1)S(1)}, u32[]{:S(2)}, u32[]{:S(2)}) %collective-permute-start.8) | collective-permute-done | bytes 356384 | tf_op jit(solution)/shard_map/ppermute | solution.py:41
  36.5 0.5 collective-permute-start.11
  37.0 4.8 %fetch.1 = (bf16[3584,512]{1,0:T(8,128)(2,1)S(1)}, bf16[3584,512]{1,0:T(8,128)(2,1)S(1)}, bf16[512,3584]{1,0:T(8,128)(2,1)S(1)}, s32[8,128]{1,0:T(8,128)}) custom-call(bf16[48,3712]{1,0:T(8,128)(2,1)S(1)} %line_rows.1.refs_0_.refs_4_, bf16[1,3584,512]{2,1,0:T(8,128)(2,1)} %refs_1_.3, bf16[1,3584,512]{2,1,0:T(8,128)(2,1)} %refs_2_.3, ...), custom_call_target="tpu_custom_call" | custom-call | flops 1 | bytes 100000000 | tf_op jit(solution)/shard_map/fetch/pallas_call | solution.py:294
  41.8 3.5 %expert.2 = (bf16[48,3584]{1,0:T(8,128)(2,1)S(1)}, bf16[48,3584]{1,0:T(8,128)(2,1)S(1)}, bf16[48,3584]{1,0:T(8,128)(2,1)S(1)}, bf16[48,3584]{1,0:T(8,128)(2,1)S(...) custom-call(s32[1]{0:T(128)} %bitcast.3.refs_0_.refs_3_, ...), custom_call_target="tpu_custom_call" | custom-call | flops 1 | bytes 100000000 | tf_op jit(solution)/shard_map/expert/pallas_call | solution.py:375
  45.3 0.6 collective-permute-start.14
  45.9 0.1 collective-permute-start.15
  46.0 0.4 collective-permute-start.13
  46.4 0.1 collective-permute-start.12
  46.5 0.7 collective-permute-done.14
  47.2 0.1 add_convert_fusion.1.refs_2_.refs_5_
  47.2 0.9 %collective-permute-done.13 = bf16[48,3584]{1,0:T(8,128)(2,1)S(1)} collective-permute-done((bf16[48,3584]{1,0:T(8,128)(2,1)S(1)}, bf16[48,3584]{1,0:T(8,128)(2,1)S(1)}, u32[]{:S(2)}, u32[]{:S(2)}) %collective-permute-start.13) | collective-permute-done | bytes 344096 | tf_op jit(solution)/shard_map/ppermute | solution.py:41
  48.2 0.1 add_convert_fusion.2.refs_1_.refs_4_
  48.3 0.4 collective-permute-done.12
  48.7 0.1 add_convert_fusion.3.refs_0_.refs_3_
  48.7 0.0 copy-start
  48.8 0.0 copy-start.1
  48.8 0.0 copy-start.2
  48.8 0.0 copy-start.3
  48.8 2.0 %expert.3 = (bf16[48,3584]{1,0:T(8,128)(2,1)S(1)}, bf16[48,3584]{1,0:T(8,128)(2,1)S(1)}) custom-call(bf16[48,3584]{1,0:T(8,128)(2,1)S(1)} %add_convert_fusion.3.refs_0_.refs_3_, bf16[48,3584]{1,0:T(8,128)(2,1)S(1)} %add_convert_fusion.2.refs_1_.refs_4_, bf16[48,3584]{1,0:T(8,128)(2,1)S(1)} %add_convert_fusion.1.refs_2_.refs_5_, s32[1]{0:T(128)} %bitcast.3.refs_0_.refs_3_, ...), custom_call_target="tpu_custom_call" | custom-call | flops 1 | bytes 100000000 | tf_op jit(solution)/shard_map/expert/pallas_call | solution.py:375
  50.8 0.4 collective-permute-start.16
  51.2 2.5 %collective-permute-start.19 = (bf16[48,3584]{1,0:T(8,128)(2,1)S(1)}, bf16[48,3584]{1,0:T(8,128)(2,1)S(1)}, u32[]{:S(2)}, u32[]{:S(2)}) collective-permute-start(bf16[48,3584]{1,0:T(8,128)(2,1)S(1)} %add_convert_fusion.1.refs_2_.refs_5_), channel_id=1, source_target_pairs={{0,17},{1,16},{2,19},{3,18},{4,21},{5,20},{6,23},{7,22},{8,25},{9,... | collective-permute-start | bytes 1032200 | tf_op jit(solution)/shard_map/ppermute | solution.py:41
  53.7 0.5 collective-permute-start.18
  54.2 0.5 collective-permute-start.17
  54.7 0.1 add_convert_fusion.refs_6_.refs_1_
  54.9 4.8 %attention.1 = (bf16[3,4,128,512]{3,2,1,0:T(8,128)(2,1)}, bf16[4,576,128]{2,1,0:T(8,128)(2,1)}, s32[8,128]{1,0:T(8,128)S(1)}) custom-call(s32[4]{0:T(128)S(1)} %copy-done.3, s32[2,2,4]{2,1,0:T(2,128)S(1)} %bitcast.12, s32[1]{0:T(128)} %bitcast.2.group_ref.refs_2_, bf16[48,3584]{1,0:T(8,128)(2,1)S(1)} %add_convert_fusion.3.refs_0_.refs_3_, ...), custom_call_target="tpu_custom_call" | custom-call | flops 1 | bytes 100000000 | tf_op jit(solution)/shard_map/attention/pallas_call | solution.py:312
  59.6 3.5 %collective-permute-done.19.refs_4_ = bf16[48,3584]{1,0:T(8,128)(2,1)S(1)} collective-permute-done((bf16[48,3584]{1,0:T(8,128)(2,1)S(1)}, bf16[48,3584]{1,0:T(8,128)(2,1)S(1)}, u32[]{:S(2)}, u32[]{:S(2)}) %collective-permute-start.19) | collective-permute-done | bytes 344096 | tf_op jit(solution)/shard_map/ppermute | solution.py:41
  63.1 6.6 %collective-permute-done.18.refs_3_ = bf16[48,3584]{1,0:T(8,128)(2,1)S(1)} collective-permute-done((bf16[48,3584]{1,0:T(8,128)(2,1)S(1)}, bf16[48,3584]{1,0:T(8,128)(2,1)S(1)}, u32[]{:S(2)}, u32[]{:S(2)}) %collective-permute-start.18) | collective-permute-done | bytes 344096 | tf_op jit(solution)/shard_map/ppermute | solution.py:41
  69.7 0.2 line_sums.1
  69.9 0.9 %collective-permute-start.20 = (bf16[3,4,3584]{2,1,0:T(4,128)(2,1)S(1)}, bf16[3,4,3584]{2,1,0:T(4,128)(2,1)S(1)}, u32[]{:S(2)}, u32[]{:S(2)}) collective-permute-start(bf16[3,4,3584]{2,1,0:T(4,128)(2,1)S(1)} %get-tuple-element.52), channel_id=1, source_target_pairs={{0,6},{1,7},{2,4},{3,5},{4,2},{5,3},{6,0},{7,1},{8,14},{9,15},{10,... | collective-permute-start | bytes 258056 | tf_op jit(solution)/shard_map/ppermute | solution.py:41
  70.8 0.4 collective-permute-start.21
  71.2 3.2 %collective-permute-start.22 = (bf16[3,4,3584]{2,1,0:T(4,128)(2,1)S(1)}, bf16[3,4,3584]{2,1,0:T(4,128)(2,1)S(1)}, u32[]{:S(2)}, u32[]{:S(2)}) collective-permute-start(bf16[3,4,3584]{2,1,0:T(4,128)(2,1)S(1)} %get-tuple-element.54), channel_id=1, source_target_pairs={{0,2},{1,3},{2,0},{3,1},{4,6},{5,7},{6,4},{7,5},{8,10},{9,11},{10,... | collective-permute-start | bytes 258056 | tf_op jit(solution)/shard_map/ppermute | solution.py:41
  74.4 2.8 %collective-permute-done.20 = bf16[3,4,3584]{2,1,0:T(4,128)(2,1)S(1)} collective-permute-done((bf16[3,4,3584]{2,1,0:T(4,128)(2,1)S(1)}, bf16[3,4,3584]{2,1,0:T(4,128)(2,1)S(1)}, u32[]{:S(2)}, u32[]{:S(2)}) %collective-permute-start.20) | collective-permute-done | bytes 86048 | tf_op jit(solution)/shard_map/ppermute | solution.py:41
  77.2 2.3 %collective-permute-done.21 = bf16[3,4,3584]{2,1,0:T(4,128)(2,1)S(1)} collective-permute-done((bf16[3,4,3584]{2,1,0:T(4,128)(2,1)S(1)}, bf16[3,4,3584]{2,1,0:T(4,128)(2,1)S(1)}, u32[]{:S(2)}, u32[]{:S(2)}) %collective-permute-start.21) | collective-permute-done | bytes 86048 | tf_op jit(solution)/shard_map/ppermute | solution.py:41
  79.6 0.7 add_convert_fusion.4
  (18 shorter events, 0.0 us)
Async XLA Ops:
  2.9 7.8 %collective-permute-start.3 = (bf16[3,4,3712]{2,1,0:T(4,128)(2,1)S(1)}, bf16[3,4,3712]{2,1,0:T(4,128)(2,1)S(1)}, u32[]{:S(2)}, u32[]{:S(2)}) collective-permute-start(bf16[3,4,3712]{2,1,0:T(4,128)(2,1)S(1)} %get-tuple-element.32.refs_3_), channel_id=1, source_target_pairs={{0,6},{1,7},{2,4},{3,5},{4,2},{5,3},{6,0},{7,1},{8,14},{9,15},{10,... | collective-permute-start | bytes 267272 | tf_op jit(solution)/shard_map/ppermute | solution.py:41
  8.0 9.1 %collective-permute-start = (bf16[576,128]{1,0:T(8,128)(2,1)S(1)}, bf16[576,128]{1,0:T(8,128)(2,1)S(1)}, u32[]{:S(2)}, u32[]{:S(2)}) collective-permute-start(bf16[576,128]{1,0:T(8,128)(2,1)S(1)} %get-tuple-element.29), channel_id=1, source_target_pairs={{0,8},{1,9},{2,10},{3,11},{4,12},{5,13},{6,14},{7,15},{8,0},{9,1},... | collective-permute-start | bytes 442376 | tf_op jit(solution)/shard_map/ppermute | solution.py:41
  8.0 9.1 %collective-permute-start.1 = (bf16[576,128]{1,0:T(8,128)(2,1)S(1)}, bf16[576,128]{1,0:T(8,128)(2,1)S(1)}, u32[]{:S(2)}, u32[]{:S(2)}) collective-permute-start(bf16[576,128]{1,0:T(8,128)(2,1)S(1)} %get-tuple-element.30), channel_id=1, source_target_pairs={{0,16},{1,17},{2,18},{3,19},{4,20},{5,21},{6,22},{7,23},{8,24},{9,... | collective-permute-start | bytes 442376 | tf_op jit(solution)/shard_map/ppermute | solution.py:41
  9.5 7.6 %collective-permute-start.2 = (bf16[576,128]{1,0:T(8,128)(2,1)S(1)}, bf16[576,128]{1,0:T(8,128)(2,1)S(1)}, u32[]{:S(2)}, u32[]{:S(2)}) collective-permute-start(bf16[576,128]{1,0:T(8,128)(2,1)S(1)} %get-tuple-element.31), channel_id=1, source_target_pairs={{0,24},{1,25},{2,26},{3,27},{4,28},{5,29},{6,30},{7,31},{8,16},{9,... | collective-permute-start | bytes 442376 | tf_op jit(solution)/shard_map/ppermute | solution.py:41
  9.9 6.7 %collective-permute-start.4 = (bf16[3,4,3712]{2,1,0:T(4,128)(2,1)S(1)}, bf16[3,4,3712]{2,1,0:T(4,128)(2,1)S(1)}, u32[]{:S(2)}, u32[]{:S(2)}) collective-permute-start(bf16[3,4,3712]{2,1,0:T(4,128)(2,1)S(1)} %get-tuple-element.32.refs_3_), channel_id=1, source_target_pairs={{0,4},{1,5},{2,6},{3,7},{4,0},{5,1},{6,2},{7,3},{8,12},{9,13},{10,... | collective-permute-start | bytes 267272 | tf_op jit(solution)/shard_map/ppermute | solution.py:41
  10.7 6.4 %collective-permute-start.5 = (bf16[3,4,3712]{2,1,0:T(4,128)(2,1)S(1)}, bf16[3,4,3712]{2,1,0:T(4,128)(2,1)S(1)}, u32[]{:S(2)}, u32[]{:S(2)}) collective-permute-start(bf16[3,4,3712]{2,1,0:T(4,128)(2,1)S(1)} %get-tuple-element.32.refs_3_), channel_id=1, source_target_pairs={{0,2},{1,3},{2,0},{3,1},{4,6},{5,7},{6,4},{7,5},{8,10},{9,11},{10,... | collective-permute-start | bytes 267272 | tf_op jit(solution)/shard_map/ppermute | solution.py:41
  17.2 10.4 %collective-permute-start.6 = (bf16[48,3712]{1,0:T(8,128)(2,1)S(1)}, bf16[48,3712]{1,0:T(8,128)(2,1)S(1)}, u32[]{:S(2)}, u32[]{:S(2)}) collective-permute-start(bf16[48,3712]{1,0:T(8,128)(2,1)S(1)} %line_rows.1.refs_0_.refs_4_), channel_id=1, source_target_pairs={{0,1},{1,0},{2,3},{3,2},{4,5},{5,4},{6,7},{7,6},{8,9},{9,8},{10,11... | collective-permute-start | bytes 1069064 | tf_op jit(solution)/shard_map/ppermute | solution.py:41
  18.8 11.2 %collective-permute-start.7 = (bf16[48,3712]{1,0:T(8,128)(2,1)S(1)}, bf16[48,3712]{1,0:T(8,128)(2,1)S(1)}, u32[]{:S(2)}, u32[]{:S(2)}) collective-permute-start(bf16[48,3712]{1,0:T(8,128)(2,1)S(1)} %line_rows.1.refs_0_.refs_4_), channel_id=1, source_target_pairs={{0,16},{1,17},{2,18},{3,19},{4,20},{5,21},{6,22},{7,23},{8,24},{9,... | collective-permute-start | bytes 1069064 | tf_op jit(solution)/shard_map/ppermute | solution.py:41
  20.3 16.1 %collective-permute-start.8 = (bf16[48,3712]{1,0:T(8,128)(2,1)S(1)}, bf16[48,3712]{1,0:T(8,128)(2,1)S(1)}, u32[]{:S(2)}, u32[]{:S(2)}) collective-permute-start(bf16[48,3712]{1,0:T(8,128)(2,1)S(1)} %line_rows.1.refs_0_.refs_4_), channel_id=1, source_target_pairs={{0,17},{1,16},{2,19},{3,18},{4,21},{5,20},{6,23},{7,22},{8,25},{9,... | collective-permute-start | bytes 1069064 | tf_op jit(solution)/shard_map/ppermute | solution.py:41
  36.5 5.3 %collective-permute-start.10 = (bf16[48,3712]{1,0:T(8,128)(2,1)S(1)}, bf16[48,3712]{1,0:T(8,128)(2,1)S(1)}, u32[]{:S(2)}, u32[]{:S(2)}) collective-permute-start(bf16[48,3712]{1,0:T(8,128)(2,1)S(1)} %collective-permute-done.7.refs_2_), channel_id=1, source_target_pairs={{0,8},{1,9},{2,10},{3,11},{4,12},{5,13},{6,14},{7,15},{8,0},{9,1},... | collective-permute-start | bytes 1069064 | tf_op jit(solution)/shard_map/ppermute | solution.py:41
  36.5 5.3 %collective-permute-start.11 = (bf16[48,3712]{1,0:T(8,128)(2,1)S(1)}, bf16[48,3712]{1,0:T(8,128)(2,1)S(1)}, u32[]{:S(2)}, u32[]{:S(2)}) collective-permute-start(bf16[48,3712]{1,0:T(8,128)(2,1)S(1)} %collective-permute-done.8.refs_3_), channel_id=1, source_target_pairs={{0,8},{1,9},{2,10},{3,11},{4,12},{5,13},{6,14},{7,15},{8,0},{9,1},... | collective-permute-start | bytes 1069064 | tf_op jit(solution)/shard_map/ppermute | solution.py:41
  37.0 4.9 %collective-permute-start.9 = (bf16[48,3712]{1,0:T(8,128)(2,1)S(1)}, bf16[48,3712]{1,0:T(8,128)(2,1)S(1)}, u32[]{:S(2)}, u32[]{:S(2)}) collective-permute-start(bf16[48,3712]{1,0:T(8,128)(2,1)S(1)} %collective-permute-done.6.refs_1_), channel_id=1, source_target_pairs={{0,8},{1,9},{2,10},{3,11},{4,12},{5,13},{6,14},{7,15},{8,0},{9,1},... | collective-permute-start | bytes 1069064 | tf_op jit(solution)/shard_map/ppermute | solution.py:41
  45.3 1.9 %collective-permute-start.14 = (bf16[48,3584]{1,0:T(8,128)(2,1)S(1)}, bf16[48,3584]{1,0:T(8,128)(2,1)S(1)}, u32[]{:S(2)}, u32[]{:S(2)}) collective-permute-start(bf16[48,3584]{1,0:T(8,128)(2,1)S(1)} %get-tuple-element.44), channel_id=1, source_target_pairs={{0,8},{1,9},{2,10},{3,11},{4,12},{5,13},{6,14},{7,15},{8,0},{9,1},... | collective-permute-start | bytes 1032200 | tf_op jit(solution)/shard_map/ppermute | solution.py:41
  45.9 2.9 %collective-permute-start.15 = (bf16[48,3712]{1,0:T(8,128)(2,1)S(1)}, bf16[48,3712]{1,0:T(8,128)(2,1)S(1)}, u32[]{:S(2)}, u32[]{:S(2)}) collective-permute-start(bf16[48,3712]{1,0:T(8,128)(2,1)S(1)} %line_rows.1.refs_0_.refs_4_), channel_id=1, source_target_pairs={{0,8},{1,9},{2,10},{3,11},{4,12},{5,13},{6,14},{7,15},{8,0},{9,1},... | collective-permute-start | bytes 1069064 | tf_op jit(solution)/shard_map/ppermute | solution.py:41
  46.0 2.2 %collective-permute-start.13 = (bf16[48,3584]{1,0:T(8,128)(2,1)S(1)}, bf16[48,3584]{1,0:T(8,128)(2,1)S(1)}, u32[]{:S(2)}, u32[]{:S(2)}) collective-permute-start(bf16[48,3584]{1,0:T(8,128)(2,1)S(1)} %get-tuple-element.42), channel_id=1, source_target_pairs={{0,8},{1,9},{2,10},{3,11},{4,12},{5,13},{6,14},{7,15},{8,0},{9,1},... | collective-permute-start | bytes 1032200 | tf_op jit(solution)/shard_map/ppermute | solution.py:41
  46.4 2.3 %collective-permute-start.12 = (bf16[48,3584]{1,0:T(8,128)(2,1)S(1)}, bf16[48,3584]{1,0:T(8,128)(2,1)S(1)}, u32[]{:S(2)}, u32[]{:S(2)}) collective-permute-start(bf16[48,3584]{1,0:T(8,128)(2,1)S(1)} %get-tuple-element.40), channel_id=1, source_target_pairs={{0,8},{1,9},{2,10},{3,11},{4,12},{5,13},{6,14},{7,15},{8,0},{9,1},... | collective-permute-start | bytes 1032200 | tf_op jit(solution)/shard_map/ppermute | solution.py:41
  48.7 6.1 %copy-start = (bf16[4,128,576]{1,2,0:T(8,128)(2,1)S(1)}, bf16[4,128,576]{1,2,0:T(8,128)(2,1)}, u32[]{:S(2)}) copy-start(bf16[4,128,576]{1,2,0:T(8,128)(2,1)} %param.12) | copy-start | bytes 1769476
  48.8 6.1 %copy-start.1 = (bf16[3,4,128,576]{2,3,1,0:T(8,128)(2,1)S(1)}, bf16[3,4,128,576]{2,3,1,0:T(8,128)(2,1)}, u32[]{:S(2)}) copy-start(bf16[3,4,128,576]{2,3,1,0:T(8,128)(2,1)} %param.11) | copy-start | bytes 5308420
  48.8 6.1 %copy-start.2 = (s32[4,1,2,2]{0,3,2,1:T(2,128)S(1)}, s32[4,1,2,2]{0,3,2,1:T(2,128)}, u32[]{:S(2)}) copy-start(s32[4,1,2,2]{0,3,2,1:T(2,128)} %param.21) | copy-start | bytes 196
  48.8 6.1 %copy-start.3 = (s32[4]{0:T(128)S(1)}, s32[4]{0:T(128)}, u32[]{:S(2)}) copy-start(s32[4]{0:T(128)} %refs_0_.1) | copy-start | bytes 52
  50.8 3.9 %collective-permute-start.16 = (bf16[48,3584]{1,0:T(8,128)(2,1)S(1)}, bf16[48,3584]{1,0:T(8,128)(2,1)S(1)}, u32[]{:S(2)}, u32[]{:S(2)}) collective-permute-start(bf16[48,3584]{1,0:T(8,128)(2,1)S(1)} %get-tuple-element.46), channel_id=1, source_target_pairs={{0,8},{1,9},{2,10},{3,11},{4,12},{5,13},{6,14},{7,15},{8,0},{9,1},... | collective-permute-start | bytes 1032200 | tf_op jit(solution)/shard_map/ppermute | solution.py:41
  51.2 11.9 %collective-permute-start.19 = (bf16[48,3584]{1,0:T(8,128)(2,1)S(1)}, bf16[48,3584]{1,0:T(8,128)(2,1)S(1)}, u32[]{:S(2)}, u32[]{:S(2)}) collective-permute-start(bf16[48,3584]{1,0:T(8,128)(2,1)S(1)} %add_convert_fusion.1.refs_2_.refs_5_), channel_id=1, source_target_pairs={{0,17},{1,16},{2,19},{3,18},{4,21},{5,20},{6,23},{7,22},{8,25},{9,... | collective-permute-start | bytes 1032200 | tf_op jit(solution)/shard_map/ppermute | solution.py:41
  53.7 16.0 %collective-permute-start.18 = (bf16[48,3584]{1,0:T(8,128)(2,1)S(1)}, bf16[48,3584]{1,0:T(8,128)(2,1)S(1)}, u32[]{:S(2)}, u32[]{:S(2)}) collective-permute-start(bf16[48,3584]{1,0:T(8,128)(2,1)S(1)} %add_convert_fusion.2.refs_1_.refs_4_), channel_id=1, source_target_pairs={{0,16},{1,17},{2,18},{3,19},{4,20},{5,21},{6,22},{7,23},{8,24},{9,... | collective-permute-start | bytes 1032200 | tf_op jit(solution)/shard_map/ppermute | solution.py:41
  54.2 15.5 %collective-permute-start.17 = (bf16[48,3584]{1,0:T(8,128)(2,1)S(1)}, bf16[48,3584]{1,0:T(8,128)(2,1)S(1)}, u32[]{:S(2)}, u32[]{:S(2)}) collective-permute-start(bf16[48,3584]{1,0:T(8,128)(2,1)S(1)} %add_convert_fusion.3.refs_0_.refs_3_), channel_id=1, source_target_pairs={{0,1},{1,0},{2,3},{3,2},{4,5},{5,4},{6,7},{7,6},{8,9},{9,8},{10,11... | collective-permute-start | bytes 1032200 | tf_op jit(solution)/shard_map/ppermute | solution.py:41
  69.9 7.3 %collective-permute-start.20 = (bf16[3,4,3584]{2,1,0:T(4,128)(2,1)S(1)}, bf16[3,4,3584]{2,1,0:T(4,128)(2,1)S(1)}, u32[]{:S(2)}, u32[]{:S(2)}) collective-permute-start(bf16[3,4,3584]{2,1,0:T(4,128)(2,1)S(1)} %get-tuple-element.52), channel_id=1, source_target_pairs={{0,6},{1,7},{2,4},{3,5},{4,2},{5,3},{6,0},{7,1},{8,14},{9,15},{10,... | collective-permute-start | bytes 258056 | tf_op jit(solution)/shard_map/ppermute | solution.py:41
  70.8 8.8 %collective-permute-start.21 = (bf16[3,4,3584]{2,1,0:T(4,128)(2,1)S(1)}, bf16[3,4,3584]{2,1,0:T(4,128)(2,1)S(1)}, u32[]{:S(2)}, u32[]{:S(2)}) collective-permute-start(bf16[3,4,3584]{2,1,0:T(4,128)(2,1)S(1)} %get-tuple-element.53), channel_id=1, source_target_pairs={{0,4},{1,5},{2,6},{3,7},{4,0},{5,1},{6,2},{7,3},{8,12},{9,13},{10,... | collective-permute-start | bytes 258056 | tf_op jit(solution)/shard_map/ppermute | solution.py:41
  71.2 8.4 %collective-permute-start.22 = (bf16[3,4,3584]{2,1,0:T(4,128)(2,1)S(1)}, bf16[3,4,3584]{2,1,0:T(4,128)(2,1)S(1)}, u32[]{:S(2)}, u32[]{:S(2)}) collective-permute-start(bf16[3,4,3584]{2,1,0:T(4,128)(2,1)S(1)} %get-tuple-element.54), channel_id=1, source_target_pairs={{0,2},{1,3},{2,0},{3,1},{4,6},{5,7},{6,4},{7,5},{8,10},{9,11},{10,... | collective-permute-start | bytes 258056 | tf_op jit(solution)/shard_map/ppermute | solution.py:41

commit v4 on v3

--- a/solution.py
+++ b/solution.py
@@ -31,13 +31,14 @@
 KERNEL_PARAMS = pltpu.CompilerParams(vmem_limit_bytes=12 * 1024 * 1024)
 
 
-def across(values, grp_flip, ep_flip):
+def across(values, even_flip, odd_flip=None):
     groups, columns = lax.axis_size("grp"), lax.axis_size("ep")
-    pairs = [
-        (g * columns + e, (g ^ grp_flip) * columns + (e ^ ep_flip))
-        for g in range(groups)
-        for e in range(columns)
-    ]
+    flips = (even_flip, odd_flip or even_flip)
+    pairs = []
+    for g in range(groups):
+        for e in range(columns):
+            grp_flip, ep_flip = flips[g % 2]
+            pairs.append((g * columns + e, (g ^ grp_flip) * columns + (e ^ ep_flip)))
     return lax.ppermute(values, BOTH, pairs)
 
 
@@ -114,31 +115,55 @@
     return parts.astype(jnp.bfloat16)
 
 
-def prepare_kernel(others, lengths_ref, plan_ref, group_ref, *refs):
-    cache_hbm, sources, refs = refs[0], refs[1:5], refs[5:]
-    rows_ref, entries_ref, out_refs = refs[0], refs[1], refs[2 : 2 + others]
-    slots_ref, targets, stack_ref, semaphores = refs[2 + others], refs[3 + others : -2], refs[-2], refs[-1]
+def token_rows_kernel(group_ref, *refs):
+    sources, rows_ref, targets, semaphores = refs[:3], refs[3], refs[4:7], refs[7]
     copies = [
-        pltpu.make_async_copy(source, target, semaphores.at[others + number])
+        pltpu.make_async_copy(source, target, semaphores.at[number])
         for number, (source, target) in enumerate(zip(sources, targets))
     ]
-    slots = [outgoing_slot(number, plan_ref, group_ref) for number in range(others)]
-    for number, slot in enumerate(slots):
-        copies.append(
-            pltpu.make_async_copy(
-                cache_hbm.at[slot], slots_ref.at[number], semaphores.at[number]
-            )
-        )
     for copy in copies:
         copy.start()
     for copy in copies:
         copy.wait()
-    ids_ref, gains_ref, tokens_ref, new_entries_ref = targets
-    steps, traces, width = tokens_ref.shape
+    ids_ref, gains_ref, tokens_ref = targets
+    steps, _, width = tokens_ref.shape
     group = group_ref[0]
     for step in range(steps):
         rows_ref[step, :, :width] = tokens_ref[step]
         rows_ref[step, :, width:] = gain_lanes(ids_ref[step, group], gains_ref[step, group])
+
+
+def token_rows(group, expert_ids, route_gains, moe_input):
+    steps, traces, width = moe_input.shape
+    sources = [expert_ids, route_gains, moe_input]
+    return pl.pallas_call(
+        token_rows_kernel,
+        in_specs=[pl.BlockSpec(memory_space=pltpu.SMEM)]
+        + [pl.BlockSpec(memory_space=pltpu.HBM)] * len(sources),
+        out_specs=pl.BlockSpec(memory_space=pltpu.VMEM),
+        out_shape=jax.ShapeDtypeStruct((steps, traces, width + GAIN_LANES), moe_input.dtype),
+        scratch_shapes=[pltpu.VMEM(source.shape, source.dtype) for source in sources]
+        + [pltpu.SemaphoreType.DMA((len(sources),))],
+        compiler_params=KERNEL_PARAMS,
+        cost_estimate=LARGE_COST,
+        name="token_rows",
+    )(group, *(pltpu.with_memory_space_constraint(source, pltpu.HBM) for source in sources))
+
+
+def outgoing_kernel(others, lengths_ref, plan_ref, group_ref, cache_hbm, entries_hbm, *refs):
+    entries_ref, out_refs = refs[0], refs[1 : 1 + others]
+    slots_ref, new_entries_ref, stack_ref, semaphores = refs[1 + others :]
+    slots = [outgoing_slot(number, plan_ref, group_ref) for number in range(others)]
+    copies = [pltpu.make_async_copy(entries_hbm, new_entries_ref, semaphores.at[others])]
+    for number, slot in enumerate(slots):
+        copies.append(
+            pltpu.make_async_copy(cache_hbm.at[slot], slots_ref.at[number], semaphores.at[number])
+        )
+    for copy in copies:
+        copy.start()
+    for copy in copies:
+        copy.wait()
+    steps, traces, _ = new_entries_ref.shape
     stack_ref[...] = jnp.zeros_like(stack_ref)
     for step in range(steps):
         stack_ref[step * traces : (step + 1) * traces, :] = new_entries_ref[step].astype(jnp.float32)
@@ -150,38 +175,36 @@
         )
 
 
-def prepare(cache, new_entries, lengths, plan, group, moe_input, expert_ids, route_gains):
+def outgoing(cache, new_entries, lengths, plan, group, behind=()):
     traces, width, capacity = cache.shape
-    steps, _, model_width = moe_input.shape
     others = lax.axis_size("grp") - 1
-    entry_rows = -(-steps * traces // 16) * 16
+    entry_rows = -(-new_entries.shape[0] * traces // 16) * 16
     smem, vmem = pl.BlockSpec(memory_space=pltpu.SMEM), pl.BlockSpec(memory_space=pltpu.VMEM)
-    sources = [cache, expert_ids, route_gains, moe_input, new_entries]
-    rows, entries, *leaving = pl.pallas_call(
-        partial(prepare_kernel, others),
-        in_specs=[smem] * 3 + [pl.BlockSpec(memory_space=pltpu.HBM)] * len(sources),
-        out_specs=[vmem] * (others + 2),
-        out_shape=[
-            jax.ShapeDtypeStruct((steps, traces, model_width + GAIN_LANES), moe_input.dtype),
-            jax.ShapeDtypeStruct((entry_rows, width), cache.dtype),
-        ]
+    hbm = pl.BlockSpec(memory_space=pltpu.HBM)
+    entries, *leaving = pl.pallas_call(
+        ignoring(partial(outgoing_kernel, others), 0, len(behind)),
+        in_specs=[ANYWHERE] * len(behind) + [smem, smem, smem, hbm, hbm],
+        out_specs=[vmem] * (others + 1),
+        out_shape=[jax.ShapeDtypeStruct((entry_rows, width), cache.dtype)]
         + [jax.ShapeDtypeStruct((width, capacity), cache.dtype)] * others,
-        scratch_shapes=[pltpu.VMEM((others, width, capacity), cache.dtype)]
-        + [pltpu.VMEM(source.shape, source.dtype) for source in sources[1:]]
-        + [
+        scratch_shapes=[
+            pltpu.VMEM((others, width, capacity), cache.dtype),
+            pltpu.VMEM(new_entries.shape, new_entries.dtype),
             pltpu.VMEM((entry_rows, width), jnp.float32),
-            pltpu.SemaphoreType.DMA((others + len(sources) - 1,)),
+            pltpu.SemaphoreType.DMA((others + 1,)),
         ],
         compiler_params=KERNEL_PARAMS,
         cost_estimate=LARGE_COST,
-        name="prepare",
+        name="outgoing",
     )(
+        *behind,
         pltpu.with_memory_space_constraint(lengths, pltpu.HBM),
         pltpu.with_memory_space_constraint(plan, pltpu.HBM),
         group,
-        *(pltpu.with_memory_space_constraint(source, pltpu.HBM) for source in sources),
-    )
-    return rows, entries, leaving
+        pltpu.with_memory_space_constraint(cache, pltpu.HBM),
+        pltpu.with_memory_space_constraint(new_entries, pltpu.HBM),
+    )
+    return entries, leaving
 
 
 def line_kernel(*refs):
@@ -400,30 +423,29 @@
     far_flips = [(0, 2 * z) for z in range(1, experts // 2)][::-1]
     near_flips = [(2 * x, y) for x in range(groups // 2) for y in range(2)][1:]
     steps, trace_count, width = moe_input.shape
-    rows, entries, leaving = prepare(
-        cache, new_entries, lengths, plan, group, moe_input, expert_ids, route_gains
-    )
-    received = [across(leaving[flip - 1], flip, 0) for flip in range(1, groups)]
-    line = [rows] + [across(rows, *flip) for flip in far_flips]
-    own_line = line_rows(line, received)
-    plane = [across(own_line, *flip) for flip in near_flips]
-    *weights, fetched = fetch(weights, [own_line])
-    plane = [own_line] + list(lax.optimization_barrier((plane, fetched))[0])
-    other_plane = [across(piece, 1, 0) for piece in plane]
-    terms, sums = [None] * len(plane), []
-    for members in PLANE_GROUPS:
-        pieces = [half[member] for half in (plane, other_plane) for member in members]
-        outputs = expert(pieces, weights, sums)
-        for member, own, other in zip(members, outputs, outputs[len(members) :]):
-            term = add_up([own, across(other, 1, 0)])
-            terms[member] = across(term, *near_flips[member - 1]) if member else term
-            sums = sums + [term]
+    rows = token_rows(group, expert_ids, route_gains, moe_input)
+    first_flips = list(zip(far_flips, near_flips))
+    last_flips = list(zip(near_flips, far_flips))
+    line = [rows] + [across(rows, *flips) for flips in first_flips]
+    own_line = line_rows(line, [])
+    plane = [across(own_line, *flips) for flips in last_flips]
+    entries, leaving = outgoing(cache, new_entries, lengths, plan, group, [own_line])
+    received = [across(leaving[flip - 1], (flip, 0)) for flip in range(1, groups)]
+    *weights, _ = fetch(weights, [own_line])
+    own_sums, other_sums = expert([own_line, across(own_line, (1, 0))], weights)
+    plane = gate(plane, [*received, own_sums])
+    other_plane = [across(piece, (1, 0)) for piece in plane]
+    own = expert(plane, weights)
+    other = expert(other_plane, weights, own[:1])
+    sums = [add_up([mine, across(theirs, (1, 0))]) for mine, theirs in zip(own, other)]
+    terms = [across(term, *flips) for term, flips in zip(sums, last_flips)]
     contexts, migrated_cache, attended = attention(
         queries, cache, entries, lengths, plan, group, received, sums
     )
-    parts = line_sums(terms, steps, trace_count, len(line), [attended])
+    own_term = add_up([own_sums, across(other_sums, (1, 0))])
+    parts = line_sums([*terms, own_term], steps, trace_count, len(line), [attended])
     moe_output = add_up(
-        [parts[0]] + [across(part, *flip) for part, flip in zip(parts[1:], far_flips)]
+        [parts[0]] + [across(part, *flips) for part, flips in zip(parts[1:], first_flips)]
     )
     return contexts, migrated_cache, moe_output
 
@@ -431,10 +453,8 @@
 def routed_layer(
     queries, cache, new_entries, lengths, moe_input, expert_ids, route_gains, weights, plan, group
 ):
-    _, entries, leaving = prepare(
-        cache, new_entries, lengths, plan, group, moe_input, expert_ids, route_gains
-    )
-    received = [across(leaving[flip - 1], flip, 0) for flip in range(1, lax.axis_size("grp"))]
+    entries, leaving = outgoing(cache, new_entries, lengths, plan, group)
+    received = [across(leaving[flip - 1], (flip, 0)) for flip in range(1, lax.axis_size("grp"))]
     contexts, migrated_cache, _ = attention(
         queries, cache, entries, lengths, plan, group, received
     )

time: 80.5 us -> 66.1 us (0.82)
  the two profiles are of different devices: /device:TPU:0 before, /device:TPU:9 now
where the time goes in v4:
time: 66.1 us; the launch traced here: 65.9 us
  waiting for transfers between devices  27.1 us (41%)
  Pallas kernels  18.9 us (29%)
  starting transfers between devices  17.9 us (27%)
  other arithmetic  1.06 us (2%)
  between operations  0.83 us (1%)
    ppermute x23, waiting for transfers between devices, across(): return lax.ppermute(values, BOTH, pairs)  27.1 us
    ppermute x23, starting transfers between devices, across(): return lax.ppermute(values, BOTH, pairs)  17.9 us
    pallas_call x3, Pallas kernels, expert(): pl.pallas_call(ignoring(expert_kernel, 0, len(others)), in_specs=[ANYWHER...  5.78 us
    pallas_call x1, Pallas kernels, fetch(): pl.pallas_call(ignoring(fetch_kernel, 0, len(others)), in_specs=[ANYWHERE...  4.82 us
    pallas_call x1, Pallas kernels, attention(): pl.pallas_call(ignoring(partial(attention_kernel, block), 3, len(others))...  4.78 us
    pallas_call x1, Pallas kernels, outgoing(): pl.pallas_call(ignoring(partial(outgoing_kernel, others), 0, len(behind))...  2.12 us
  transfers between devices with their start and end apart: 23, of which 14 were waited for; matrix products, arithmetic and copies ran while one was open for 0% of the time, Pallas kernels for 24%

profile of v4, /device:TPU:9, one launch (start us, length us, event | category | flops | bytes accessed | tf_op | source)
XLA Modules:
  0.0 65.9 jit_solution(3576910778137256429)
XLA Ops:
  0.6 1.1 %token_rows.1.refs_0_ = bf16[3,4,3712]{2,1,0:T(4,128)(2,1)S(1)} custom-call(s32[1]{0:T(128)} %bitcast.2.group_ref.refs_3_.refs_2_, s32[3,4,4,8]{3,2,1,0:T(4,128)} %refs_0_.2, f32[3,4,4,8]{3,2,1,0:T(4,128)} %refs_1_.3, bf16[3,4,3584]{2,1,0:T(4,128)(2,1)} %refs_2_.2), custom_call_target="tpu_custom_call" | custom-call | flops 1 | bytes 100000000 | tf_op jit(solution)/shard_map/token_rows/pallas_call | solution.py:139
  1.8 1.3 %collective-permute-start = (bf16[3,4,3712]{2,1,0:T(4,128)(2,1)S(1)}, bf16[3,4,3712]{2,1,0:T(4,128)(2,1)S(1)}, u32[]{:S(2)}, u32[]{:S(2)}) collective-permute-start(bf16[3,4,3712]{2,1,0:T(4,128)(2,1)S(1)} %token_rows.1.refs_0_), channel_id=1, source_target_pairs={{0,6},{1,7},{2,4},{3,5},{4,2},{5,3},{6,0},{7,1},{8,9},{9,8},{10,11... | collective-permute-start | bytes 267272 | tf_op jit(solution)/shard_map/ppermute | solution.py:42
  3.1 1.2 %collective-permute-start.1 = (bf16[3,4,3712]{2,1,0:T(4,128)(2,1)S(1)}, bf16[3,4,3712]{2,1,0:T(4,128)(2,1)S(1)}, u32[]{:S(2)}, u32[]{:S(2)}) collective-permute-start(bf16[3,4,3712]{2,1,0:T(4,128)(2,1)S(1)} %token_rows.1.refs_0_), channel_id=1, source_target_pairs={{0,4},{1,5},{2,6},{3,7},{4,0},{5,1},{6,2},{7,3},{8,24},{9,25},{10,... | collective-permute-start | bytes 267272 | tf_op jit(solution)/shard_map/ppermute | solution.py:42
  4.3 0.2 collective-permute-start.2
  4.5 0.7 %collective-permute-done.refs_1_ = bf16[3,4,3712]{2,1,0:T(4,128)(2,1)S(1)} collective-permute-done((bf16[3,4,3712]{2,1,0:T(4,128)(2,1)S(1)}, bf16[3,4,3712]{2,1,0:T(4,128)(2,1)S(1)}, u32[]{:S(2)}, u32[]{:S(2)}) %collective-permute-start) | collective-permute-done | bytes 89120 | tf_op jit(solution)/shard_map/ppermute | solution.py:42
  5.2 1.5 %collective-permute-done.1.refs_2_ = bf16[3,4,3712]{2,1,0:T(4,128)(2,1)S(1)} collective-permute-done((bf16[3,4,3712]{2,1,0:T(4,128)(2,1)S(1)}, bf16[3,4,3712]{2,1,0:T(4,128)(2,1)S(1)}, u32[]{:S(2)}, u32[]{:S(2)}) %collective-permute-start.1) | collective-permute-done | bytes 89120 | tf_op jit(solution)/shard_map/ppermute | solution.py:42
  6.8 2.1 %collective-permute-done.2.refs_3_ = bf16[3,4,3712]{2,1,0:T(4,128)(2,1)S(1)} collective-permute-done((bf16[3,4,3712]{2,1,0:T(4,128)(2,1)S(1)}, bf16[3,4,3712]{2,1,0:T(4,128)(2,1)S(1)}, u32[]{:S(2)}, u32[]{:S(2)}) %collective-permute-start.2) | collective-permute-done | bytes 89120 | tf_op jit(solution)/shard_map/ppermute | solution.py:42
  8.9 0.1 line_rows.1.refs_0_.refs_1_
  9.0 2.2 %collective-permute-start.9 = (bf16[48,3712]{1,0:T(8,128)(2,1)S(1)}, bf16[48,3712]{1,0:T(8,128)(2,1)S(1)}, u32[]{:S(2)}, u32[]{:S(2)}) collective-permute-start(bf16[48,3712]{1,0:T(8,128)(2,1)S(1)} %line_rows.1.refs_0_.refs_1_), channel_id=1, source_target_pairs={{0,8},{1,9},{2,10},{3,11},{4,12},{5,13},{6,14},{7,15},{8,0},{9,1},... | collective-permute-start | bytes 1069064 | tf_op jit(solution)/shard_map/ppermute | solution.py:42
  11.2 1.3 %collective-permute-start.3 = (bf16[48,3712]{1,0:T(8,128)(2,1)S(1)}, bf16[48,3712]{1,0:T(8,128)(2,1)S(1)}, u32[]{:S(2)}, u32[]{:S(2)}) collective-permute-start(bf16[48,3712]{1,0:T(8,128)(2,1)S(1)} %line_rows.1.refs_0_.refs_1_), channel_id=1, source_target_pairs={{0,1},{1,0},{2,3},{3,2},{4,5},{5,4},{6,7},{7,6},{8,14},{9,15},{10,... | collective-permute-start | bytes 1069064 | tf_op jit(solution)/shard_map/ppermute | solution.py:42
  12.4 1.6 %collective-permute-start.4 = (bf16[48,3712]{1,0:T(8,128)(2,1)S(1)}, bf16[48,3712]{1,0:T(8,128)(2,1)S(1)}, u32[]{:S(2)}, u32[]{:S(2)}) collective-permute-start(bf16[48,3712]{1,0:T(8,128)(2,1)S(1)} %line_rows.1.refs_0_.refs_1_), channel_id=1, source_target_pairs={{0,16},{1,17},{2,18},{3,19},{4,20},{5,21},{6,22},{7,23},{8,12},{9,... | collective-permute-start | bytes 1069064 | tf_op jit(solution)/shard_map/ppermute | solution.py:42
  14.0 2.1 %outgoing.1 = (bf16[16,576]{1,0:T(8,128)(2,1)S(1)}, bf16[576,128]{1,0:T(8,128)(2,1)S(1)}, bf16[576,128]{1,0:T(8,128)(2,1)S(1)}, bf16[576,128]{1,0:T(8,128)(2,1)S(1)}) custom-call(bf16[48,3712]{1,0:T(8,128)(2,1)S(1)} %line_rows.1.refs_0_.refs_1_, s32[4]{0:T(128)} %refs_0_.3, s32[2,2,4]{2,1,0:T(2,128)} %bitcast.11, s32[1]{0:T(128)} %bitcast.2.group_ref.refs_3_.refs_2_, ...), custom_call_target="tpu_custom_call" | custom-call | flops 1 | bytes 100000000 | tf_op jit(solution)/shard_map/outgoing/pallas_call | solution.py:184
  16.2 0.8 %collective-permute-start.6 = (bf16[576,128]{1,0:T(8,128)(2,1)S(1)}, bf16[576,128]{1,0:T(8,128)(2,1)S(1)}, u32[]{:S(2)}, u32[]{:S(2)}) collective-permute-start(bf16[576,128]{1,0:T(8,128)(2,1)S(1)} %get-tuple-element.28), channel_id=1, source_target_pairs={{0,8},{1,9},{2,10},{3,11},{4,12},{5,13},{6,14},{7,15},{8,0},{9,1},... | collective-permute-start | bytes 442376 | tf_op jit(solution)/shard_map/ppermute | solution.py:42
  16.9 1.0 %collective-permute-done.6.refs_3_.refs_9_ = bf16[576,128]{1,0:T(8,128)(2,1)S(1)} collective-permute-done((bf16[576,128]{1,0:T(8,128)(2,1)S(1)}, bf16[576,128]{1,0:T(8,128)(2,1)S(1)}, u32[]{:S(2)}, u32[]{:S(2)}) %collective-permute-start.6) | collective-permute-done | bytes 147488 | tf_op jit(solution)/shard_map/ppermute | solution.py:42
  18.0 1.2 %collective-permute-start.7 = (bf16[576,128]{1,0:T(8,128)(2,1)S(1)}, bf16[576,128]{1,0:T(8,128)(2,1)S(1)}, u32[]{:S(2)}, u32[]{:S(2)}) collective-permute-start(bf16[576,128]{1,0:T(8,128)(2,1)S(1)} %get-tuple-element.29), channel_id=1, source_target_pairs={{0,16},{1,17},{2,18},{3,19},{4,20},{5,21},{6,22},{7,23},{8,24},{9,... | collective-permute-start | bytes 442376 | tf_op jit(solution)/shard_map/ppermute | solution.py:42
  19.2 0.8 %collective-permute-start.8 = (bf16[576,128]{1,0:T(8,128)(2,1)S(1)}, bf16[576,128]{1,0:T(8,128)(2,1)S(1)}, u32[]{:S(2)}, u32[]{:S(2)}) collective-permute-start(bf16[576,128]{1,0:T(8,128)(2,1)S(1)} %get-tuple-element.30), channel_id=1, source_target_pairs={{0,24},{1,25},{2,26},{3,27},{4,28},{5,29},{6,30},{7,31},{8,16},{9,... | collective-permute-start | bytes 442376 | tf_op jit(solution)/shard_map/ppermute | solution.py:42
  20.0 4.8 %fetch.1 = (bf16[3584,512]{1,0:T(8,128)(2,1)S(1)}, bf16[3584,512]{1,0:T(8,128)(2,1)S(1)}, bf16[512,3584]{1,0:T(8,128)(2,1)S(1)}, s32[8,128]{1,0:T(8,128)}) custom-call(bf16[48,3712]{1,0:T(8,128)(2,1)S(1)} %line_rows.1.refs_0_.refs_1_, bf16[1,3584,512]{2,1,0:T(8,128)(2,1)} %refs_1_.5, bf16[1,3584,512]{2,1,0:T(8,128)(2,1)} %refs_2_.3, ...), custom_call_target="tpu_custom_call" | custom-call | flops 1 | bytes 100000000 | tf_op jit(solution)/shard_map/fetch/pallas_call | solution.py:317
  24.8 2.0 %expert.3 = (bf16[48,3584]{1,0:T(8,128)(2,1)S(1)}, bf16[48,3584]{1,0:T(8,128)(2,1)S(1)}) custom-call(s32[1]{0:T(128)} %bitcast.3.refs_0_.refs_1_, bf16[48,3712]{1,0:T(8,128)(2,1)S(1)} %line_rows.1.refs_0_.refs_1_, bf16[48,3712]{1,0:T(8,128)(2,1)S(1)} %collective-permute-done.9.refs_2_, bf16[3584,512]{1,0:T(8,128)(2,1)S(1)} %get-tuple-element.31.refs_3_.refs_4_.refs_5_, ...), custom_call_target="tpu_custom_call" | custom-call | flops 1 | bytes 100000000 | tf_op jit(solution)/shard_map/expert/pallas_call | solution.py:398
  26.8 2.9 %collective-permute-done.8.refs_5_.refs_11_ = bf16[576,128]{1,0:T(8,128)(2,1)S(1)} collective-permute-done((bf16[576,128]{1,0:T(8,128)(2,1)S(1)}, bf16[576,128]{1,0:T(8,128)(2,1)S(1)}, u32[]{:S(2)}, u32[]{:S(2)}) %collective-permute-start.8) | collective-permute-done | bytes 147488 | tf_op jit(solution)/shard_map/ppermute | solution.py:42
  29.7 0.5 collective-permute-start.11
  30.3 1.9 %expert.4 = (bf16[48,3584]{1,0:T(8,128)(2,1)S(1)}, bf16[48,3584]{1,0:T(8,128)(2,1)S(1)}, bf16[48,3584]{1,0:T(8,128)(2,1)S(1)}) custom-call(s32[1]{0:T(128)} %bitcast.3.refs_0_.refs_1_, bf16[48,3712]{1,0:T(8,128)(2,1)S(1)} %get-tuple-element.35.refs_1_, bf16[48,3712]{1,0:T(8,128)(2,1)S(1)} %get-tuple-element.36.refs_2_, ...), custom_call_target="tpu_custom_call" | custom-call | flops 1 | bytes 100000000 | tf_op jit(solution)/shard_map/expert/pallas_call | solution.py:398
  32.2 0.2 collective-permute-done.12.refs_4_
  32.4 1.9 %expert.5 = (bf16[48,3584]{1,0:T(8,128)(2,1)S(1)}, bf16[48,3584]{1,0:T(8,128)(2,1)S(1)}, bf16[48,3584]{1,0:T(8,128)(2,1)S(1)}) custom-call(bf16[48,3584]{1,0:T(8,128)(2,1)S(1)} %get-tuple-element.38.refs_0_, s32[1]{0:T(128)} %bitcast.3.refs_0_.refs_1_, bf16[48,3712]{1,0:T(8,128)(2,1)S(1)} %collective-permute-done.10.refs_2_, ...), custom_call_target="tpu_custom_call" | custom-call | flops 1 | bytes 100000000 | tf_op jit(solution)/shard_map/expert/pallas_call | solution.py:398
  34.4 0.4 collective-permute-start.15
  34.7 0.2 collective-permute-start.19
  34.9 0.3 collective-permute-start.14
  35.2 0.2 collective-permute-start.13
  35.4 0.6 collective-permute-done.15
  36.1 0.1 add_convert_fusion.1.refs_5_
  36.2 0.8 %collective-permute-start.18 = (bf16[48,3584]{1,0:T(8,128)(2,1)S(1)}, bf16[48,3584]{1,0:T(8,128)(2,1)S(1)}, u32[]{:S(2)}, u32[]{:S(2)}) collective-permute-start(bf16[48,3584]{1,0:T(8,128)(2,1)S(1)} %add_convert_fusion.1.refs_5_), channel_id=1, source_target_pairs={{0,17},{1,16},{2,19},{3,18},{4,21},{5,20},{6,23},{7,22},{8,10},{9,... | collective-permute-start | bytes 1032200 | tf_op jit(solution)/shard_map/ppermute | solution.py:42
  37.0 0.1 collective-permute-done.14
  37.1 0.1 add_convert_fusion.2.refs_4_
  37.1 1.7 %collective-permute-start.17 = (bf16[48,3584]{1,0:T(8,128)(2,1)S(1)}, bf16[48,3584]{1,0:T(8,128)(2,1)S(1)}, u32[]{:S(2)}, u32[]{:S(2)}) collective-permute-start(bf16[48,3584]{1,0:T(8,128)(2,1)S(1)} %add_convert_fusion.2.refs_4_), channel_id=1, source_target_pairs={{0,16},{1,17},{2,18},{3,19},{4,20},{5,21},{6,22},{7,23},{8,12},{9,... | collective-permute-start | bytes 1032200 | tf_op jit(solution)/shard_map/ppermute | solution.py:42
  38.8 0.1 add_convert_fusion.3.refs_3_
  38.9 0.4 collective-permute-start.16
  39.3 0.1 add_convert_fusion.refs_4_
  39.4 4.8 %attention.1 = (bf16[3,4,128,512]{3,2,1,0:T(8,128)(2,1)}, bf16[4,576,128]{2,1,0:T(8,128)(2,1)}, s32[8,128]{1,0:T(8,128)S(1)}) custom-call(s32[4]{0:T(128)S(1)} %copy-done.3, s32[2,2,4]{2,1,0:T(2,128)S(1)} %bitcast.12, s32[1]{0:T(128)} %bitcast.2.group_ref.refs_3_.refs_2_, bf16[48,3584]{1,0:T(8,128)(2,1)S(1)} %add_convert_fusion.3.refs_3_, ...), custom_call_target="tpu_custom_call" | custom-call | flops 1 | bytes 100000000 | tf_op jit(solution)/shard_map/attention/pallas_call | solution.py:335
  44.2 0.2 collective-permute-done.18.refs_3_
  44.4 6.0 %collective-permute-done.17.refs_2_ = bf16[48,3584]{1,0:T(8,128)(2,1)S(1)} collective-permute-done((bf16[48,3584]{1,0:T(8,128)(2,1)S(1)}, bf16[48,3584]{1,0:T(8,128)(2,1)S(1)}, u32[]{:S(2)}, u32[]{:S(2)}) %collective-permute-start.17) | collective-permute-done | bytes 344096 | tf_op jit(solution)/shard_map/ppermute | solution.py:42
  50.4 8.1 %collective-permute-done.16.refs_1_ = bf16[48,3584]{1,0:T(8,128)(2,1)S(1)} collective-permute-done((bf16[48,3584]{1,0:T(8,128)(2,1)S(1)}, bf16[48,3584]{1,0:T(8,128)(2,1)S(1)}, u32[]{:S(2)}, u32[]{:S(2)}) %collective-permute-start.16) | collective-permute-done | bytes 344096 | tf_op jit(solution)/shard_map/ppermute | solution.py:42
  58.6 0.2 line_sums.1
  58.8 0.9 %collective-permute-start.20 = (bf16[3,4,3584]{2,1,0:T(4,128)(2,1)S(1)}, bf16[3,4,3584]{2,1,0:T(4,128)(2,1)S(1)}, u32[]{:S(2)}, u32[]{:S(2)}) collective-permute-start(bf16[3,4,3584]{2,1,0:T(4,128)(2,1)S(1)} %get-tuple-element.50), channel_id=1, source_target_pairs={{0,6},{1,7},{2,4},{3,5},{4,2},{5,3},{6,0},{7,1},{8,9},{9,8},{10,11... | collective-permute-start | bytes 258056 | tf_op jit(solution)/shard_map/ppermute | solution.py:42
  59.7 1.2 %collective-permute-start.21 = (bf16[3,4,3584]{2,1,0:T(4,128)(2,1)S(1)}, bf16[3,4,3584]{2,1,0:T(4,128)(2,1)S(1)}, u32[]{:S(2)}, u32[]{:S(2)}) collective-permute-start(bf16[3,4,3584]{2,1,0:T(4,128)(2,1)S(1)} %get-tuple-element.51), channel_id=1, source_target_pairs={{0,4},{1,5},{2,6},{3,7},{4,0},{5,1},{6,2},{7,3},{8,24},{9,25},{10,... | collective-permute-start | bytes 258056 | tf_op jit(solution)/shard_map/ppermute | solution.py:42
  60.9 0.6 collective-permute-start.22
  61.5 0.7 %collective-permute-done.20 = bf16[3,4,3584]{2,1,0:T(4,128)(2,1)S(1)} collective-permute-done((bf16[3,4,3584]{2,1,0:T(4,128)(2,1)S(1)}, bf16[3,4,3584]{2,1,0:T(4,128)(2,1)S(1)}, u32[]{:S(2)}, u32[]{:S(2)}) %collective-permute-start.20) | collective-permute-done | bytes 86048 | tf_op jit(solution)/shard_map/ppermute | solution.py:42
  62.2 0.8 %collective-permute-done.21 = bf16[3,4,3584]{2,1,0:T(4,128)(2,1)S(1)} collective-permute-done((bf16[3,4,3584]{2,1,0:T(4,128)(2,1)S(1)}, bf16[3,4,3584]{2,1,0:T(4,128)(2,1)S(1)}, u32[]{:S(2)}, u32[]{:S(2)}) %collective-permute-start.21) | collective-permute-done | bytes 86048 | tf_op jit(solution)/shard_map/ppermute | solution.py:42
  63.0 2.1 %collective-permute-done.22 = bf16[3,4,3584]{2,1,0:T(4,128)(2,1)S(1)} collective-permute-done((bf16[3,4,3584]{2,1,0:T(4,128)(2,1)S(1)}, bf16[3,4,3584]{2,1,0:T(4,128)(2,1)S(1)}, u32[]{:S(2)}, u32[]{:S(2)}) %collective-permute-start.22) | collective-permute-done | bytes 86048 | tf_op jit(solution)/shard_map/ppermute | solution.py:42
  65.1 0.7 %add_convert_fusion.4 = bf16[3,4,3584]{2,1,0:T(4,128)(2,1)} fusion(bf16[3,4,3584]{2,1,0:T(4,128)(2,1)S(1)} %collective-permute-done.22, bf16[3,4,3584]{2,1,0:T(4,128)(2,1)S(1)} %collective-permute-done.21, bf16[3,4,3584]{2,1,0:T(4,128)(2,1)S(1)} %collective-permute-done.20, bf16[3,4,3584]{2,1,0:T(4,128)(2,1)S(1)} %get-tuple-element.49), kind=kLoop, calls=%fused_computation.4 | loop fusion | flops 344064 | bytes 430080 | tf_op jit(solution)/shard_map/convert_element_type | solution.py:416
  (21 shorter events, 0.2 us)
Async XLA Ops:
  1.8 3.4 %collective-permute-start = (bf16[3,4,3712]{2,1,0:T(4,128)(2,1)S(1)}, bf16[3,4,3712]{2,1,0:T(4,128)(2,1)S(1)}, u32[]{:S(2)}, u32[]{:S(2)}) collective-permute-start(bf16[3,4,3712]{2,1,0:T(4,128)(2,1)S(1)} %token_rows.1.refs_0_), channel_id=1, source_target_pairs={{0,6},{1,7},{2,4},{3,5},{4,2},{5,3},{6,0},{7,1},{8,9},{9,8},{10,11... | collective-permute-start | bytes 267272 | tf_op jit(solution)/shard_map/ppermute | solution.py:42
  3.1 3.7 %collective-permute-start.1 = (bf16[3,4,3712]{2,1,0:T(4,128)(2,1)S(1)}, bf16[3,4,3712]{2,1,0:T(4,128)(2,1)S(1)}, u32[]{:S(2)}, u32[]{:S(2)}) collective-permute-start(bf16[3,4,3712]{2,1,0:T(4,128)(2,1)S(1)} %token_rows.1.refs_0_), channel_id=1, source_target_pairs={{0,4},{1,5},{2,6},{3,7},{4,0},{5,1},{6,2},{7,3},{8,24},{9,25},{10,... | collective-permute-start | bytes 267272 | tf_op jit(solution)/shard_map/ppermute | solution.py:42
  4.3 4.6 %collective-permute-start.2 = (bf16[3,4,3712]{2,1,0:T(4,128)(2,1)S(1)}, bf16[3,4,3712]{2,1,0:T(4,128)(2,1)S(1)}, u32[]{:S(2)}, u32[]{:S(2)}) collective-permute-start(bf16[3,4,3712]{2,1,0:T(4,128)(2,1)S(1)} %token_rows.1.refs_0_), channel_id=1, source_target_pairs={{0,2},{1,3},{2,0},{3,1},{4,6},{5,7},{6,4},{7,5},{8,25},{9,24},{10,... | collective-permute-start | bytes 267272 | tf_op jit(solution)/shard_map/ppermute | solution.py:42
  9.0 10.2 %collective-permute-start.9 = (bf16[48,3712]{1,0:T(8,128)(2,1)S(1)}, bf16[48,3712]{1,0:T(8,128)(2,1)S(1)}, u32[]{:S(2)}, u32[]{:S(2)}) collective-permute-start(bf16[48,3712]{1,0:T(8,128)(2,1)S(1)} %line_rows.1.refs_0_.refs_1_), channel_id=1, source_target_pairs={{0,8},{1,9},{2,10},{3,11},{4,12},{5,13},{6,14},{7,15},{8,0},{9,1},... | collective-permute-start | bytes 1069064 | tf_op jit(solution)/shard_map/ppermute | solution.py:42
  11.2 18.4 %collective-permute-start.3 = (bf16[48,3712]{1,0:T(8,128)(2,1)S(1)}, bf16[48,3712]{1,0:T(8,128)(2,1)S(1)}, u32[]{:S(2)}, u32[]{:S(2)}) collective-permute-start(bf16[48,3712]{1,0:T(8,128)(2,1)S(1)} %line_rows.1.refs_0_.refs_1_), channel_id=1, source_target_pairs={{0,1},{1,0},{2,3},{3,2},{4,5},{5,4},{6,7},{7,6},{8,14},{9,15},{10,... | collective-permute-start | bytes 1069064 | tf_op jit(solution)/shard_map/ppermute | solution.py:42
  12.4 17.2 %collective-permute-start.4 = (bf16[48,3712]{1,0:T(8,128)(2,1)S(1)}, bf16[48,3712]{1,0:T(8,128)(2,1)S(1)}, u32[]{:S(2)}, u32[]{:S(2)}) collective-permute-start(bf16[48,3712]{1,0:T(8,128)(2,1)S(1)} %line_rows.1.refs_0_.refs_1_), channel_id=1, source_target_pairs={{0,16},{1,17},{2,18},{3,19},{4,20},{5,21},{6,22},{7,23},{8,12},{9,... | collective-permute-start | bytes 1069064 | tf_op jit(solution)/shard_map/ppermute | solution.py:42
  14.0 15.6 %collective-permute-start.5 = (bf16[48,3712]{1,0:T(8,128)(2,1)S(1)}, bf16[48,3712]{1,0:T(8,128)(2,1)S(1)}, u32[]{:S(2)}, u32[]{:S(2)}) collective-permute-start(bf16[48,3712]{1,0:T(8,128)(2,1)S(1)} %line_rows.1.refs_0_.refs_1_), channel_id=1, source_target_pairs={{0,17},{1,16},{2,19},{3,18},{4,21},{5,20},{6,23},{7,22},{8,10},{9,... | collective-permute-start | bytes 1069064 | tf_op jit(solution)/shard_map/ppermute | solution.py:42
  16.2 1.8 %collective-permute-start.6 = (bf16[576,128]{1,0:T(8,128)(2,1)S(1)}, bf16[576,128]{1,0:T(8,128)(2,1)S(1)}, u32[]{:S(2)}, u32[]{:S(2)}) collective-permute-start(bf16[576,128]{1,0:T(8,128)(2,1)S(1)} %get-tuple-element.28), channel_id=1, source_target_pairs={{0,8},{1,9},{2,10},{3,11},{4,12},{5,13},{6,14},{7,15},{8,0},{9,1},... | collective-permute-start | bytes 442376 | tf_op jit(solution)/shard_map/ppermute | solution.py:42
  18.0 8.8 %collective-permute-start.7 = (bf16[576,128]{1,0:T(8,128)(2,1)S(1)}, bf16[576,128]{1,0:T(8,128)(2,1)S(1)}, u32[]{:S(2)}, u32[]{:S(2)}) collective-permute-start(bf16[576,128]{1,0:T(8,128)(2,1)S(1)} %get-tuple-element.29), channel_id=1, source_target_pairs={{0,16},{1,17},{2,18},{3,19},{4,20},{5,21},{6,22},{7,23},{8,24},{9,... | collective-permute-start | bytes 442376 | tf_op jit(solution)/shard_map/ppermute | solution.py:42
  19.2 10.4 %collective-permute-start.8 = (bf16[576,128]{1,0:T(8,128)(2,1)S(1)}, bf16[576,128]{1,0:T(8,128)(2,1)S(1)}, u32[]{:S(2)}, u32[]{:S(2)}) collective-permute-start(bf16[576,128]{1,0:T(8,128)(2,1)S(1)} %get-tuple-element.30), channel_id=1, source_target_pairs={{0,24},{1,25},{2,26},{3,27},{4,28},{5,29},{6,30},{7,31},{8,16},{9,... | collective-permute-start | bytes 442376 | tf_op jit(solution)/shard_map/ppermute | solution.py:42
  29.6 2.6 %collective-permute-start.10 = (bf16[48,3712]{1,0:T(8,128)(2,1)S(1)}, bf16[48,3712]{1,0:T(8,128)(2,1)S(1)}, u32[]{:S(2)}, u32[]{:S(2)}) collective-permute-start(bf16[48,3712]{1,0:T(8,128)(2,1)S(1)} %get-tuple-element.35.refs_1_), channel_id=1, source_target_pairs={{0,8},{1,9},{2,10},{3,11},{4,12},{5,13},{6,14},{7,15},{8,0},{9,1},... | collective-permute-start | bytes 1069064 | tf_op jit(solution)/shard_map/ppermute | solution.py:42
  29.7 2.5 %collective-permute-start.11 = (bf16[48,3712]{1,0:T(8,128)(2,1)S(1)}, bf16[48,3712]{1,0:T(8,128)(2,1)S(1)}, u32[]{:S(2)}, u32[]{:S(2)}) collective-permute-start(bf16[48,3712]{1,0:T(8,128)(2,1)S(1)} %get-tuple-element.36.refs_2_), channel_id=1, source_target_pairs={{0,8},{1,9},{2,10},{3,11},{4,12},{5,13},{6,14},{7,15},{8,0},{9,1},... | collective-permute-start | bytes 1069064 | tf_op jit(solution)/shard_map/ppermute | solution.py:42
  30.2 2.2 %collective-permute-start.12 = (bf16[48,3712]{1,0:T(8,128)(2,1)S(1)}, bf16[48,3712]{1,0:T(8,128)(2,1)S(1)}, u32[]{:S(2)}, u32[]{:S(2)}) collective-permute-start(bf16[48,3712]{1,0:T(8,128)(2,1)S(1)} %get-tuple-element.37.refs_3_), channel_id=1, source_target_pairs={{0,8},{1,9},{2,10},{3,11},{4,12},{5,13},{6,14},{7,15},{8,0},{9,1},... | collective-permute-start | bytes 1069064 | tf_op jit(solution)/shard_map/ppermute | solution.py:42
  34.3 5.1 %copy-start = (bf16[4,128,576]{1,2,0:T(8,128)(2,1)S(1)}, bf16[4,128,576]{1,2,0:T(8,128)(2,1)}, u32[]{:S(2)}) copy-start(bf16[4,128,576]{1,2,0:T(8,128)(2,1)} %param.12) | copy-start | bytes 1769476
  34.3 5.1 %copy-start.1 = (bf16[3,4,128,576]{2,3,1,0:T(8,128)(2,1)S(1)}, bf16[3,4,128,576]{2,3,1,0:T(8,128)(2,1)}, u32[]{:S(2)}) copy-start(bf16[3,4,128,576]{2,3,1,0:T(8,128)(2,1)} %param.11) | copy-start | bytes 5308420
  34.3 5.1 %copy-start.2 = (s32[4,1,2,2]{0,3,2,1:T(2,128)S(1)}, s32[4,1,2,2]{0,3,2,1:T(2,128)}, u32[]{:S(2)}) copy-start(s32[4,1,2,2]{0,3,2,1:T(2,128)} %param.21) | copy-start | bytes 196
  34.4 5.1 %copy-start.3 = (s32[4]{0:T(128)S(1)}, s32[4]{0:T(128)}, u32[]{:S(2)}) copy-start(s32[4]{0:T(128)} %refs_0_.3) | copy-start | bytes 52
  34.4 1.7 %collective-permute-start.15 = (bf16[48,3584]{1,0:T(8,128)(2,1)S(1)}, bf16[48,3584]{1,0:T(8,128)(2,1)S(1)}, u32[]{:S(2)}, u32[]{:S(2)}) collective-permute-start(bf16[48,3584]{1,0:T(8,128)(2,1)S(1)} %get-tuple-element.43), channel_id=1, source_target_pairs={{0,8},{1,9},{2,10},{3,11},{4,12},{5,13},{6,14},{7,15},{8,0},{9,1},... | collective-permute-start | bytes 1032200 | tf_op jit(solution)/shard_map/ppermute | solution.py:42
  34.7 4.6 %collective-permute-start.19 = (bf16[48,3584]{1,0:T(8,128)(2,1)S(1)}, bf16[48,3584]{1,0:T(8,128)(2,1)S(1)}, u32[]{:S(2)}, u32[]{:S(2)}) collective-permute-start(bf16[48,3584]{1,0:T(8,128)(2,1)S(1)} %get-tuple-element.48), channel_id=1, source_target_pairs={{0,8},{1,9},{2,10},{3,11},{4,12},{5,13},{6,14},{7,15},{8,0},{9,1},... | collective-permute-start | bytes 1032200 | tf_op jit(solution)/shard_map/ppermute | solution.py:42
  34.9 2.1 %collective-permute-start.14 = (bf16[48,3584]{1,0:T(8,128)(2,1)S(1)}, bf16[48,3584]{1,0:T(8,128)(2,1)S(1)}, u32[]{:S(2)}, u32[]{:S(2)}) collective-permute-start(bf16[48,3584]{1,0:T(8,128)(2,1)S(1)} %get-tuple-element.41), channel_id=1, source_target_pairs={{0,8},{1,9},{2,10},{3,11},{4,12},{5,13},{6,14},{7,15},{8,0},{9,1},... | collective-permute-start | bytes 1032200 | tf_op jit(solution)/shard_map/ppermute | solution.py:42
  35.2 3.6 %collective-permute-start.13 = (bf16[48,3584]{1,0:T(8,128)(2,1)S(1)}, bf16[48,3584]{1,0:T(8,128)(2,1)S(1)}, u32[]{:S(2)}, u32[]{:S(2)}) collective-permute-start(bf16[48,3584]{1,0:T(8,128)(2,1)S(1)} %get-tuple-element.39), channel_id=1, source_target_pairs={{0,8},{1,9},{2,10},{3,11},{4,12},{5,13},{6,14},{7,15},{8,0},{9,1},... | collective-permute-start | bytes 1032200 | tf_op jit(solution)/shard_map/ppermute | solution.py:42
  36.2 8.3 %collective-permute-start.18 = (bf16[48,3584]{1,0:T(8,128)(2,1)S(1)}, bf16[48,3584]{1,0:T(8,128)(2,1)S(1)}, u32[]{:S(2)}, u32[]{:S(2)}) collective-permute-start(bf16[48,3584]{1,0:T(8,128)(2,1)S(1)} %add_convert_fusion.1.refs_5_), channel_id=1, source_target_pairs={{0,17},{1,16},{2,19},{3,18},{4,21},{5,20},{6,23},{7,22},{8,10},{9,... | collective-permute-start | bytes 1032200 | tf_op jit(solution)/shard_map/ppermute | solution.py:42
  37.1 13.3 %collective-permute-start.17 = (bf16[48,3584]{1,0:T(8,128)(2,1)S(1)}, bf16[48,3584]{1,0:T(8,128)(2,1)S(1)}, u32[]{:S(2)}, u32[]{:S(2)}) collective-permute-start(bf16[48,3584]{1,0:T(8,128)(2,1)S(1)} %add_convert_fusion.2.refs_4_), channel_id=1, source_target_pairs={{0,16},{1,17},{2,18},{3,19},{4,20},{5,21},{6,22},{7,23},{8,12},{9,... | collective-permute-start | bytes 1032200 | tf_op jit(solution)/shard_map/ppermute | solution.py:42
  38.9 19.7 %collective-permute-start.16 = (bf16[48,3584]{1,0:T(8,128)(2,1)S(1)}, bf16[48,3584]{1,0:T(8,128)(2,1)S(1)}, u32[]{:S(2)}, u32[]{:S(2)}) collective-permute-start(bf16[48,3584]{1,0:T(8,128)(2,1)S(1)} %add_convert_fusion.3.refs_3_), channel_id=1, source_target_pairs={{0,1},{1,0},{2,3},{3,2},{4,5},{5,4},{6,7},{7,6},{8,14},{9,15},{10,... | collective-permute-start | bytes 1032200 | tf_op jit(solution)/shard_map/ppermute | solution.py:42
  58.8 3.4 %collective-permute-start.20 = (bf16[3,4,3584]{2,1,0:T(4,128)(2,1)S(1)}, bf16[3,4,3584]{2,1,0:T(4,128)(2,1)S(1)}, u32[]{:S(2)}, u32[]{:S(2)}) collective-permute-start(bf16[3,4,3584]{2,1,0:T(4,128)(2,1)S(1)} %get-tuple-element.50), channel_id=1, source_target_pairs={{0,6},{1,7},{2,4},{3,5},{4,2},{5,3},{6,0},{7,1},{8,9},{9,8},{10,11... | collective-permute-start | bytes 258056 | tf_op jit(solution)/shard_map/ppermute | solution.py:42
  59.7 3.3 %collective-permute-start.21 = (bf16[3,4,3584]{2,1,0:T(4,128)(2,1)S(1)}, bf16[3,4,3584]{2,1,0:T(4,128)(2,1)S(1)}, u32[]{:S(2)}, u32[]{:S(2)}) collective-permute-start(bf16[3,4,3584]{2,1,0:T(4,128)(2,1)S(1)} %get-tuple-element.51), channel_id=1, source_target_pairs={{0,4},{1,5},{2,6},{3,7},{4,0},{5,1},{6,2},{7,3},{8,24},{9,25},{10,... | collective-permute-start | bytes 258056 | tf_op jit(solution)/shard_map/ppermute | solution.py:42
  60.9 4.2 %collective-permute-start.22 = (bf16[3,4,3584]{2,1,0:T(4,128)(2,1)S(1)}, bf16[3,4,3584]{2,1,0:T(4,128)(2,1)S(1)}, u32[]{:S(2)}, u32[]{:S(2)}) collective-permute-start(bf16[3,4,3584]{2,1,0:T(4,128)(2,1)S(1)} %get-tuple-element.52), channel_id=1, source_target_pairs={{0,2},{1,3},{2,0},{3,1},{4,6},{5,7},{6,4},{7,5},{8,25},{9,24},{10,... | collective-permute-start | bytes 258056 | tf_op jit(solution)/shard_map/ppermute | solution.py:42

commit v5 on v4

--- a/solution.py
+++ b/solution.py
@@ -70,8 +70,59 @@
     )(*arrays, *others)
 
 
+def choose_kernel(odd_ref, even_rows_ref, odd_rows_ref, out_ref):
+    odd = odd_ref[0] == 1
+
+    @pl.when(odd)
+    def _():
+        out_ref[...] = odd_rows_ref[...]
+
+    @pl.when(jnp.logical_not(odd))
+    def _():
+        out_ref[...] = even_rows_ref[...]
+
+
+def choose(odd, even_rows, odd_rows, others):
+    vmem = pl.BlockSpec(memory_space=pltpu.VMEM)
+    return pl.pallas_call(
+        ignoring(choose_kernel, 0, len(others)),
+        in_specs=[ANYWHERE] * len(others) + [pl.BlockSpec(memory_space=pltpu.SMEM), vmem, vmem],
+        out_specs=vmem,
+        out_shape=jax.ShapeDtypeStruct(even_rows.shape, even_rows.dtype),
+        compiler_params=KERNEL_PARAMS,
+        cost_estimate=SMALL_COST,
+        name="choose",
+    )(*others, odd, even_rows, odd_rows)
+
+
+def add_if_odd_kernel(odd_ref, rows_ref, more_ref, out_ref):
+    more = jnp.where(odd_ref[0] == 1, more_ref[...].astype(jnp.float32), 0.0)
+    out_ref[...] = (rows_ref[...].astype(jnp.float32) + more).astype(out_ref.dtype)
+
+
+def add_if_odd(odd, rows, more):
+    vmem = pl.BlockSpec(memory_space=pltpu.VMEM)
+    return pl.pallas_call(
+        add_if_odd_kernel,
+        in_specs=[pl.BlockSpec(memory_space=pltpu.SMEM), vmem, vmem],
+        out_specs=vmem,
+        out_shape=jax.ShapeDtypeStruct(rows.shape, rows.dtype),
+        compiler_params=KERNEL_PARAMS,
+        cost_estimate=SMALL_COST,
+        name="add_if_odd",
+    )(odd, rows, more)
+
+
 def plan_entry(plan_ref, group, entry, field):
     return plan_ref[entry, field, group]
+
+
+def stack_entries(new_entries_ref, stack_ref):
+    steps, traces = new_entries_ref.shape[:2]
+    stack_ref[...] = jnp.zeros_like(stack_ref)
+    for step in range(steps):
+        stack_ref[step * traces : (step + 1) * traces, :] = new_entries_ref[step].astype(jnp.float32)
+    return stack_ref[...].astype(jnp.bfloat16)
 
 
 def insert_entries(keys, entries, filled, trace, steps, traces):
@@ -151,8 +202,8 @@
 
 
 def outgoing_kernel(others, lengths_ref, plan_ref, group_ref, cache_hbm, entries_hbm, *refs):
-    entries_ref, out_refs = refs[0], refs[1 : 1 + others]
-    slots_ref, new_entries_ref, stack_ref, semaphores = refs[1 + others :]
+    out_refs = refs[:others]
+    slots_ref, new_entries_ref, stack_ref, semaphores = refs[others:]
     slots = [outgoing_slot(number, plan_ref, group_ref) for number in range(others)]
     copies = [pltpu.make_async_copy(entries_hbm, new_entries_ref, semaphores.at[others])]
     for number, slot in enumerate(slots):
@@ -164,11 +215,7 @@
     for copy in copies:
         copy.wait()
     steps, traces, _ = new_entries_ref.shape
-    stack_ref[...] = jnp.zeros_like(stack_ref)
-    for step in range(steps):
-        stack_ref[step * traces : (step + 1) * traces, :] = new_entries_ref[step].astype(jnp.float32)
-    entries = stack_ref[...].astype(jnp.bfloat16)
-    entries_ref[...] = entries
+    entries = stack_entries(new_entries_ref, stack_ref)
     for number, slot in enumerate(slots):
         out_refs[number][...] = insert_entries(
             slots_ref[number], entries, lengths_ref[slot], slot, steps, traces
@@ -181,12 +228,11 @@
     entry_rows = -(-new_entries.shape[0] * traces // 16) * 16
     smem, vmem = pl.BlockSpec(memory_space=pltpu.SMEM), pl.BlockSpec(memory_space=pltpu.VMEM)
     hbm = pl.BlockSpec(memory_space=pltpu.HBM)
-    entries, *leaving = pl.pallas_call(
+    return pl.pallas_call(
         ignoring(partial(outgoing_kernel, others), 0, len(behind)),
         in_specs=[ANYWHERE] * len(behind) + [smem, smem, smem, hbm, hbm],
-        out_specs=[vmem] * (others + 1),
-        out_shape=[jax.ShapeDtypeStruct((entry_rows, width), cache.dtype)]
-        + [jax.ShapeDtypeStruct((width, capacity), cache.dtype)] * others,
+        out_specs=[vmem] * others,
+        out_shape=[jax.ShapeDtypeStruct((width, capacity), cache.dtype)] * others,
         scratch_shapes=[
             pltpu.VMEM((others, width, capacity), cache.dtype),
             pltpu.VMEM(new_entries.shape, new_entries.dtype),
@@ -204,7 +250,6 @@
         pltpu.with_memory_space_constraint(cache, pltpu.HBM),
         pltpu.with_memory_space_constraint(new_entries, pltpu.HBM),
     )
-    return entries, leaving
 
 
 def line_kernel(*refs):
@@ -227,10 +272,10 @@
     )(*others, *pieces)
 
 
-def line_sums_kernel(*refs):
+def line_sums_kernel(odd_ref, *refs):
     steps, traces, _ = refs[-1].shape
     count = len(refs) - refs[0].shape[0] // (steps * traces)
-    total = refs[0][...].astype(jnp.float32)
+    total = jnp.where(odd_ref[0] == 1, 0.0, refs[0][...].astype(jnp.float32))
     for term_ref in refs[1:count]:
         total = total + term_ref[...].astype(jnp.float32)
     for number, out_ref in enumerate(refs[count:]):
@@ -239,45 +284,38 @@
             out_ref[step] = total[first : first + traces].astype(out_ref.dtype)
 
 
-def line_sums(terms, steps, traces, pieces, others):
+def line_sums(odd, terms, steps, traces, pieces, others):
     lanes = terms[0].shape[1]
     vmem = pl.BlockSpec(memory_space=pltpu.VMEM)
     return pl.pallas_call(
         ignoring(line_sums_kernel, 0, len(others)),
-        in_specs=[ANYWHERE] * len(others) + [vmem] * len(terms),
+        in_specs=[ANYWHERE] * len(others)
+        + [pl.BlockSpec(memory_space=pltpu.SMEM)]
+        + [vmem] * len(terms),
         out_specs=[vmem] * pieces,
         out_shape=[jax.ShapeDtypeStruct((steps, traces, lanes), terms[0].dtype)] * pieces,
-        cost_estimate=LARGE_COST,
-        compiler_params=KERNEL_PARAMS,
+        compiler_params=KERNEL_PARAMS,
+        cost_estimate=LARGE_COST,
         name="line_sums",
-    )(*others, *terms)
+    )(*others, odd, *terms)
 
 
 def attention_kernel(
-    block, lengths_ref, plan_ref, group_ref, queries_ref, cache_ref, entries_ref, *rest
+    block, lengths_ref, queries_ref, cache_ref, entries_ref, contexts_ref, grown_ref, done_ref, stack_ref
 ):
-    received_refs, (contexts_ref, migrated_ref, done_ref) = rest[:-3], rest[-3:]
     done_ref[...] = jnp.zeros_like(done_ref)
     grid_index = pl.program_id(0)
     step_count, _, width, heads = queries_ref.shape
     latent = contexts_ref.shape[3]
     traces = block * pl.num_programs(0)
-    group = group_ref[0]
+    entries = stack_entries(entries_ref, stack_ref)
     for member in range(block):
         trace = grid_index * block + member
         filled = lengths_ref[trace]
         keys = insert_entries(
-            cache_ref[member], entries_ref[...], filled, trace, step_count, traces
-        )
-        migrated = keys
-        for number, received_ref in enumerate(received_refs):
-            partner = group ^ (number + 1)
-            for entry in range(2):
-                lands = (plan_entry(plan_ref, partner, entry, 1) == group) & (
-                    plan_entry(plan_ref, group, entry, 0) == trace
-                )
-                migrated = jnp.where(lands, received_ref[...], migrated)
-        migrated_ref[member] = migrated
+            cache_ref[member], entries, filled, trace, step_count, traces
+        )
+        grown_ref[member] = keys
         key_rows = jnp.transpose(keys)
         flat_queries = jnp.concatenate(
             [queries_ref[s, member] for s in range(step_count)], axis=1
@@ -295,6 +333,44 @@
             preferred_element_type=jnp.float32,
         )
         contexts_ref[:, member] = context.astype(jnp.bfloat16).reshape(step_count, heads, latent)
+
+
+def place_kernel(plan_ref, group_ref, *refs):
+    received_refs, (_, migrated_ref, semaphores) = refs[:-3], refs[-3:]
+    group = group_ref[0]
+    copies = []
+    for number, received_ref in enumerate(received_refs):
+        partner = group ^ (number + 1)
+        lands, slot = jnp.bool_(False), jnp.int32(0)
+        for entry in range(2):
+            here = plan_entry(plan_ref, partner, entry, 1) == group
+            lands = lands | here
+            slot = jnp.where(here, plan_entry(plan_ref, group, entry, 0), slot)
+        copies.append(
+            (
+                lands,
+                pltpu.make_async_copy(received_ref, migrated_ref.at[slot], semaphores.at[number]),
+            )
+        )
+    for lands, copy in copies:
+        pl.when(lands)(copy.start)
+    for lands, copy in copies:
+        pl.when(lands)(copy.wait)
+
+
+def place(grown, received, plan, group):
+    smem = pl.BlockSpec(memory_space=pltpu.SMEM)
+    return pl.pallas_call(
+        place_kernel,
+        in_specs=[smem, smem] + [ANYWHERE] * (len(received) + 1),
+        out_specs=ANYWHERE,
+        out_shape=jax.ShapeDtypeStruct(grown.shape, grown.dtype),
+        input_output_aliases={len(received) + 2: 0},
+        scratch_shapes=[pltpu.SemaphoreType.DMA((len(received),))],
+        compiler_params=KERNEL_PARAMS,
+        cost_estimate=LARGE_COST,
+        name="place",
+    )(plan, group, *received, grown)
 
 
 def fetch_kernel(*refs):
@@ -327,28 +403,29 @@
     )(*others, *weights)
 
 
-def attention(queries, cache, entries, lengths, plan, group, received, others=(), block=2):
+def attention(queries, cache, new_entries, lengths, others=(), block=2):
     step_count, traces, width, heads = queries.shape
     capacity = cache.shape[2]
     latent = width - ROPE
+    entry_rows = -(-step_count * traces // 16) * 16
     whole = lambda shape: pl.BlockSpec(shape, lambda t, *_: (0,) * len(shape))
     return pl.pallas_call(
-        ignoring(partial(attention_kernel, block), 3, len(others)),
+        ignoring(partial(attention_kernel, block), 1, len(others)),
         grid_spec=pltpu.PrefetchScalarGridSpec(
-            num_scalar_prefetch=3,
+            num_scalar_prefetch=1,
             grid=(traces // block,),
             in_specs=[ANYWHERE] * len(others)
             + [
                 pl.BlockSpec((step_count, block, width, heads), lambda t, *_: (0, t, 0, 0)),
                 pl.BlockSpec((block, width, capacity), lambda t, *_: (t, 0, 0)),
-                whole(entries.shape),
-            ]
-            + [whole((width, capacity))] * len(received),
+                whole(new_entries.shape),
+            ],
             out_specs=[
                 pl.BlockSpec((step_count, block, heads, latent), lambda t, *_: (0, t, 0, 0)),
                 pl.BlockSpec((block, width, capacity), lambda t, *_: (t, 0, 0)),
                 whole(DONE.shape),
             ],
+            scratch_shapes=[pltpu.VMEM((entry_rows, width), jnp.float32)],
         ),
         out_shape=[
             jax.ShapeDtypeStruct((step_count, traces, heads, latent), jnp.bfloat16),
@@ -358,7 +435,13 @@
         cost_estimate=LARGE_COST,
         compiler_params=KERNEL_PARAMS,
         name="attention",
-    )(lengths, plan, group, *others, queries, cache, entries, *received)
+    )(
+        lengths,
+        *others,
+        pltpu.with_memory_space_constraint(queries, pltpu.HBM),
+        pltpu.with_memory_space_constraint(cache, pltpu.HBM),
+        new_entries,
+    )
 
 
 def expert_kernel(column_ref, *refs):
@@ -419,45 +502,54 @@
 def dense_layer(
     queries, cache, new_entries, lengths, moe_input, expert_ids, route_gains, weights, plan, group
 ):
-    groups, experts = lax.axis_size("grp"), lax.axis_size("ep")
-    far_flips = [(0, 2 * z) for z in range(1, experts // 2)][::-1]
-    near_flips = [(2 * x, y) for x in range(groups // 2) for y in range(2)][1:]
-    steps, trace_count, width = moe_input.shape
+    groups = lax.axis_size("grp")
+    steps, trace_count, _ = moe_input.shape
+    core, neighbour, skip, opposite = (1, 0), (0, 2), (0, 4), (0, 6)
+    beside, above, diagonal = (0, 1), (2, 0), (2, 1)
+    first_flips = [(opposite, beside), (skip, above), (neighbour, diagonal)]
+    odd = (lax.axis_index("grp") % 2).reshape(1)
     rows = token_rows(group, expert_ids, route_gains, moe_input)
-    first_flips = list(zip(far_flips, near_flips))
-    last_flips = list(zip(near_flips, far_flips))
     line = [rows] + [across(rows, *flips) for flips in first_flips]
-    own_line = line_rows(line, [])
-    plane = [across(own_line, *flips) for flips in last_flips]
-    entries, leaving = outgoing(cache, new_entries, lengths, plan, group, [own_line])
+    own = line_rows(line, [])
+
+    pieces = [
+        across(own, *flips)
+        for flips in ((beside, skip), (above, neighbour), (diagonal, opposite))
+    ]
+    *weights, _ = fetch(weights, [own])
+    own_sums, other_sums = expert([own, across(own, core)], weights)
+    pieces = gate(pieces, [own_sums])
+    other_pieces = [across(piece, core) for piece in pieces]
+    mine = expert(pieces, weights)
+    theirs = expert(other_pieces, weights, mine[:1])
+    sums_3, sums_2, sums_1 = [
+        add_up([own_part, across(part, core)]) for own_part, part in zip(mine[::-1], theirs[::-1])
+    ]
+
+    term_3 = across(sums_3, diagonal, neighbour)
+    contexts, grown, attended = attention(queries, cache, new_entries, lengths, [sums_3])
+    (sums_2,) = gate([sums_2], [term_3, attended])
+    term_2 = across(sums_2, above, neighbour)
+    term_1 = across(add_if_odd(odd, sums_1, term_3), beside, skip)
+    leaving = outgoing(cache, new_entries, lengths, plan, group, [sums_2])
     received = [across(leaving[flip - 1], (flip, 0)) for flip in range(1, groups)]
-    *weights, _ = fetch(weights, [own_line])
-    own_sums, other_sums = expert([own_line, across(own_line, (1, 0))], weights)
-    plane = gate(plane, [*received, own_sums])
-    other_plane = [across(piece, (1, 0)) for piece in plane]
-    own = expert(plane, weights)
-    other = expert(other_plane, weights, own[:1])
-    sums = [add_up([mine, across(theirs, (1, 0))]) for mine, theirs in zip(own, other)]
-    terms = [across(term, *flips) for term, flips in zip(sums, last_flips)]
-    contexts, migrated_cache, attended = attention(
-        queries, cache, entries, lengths, plan, group, received, sums
-    )
-    own_term = add_up([own_sums, across(other_sums, (1, 0))])
-    parts = line_sums([*terms, own_term], steps, trace_count, len(line), [attended])
+    own_term = add_up([own_sums, across(other_sums, core)])
+    parts = line_sums(
+        odd, [term_3, term_1, term_2, own_term], steps, trace_count, len(line), leaving[:1]
+    )
     moe_output = add_up(
         [parts[0]] + [across(part, *flips) for part, flips in zip(parts[1:], first_flips)]
     )
-    return contexts, migrated_cache, moe_output
+    return contexts, place(grown, received, plan, group), moe_output
 
 
 def routed_layer(
     queries, cache, new_entries, lengths, moe_input, expert_ids, route_gains, weights, plan, group
 ):
-    entries, leaving = outgoing(cache, new_entries, lengths, plan, group)
+    leaving = outgoing(cache, new_entries, lengths, plan, group)
     received = [across(leaving[flip - 1], (flip, 0)) for flip in range(1, lax.axis_size("grp"))]
-    contexts, migrated_cache, _ = attention(
-        queries, cache, entries, lengths, plan, group, received
-    )
+    contexts, grown, _ = attention(queries, cache, new_entries, lengths)
+    migrated_cache = place(grown, received, plan, group)
     moe_output = routed_experts(moe_input, expert_ids, route_gains, *weights)
     return contexts, migrated_cache, moe_output
 
@@ -540,6 +632,7 @@
     queries, cache = jnp.swapaxes(queries, 2, 3), jnp.swapaxes(cache, 1, 2)
     plan, group = jnp.transpose(plan[:, 0], (1, 2, 0)), lax.axis_index("grp").reshape(1)
     every_expert = expert_ids.shape[3] == lax.axis_size("ep")
+    every_expert = every_expert and (lax.axis_size("grp"), lax.axis_size("ep")) == (4, 8)
     layer = dense_layer if every_expert else routed_layer
     contexts, migrated_cache, moe_output = layer(
         queries,

time: 66.1 us -> 63.3 us (0.958)
  the two profiles are of different devices: /device:TPU:9 before, /device:TPU:0 now
where the time goes in v5:
time: 63.3 us; the launch traced here: 63 us
  starting transfers between devices  27 us (43%)
  Pallas kernels  21.4 us (34%)
  waiting for transfers between devices  12.7 us (20%)
  other arithmetic  1.08 us (2%)
  between operations  0.87 us (1%)
    ppermute x23, starting transfers between devices, across(): return lax.ppermute(values, BOTH, pairs)  27 us
    ppermute x23, waiting for transfers between devices, across(): return lax.ppermute(values, BOTH, pairs)  12.7 us
    pallas_call x3, Pallas kernels, expert(): pl.pallas_call(ignoring(expert_kernel, 0, len(others)), in_specs=[ANYWHER...  5.79 us
    pallas_call x1, Pallas kernels, attention(): pl.pallas_call(ignoring(partial(attention_kernel, block), 1, len(others))...  5.77 us
    pallas_call x1, Pallas kernels, fetch(): pl.pallas_call(ignoring(fetch_kernel, 0, len(others)), in_specs=[ANYWHERE...  4.82 us
    pallas_call x1, Pallas kernels, outgoing(): pl.pallas_call(ignoring(partial(outgoing_kernel, others), 0, len(behind))...  2.12 us
    pallas_call x1, Pallas kernels, place(): pl.pallas_call(place_kernel, in_specs=[smem, smem] + [ANYWHERE] * (len(re...  1.32 us
  transfers between devices with their start and end apart: 23, of which 8 were waited for; matrix products, arithmetic and copies ran while one was open for 1% of the time, Pallas kernels for 29%

profile of v5, /device:TPU:0, one launch (start us, length us, event | category | flops | bytes accessed | tf_op | source)
XLA Modules:
  0.0 63.0 jit_solution(8373686451053278549)
XLA Ops:
  0.6 1.1 %token_rows.1.refs_0_ = bf16[3,4,3712]{2,1,0:T(4,128)(2,1)S(1)} custom-call(s32[1]{0:T(128)} %bitcast.1.group_ref.refs_3_, s32[3,4,4,8]{3,2,1,0:T(4,128)} %refs_0_.2, f32[3,4,4,8]{3,2,1,0:T(4,128)} %refs_1_.3, bf16[3,4,3584]{2,1,0:T(4,128)(2,1)} %refs_2_.2), custom_call_target="tpu_custom_call" | custom-call | flops 1 | bytes 100000000 | tf_op jit(solution)/shard_map/token_rows/pallas_call | solution.py:190
  1.8 5.1 %collective-permute-start = (bf16[3,4,3712]{2,1,0:T(4,128)(2,1)S(1)}, bf16[3,4,3712]{2,1,0:T(4,128)(2,1)S(1)}, u32[]{:S(2)}, u32[]{:S(2)}) collective-permute-start(bf16[3,4,3712]{2,1,0:T(4,128)(2,1)S(1)} %token_rows.1.refs_0_), channel_id=1, source_target_pairs={{0,6},{1,7},{2,4},{3,5},{4,2},{5,3},{6,0},{7,1},{8,9},{9,8},{10,11... | collective-permute-start | bytes 267272 | tf_op jit(solution)/shard_map/ppermute | solution.py:42
  6.9 0.0 collective-permute-start.1
  6.9 0.6 %collective-permute-start.2 = (bf16[3,4,3712]{2,1,0:T(4,128)(2,1)S(1)}, bf16[3,4,3712]{2,1,0:T(4,128)(2,1)S(1)}, u32[]{:S(2)}, u32[]{:S(2)}) collective-permute-start(bf16[3,4,3712]{2,1,0:T(4,128)(2,1)S(1)} %token_rows.1.refs_0_), channel_id=1, source_target_pairs={{0,2},{1,3},{2,0},{3,1},{4,6},{5,7},{6,4},{7,5},{8,25},{9,24},{10,... | collective-permute-start | bytes 267272 | tf_op jit(solution)/shard_map/ppermute | solution.py:42
  7.5 2.0 %collective-permute-done.refs_1_ = bf16[3,4,3712]{2,1,0:T(4,128)(2,1)S(1)} collective-permute-done((bf16[3,4,3712]{2,1,0:T(4,128)(2,1)S(1)}, bf16[3,4,3712]{2,1,0:T(4,128)(2,1)S(1)}, u32[]{:S(2)}, u32[]{:S(2)}) %collective-permute-start) | collective-permute-done | bytes 89120 | tf_op jit(solution)/shard_map/ppermute | solution.py:42
  9.5 2.9 %collective-permute-done.1.refs_2_ = bf16[3,4,3712]{2,1,0:T(4,128)(2,1)S(1)} collective-permute-done((bf16[3,4,3712]{2,1,0:T(4,128)(2,1)S(1)}, bf16[3,4,3712]{2,1,0:T(4,128)(2,1)S(1)}, u32[]{:S(2)}, u32[]{:S(2)}) %collective-permute-start.1) | collective-permute-done | bytes 89120 | tf_op jit(solution)/shard_map/ppermute | solution.py:42
  12.4 0.1 line_rows.1.refs_0_.refs_1_
  12.5 0.1 collective-permute-start.6
  12.6 1.6 %collective-permute-start.3 = (bf16[48,3712]{1,0:T(8,128)(2,1)S(1)}, bf16[48,3712]{1,0:T(8,128)(2,1)S(1)}, u32[]{:S(2)}, u32[]{:S(2)}) collective-permute-start(bf16[48,3712]{1,0:T(8,128)(2,1)S(1)} %line_rows.1.refs_0_.refs_1_), channel_id=1, source_target_pairs={{0,1},{1,0},{2,3},{3,2},{4,5},{5,4},{6,7},{7,6},{8,12},{9,13},{10,... | collective-permute-start | bytes 1069064 | tf_op jit(solution)/shard_map/ppermute | solution.py:42
  14.1 1.5 %collective-permute-start.4 = (bf16[48,3712]{1,0:T(8,128)(2,1)S(1)}, bf16[48,3712]{1,0:T(8,128)(2,1)S(1)}, u32[]{:S(2)}, u32[]{:S(2)}) collective-permute-start(bf16[48,3712]{1,0:T(8,128)(2,1)S(1)} %line_rows.1.refs_0_.refs_1_), channel_id=1, source_target_pairs={{0,16},{1,17},{2,18},{3,19},{4,20},{5,21},{6,22},{7,23},{8,10},{9,... | collective-permute-start | bytes 1069064 | tf_op jit(solution)/shard_map/ppermute | solution.py:42
  15.6 0.5 collective-permute-start.5
  16.1 4.8 %fetch.1 = (bf16[3584,512]{1,0:T(8,128)(2,1)S(1)}, bf16[3584,512]{1,0:T(8,128)(2,1)S(1)}, bf16[512,3584]{1,0:T(8,128)(2,1)S(1)}, s32[8,128]{1,0:T(8,128)}) custom-call(bf16[48,3712]{1,0:T(8,128)(2,1)S(1)} %line_rows.1.refs_0_.refs_1_, bf16[1,3584,512]{2,1,0:T(8,128)(2,1)} %refs_1_.4, bf16[1,3584,512]{2,1,0:T(8,128)(2,1)} %refs_2_.3, ...), custom_call_target="tpu_custom_call" | custom-call | flops 1 | bytes 100000000 | tf_op jit(solution)/shard_map/fetch/pallas_call | solution.py:393
  20.9 2.0 %expert.3 = (bf16[48,3584]{1,0:T(8,128)(2,1)S(1)}, bf16[48,3584]{1,0:T(8,128)(2,1)S(1)}) custom-call(s32[1]{0:T(128)} %bitcast.refs_0_.refs_1_, bf16[48,3712]{1,0:T(8,128)(2,1)S(1)} %line_rows.1.refs_0_.refs_1_, bf16[48,3712]{1,0:T(8,128)(2,1)S(1)} %collective-permute-done.6.refs_2_, bf16[3584,512]{1,0:T(8,128)(2,1)S(1)} %get-tuple-element.27.refs_3_.refs_4_.refs_5_, ...), custom_call_target="tpu_custom_call" | custom-call | flops 1 | bytes 100000000 | tf_op jit(solution)/shard_map/expert/pallas_call | solution.py:481
  22.9 2.3 %collective-permute-done.5.refs_2_ = bf16[48,3712]{1,0:T(8,128)(2,1)S(1)} collective-permute-done((bf16[48,3712]{1,0:T(8,128)(2,1)S(1)}, bf16[48,3712]{1,0:T(8,128)(2,1)S(1)}, u32[]{:S(2)}, u32[]{:S(2)}) %collective-permute-start.5) | collective-permute-done | bytes 356384 | tf_op jit(solution)/shard_map/ppermute | solution.py:42
  25.3 3.1 %collective-permute-start.7 = (bf16[48,3712]{1,0:T(8,128)(2,1)S(1)}, bf16[48,3712]{1,0:T(8,128)(2,1)S(1)}, u32[]{:S(2)}, u32[]{:S(2)}) collective-permute-start(bf16[48,3712]{1,0:T(8,128)(2,1)S(1)} %get-tuple-element.31.refs_1_), channel_id=1, source_target_pairs={{0,8},{1,9},{2,10},{3,11},{4,12},{5,13},{6,14},{7,15},{8,0},{9,1},... | collective-permute-start | bytes 1069064 | tf_op jit(solution)/shard_map/ppermute | solution.py:42
  28.4 0.0 collective-permute-start.8
  28.4 0.5 collective-permute-start.9
  28.9 1.9 %expert.4 = (bf16[48,3584]{1,0:T(8,128)(2,1)S(1)}, bf16[48,3584]{1,0:T(8,128)(2,1)S(1)}, bf16[48,3584]{1,0:T(8,128)(2,1)S(1)}) custom-call(s32[1]{0:T(128)} %bitcast.refs_0_.refs_1_, bf16[48,3712]{1,0:T(8,128)(2,1)S(1)} %get-tuple-element.31.refs_1_, bf16[48,3712]{1,0:T(8,128)(2,1)S(1)} %get-tuple-element.32.refs_2_, ...), custom_call_target="tpu_custom_call" | custom-call | flops 1 | bytes 100000000 | tf_op jit(solution)/shard_map/expert/pallas_call | solution.py:481
  30.9 0.0 copy-start
  30.9 0.0 copy-start.2
  30.9 1.9 %expert.5 = (bf16[48,3584]{1,0:T(8,128)(2,1)S(1)}, bf16[48,3584]{1,0:T(8,128)(2,1)S(1)}, bf16[48,3584]{1,0:T(8,128)(2,1)S(1)}) custom-call(bf16[48,3584]{1,0:T(8,128)(2,1)S(1)} %get-tuple-element.35.refs_0_, s32[1]{0:T(128)} %bitcast.refs_0_.refs_1_, bf16[48,3712]{1,0:T(8,128)(2,1)S(1)} %collective-permute-done.7.refs_2_, ...), custom_call_target="tpu_custom_call" | custom-call | flops 1 | bytes 100000000 | tf_op jit(solution)/shard_map/expert/pallas_call | solution.py:481
  32.8 0.2 collective-permute-start.10
  33.1 0.3 collective-permute-start.19
  33.4 0.2 collective-permute-start.16
  33.6 0.3 collective-permute-start.11
  33.9 0.6 %collective-permute-done.10 = bf16[48,3584]{1,0:T(8,128)(2,1)S(1)} collective-permute-done((bf16[48,3584]{1,0:T(8,128)(2,1)S(1)}, bf16[48,3584]{1,0:T(8,128)(2,1)S(1)}, u32[]{:S(2)}, u32[]{:S(2)}) %collective-permute-start.10) | collective-permute-done | bytes 344096 | tf_op jit(solution)/shard_map/ppermute | solution.py:42
  34.5 0.1 add_convert_fusion.3.refs_1_
  34.6 2.5 %collective-permute-start.12 = (bf16[48,3584]{1,0:T(8,128)(2,1)S(1)}, bf16[48,3584]{1,0:T(8,128)(2,1)S(1)}, u32[]{:S(2)}, u32[]{:S(2)}) collective-permute-start(bf16[48,3584]{1,0:T(8,128)(2,1)S(1)} %add_convert_fusion.3.refs_1_), channel_id=1, source_target_pairs={{0,17},{1,16},{2,19},{3,18},{4,21},{5,20},{6,23},{7,22},{8,10},{9,... | collective-permute-start | bytes 1032200 | tf_op jit(solution)/shard_map/ppermute | solution.py:42
  37.1 0.1 add_convert_fusion.1.rows_ref
  37.2 0.1 add_convert_fusion.2.refs_0_
  37.3 0.0 copy-start.1
  37.3 5.8 %attention.1 = (bf16[3,4,128,512]{3,2,1,0:T(8,128)(2,1)}, bf16[4,576,128]{2,1,0:T(8,128)(2,1)}, s32[8,128]{1,0:T(8,128)S(1)}) custom-call(s32[4]{0:T(128)S(1)} %copy-done.2, bf16[48,3584]{1,0:T(8,128)(2,1)S(1)} %add_convert_fusion.3.refs_1_, bf16[3,4,576,128]{3,2,1,0:T(8,128)(2,1)} %bitcast.13, bf16[4,576,128]{2,1,0:T(8,128)(2,1)} %bitcast.11, ...), custom_call_target="tpu_custom_call" | custom-call | flops 1 | bytes 100000000 | tf_op jit(solution)/shard_map/attention/pallas_call | solution.py:412
  43.1 0.1 add_if_odd.1
  43.2 1.3 %collective-permute-start.17 = (bf16[48,3584]{1,0:T(8,128)(2,1)S(1)}, bf16[48,3584]{1,0:T(8,128)(2,1)S(1)}, u32[]{:S(2)}, u32[]{:S(2)}) collective-permute-start(bf16[48,3584]{1,0:T(8,128)(2,1)S(1)} %add_if_odd.1), channel_id=1, source_target_pairs={{0,1},{1,0},{2,3},{3,2},{4,5},{5,4},{6,7},{7,6},{8,12},{9,13},{10,... | collective-permute-start | bytes 1032200 | tf_op jit(solution)/shard_map/ppermute | solution.py:42
  44.5 1.5 %collective-permute-start.18 = (bf16[48,3584]{1,0:T(8,128)(2,1)S(1)}, bf16[48,3584]{1,0:T(8,128)(2,1)S(1)}, u32[]{:S(2)}, u32[]{:S(2)}) collective-permute-start(bf16[48,3584]{1,0:T(8,128)(2,1)S(1)} %gate.3.refs_0_), channel_id=1, source_target_pairs={{0,16},{1,17},{2,18},{3,19},{4,20},{5,21},{6,22},{7,23},{8,10},{9,... | collective-permute-start | bytes 1032200 | tf_op jit(solution)/shard_map/ppermute | solution.py:42
  46.0 2.1 %outgoing.1 = (bf16[576,128]{1,0:T(8,128)(2,1)S(1)}, bf16[576,128]{1,0:T(8,128)(2,1)S(1)}, bf16[576,128]{1,0:T(8,128)(2,1)S(1)}) custom-call(bf16[48,3584]{1,0:T(8,128)(2,1)S(1)} %gate.3.refs_0_, s32[4]{0:T(128)} %refs_1_.5, s32[2,2,4]{2,1,0:T(2,128)} %bitcast.9, s32[1]{0:T(128)} %bitcast.1.group_ref.refs_3_, bf16[4,576,128]{2,1,0:T(8,128)(2,1)} %bitcast.12, ...), custom_call_target="tpu_custom_call" | custom-call | flops 1 | bytes 100000000 | tf_op jit(solution)/shard_map/outgoing/pallas_call | solution.py:231
  48.1 0.6 collective-permute-start.13
  48.7 1.6 %collective-permute-start.14 = (bf16[576,128]{1,0:T(8,128)(2,1)S(1)}, bf16[576,128]{1,0:T(8,128)(2,1)S(1)}, u32[]{:S(2)}, u32[]{:S(2)}) collective-permute-start(bf16[576,128]{1,0:T(8,128)(2,1)S(1)} %get-tuple-element.42), channel_id=1, source_target_pairs={{0,16},{1,17},{2,18},{3,19},{4,20},{5,21},{6,22},{7,23},{8,24},{9,... | collective-permute-start | bytes 442376 | tf_op jit(solution)/shard_map/ppermute | solution.py:42
  50.3 0.1 add_convert_fusion.refs_5_
  50.4 0.1 collective-permute-done.17.refs_3_
  50.5 1.6 %collective-permute-done.18.refs_4_ = bf16[48,3584]{1,0:T(8,128)(2,1)S(1)} collective-permute-done((bf16[48,3584]{1,0:T(8,128)(2,1)S(1)}, bf16[48,3584]{1,0:T(8,128)(2,1)S(1)}, u32[]{:S(2)}, u32[]{:S(2)}) %collective-permute-start.18) | collective-permute-done | bytes 344096 | tf_op jit(solution)/shard_map/ppermute | solution.py:42
  52.1 0.2 line_sums.1
  52.3 2.5 %collective-permute-start.20 = (bf16[3,4,3584]{2,1,0:T(4,128)(2,1)S(1)}, bf16[3,4,3584]{2,1,0:T(4,128)(2,1)S(1)}, u32[]{:S(2)}, u32[]{:S(2)}) collective-permute-start(bf16[3,4,3584]{2,1,0:T(4,128)(2,1)S(1)} %get-tuple-element.48), channel_id=1, source_target_pairs={{0,6},{1,7},{2,4},{3,5},{4,2},{5,3},{6,0},{7,1},{8,9},{9,8},{10,11... | collective-permute-start | bytes 258056 | tf_op jit(solution)/shard_map/ppermute | solution.py:42
  54.8 2.9 %collective-permute-start.21 = (bf16[3,4,3584]{2,1,0:T(4,128)(2,1)S(1)}, bf16[3,4,3584]{2,1,0:T(4,128)(2,1)S(1)}, u32[]{:S(2)}, u32[]{:S(2)}) collective-permute-start(bf16[3,4,3584]{2,1,0:T(4,128)(2,1)S(1)} %get-tuple-element.49), channel_id=1, source_target_pairs={{0,4},{1,5},{2,6},{3,7},{4,0},{5,1},{6,2},{7,3},{8,24},{9,25},{10,... | collective-permute-start | bytes 258056 | tf_op jit(solution)/shard_map/ppermute | solution.py:42
  57.8 1.3 %place.1 = bf16[4,576,128]{2,1,0:T(8,128)(2,1)} custom-call(s32[2,2,4]{2,1,0:T(2,128)S(1)} %bitcast.10, s32[1]{0:T(128)} %bitcast.1.group_ref.refs_3_, bf16[576,128]{1,0:T(8,128)(2,1)S(1)} %collective-permute-done.13.refs_0_, bf16[576,128]{1,0:T(8,128)(2,1)S(1)} %collective-permute-done.14.refs_1_, ...), custom_call_target="tpu_custom_call", output_to_operand_aliasing={{}: (5, {})} | custom-call | flops 1 | bytes 100000000 | tf_op jit(solution)/shard_map/place/pallas_call | solution.py:363
  59.1 2.0 %collective-permute-done.21 = bf16[3,4,3584]{2,1,0:T(4,128)(2,1)S(1)} collective-permute-done((bf16[3,4,3584]{2,1,0:T(4,128)(2,1)S(1)}, bf16[3,4,3584]{2,1,0:T(4,128)(2,1)S(1)}, u32[]{:S(2)}, u32[]{:S(2)}) %collective-permute-start.21) | collective-permute-done | bytes 86048 | tf_op jit(solution)/shard_map/ppermute | solution.py:42
  61.1 1.1 %collective-permute-done.22 = bf16[3,4,3584]{2,1,0:T(4,128)(2,1)S(1)} collective-permute-done((bf16[3,4,3584]{2,1,0:T(4,128)(2,1)S(1)}, bf16[3,4,3584]{2,1,0:T(4,128)(2,1)S(1)}, u32[]{:S(2)}, u32[]{:S(2)}) %collective-permute-start.22) | collective-permute-done | bytes 86048 | tf_op jit(solution)/shard_map/ppermute | solution.py:42
  62.2 0.7 %add_convert_fusion.4 = bf16[3,4,3584]{2,1,0:T(4,128)(2,1)} fusion(bf16[3,4,3584]{2,1,0:T(4,128)(2,1)S(1)} %collective-permute-done.22, bf16[3,4,3584]{2,1,0:T(4,128)(2,1)S(1)} %collective-permute-done.21, bf16[3,4,3584]{2,1,0:T(4,128)(2,1)S(1)} %collective-permute-done.20, bf16[3,4,3584]{2,1,0:T(4,128)(2,1)S(1)} %get-tuple-element.47), kind=kLoop, calls=%fused_computation.4 | loop fusion | flops 344064 | bytes 430080 | tf_op jit(solution)/shard_map/convert_element_type | solution.py:499
  (22 shorter events, 0.1 us)
Async XLA Ops:
  1.8 7.7 %collective-permute-start = (bf16[3,4,3712]{2,1,0:T(4,128)(2,1)S(1)}, bf16[3,4,3712]{2,1,0:T(4,128)(2,1)S(1)}, u32[]{:S(2)}, u32[]{:S(2)}) collective-permute-start(bf16[3,4,3712]{2,1,0:T(4,128)(2,1)S(1)} %token_rows.1.refs_0_), channel_id=1, source_target_pairs={{0,6},{1,7},{2,4},{3,5},{4,2},{5,3},{6,0},{7,1},{8,9},{9,8},{10,11... | collective-permute-start | bytes 267272 | tf_op jit(solution)/shard_map/ppermute | solution.py:42
  6.9 5.5 %collective-permute-start.1 = (bf16[3,4,3712]{2,1,0:T(4,128)(2,1)S(1)}, bf16[3,4,3712]{2,1,0:T(4,128)(2,1)S(1)}, u32[]{:S(2)}, u32[]{:S(2)}) collective-permute-start(bf16[3,4,3712]{2,1,0:T(4,128)(2,1)S(1)} %token_rows.1.refs_0_), channel_id=1, source_target_pairs={{0,4},{1,5},{2,6},{3,7},{4,0},{5,1},{6,2},{7,3},{8,24},{9,25},{10,... | collective-permute-start | bytes 267272 | tf_op jit(solution)/shard_map/ppermute | solution.py:42
  6.9 5.5 %collective-permute-start.2 = (bf16[3,4,3712]{2,1,0:T(4,128)(2,1)S(1)}, bf16[3,4,3712]{2,1,0:T(4,128)(2,1)S(1)}, u32[]{:S(2)}, u32[]{:S(2)}) collective-permute-start(bf16[3,4,3712]{2,1,0:T(4,128)(2,1)S(1)} %token_rows.1.refs_0_), channel_id=1, source_target_pairs={{0,2},{1,3},{2,0},{3,1},{4,6},{5,7},{6,4},{7,5},{8,25},{9,24},{10,... | collective-permute-start | bytes 267272 | tf_op jit(solution)/shard_map/ppermute | solution.py:42
  12.5 8.5 %collective-permute-start.6 = (bf16[48,3712]{1,0:T(8,128)(2,1)S(1)}, bf16[48,3712]{1,0:T(8,128)(2,1)S(1)}, u32[]{:S(2)}, u32[]{:S(2)}) collective-permute-start(bf16[48,3712]{1,0:T(8,128)(2,1)S(1)} %line_rows.1.refs_0_.refs_1_), channel_id=1, source_target_pairs={{0,8},{1,9},{2,10},{3,11},{4,12},{5,13},{6,14},{7,15},{8,0},{9,1},... | collective-permute-start | bytes 1069064 | tf_op jit(solution)/shard_map/ppermute | solution.py:42
  12.6 10.4 %collective-permute-start.3 = (bf16[48,3712]{1,0:T(8,128)(2,1)S(1)}, bf16[48,3712]{1,0:T(8,128)(2,1)S(1)}, u32[]{:S(2)}, u32[]{:S(2)}) collective-permute-start(bf16[48,3712]{1,0:T(8,128)(2,1)S(1)} %line_rows.1.refs_0_.refs_1_), channel_id=1, source_target_pairs={{0,1},{1,0},{2,3},{3,2},{4,5},{5,4},{6,7},{7,6},{8,12},{9,13},{10,... | collective-permute-start | bytes 1069064 | tf_op jit(solution)/shard_map/ppermute | solution.py:42
  14.1 8.8 %collective-permute-start.4 = (bf16[48,3712]{1,0:T(8,128)(2,1)S(1)}, bf16[48,3712]{1,0:T(8,128)(2,1)S(1)}, u32[]{:S(2)}, u32[]{:S(2)}) collective-permute-start(bf16[48,3712]{1,0:T(8,128)(2,1)S(1)} %line_rows.1.refs_0_.refs_1_), channel_id=1, source_target_pairs={{0,16},{1,17},{2,18},{3,19},{4,20},{5,21},{6,22},{7,23},{8,10},{9,... | collective-permute-start | bytes 1069064 | tf_op jit(solution)/shard_map/ppermute | solution.py:42
  15.6 9.7 %collective-permute-start.5 = (bf16[48,3712]{1,0:T(8,128)(2,1)S(1)}, bf16[48,3712]{1,0:T(8,128)(2,1)S(1)}, u32[]{:S(2)}, u32[]{:S(2)}) collective-permute-start(bf16[48,3712]{1,0:T(8,128)(2,1)S(1)} %line_rows.1.refs_0_.refs_1_), channel_id=1, source_target_pairs={{0,17},{1,16},{2,19},{3,18},{4,21},{5,20},{6,23},{7,22},{8,14},{9,... | collective-permute-start | bytes 1069064 | tf_op jit(solution)/shard_map/ppermute | solution.py:42
  25.3 5.6 %collective-permute-start.7 = (bf16[48,3712]{1,0:T(8,128)(2,1)S(1)}, bf16[48,3712]{1,0:T(8,128)(2,1)S(1)}, u32[]{:S(2)}, u32[]{:S(2)}) collective-permute-start(bf16[48,3712]{1,0:T(8,128)(2,1)S(1)} %get-tuple-element.31.refs_1_), channel_id=1, source_target_pairs={{0,8},{1,9},{2,10},{3,11},{4,12},{5,13},{6,14},{7,15},{8,0},{9,1},... | collective-permute-start | bytes 1069064 | tf_op jit(solution)/shard_map/ppermute | solution.py:42
  28.4 2.5 %collective-permute-start.8 = (bf16[48,3712]{1,0:T(8,128)(2,1)S(1)}, bf16[48,3712]{1,0:T(8,128)(2,1)S(1)}, u32[]{:S(2)}, u32[]{:S(2)}) collective-permute-start(bf16[48,3712]{1,0:T(8,128)(2,1)S(1)} %get-tuple-element.32.refs_2_), channel_id=1, source_target_pairs={{0,8},{1,9},{2,10},{3,11},{4,12},{5,13},{6,14},{7,15},{8,0},{9,1},... | collective-permute-start | bytes 1069064 | tf_op jit(solution)/shard_map/ppermute | solution.py:42
  28.4 2.5 %collective-permute-start.9 = (bf16[48,3712]{1,0:T(8,128)(2,1)S(1)}, bf16[48,3712]{1,0:T(8,128)(2,1)S(1)}, u32[]{:S(2)}, u32[]{:S(2)}) collective-permute-start(bf16[48,3712]{1,0:T(8,128)(2,1)S(1)} %get-tuple-element.33.refs_3_), channel_id=1, source_target_pairs={{0,8},{1,9},{2,10},{3,11},{4,12},{5,13},{6,14},{7,15},{8,0},{9,1},... | collective-permute-start | bytes 1069064 | tf_op jit(solution)/shard_map/ppermute | solution.py:42
  30.9 6.4 %copy-start = (bf16[3,4,576]{2,1,0:T(4,128)(2,1)S(1)}, bf16[3,4,576]{2,1,0:T(4,128)(2,1)}, u32[]{:S(2)}) copy-start(bf16[3,4,576]{2,1,0:T(4,128)(2,1)} %refs_5_.1) | copy-start | bytes 41476
  30.9 6.4 %copy-start.2 = (s32[4]{0:T(128)S(1)}, s32[4]{0:T(128)}, u32[]{:S(2)}) copy-start(s32[4]{0:T(128)} %refs_1_.5) | copy-start | bytes 52
  32.8 1.7 %collective-permute-start.10 = (bf16[48,3584]{1,0:T(8,128)(2,1)S(1)}, bf16[48,3584]{1,0:T(8,128)(2,1)S(1)}, u32[]{:S(2)}, u32[]{:S(2)}) collective-permute-start(bf16[48,3584]{1,0:T(8,128)(2,1)S(1)} %get-tuple-element.36), channel_id=1, source_target_pairs={{0,8},{1,9},{2,10},{3,11},{4,12},{5,13},{6,14},{7,15},{8,0},{9,1},... | collective-permute-start | bytes 1032200 | tf_op jit(solution)/shard_map/ppermute | solution.py:42
  33.1 17.3 %collective-permute-start.19 = (bf16[48,3584]{1,0:T(8,128)(2,1)S(1)}, bf16[48,3584]{1,0:T(8,128)(2,1)S(1)}, u32[]{:S(2)}, u32[]{:S(2)}) collective-permute-start(bf16[48,3584]{1,0:T(8,128)(2,1)S(1)} %get-tuple-element.46), channel_id=1, source_target_pairs={{0,8},{1,9},{2,10},{3,11},{4,12},{5,13},{6,14},{7,15},{8,0},{9,1},... | collective-permute-start | bytes 1032200 | tf_op jit(solution)/shard_map/ppermute | solution.py:42
  33.4 3.7 %collective-permute-start.16 = (bf16[48,3584]{1,0:T(8,128)(2,1)S(1)}, bf16[48,3584]{1,0:T(8,128)(2,1)S(1)}, u32[]{:S(2)}, u32[]{:S(2)}) collective-permute-start(bf16[48,3584]{1,0:T(8,128)(2,1)S(1)} %get-tuple-element.45), channel_id=1, source_target_pairs={{0,8},{1,9},{2,10},{3,11},{4,12},{5,13},{6,14},{7,15},{8,0},{9,1},... | collective-permute-start | bytes 1032200 | tf_op jit(solution)/shard_map/ppermute | solution.py:42
  33.6 3.6 %collective-permute-start.11 = (bf16[48,3584]{1,0:T(8,128)(2,1)S(1)}, bf16[48,3584]{1,0:T(8,128)(2,1)S(1)}, u32[]{:S(2)}, u32[]{:S(2)}) collective-permute-start(bf16[48,3584]{1,0:T(8,128)(2,1)S(1)} %get-tuple-element.39), channel_id=1, source_target_pairs={{0,8},{1,9},{2,10},{3,11},{4,12},{5,13},{6,14},{7,15},{8,0},{9,1},... | collective-permute-start | bytes 1032200 | tf_op jit(solution)/shard_map/ppermute | solution.py:42
  34.6 8.5 %collective-permute-start.12 = (bf16[48,3584]{1,0:T(8,128)(2,1)S(1)}, bf16[48,3584]{1,0:T(8,128)(2,1)S(1)}, u32[]{:S(2)}, u32[]{:S(2)}) collective-permute-start(bf16[48,3584]{1,0:T(8,128)(2,1)S(1)} %add_convert_fusion.3.refs_1_), channel_id=1, source_target_pairs={{0,17},{1,16},{2,19},{3,18},{4,21},{5,20},{6,23},{7,22},{8,10},{9,... | collective-permute-start | bytes 1032200 | tf_op jit(solution)/shard_map/ppermute | solution.py:42
  37.3 20.4 %copy-start.1 = (s32[4,1,2,2]{0,3,2,1:T(2,128)S(1)}, s32[4,1,2,2]{0,3,2,1:T(2,128)}, u32[]{:S(2)}) copy-start(s32[4,1,2,2]{0,3,2,1:T(2,128)} %param.21) | copy-start | bytes 196
  43.2 7.3 %collective-permute-start.17 = (bf16[48,3584]{1,0:T(8,128)(2,1)S(1)}, bf16[48,3584]{1,0:T(8,128)(2,1)S(1)}, u32[]{:S(2)}, u32[]{:S(2)}) collective-permute-start(bf16[48,3584]{1,0:T(8,128)(2,1)S(1)} %add_if_odd.1), channel_id=1, source_target_pairs={{0,1},{1,0},{2,3},{3,2},{4,5},{5,4},{6,7},{7,6},{8,12},{9,13},{10,... | collective-permute-start | bytes 1032200 | tf_op jit(solution)/shard_map/ppermute | solution.py:42
  44.5 7.6 %collective-permute-start.18 = (bf16[48,3584]{1,0:T(8,128)(2,1)S(1)}, bf16[48,3584]{1,0:T(8,128)(2,1)S(1)}, u32[]{:S(2)}, u32[]{:S(2)}) collective-permute-start(bf16[48,3584]{1,0:T(8,128)(2,1)S(1)} %gate.3.refs_0_), channel_id=1, source_target_pairs={{0,16},{1,17},{2,18},{3,19},{4,20},{5,21},{6,22},{7,23},{8,10},{9,... | collective-permute-start | bytes 1032200 | tf_op jit(solution)/shard_map/ppermute | solution.py:42
  48.1 9.6 %collective-permute-start.13 = (bf16[576,128]{1,0:T(8,128)(2,1)S(1)}, bf16[576,128]{1,0:T(8,128)(2,1)S(1)}, u32[]{:S(2)}, u32[]{:S(2)}) collective-permute-start(bf16[576,128]{1,0:T(8,128)(2,1)S(1)} %get-tuple-element.41.refs_0_), channel_id=1, source_target_pairs={{0,8},{1,9},{2,10},{3,11},{4,12},{5,13},{6,14},{7,15},{8,0},{9,1},... | collective-permute-start | bytes 442376 | tf_op jit(solution)/shard_map/ppermute | solution.py:42
  48.7 9.1 %collective-permute-start.14 = (bf16[576,128]{1,0:T(8,128)(2,1)S(1)}, bf16[576,128]{1,0:T(8,128)(2,1)S(1)}, u32[]{:S(2)}, u32[]{:S(2)}) collective-permute-start(bf16[576,128]{1,0:T(8,128)(2,1)S(1)} %get-tuple-element.42), channel_id=1, source_target_pairs={{0,16},{1,17},{2,18},{3,19},{4,20},{5,21},{6,22},{7,23},{8,24},{9,... | collective-permute-start | bytes 442376 | tf_op jit(solution)/shard_map/ppermute | solution.py:42
  50.3 7.4 %collective-permute-start.15 = (bf16[576,128]{1,0:T(8,128)(2,1)S(1)}, bf16[576,128]{1,0:T(8,128)(2,1)S(1)}, u32[]{:S(2)}, u32[]{:S(2)}) collective-permute-start(bf16[576,128]{1,0:T(8,128)(2,1)S(1)} %get-tuple-element.43), channel_id=1, source_target_pairs={{0,24},{1,25},{2,26},{3,27},{4,28},{5,29},{6,30},{7,31},{8,16},{9,... | collective-permute-start | bytes 442376 | tf_op jit(solution)/shard_map/ppermute | solution.py:42
  52.3 6.8 %collective-permute-start.20 = (bf16[3,4,3584]{2,1,0:T(4,128)(2,1)S(1)}, bf16[3,4,3584]{2,1,0:T(4,128)(2,1)S(1)}, u32[]{:S(2)}, u32[]{:S(2)}) collective-permute-start(bf16[3,4,3584]{2,1,0:T(4,128)(2,1)S(1)} %get-tuple-element.48), channel_id=1, source_target_pairs={{0,6},{1,7},{2,4},{3,5},{4,2},{5,3},{6,0},{7,1},{8,9},{9,8},{10,11... | collective-permute-start | bytes 258056 | tf_op jit(solution)/shard_map/ppermute | solution.py:42
  54.8 6.3 %collective-permute-start.21 = (bf16[3,4,3584]{2,1,0:T(4,128)(2,1)S(1)}, bf16[3,4,3584]{2,1,0:T(4,128)(2,1)S(1)}, u32[]{:S(2)}, u32[]{:S(2)}) collective-permute-start(bf16[3,4,3584]{2,1,0:T(4,128)(2,1)S(1)} %get-tuple-element.49), channel_id=1, source_target_pairs={{0,4},{1,5},{2,6},{3,7},{4,0},{5,1},{6,2},{7,3},{8,24},{9,25},{10,... | collective-permute-start | bytes 258056 | tf_op jit(solution)/shard_map/ppermute | solution.py:42
  57.7 4.5 %collective-permute-start.22 = (bf16[3,4,3584]{2,1,0:T(4,128)(2,1)S(1)}, bf16[3,4,3584]{2,1,0:T(4,128)(2,1)S(1)}, u32[]{:S(2)}, u32[]{:S(2)}) collective-permute-start(bf16[3,4,3584]{2,1,0:T(4,128)(2,1)S(1)} %get-tuple-element.50), channel_id=1, source_target_pairs={{0,2},{1,3},{2,0},{3,1},{4,6},{5,7},{6,4},{7,5},{8,25},{9,24},{10,... | collective-permute-start | bytes 258056 | tf_op jit(solution)/shard_map/ppermute | solution.py:42

commit v6 on v5

--- a/solution.py
+++ b/solution.py
@@ -517,11 +517,11 @@
         for flips in ((beside, skip), (above, neighbour), (diagonal, opposite))
     ]
     *weights, _ = fetch(weights, [own])
-    own_sums, other_sums = expert([own, across(own, core)], weights)
+    (own_sums,) = expert([own], weights)
     pieces = gate(pieces, [own_sums])
-    other_pieces = [across(piece, core) for piece in pieces]
+    other_pieces = [across(piece, core) for piece in [*pieces, own]]
     mine = expert(pieces, weights)
-    theirs = expert(other_pieces, weights, mine[:1])
+    *theirs, other_sums = expert(other_pieces, weights, mine[:1])
     sums_3, sums_2, sums_1 = [
         add_up([own_part, across(part, core)]) for own_part, part in zip(mine[::-1], theirs[::-1])
     ]

time: 63.3 us -> 61.4 us (0.970); the launches traced: 63 us -> 60.2 us
  waiting for transfers between devices: 12.7 us -> 10.9 us
  starting transfers between devices: 27 us -> 25.4 us
    ppermute x23, waiting for transfers between devices: 12.7 us -> 10.9 us  [across(): return lax.ppermute(values, BOTH, pairs)]
    ppermute x23, starting transfers between devices: 27 us -> 25.4 us  [across(): return lax.ppermute(values, BOTH, pairs)]
  transfers between devices with their start and end apart: 23 -> 23, of which waited for: 8 -> 8; matrix products, arithmetic and copies ran while one was open for 1% -> 1% of each run, Pallas kernels for 29% -> 30%
where the time goes in v6:
time: 61.4 us; the launch traced here: 60.2 us
  starting transfers between devices  25.4 us (41%)
  Pallas kernels  22 us (36%)
  waiting for transfers between devices  10.9 us (18%)
  other arithmetic  1.08 us (2%)
  between operations  0.86 us (1%)
    ppermute x23, starting transfers between devices, across(): return lax.ppermute(values, BOTH, pairs)  25.4 us
    ppermute x23, waiting for transfers between devices, across(): return lax.ppermute(values, BOTH, pairs)  10.9 us
    pallas_call x3, Pallas kernels, expert(): pl.pallas_call(ignoring(expert_kernel, 0, len(others)), in_specs=[ANYWHER...  6.4 us
    pallas_call x1, Pallas kernels, attention(): pl.pallas_call(ignoring(partial(attention_kernel, block), 1, len(others))...  5.78 us
    pallas_call x1, Pallas kernels, fetch(): pl.pallas_call(ignoring(fetch_kernel, 0, len(others)), in_specs=[ANYWHERE...  4.82 us
    pallas_call x1, Pallas kernels, outgoing(): pl.pallas_call(ignoring(partial(outgoing_kernel, others), 0, len(behind))...  2.12 us
    pallas_call x1, Pallas kernels, place(): pl.pallas_call(place_kernel, in_specs=[smem, smem] + [ANYWHERE] * (len(re...  1.31 us
  transfers between devices with their start and end apart: 23, of which 8 were waited for; matrix products, arithmetic and copies ran while one was open for 1% of the time, Pallas kernels for 30%

profile of v6, /device:TPU:0, one launch (start us, length us, event | category | flops | bytes accessed | tf_op | source)
XLA Modules:
  0.0 60.2 jit_solution(6091414268251186627)
XLA Ops:
  0.6 1.1 %token_rows.1.refs_0_ = bf16[3,4,3712]{2,1,0:T(4,128)(2,1)S(1)} custom-call(s32[1]{0:T(128)} %bitcast.1.group_ref.refs_3_, s32[3,4,4,8]{3,2,1,0:T(4,128)} %refs_0_.2, f32[3,4,4,8]{3,2,1,0:T(4,128)} %refs_1_.3, bf16[3,4,3584]{2,1,0:T(4,128)(2,1)} %refs_2_.2), custom_call_target="tpu_custom_call" | custom-call | flops 1 | bytes 100000000 | tf_op jit(solution)/shard_map/token_rows/pallas_call | solution.py:190
  1.8 5.1 %collective-permute-start = (bf16[3,4,3712]{2,1,0:T(4,128)(2,1)S(1)}, bf16[3,4,3712]{2,1,0:T(4,128)(2,1)S(1)}, u32[]{:S(2)}, u32[]{:S(2)}) collective-permute-start(bf16[3,4,3712]{2,1,0:T(4,128)(2,1)S(1)} %token_rows.1.refs_0_), channel_id=1, source_target_pairs={{0,6},{1,7},{2,4},{3,5},{4,2},{5,3},{6,0},{7,1},{8,9},{9,8},{10,11... | collective-permute-start | bytes 267272 | tf_op jit(solution)/shard_map/ppermute | solution.py:42
  6.9 0.6 %collective-permute-start.2 = (bf16[3,4,3712]{2,1,0:T(4,128)(2,1)S(1)}, bf16[3,4,3712]{2,1,0:T(4,128)(2,1)S(1)}, u32[]{:S(2)}, u32[]{:S(2)}) collective-permute-start(bf16[3,4,3712]{2,1,0:T(4,128)(2,1)S(1)} %token_rows.1.refs_0_), channel_id=1, source_target_pairs={{0,2},{1,3},{2,0},{3,1},{4,6},{5,7},{6,4},{7,5},{8,25},{9,24},{10,... | collective-permute-start | bytes 267272 | tf_op jit(solution)/shard_map/ppermute | solution.py:42
  7.5 2.0 %collective-permute-done.refs_1_ = bf16[3,4,3712]{2,1,0:T(4,128)(2,1)S(1)} collective-permute-done((bf16[3,4,3712]{2,1,0:T(4,128)(2,1)S(1)}, bf16[3,4,3712]{2,1,0:T(4,128)(2,1)S(1)}, u32[]{:S(2)}, u32[]{:S(2)}) %collective-permute-start) | collective-permute-done | bytes 89120 | tf_op jit(solution)/shard_map/ppermute | solution.py:42
  9.5 2.9 %collective-permute-done.1.refs_2_ = bf16[3,4,3712]{2,1,0:T(4,128)(2,1)S(1)} collective-permute-done((bf16[3,4,3712]{2,1,0:T(4,128)(2,1)S(1)}, bf16[3,4,3712]{2,1,0:T(4,128)(2,1)S(1)}, u32[]{:S(2)}, u32[]{:S(2)}) %collective-permute-start.1) | collective-permute-done | bytes 89120 | tf_op jit(solution)/shard_map/ppermute | solution.py:42
  12.4 0.1 line_rows.1.refs_0_.refs_1_
  12.5 1.6 %collective-permute-start.3 = (bf16[48,3712]{1,0:T(8,128)(2,1)S(1)}, bf16[48,3712]{1,0:T(8,128)(2,1)S(1)}, u32[]{:S(2)}, u32[]{:S(2)}) collective-permute-start(bf16[48,3712]{1,0:T(8,128)(2,1)S(1)} %line_rows.1.refs_0_.refs_1_), channel_id=1, source_target_pairs={{0,1},{1,0},{2,3},{3,2},{4,5},{5,4},{6,7},{7,6},{8,12},{9,13},{10,... | collective-permute-start | bytes 1069064 | tf_op jit(solution)/shard_map/ppermute | solution.py:42
  14.1 1.5 %collective-permute-start.4 = (bf16[48,3712]{1,0:T(8,128)(2,1)S(1)}, bf16[48,3712]{1,0:T(8,128)(2,1)S(1)}, u32[]{:S(2)}, u32[]{:S(2)}) collective-permute-start(bf16[48,3712]{1,0:T(8,128)(2,1)S(1)} %line_rows.1.refs_0_.refs_1_), channel_id=1, source_target_pairs={{0,16},{1,17},{2,18},{3,19},{4,20},{5,21},{6,22},{7,23},{8,10},{9,... | collective-permute-start | bytes 1069064 | tf_op jit(solution)/shard_map/ppermute | solution.py:42
  15.6 0.5 collective-permute-start.5
  16.0 4.8 %fetch.1 = (bf16[3584,512]{1,0:T(8,128)(2,1)S(1)}, bf16[3584,512]{1,0:T(8,128)(2,1)S(1)}, bf16[512,3584]{1,0:T(8,128)(2,1)S(1)}, s32[8,128]{1,0:T(8,128)}) custom-call(bf16[48,3712]{1,0:T(8,128)(2,1)S(1)} %line_rows.1.refs_0_.refs_1_, bf16[1,3584,512]{2,1,0:T(8,128)(2,1)} %refs_1_.4, bf16[1,3584,512]{2,1,0:T(8,128)(2,1)} %refs_2_.3, ...), custom_call_target="tpu_custom_call" | custom-call | flops 1 | bytes 100000000 | tf_op jit(solution)/shard_map/fetch/pallas_call | solution.py:393
  20.9 2.1 %expert.3.refs_3_ = bf16[48,3584]{1,0:T(8,128)(2,1)S(1)} custom-call(s32[1]{0:T(128)} %bitcast.refs_0_.refs_1_, bf16[48,3712]{1,0:T(8,128)(2,1)S(1)} %line_rows.1.refs_0_.refs_1_, bf16[3584,512]{1,0:T(8,128)(2,1)S(1)} %get-tuple-element.26.refs_2_.refs_4_.refs_6_, bf16[3584,512]{1,0:T(8,128)(2,1)S(1)} %get-tuple-element.27.refs_3_.refs_5_.refs_7_, ...), custom_call_target="tpu_custom_call" | custom-call | flops 1 | bytes 100000000 | tf_op jit(solution)/shard_map/expert/pallas_call | solution.py:481
  23.0 2.2 %collective-permute-done.5.refs_2_ = bf16[48,3712]{1,0:T(8,128)(2,1)S(1)} collective-permute-done((bf16[48,3712]{1,0:T(8,128)(2,1)S(1)}, bf16[48,3712]{1,0:T(8,128)(2,1)S(1)}, u32[]{:S(2)}, u32[]{:S(2)}) %collective-permute-start.5) | collective-permute-done | bytes 356384 | tf_op jit(solution)/shard_map/ppermute | solution.py:42
  25.2 1.0 %collective-permute-start.6 = (bf16[48,3712]{1,0:T(8,128)(2,1)S(1)}, bf16[48,3712]{1,0:T(8,128)(2,1)S(1)}, u32[]{:S(2)}, u32[]{:S(2)}) collective-permute-start(bf16[48,3712]{1,0:T(8,128)(2,1)S(1)} %get-tuple-element.29.refs_1_), channel_id=1, source_target_pairs={{0,8},{1,9},{2,10},{3,11},{4,12},{5,13},{6,14},{7,15},{8,0},{9,1},... | collective-permute-start | bytes 1069064 | tf_op jit(solution)/shard_map/ppermute | solution.py:42
  26.2 0.0 collective-permute-start.7
  26.2 0.5 collective-permute-start.8
  26.8 1.9 %expert.4 = (bf16[48,3584]{1,0:T(8,128)(2,1)S(1)}, bf16[48,3584]{1,0:T(8,128)(2,1)S(1)}, bf16[48,3584]{1,0:T(8,128)(2,1)S(1)}) custom-call(s32[1]{0:T(128)} %bitcast.refs_0_.refs_1_, bf16[48,3712]{1,0:T(8,128)(2,1)S(1)} %get-tuple-element.29.refs_1_, bf16[48,3712]{1,0:T(8,128)(2,1)S(1)} %get-tuple-element.30.refs_2_, ...), custom_call_target="tpu_custom_call" | custom-call | flops 1 | bytes 100000000 | tf_op jit(solution)/shard_map/expert/pallas_call | solution.py:481
  28.7 0.0 copy-start
  28.7 0.0 copy-start.2
  28.7 2.4 %expert.5 = (bf16[48,3584]{1,0:T(8,128)(2,1)S(1)}, bf16[48,3584]{1,0:T(8,128)(2,1)S(1)}, bf16[48,3584]{1,0:T(8,128)(2,1)S(1)}, bf16[48,3584]{1,0:T(8,128)(2,1)S(1)}) custom-call(bf16[48,3584]{1,0:T(8,128)(2,1)S(1)} %get-tuple-element.33.refs_0_, s32[1]{0:T(128)} %bitcast.refs_0_.refs_1_, bf16[48,3712]{1,0:T(8,128)(2,1)S(1)} %collective-permute-done.6.refs_2_, ...), custom_call_target="tpu_custom_call" | custom-call | flops 1 | bytes 100000000 | tf_op jit(solution)/shard_map/expert/pallas_call | solution.py:481
  31.2 0.3 collective-permute-start.10
  31.4 0.3 collective-permute-start.19
  31.7 0.2 collective-permute-start.16
  31.9 0.3 collective-permute-start.11
  32.2 0.6 %collective-permute-done.10 = bf16[48,3584]{1,0:T(8,128)(2,1)S(1)} collective-permute-done((bf16[48,3584]{1,0:T(8,128)(2,1)S(1)}, bf16[48,3584]{1,0:T(8,128)(2,1)S(1)}, u32[]{:S(2)}, u32[]{:S(2)}) %collective-permute-start.10) | collective-permute-done | bytes 344096 | tf_op jit(solution)/shard_map/ppermute | solution.py:42
  32.9 0.1 add_convert_fusion.3.refs_1_
  33.0 1.7 %collective-permute-start.12 = (bf16[48,3584]{1,0:T(8,128)(2,1)S(1)}, bf16[48,3584]{1,0:T(8,128)(2,1)S(1)}, u32[]{:S(2)}, u32[]{:S(2)}) collective-permute-start(bf16[48,3584]{1,0:T(8,128)(2,1)S(1)} %add_convert_fusion.3.refs_1_), channel_id=1, source_target_pairs={{0,17},{1,16},{2,19},{3,18},{4,21},{5,20},{6,23},{7,22},{8,10},{9,... | collective-permute-start | bytes 1032200 | tf_op jit(solution)/shard_map/ppermute | solution.py:42
  34.7 0.1 add_convert_fusion.1.rows_ref
  34.7 0.1 add_convert_fusion.2.refs_0_
  34.9 0.0 copy-start.1
  34.9 5.8 %attention.1 = (bf16[3,4,128,512]{3,2,1,0:T(8,128)(2,1)}, bf16[4,576,128]{2,1,0:T(8,128)(2,1)}, s32[8,128]{1,0:T(8,128)S(1)}) custom-call(s32[4]{0:T(128)S(1)} %copy-done.2, bf16[48,3584]{1,0:T(8,128)(2,1)S(1)} %add_convert_fusion.3.refs_1_, bf16[3,4,576,128]{3,2,1,0:T(8,128)(2,1)} %bitcast.13, bf16[4,576,128]{2,1,0:T(8,128)(2,1)} %bitcast.11, ...), custom_call_target="tpu_custom_call" | custom-call | flops 1 | bytes 100000000 | tf_op jit(solution)/shard_map/attention/pallas_call | solution.py:412
  40.7 0.5 collective-permute-done.12.refs_1_.more_ref.refs_2_
  41.2 0.1 add_if_odd.1
  41.3 0.8 %collective-permute-start.17 = (bf16[48,3584]{1,0:T(8,128)(2,1)S(1)}, bf16[48,3584]{1,0:T(8,128)(2,1)S(1)}, u32[]{:S(2)}, u32[]{:S(2)}) collective-permute-start(bf16[48,3584]{1,0:T(8,128)(2,1)S(1)} %add_if_odd.1), channel_id=1, source_target_pairs={{0,1},{1,0},{2,3},{3,2},{4,5},{5,4},{6,7},{7,6},{8,12},{9,13},{10,... | collective-permute-start | bytes 1032200 | tf_op jit(solution)/shard_map/ppermute | solution.py:42
  42.0 1.5 %collective-permute-start.18 = (bf16[48,3584]{1,0:T(8,128)(2,1)S(1)}, bf16[48,3584]{1,0:T(8,128)(2,1)S(1)}, u32[]{:S(2)}, u32[]{:S(2)}) collective-permute-start(bf16[48,3584]{1,0:T(8,128)(2,1)S(1)} %gate.3.refs_0_), channel_id=1, source_target_pairs={{0,16},{1,17},{2,18},{3,19},{4,20},{5,21},{6,22},{7,23},{8,10},{9,... | collective-permute-start | bytes 1032200 | tf_op jit(solution)/shard_map/ppermute | solution.py:42
  43.5 2.1 %outgoing.1 = (bf16[576,128]{1,0:T(8,128)(2,1)S(1)}, bf16[576,128]{1,0:T(8,128)(2,1)S(1)}, bf16[576,128]{1,0:T(8,128)(2,1)S(1)}) custom-call(bf16[48,3584]{1,0:T(8,128)(2,1)S(1)} %gate.3.refs_0_, s32[4]{0:T(128)} %refs_1_.5, s32[2,2,4]{2,1,0:T(2,128)} %bitcast.9, s32[1]{0:T(128)} %bitcast.1.group_ref.refs_3_, bf16[4,576,128]{2,1,0:T(8,128)(2,1)} %bitcast.12, ...), custom_call_target="tpu_custom_call" | custom-call | flops 1 | bytes 100000000 | tf_op jit(solution)/shard_map/outgoing/pallas_call | solution.py:231
  45.7 2.4 %collective-permute-start.13 = (bf16[576,128]{1,0:T(8,128)(2,1)S(1)}, bf16[576,128]{1,0:T(8,128)(2,1)S(1)}, u32[]{:S(2)}, u32[]{:S(2)}) collective-permute-start(bf16[576,128]{1,0:T(8,128)(2,1)S(1)} %get-tuple-element.39.refs_0_), channel_id=1, source_target_pairs={{0,8},{1,9},{2,10},{3,11},{4,12},{5,13},{6,14},{7,15},{8,0},{9,1},... | collective-permute-start | bytes 442376 | tf_op jit(solution)/shard_map/ppermute | solution.py:42
  48.0 0.3 collective-permute-start.14
  48.3 1.2 %collective-permute-start.15 = (bf16[576,128]{1,0:T(8,128)(2,1)S(1)}, bf16[576,128]{1,0:T(8,128)(2,1)S(1)}, u32[]{:S(2)}, u32[]{:S(2)}) collective-permute-start(bf16[576,128]{1,0:T(8,128)(2,1)S(1)} %get-tuple-element.41), channel_id=1, source_target_pairs={{0,24},{1,25},{2,26},{3,27},{4,28},{5,29},{6,30},{7,31},{8,16},{9,... | collective-permute-start | bytes 442376 | tf_op jit(solution)/shard_map/ppermute | solution.py:42
  49.5 0.1 add_convert_fusion.refs_5_
  49.6 0.2 line_sums.1
  49.8 1.8 %collective-permute-start.20 = (bf16[3,4,3584]{2,1,0:T(4,128)(2,1)S(1)}, bf16[3,4,3584]{2,1,0:T(4,128)(2,1)S(1)}, u32[]{:S(2)}, u32[]{:S(2)}) collective-permute-start(bf16[3,4,3584]{2,1,0:T(4,128)(2,1)S(1)} %get-tuple-element.46), channel_id=1, source_target_pairs={{0,6},{1,7},{2,4},{3,5},{4,2},{5,3},{6,0},{7,1},{8,9},{9,8},{10,11... | collective-permute-start | bytes 258056 | tf_op jit(solution)/shard_map/ppermute | solution.py:42
  51.7 3.4 %collective-permute-start.21 = (bf16[3,4,3584]{2,1,0:T(4,128)(2,1)S(1)}, bf16[3,4,3584]{2,1,0:T(4,128)(2,1)S(1)}, u32[]{:S(2)}, u32[]{:S(2)}) collective-permute-start(bf16[3,4,3584]{2,1,0:T(4,128)(2,1)S(1)} %get-tuple-element.47), channel_id=1, source_target_pairs={{0,4},{1,5},{2,6},{3,7},{4,0},{5,1},{6,2},{7,3},{8,24},{9,25},{10,... | collective-permute-start | bytes 258056 | tf_op jit(solution)/shard_map/ppermute | solution.py:42
  55.0 0.5 collective-permute-start.22
  55.5 0.6 %collective-permute-done.15.refs_2_ = bf16[576,128]{1,0:T(8,128)(2,1)S(1)} collective-permute-done((bf16[576,128]{1,0:T(8,128)(2,1)S(1)}, bf16[576,128]{1,0:T(8,128)(2,1)S(1)}, u32[]{:S(2)}, u32[]{:S(2)}) %collective-permute-start.15) | collective-permute-done | bytes 147488 | tf_op jit(solution)/shard_map/ppermute | solution.py:42
  56.2 1.3 %place.1 = bf16[4,576,128]{2,1,0:T(8,128)(2,1)} custom-call(s32[2,2,4]{2,1,0:T(2,128)S(1)} %bitcast.10, s32[1]{0:T(128)} %bitcast.1.group_ref.refs_3_, bf16[576,128]{1,0:T(8,128)(2,1)S(1)} %collective-permute-done.13.refs_0_, bf16[576,128]{1,0:T(8,128)(2,1)S(1)} %collective-permute-done.14.refs_1_, ...), custom_call_target="tpu_custom_call", output_to_operand_aliasing={{}: (5, {})} | custom-call | flops 1 | bytes 100000000 | tf_op jit(solution)/shard_map/place/pallas_call | solution.py:363
  57.5 0.8 %collective-permute-done.21 = bf16[3,4,3584]{2,1,0:T(4,128)(2,1)S(1)} collective-permute-done((bf16[3,4,3584]{2,1,0:T(4,128)(2,1)S(1)}, bf16[3,4,3584]{2,1,0:T(4,128)(2,1)S(1)}, u32[]{:S(2)}, u32[]{:S(2)}) %collective-permute-start.21) | collective-permute-done | bytes 86048 | tf_op jit(solution)/shard_map/ppermute | solution.py:42
  58.3 1.2 %collective-permute-done.22 = bf16[3,4,3584]{2,1,0:T(4,128)(2,1)S(1)} collective-permute-done((bf16[3,4,3584]{2,1,0:T(4,128)(2,1)S(1)}, bf16[3,4,3584]{2,1,0:T(4,128)(2,1)S(1)}, u32[]{:S(2)}, u32[]{:S(2)}) %collective-permute-start.22) | collective-permute-done | bytes 86048 | tf_op jit(solution)/shard_map/ppermute | solution.py:42
  59.5 0.7 %add_convert_fusion.4 = bf16[3,4,3584]{2,1,0:T(4,128)(2,1)} fusion(bf16[3,4,3584]{2,1,0:T(4,128)(2,1)S(1)} %collective-permute-done.22, bf16[3,4,3584]{2,1,0:T(4,128)(2,1)S(1)} %collective-permute-done.21, bf16[3,4,3584]{2,1,0:T(4,128)(2,1)S(1)} %collective-permute-done.20, bf16[3,4,3584]{2,1,0:T(4,128)(2,1)S(1)} %get-tuple-element.45), kind=kLoop, calls=%fused_computation.4 | loop fusion | flops 344064 | bytes 430080 | tf_op jit(solution)/shard_map/convert_element_type | solution.py:499
  (22 shorter events, 0.1 us)
Async XLA Ops:
  1.8 7.7 %collective-permute-start = (bf16[3,4,3712]{2,1,0:T(4,128)(2,1)S(1)}, bf16[3,4,3712]{2,1,0:T(4,128)(2,1)S(1)}, u32[]{:S(2)}, u32[]{:S(2)}) collective-permute-start(bf16[3,4,3712]{2,1,0:T(4,128)(2,1)S(1)} %token_rows.1.refs_0_), channel_id=1, source_target_pairs={{0,6},{1,7},{2,4},{3,5},{4,2},{5,3},{6,0},{7,1},{8,9},{9,8},{10,11... | collective-permute-start | bytes 267272 | tf_op jit(solution)/shard_map/ppermute | solution.py:42
  6.9 5.5 %collective-permute-start.1 = (bf16[3,4,3712]{2,1,0:T(4,128)(2,1)S(1)}, bf16[3,4,3712]{2,1,0:T(4,128)(2,1)S(1)}, u32[]{:S(2)}, u32[]{:S(2)}) collective-permute-start(bf16[3,4,3712]{2,1,0:T(4,128)(2,1)S(1)} %token_rows.1.refs_0_), channel_id=1, source_target_pairs={{0,4},{1,5},{2,6},{3,7},{4,0},{5,1},{6,2},{7,3},{8,24},{9,25},{10,... | collective-permute-start | bytes 267272 | tf_op jit(solution)/shard_map/ppermute | solution.py:42
  6.9 5.5 %collective-permute-start.2 = (bf16[3,4,3712]{2,1,0:T(4,128)(2,1)S(1)}, bf16[3,4,3712]{2,1,0:T(4,128)(2,1)S(1)}, u32[]{:S(2)}, u32[]{:S(2)}) collective-permute-start(bf16[3,4,3712]{2,1,0:T(4,128)(2,1)S(1)} %token_rows.1.refs_0_), channel_id=1, source_target_pairs={{0,2},{1,3},{2,0},{3,1},{4,6},{5,7},{6,4},{7,5},{8,25},{9,24},{10,... | collective-permute-start | bytes 267272 | tf_op jit(solution)/shard_map/ppermute | solution.py:42
  12.5 10.5 %collective-permute-start.3 = (bf16[48,3712]{1,0:T(8,128)(2,1)S(1)}, bf16[48,3712]{1,0:T(8,128)(2,1)S(1)}, u32[]{:S(2)}, u32[]{:S(2)}) collective-permute-start(bf16[48,3712]{1,0:T(8,128)(2,1)S(1)} %line_rows.1.refs_0_.refs_1_), channel_id=1, source_target_pairs={{0,1},{1,0},{2,3},{3,2},{4,5},{5,4},{6,7},{7,6},{8,12},{9,13},{10,... | collective-permute-start | bytes 1069064 | tf_op jit(solution)/shard_map/ppermute | solution.py:42
  14.1 8.9 %collective-permute-start.4 = (bf16[48,3712]{1,0:T(8,128)(2,1)S(1)}, bf16[48,3712]{1,0:T(8,128)(2,1)S(1)}, u32[]{:S(2)}, u32[]{:S(2)}) collective-permute-start(bf16[48,3712]{1,0:T(8,128)(2,1)S(1)} %line_rows.1.refs_0_.refs_1_), channel_id=1, source_target_pairs={{0,16},{1,17},{2,18},{3,19},{4,20},{5,21},{6,22},{7,23},{8,10},{9,... | collective-permute-start | bytes 1069064 | tf_op jit(solution)/shard_map/ppermute | solution.py:42
  15.6 9.7 %collective-permute-start.5 = (bf16[48,3712]{1,0:T(8,128)(2,1)S(1)}, bf16[48,3712]{1,0:T(8,128)(2,1)S(1)}, u32[]{:S(2)}, u32[]{:S(2)}) collective-permute-start(bf16[48,3712]{1,0:T(8,128)(2,1)S(1)} %line_rows.1.refs_0_.refs_1_), channel_id=1, source_target_pairs={{0,17},{1,16},{2,19},{3,18},{4,21},{5,20},{6,23},{7,22},{8,14},{9,... | collective-permute-start | bytes 1069064 | tf_op jit(solution)/shard_map/ppermute | solution.py:42
  16.0 12.6 %collective-permute-start.9 = (bf16[48,3712]{1,0:T(8,128)(2,1)S(1)}, bf16[48,3712]{1,0:T(8,128)(2,1)S(1)}, u32[]{:S(2)}, u32[]{:S(2)}) collective-permute-start(bf16[48,3712]{1,0:T(8,128)(2,1)S(1)} %line_rows.1.refs_0_.refs_1_), channel_id=1, source_target_pairs={{0,8},{1,9},{2,10},{3,11},{4,12},{5,13},{6,14},{7,15},{8,0},{9,1},... | collective-permute-start | bytes 1069064 | tf_op jit(solution)/shard_map/ppermute | solution.py:42
  25.2 3.5 %collective-permute-start.6 = (bf16[48,3712]{1,0:T(8,128)(2,1)S(1)}, bf16[48,3712]{1,0:T(8,128)(2,1)S(1)}, u32[]{:S(2)}, u32[]{:S(2)}) collective-permute-start(bf16[48,3712]{1,0:T(8,128)(2,1)S(1)} %get-tuple-element.29.refs_1_), channel_id=1, source_target_pairs={{0,8},{1,9},{2,10},{3,11},{4,12},{5,13},{6,14},{7,15},{8,0},{9,1},... | collective-permute-start | bytes 1069064 | tf_op jit(solution)/shard_map/ppermute | solution.py:42
  26.2 2.4 %collective-permute-start.7 = (bf16[48,3712]{1,0:T(8,128)(2,1)S(1)}, bf16[48,3712]{1,0:T(8,128)(2,1)S(1)}, u32[]{:S(2)}, u32[]{:S(2)}) collective-permute-start(bf16[48,3712]{1,0:T(8,128)(2,1)S(1)} %get-tuple-element.30.refs_2_), channel_id=1, source_target_pairs={{0,8},{1,9},{2,10},{3,11},{4,12},{5,13},{6,14},{7,15},{8,0},{9,1},... | collective-permute-start | bytes 1069064 | tf_op jit(solution)/shard_map/ppermute | solution.py:42
  26.2 2.4 %collective-permute-start.8 = (bf16[48,3712]{1,0:T(8,128)(2,1)S(1)}, bf16[48,3712]{1,0:T(8,128)(2,1)S(1)}, u32[]{:S(2)}, u32[]{:S(2)}) collective-permute-start(bf16[48,3712]{1,0:T(8,128)(2,1)S(1)} %get-tuple-element.31.refs_3_), channel_id=1, source_target_pairs={{0,8},{1,9},{2,10},{3,11},{4,12},{5,13},{6,14},{7,15},{8,0},{9,1},... | collective-permute-start | bytes 1069064 | tf_op jit(solution)/shard_map/ppermute | solution.py:42
  28.7 6.2 %copy-start = (bf16[3,4,576]{2,1,0:T(4,128)(2,1)S(1)}, bf16[3,4,576]{2,1,0:T(4,128)(2,1)}, u32[]{:S(2)}) copy-start(bf16[3,4,576]{2,1,0:T(4,128)(2,1)} %refs_5_.1) | copy-start | bytes 41476
  28.7 6.2 %copy-start.2 = (s32[4]{0:T(128)S(1)}, s32[4]{0:T(128)}, u32[]{:S(2)}) copy-start(s32[4]{0:T(128)} %refs_1_.5) | copy-start | bytes 52
  31.2 1.7 %collective-permute-start.10 = (bf16[48,3584]{1,0:T(8,128)(2,1)S(1)}, bf16[48,3584]{1,0:T(8,128)(2,1)S(1)}, u32[]{:S(2)}, u32[]{:S(2)}) collective-permute-start(bf16[48,3584]{1,0:T(8,128)(2,1)S(1)} %get-tuple-element.34), channel_id=1, source_target_pairs={{0,8},{1,9},{2,10},{3,11},{4,12},{5,13},{6,14},{7,15},{8,0},{9,1},... | collective-permute-start | bytes 1032200 | tf_op jit(solution)/shard_map/ppermute | solution.py:42
  31.4 16.9 %collective-permute-start.19 = (bf16[48,3584]{1,0:T(8,128)(2,1)S(1)}, bf16[48,3584]{1,0:T(8,128)(2,1)S(1)}, u32[]{:S(2)}, u32[]{:S(2)}) collective-permute-start(bf16[48,3584]{1,0:T(8,128)(2,1)S(1)} %get-tuple-element.44), channel_id=1, source_target_pairs={{0,8},{1,9},{2,10},{3,11},{4,12},{5,13},{6,14},{7,15},{8,0},{9,1},... | collective-permute-start | bytes 1032200 | tf_op jit(solution)/shard_map/ppermute | solution.py:42
  31.7 2.9 %collective-permute-start.16 = (bf16[48,3584]{1,0:T(8,128)(2,1)S(1)}, bf16[48,3584]{1,0:T(8,128)(2,1)S(1)}, u32[]{:S(2)}, u32[]{:S(2)}) collective-permute-start(bf16[48,3584]{1,0:T(8,128)(2,1)S(1)} %get-tuple-element.43), channel_id=1, source_target_pairs={{0,8},{1,9},{2,10},{3,11},{4,12},{5,13},{6,14},{7,15},{8,0},{9,1},... | collective-permute-start | bytes 1032200 | tf_op jit(solution)/shard_map/ppermute | solution.py:42
  31.9 2.8 %collective-permute-start.11 = (bf16[48,3584]{1,0:T(8,128)(2,1)S(1)}, bf16[48,3584]{1,0:T(8,128)(2,1)S(1)}, u32[]{:S(2)}, u32[]{:S(2)}) collective-permute-start(bf16[48,3584]{1,0:T(8,128)(2,1)S(1)} %get-tuple-element.37), channel_id=1, source_target_pairs={{0,8},{1,9},{2,10},{3,11},{4,12},{5,13},{6,14},{7,15},{8,0},{9,1},... | collective-permute-start | bytes 1032200 | tf_op jit(solution)/shard_map/ppermute | solution.py:42
  33.0 8.2 %collective-permute-start.12 = (bf16[48,3584]{1,0:T(8,128)(2,1)S(1)}, bf16[48,3584]{1,0:T(8,128)(2,1)S(1)}, u32[]{:S(2)}, u32[]{:S(2)}) collective-permute-start(bf16[48,3584]{1,0:T(8,128)(2,1)S(1)} %add_convert_fusion.3.refs_1_), channel_id=1, source_target_pairs={{0,17},{1,16},{2,19},{3,18},{4,21},{5,20},{6,23},{7,22},{8,10},{9,... | collective-permute-start | bytes 1032200 | tf_op jit(solution)/shard_map/ppermute | solution.py:42
  34.9 21.3 %copy-start.1 = (s32[4,1,2,2]{0,3,2,1:T(2,128)S(1)}, s32[4,1,2,2]{0,3,2,1:T(2,128)}, u32[]{:S(2)}) copy-start(s32[4,1,2,2]{0,3,2,1:T(2,128)} %param.21) | copy-start | bytes 196
  41.3 8.3 %collective-permute-start.17 = (bf16[48,3584]{1,0:T(8,128)(2,1)S(1)}, bf16[48,3584]{1,0:T(8,128)(2,1)S(1)}, u32[]{:S(2)}, u32[]{:S(2)}) collective-permute-start(bf16[48,3584]{1,0:T(8,128)(2,1)S(1)} %add_if_odd.1), channel_id=1, source_target_pairs={{0,1},{1,0},{2,3},{3,2},{4,5},{5,4},{6,7},{7,6},{8,12},{9,13},{10,... | collective-permute-start | bytes 1032200 | tf_op jit(solution)/shard_map/ppermute | solution.py:42
  42.0 7.5 %collective-permute-start.18 = (bf16[48,3584]{1,0:T(8,128)(2,1)S(1)}, bf16[48,3584]{1,0:T(8,128)(2,1)S(1)}, u32[]{:S(2)}, u32[]{:S(2)}) collective-permute-start(bf16[48,3584]{1,0:T(8,128)(2,1)S(1)} %gate.3.refs_0_), channel_id=1, source_target_pairs={{0,16},{1,17},{2,18},{3,19},{4,20},{5,21},{6,22},{7,23},{8,10},{9,... | collective-permute-start | bytes 1032200 | tf_op jit(solution)/shard_map/ppermute | solution.py:42
  45.7 9.4 %collective-permute-start.13 = (bf16[576,128]{1,0:T(8,128)(2,1)S(1)}, bf16[576,128]{1,0:T(8,128)(2,1)S(1)}, u32[]{:S(2)}, u32[]{:S(2)}) collective-permute-start(bf16[576,128]{1,0:T(8,128)(2,1)S(1)} %get-tuple-element.39.refs_0_), channel_id=1, source_target_pairs={{0,8},{1,9},{2,10},{3,11},{4,12},{5,13},{6,14},{7,15},{8,0},{9,1},... | collective-permute-start | bytes 442376 | tf_op jit(solution)/shard_map/ppermute | solution.py:42
  48.0 7.5 %collective-permute-start.14 = (bf16[576,128]{1,0:T(8,128)(2,1)S(1)}, bf16[576,128]{1,0:T(8,128)(2,1)S(1)}, u32[]{:S(2)}, u32[]{:S(2)}) collective-permute-start(bf16[576,128]{1,0:T(8,128)(2,1)S(1)} %get-tuple-element.40), channel_id=1, source_target_pairs={{0,16},{1,17},{2,18},{3,19},{4,20},{5,21},{6,22},{7,23},{8,24},{9,... | collective-permute-start | bytes 442376 | tf_op jit(solution)/shard_map/ppermute | solution.py:42
  48.3 7.8 %collective-permute-start.15 = (bf16[576,128]{1,0:T(8,128)(2,1)S(1)}, bf16[576,128]{1,0:T(8,128)(2,1)S(1)}, u32[]{:S(2)}, u32[]{:S(2)}) collective-permute-start(bf16[576,128]{1,0:T(8,128)(2,1)S(1)} %get-tuple-element.41), channel_id=1, source_target_pairs={{0,24},{1,25},{2,26},{3,27},{4,28},{5,29},{6,30},{7,31},{8,16},{9,... | collective-permute-start | bytes 442376 | tf_op jit(solution)/shard_map/ppermute | solution.py:42
  49.8 7.7 %collective-permute-start.20 = (bf16[3,4,3584]{2,1,0:T(4,128)(2,1)S(1)}, bf16[3,4,3584]{2,1,0:T(4,128)(2,1)S(1)}, u32[]{:S(2)}, u32[]{:S(2)}) collective-permute-start(bf16[3,4,3584]{2,1,0:T(4,128)(2,1)S(1)} %get-tuple-element.46), channel_id=1, source_target_pairs={{0,6},{1,7},{2,4},{3,5},{4,2},{5,3},{6,0},{7,1},{8,9},{9,8},{10,11... | collective-permute-start | bytes 258056 | tf_op jit(solution)/shard_map/ppermute | solution.py:42
  51.7 6.7 %collective-permute-start.21 = (bf16[3,4,3584]{2,1,0:T(4,128)(2,1)S(1)}, bf16[3,4,3584]{2,1,0:T(4,128)(2,1)S(1)}, u32[]{:S(2)}, u32[]{:S(2)}) collective-permute-start(bf16[3,4,3584]{2,1,0:T(4,128)(2,1)S(1)} %get-tuple-element.47), channel_id=1, source_target_pairs={{0,4},{1,5},{2,6},{3,7},{4,0},{5,1},{6,2},{7,3},{8,24},{9,25},{10,... | collective-permute-start | bytes 258056 | tf_op jit(solution)/shard_map/ppermute | solution.py:42
  55.0 4.5 %collective-permute-start.22 = (bf16[3,4,3584]{2,1,0:T(4,128)(2,1)S(1)}, bf16[3,4,3584]{2,1,0:T(4,128)(2,1)S(1)}, u32[]{:S(2)}, u32[]{:S(2)}) collective-permute-start(bf16[3,4,3584]{2,1,0:T(4,128)(2,1)S(1)} %get-tuple-element.48), channel_id=1, source_target_pairs={{0,2},{1,3},{2,0},{3,1},{4,6},{5,7},{6,4},{7,5},{8,25},{9,24},{10,... | collective-permute-start | bytes 258056 | tf_op jit(solution)/shard_map/ppermute | solution.py:42

commit v7 on v6

--- a/solution.py
+++ b/solution.py
@@ -522,12 +522,12 @@
     other_pieces = [across(piece, core) for piece in [*pieces, own]]
     mine = expert(pieces, weights)
     *theirs, other_sums = expert(other_pieces, weights, mine[:1])
-    sums_3, sums_2, sums_1 = [
-        add_up([own_part, across(part, core)]) for own_part, part in zip(mine[::-1], theirs[::-1])
-    ]
+    sums_3 = add_up([mine[2], across(theirs[2], core)])
 
     term_3 = across(sums_3, diagonal, neighbour)
     contexts, grown, attended = attention(queries, cache, new_entries, lengths, [sums_3])
+    theirs_1, theirs_2 = gate([across(part, core) for part in theirs[:2]], [attended])
+    sums_1, sums_2 = add_up([mine[0], theirs_1]), add_up([mine[1], theirs_2])
     (sums_2,) = gate([sums_2], [term_3, attended])
     term_2 = across(sums_2, above, neighbour)
     term_1 = across(add_if_odd(odd, sums_1, term_3), beside, skip)

time: 61.4 us -> 60.9 us (level)
  no operation moved by 1% of the time
where the time goes in v7:
time: 60.9 us; the launch traced here: 60.2 us
  starting transfers between devices  25.4 us (42%)
  Pallas kernels  22 us (36%)
  waiting for transfers between devices  10.9 us (18%)
  other arithmetic  1.08 us (2%)
  between operations  0.85 us (1%)
    ppermute x23, starting transfers between devices, across(): return lax.ppermute(values, BOTH, pairs)  25.4 us
    ppermute x23, waiting for transfers between devices, across(): return lax.ppermute(values, BOTH, pairs)  10.9 us
    pallas_call x3, Pallas kernels, expert(): pl.pallas_call(ignoring(expert_kernel, 0, len(others)), in_specs=[ANYWHER...  6.4 us
    pallas_call x1, Pallas kernels, attention(): pl.pallas_call(ignoring(partial(attention_kernel, block), 1, len(others))...  5.78 us
    pallas_call x1, Pallas kernels, fetch(): pl.pallas_call(ignoring(fetch_kernel, 0, len(others)), in_specs=[ANYWHERE...  4.82 us
    pallas_call x1, Pallas kernels, outgoing(): pl.pallas_call(ignoring(partial(outgoing_kernel, others), 0, len(behind))...  2.12 us
    pallas_call x1, Pallas kernels, place(): pl.pallas_call(place_kernel, in_specs=[smem, smem] + [ANYWHERE] * (len(re...  1.31 us
  transfers between devices with their start and end apart: 23, of which 8 were waited for; matrix products, arithmetic and copies ran while one was open for 1% of the time, Pallas kernels for 30%

profile of v7, /device:TPU:0, one launch (start us, length us, event | category | flops | bytes accessed | tf_op | source)
XLA Modules:
  0.0 60.2 jit_solution(8458575305414478088)
XLA Ops:
  0.6 1.1 %token_rows.1.refs_0_ = bf16[3,4,3712]{2,1,0:T(4,128)(2,1)S(1)} custom-call(s32[1]{0:T(128)} %bitcast.1.group_ref.refs_3_, s32[3,4,4,8]{3,2,1,0:T(4,128)} %refs_0_.2, f32[3,4,4,8]{3,2,1,0:T(4,128)} %refs_1_.3, bf16[3,4,3584]{2,1,0:T(4,128)(2,1)} %refs_2_.2), custom_call_target="tpu_custom_call" | custom-call | flops 1 | bytes 100000000 | tf_op jit(solution)/shard_map/token_rows/pallas_call | solution.py:190
  1.8 5.1 %collective-permute-start = (bf16[3,4,3712]{2,1,0:T(4,128)(2,1)S(1)}, bf16[3,4,3712]{2,1,0:T(4,128)(2,1)S(1)}, u32[]{:S(2)}, u32[]{:S(2)}) collective-permute-start(bf16[3,4,3712]{2,1,0:T(4,128)(2,1)S(1)} %token_rows.1.refs_0_), channel_id=1, source_target_pairs={{0,6},{1,7},{2,4},{3,5},{4,2},{5,3},{6,0},{7,1},{8,9},{9,8},{10,11... | collective-permute-start | bytes 267272 | tf_op jit(solution)/shard_map/ppermute | solution.py:42
  6.9 0.6 %collective-permute-start.2 = (bf16[3,4,3712]{2,1,0:T(4,128)(2,1)S(1)}, bf16[3,4,3712]{2,1,0:T(4,128)(2,1)S(1)}, u32[]{:S(2)}, u32[]{:S(2)}) collective-permute-start(bf16[3,4,3712]{2,1,0:T(4,128)(2,1)S(1)} %token_rows.1.refs_0_), channel_id=1, source_target_pairs={{0,2},{1,3},{2,0},{3,1},{4,6},{5,7},{6,4},{7,5},{8,25},{9,24},{10,... | collective-permute-start | bytes 267272 | tf_op jit(solution)/shard_map/ppermute | solution.py:42
  7.5 2.0 %collective-permute-done.refs_1_ = bf16[3,4,3712]{2,1,0:T(4,128)(2,1)S(1)} collective-permute-done((bf16[3,4,3712]{2,1,0:T(4,128)(2,1)S(1)}, bf16[3,4,3712]{2,1,0:T(4,128)(2,1)S(1)}, u32[]{:S(2)}, u32[]{:S(2)}) %collective-permute-start) | collective-permute-done | bytes 89120 | tf_op jit(solution)/shard_map/ppermute | solution.py:42
  9.5 2.9 %collective-permute-done.1.refs_2_ = bf16[3,4,3712]{2,1,0:T(4,128)(2,1)S(1)} collective-permute-done((bf16[3,4,3712]{2,1,0:T(4,128)(2,1)S(1)}, bf16[3,4,3712]{2,1,0:T(4,128)(2,1)S(1)}, u32[]{:S(2)}, u32[]{:S(2)}) %collective-permute-start.1) | collective-permute-done | bytes 89120 | tf_op jit(solution)/shard_map/ppermute | solution.py:42
  12.4 0.1 line_rows.1.refs_0_.refs_1_
  12.5 1.6 %collective-permute-start.3 = (bf16[48,3712]{1,0:T(8,128)(2,1)S(1)}, bf16[48,3712]{1,0:T(8,128)(2,1)S(1)}, u32[]{:S(2)}, u32[]{:S(2)}) collective-permute-start(bf16[48,3712]{1,0:T(8,128)(2,1)S(1)} %line_rows.1.refs_0_.refs_1_), channel_id=1, source_target_pairs={{0,1},{1,0},{2,3},{3,2},{4,5},{5,4},{6,7},{7,6},{8,12},{9,13},{10,... | collective-permute-start | bytes 1069064 | tf_op jit(solution)/shard_map/ppermute | solution.py:42
  14.1 1.5 %collective-permute-start.4 = (bf16[48,3712]{1,0:T(8,128)(2,1)S(1)}, bf16[48,3712]{1,0:T(8,128)(2,1)S(1)}, u32[]{:S(2)}, u32[]{:S(2)}) collective-permute-start(bf16[48,3712]{1,0:T(8,128)(2,1)S(1)} %line_rows.1.refs_0_.refs_1_), channel_id=1, source_target_pairs={{0,16},{1,17},{2,18},{3,19},{4,20},{5,21},{6,22},{7,23},{8,10},{9,... | collective-permute-start | bytes 1069064 | tf_op jit(solution)/shard_map/ppermute | solution.py:42
  15.6 0.5 collective-permute-start.5
  16.0 4.8 %fetch.1 = (bf16[3584,512]{1,0:T(8,128)(2,1)S(1)}, bf16[3584,512]{1,0:T(8,128)(2,1)S(1)}, bf16[512,3584]{1,0:T(8,128)(2,1)S(1)}, s32[8,128]{1,0:T(8,128)}) custom-call(bf16[48,3712]{1,0:T(8,128)(2,1)S(1)} %line_rows.1.refs_0_.refs_1_, bf16[1,3584,512]{2,1,0:T(8,128)(2,1)} %refs_1_.4, bf16[1,3584,512]{2,1,0:T(8,128)(2,1)} %refs_2_.3, ...), custom_call_target="tpu_custom_call" | custom-call | flops 1 | bytes 100000000 | tf_op jit(solution)/shard_map/fetch/pallas_call | solution.py:393
  20.9 2.1 %expert.3.refs_3_ = bf16[48,3584]{1,0:T(8,128)(2,1)S(1)} custom-call(s32[1]{0:T(128)} %bitcast.refs_0_.refs_1_, bf16[48,3712]{1,0:T(8,128)(2,1)S(1)} %line_rows.1.refs_0_.refs_1_, bf16[3584,512]{1,0:T(8,128)(2,1)S(1)} %get-tuple-element.28.refs_2_.refs_4_.refs_6_, bf16[3584,512]{1,0:T(8,128)(2,1)S(1)} %get-tuple-element.29.refs_3_.refs_5_.refs_7_, ...), custom_call_target="tpu_custom_call" | custom-call | flops 1 | bytes 100000000 | tf_op jit(solution)/shard_map/expert/pallas_call | solution.py:481
  23.0 2.2 %collective-permute-done.5.refs_2_ = bf16[48,3712]{1,0:T(8,128)(2,1)S(1)} collective-permute-done((bf16[48,3712]{1,0:T(8,128)(2,1)S(1)}, bf16[48,3712]{1,0:T(8,128)(2,1)S(1)}, u32[]{:S(2)}, u32[]{:S(2)}) %collective-permute-start.5) | collective-permute-done | bytes 356384 | tf_op jit(solution)/shard_map/ppermute | solution.py:42
  25.2 1.0 %collective-permute-start.6 = (bf16[48,3712]{1,0:T(8,128)(2,1)S(1)}, bf16[48,3712]{1,0:T(8,128)(2,1)S(1)}, u32[]{:S(2)}, u32[]{:S(2)}) collective-permute-start(bf16[48,3712]{1,0:T(8,128)(2,1)S(1)} %get-tuple-element.31.refs_1_), channel_id=1, source_target_pairs={{0,8},{1,9},{2,10},{3,11},{4,12},{5,13},{6,14},{7,15},{8,0},{9,1},... | collective-permute-start | bytes 1069064 | tf_op jit(solution)/shard_map/ppermute | solution.py:42
  26.2 0.0 collective-permute-start.7
  26.2 0.5 collective-permute-start.8
  26.8 1.9 %expert.4 = (bf16[48,3584]{1,0:T(8,128)(2,1)S(1)}, bf16[48,3584]{1,0:T(8,128)(2,1)S(1)}, bf16[48,3584]{1,0:T(8,128)(2,1)S(1)}) custom-call(s32[1]{0:T(128)} %bitcast.refs_0_.refs_1_, bf16[48,3712]{1,0:T(8,128)(2,1)S(1)} %get-tuple-element.31.refs_1_, bf16[48,3712]{1,0:T(8,128)(2,1)S(1)} %get-tuple-element.32.refs_2_, ...), custom_call_target="tpu_custom_call" | custom-call | flops 1 | bytes 100000000 | tf_op jit(solution)/shard_map/expert/pallas_call | solution.py:481
  28.7 0.0 copy-start
  28.7 0.0 copy-start.2
  28.7 2.4 %expert.5 = (bf16[48,3584]{1,0:T(8,128)(2,1)S(1)}, bf16[48,3584]{1,0:T(8,128)(2,1)S(1)}, bf16[48,3584]{1,0:T(8,128)(2,1)S(1)}, bf16[48,3584]{1,0:T(8,128)(2,1)S(1)}) custom-call(bf16[48,3584]{1,0:T(8,128)(2,1)S(1)} %get-tuple-element.35.refs_0_, s32[1]{0:T(128)} %bitcast.refs_0_.refs_1_, bf16[48,3712]{1,0:T(8,128)(2,1)S(1)} %collective-permute-done.6.refs_2_, ...), custom_call_target="tpu_custom_call" | custom-call | flops 1 | bytes 100000000 | tf_op jit(solution)/shard_map/expert/pallas_call | solution.py:481
  31.2 0.3 collective-permute-start.10
  31.4 0.3 collective-permute-start.19
  31.7 0.2 collective-permute-start.11
  31.9 0.3 collective-permute-start.12
  32.2 0.6 %collective-permute-done.10 = bf16[48,3584]{1,0:T(8,128)(2,1)S(1)} collective-permute-done((bf16[48,3584]{1,0:T(8,128)(2,1)S(1)}, bf16[48,3584]{1,0:T(8,128)(2,1)S(1)}, u32[]{:S(2)}, u32[]{:S(2)}) %collective-permute-start.10) | collective-permute-done | bytes 344096 | tf_op jit(solution)/shard_map/ppermute | solution.py:42
  32.9 0.1 add_convert_fusion.3.refs_1_
  33.0 1.7 %collective-permute-start.13 = (bf16[48,3584]{1,0:T(8,128)(2,1)S(1)}, bf16[48,3584]{1,0:T(8,128)(2,1)S(1)}, u32[]{:S(2)}, u32[]{:S(2)}) collective-permute-start(bf16[48,3584]{1,0:T(8,128)(2,1)S(1)} %add_convert_fusion.3.refs_1_), channel_id=1, source_target_pairs={{0,17},{1,16},{2,19},{3,18},{4,21},{5,20},{6,23},{7,22},{8,10},{9,... | collective-permute-start | bytes 1032200 | tf_op jit(solution)/shard_map/ppermute | solution.py:42
  34.7 5.8 %attention.1 = (bf16[3,4,128,512]{3,2,1,0:T(8,128)(2,1)}, bf16[4,576,128]{2,1,0:T(8,128)(2,1)}, s32[8,128]{1,0:T(8,128)S(1)}) custom-call(s32[4]{0:T(128)S(1)} %copy-done.2, bf16[48,3584]{1,0:T(8,128)(2,1)S(1)} %add_convert_fusion.3.refs_1_, bf16[3,4,576,128]{3,2,1,0:T(8,128)(2,1)} %bitcast.13, bf16[4,576,128]{2,1,0:T(8,128)(2,1)} %bitcast.11, ...), custom_call_target="tpu_custom_call" | custom-call | flops 1 | bytes 100000000 | tf_op jit(solution)/shard_map/attention/pallas_call | solution.py:412
  40.5 0.0 copy-start.1
  40.5 0.1 add_convert_fusion.1.rows_ref
  40.6 0.1 add_convert_fusion.2.refs_0_
  40.6 0.5 collective-permute-done.13.refs_1_.more_ref.refs_2_
  41.2 0.1 add_if_odd.1
  41.3 0.8 %collective-permute-start.17 = (bf16[48,3584]{1,0:T(8,128)(2,1)S(1)}, bf16[48,3584]{1,0:T(8,128)(2,1)S(1)}, u32[]{:S(2)}, u32[]{:S(2)}) collective-permute-start(bf16[48,3584]{1,0:T(8,128)(2,1)S(1)} %add_if_odd.1), channel_id=1, source_target_pairs={{0,1},{1,0},{2,3},{3,2},{4,5},{5,4},{6,7},{7,6},{8,12},{9,13},{10,... | collective-permute-start | bytes 1032200 | tf_op jit(solution)/shard_map/ppermute | solution.py:42
  42.0 1.5 %collective-permute-start.18 = (bf16[48,3584]{1,0:T(8,128)(2,1)S(1)}, bf16[48,3584]{1,0:T(8,128)(2,1)S(1)}, u32[]{:S(2)}, u32[]{:S(2)}) collective-permute-start(bf16[48,3584]{1,0:T(8,128)(2,1)S(1)} %gate.5.refs_0_), channel_id=1, source_target_pairs={{0,16},{1,17},{2,18},{3,19},{4,20},{5,21},{6,22},{7,23},{8,10},{9,... | collective-permute-start | bytes 1032200 | tf_op jit(solution)/shard_map/ppermute | solution.py:42
  43.5 2.1 %outgoing.1 = (bf16[576,128]{1,0:T(8,128)(2,1)S(1)}, bf16[576,128]{1,0:T(8,128)(2,1)S(1)}, bf16[576,128]{1,0:T(8,128)(2,1)S(1)}) custom-call(bf16[48,3584]{1,0:T(8,128)(2,1)S(1)} %gate.5.refs_0_, s32[4]{0:T(128)} %refs_1_.5, s32[2,2,4]{2,1,0:T(2,128)} %bitcast.9, s32[1]{0:T(128)} %bitcast.1.group_ref.refs_3_, bf16[4,576,128]{2,1,0:T(8,128)(2,1)} %bitcast.12, ...), custom_call_target="tpu_custom_call" | custom-call | flops 1 | bytes 100000000 | tf_op jit(solution)/shard_map/outgoing/pallas_call | solution.py:231
  45.7 2.4 %collective-permute-start.14 = (bf16[576,128]{1,0:T(8,128)(2,1)S(1)}, bf16[576,128]{1,0:T(8,128)(2,1)S(1)}, u32[]{:S(2)}, u32[]{:S(2)}) collective-permute-start(bf16[576,128]{1,0:T(8,128)(2,1)S(1)} %get-tuple-element.43.refs_0_), channel_id=1, source_target_pairs={{0,8},{1,9},{2,10},{3,11},{4,12},{5,13},{6,14},{7,15},{8,0},{9,1},... | collective-permute-start | bytes 442376 | tf_op jit(solution)/shard_map/ppermute | solution.py:42
  48.1 0.2 collective-permute-start.15
  48.3 1.2 %collective-permute-start.16 = (bf16[576,128]{1,0:T(8,128)(2,1)S(1)}, bf16[576,128]{1,0:T(8,128)(2,1)S(1)}, u32[]{:S(2)}, u32[]{:S(2)}) collective-permute-start(bf16[576,128]{1,0:T(8,128)(2,1)S(1)} %get-tuple-element.45), channel_id=1, source_target_pairs={{0,24},{1,25},{2,26},{3,27},{4,28},{5,29},{6,30},{7,31},{8,16},{9,... | collective-permute-start | bytes 442376 | tf_op jit(solution)/shard_map/ppermute | solution.py:42
  49.5 0.1 add_convert_fusion.refs_5_
  49.6 0.2 line_sums.1
  49.8 1.9 %collective-permute-start.20 = (bf16[3,4,3584]{2,1,0:T(4,128)(2,1)S(1)}, bf16[3,4,3584]{2,1,0:T(4,128)(2,1)S(1)}, u32[]{:S(2)}, u32[]{:S(2)}) collective-permute-start(bf16[3,4,3584]{2,1,0:T(4,128)(2,1)S(1)} %get-tuple-element.50), channel_id=1, source_target_pairs={{0,6},{1,7},{2,4},{3,5},{4,2},{5,3},{6,0},{7,1},{8,9},{9,8},{10,11... | collective-permute-start | bytes 258056 | tf_op jit(solution)/shard_map/ppermute | solution.py:42
  51.7 3.3 %collective-permute-start.21 = (bf16[3,4,3584]{2,1,0:T(4,128)(2,1)S(1)}, bf16[3,4,3584]{2,1,0:T(4,128)(2,1)S(1)}, u32[]{:S(2)}, u32[]{:S(2)}) collective-permute-start(bf16[3,4,3584]{2,1,0:T(4,128)(2,1)S(1)} %get-tuple-element.51), channel_id=1, source_target_pairs={{0,4},{1,5},{2,6},{3,7},{4,0},{5,1},{6,2},{7,3},{8,24},{9,25},{10,... | collective-permute-start | bytes 258056 | tf_op jit(solution)/shard_map/ppermute | solution.py:42
  55.0 0.5 collective-permute-start.22
  55.5 0.7 %collective-permute-done.16.refs_2_ = bf16[576,128]{1,0:T(8,128)(2,1)S(1)} collective-permute-done((bf16[576,128]{1,0:T(8,128)(2,1)S(1)}, bf16[576,128]{1,0:T(8,128)(2,1)S(1)}, u32[]{:S(2)}, u32[]{:S(2)}) %collective-permute-start.16) | collective-permute-done | bytes 147488 | tf_op jit(solution)/shard_map/ppermute | solution.py:42
  56.2 1.3 %place.1 = bf16[4,576,128]{2,1,0:T(8,128)(2,1)} custom-call(s32[2,2,4]{2,1,0:T(2,128)S(1)} %bitcast.10, s32[1]{0:T(128)} %bitcast.1.group_ref.refs_3_, bf16[576,128]{1,0:T(8,128)(2,1)S(1)} %collective-permute-done.14.refs_0_, bf16[576,128]{1,0:T(8,128)(2,1)S(1)} %collective-permute-done.15.refs_1_, ...), custom_call_target="tpu_custom_call", output_to_operand_aliasing={{}: (5, {})} | custom-call | flops 1 | bytes 100000000 | tf_op jit(solution)/shard_map/place/pallas_call | solution.py:363
  57.5 0.8 %collective-permute-done.21 = bf16[3,4,3584]{2,1,0:T(4,128)(2,1)S(1)} collective-permute-done((bf16[3,4,3584]{2,1,0:T(4,128)(2,1)S(1)}, bf16[3,4,3584]{2,1,0:T(4,128)(2,1)S(1)}, u32[]{:S(2)}, u32[]{:S(2)}) %collective-permute-start.21) | collective-permute-done | bytes 86048 | tf_op jit(solution)/shard_map/ppermute | solution.py:42
  58.3 1.2 %collective-permute-done.22 = bf16[3,4,3584]{2,1,0:T(4,128)(2,1)S(1)} collective-permute-done((bf16[3,4,3584]{2,1,0:T(4,128)(2,1)S(1)}, bf16[3,4,3584]{2,1,0:T(4,128)(2,1)S(1)}, u32[]{:S(2)}, u32[]{:S(2)}) %collective-permute-start.22) | collective-permute-done | bytes 86048 | tf_op jit(solution)/shard_map/ppermute | solution.py:42
  59.5 0.7 %add_convert_fusion.4 = bf16[3,4,3584]{2,1,0:T(4,128)(2,1)} fusion(bf16[3,4,3584]{2,1,0:T(4,128)(2,1)S(1)} %collective-permute-done.22, bf16[3,4,3584]{2,1,0:T(4,128)(2,1)S(1)} %collective-permute-done.21, bf16[3,4,3584]{2,1,0:T(4,128)(2,1)S(1)} %collective-permute-done.20, bf16[3,4,3584]{2,1,0:T(4,128)(2,1)S(1)} %get-tuple-element.49), kind=kLoop, calls=%fused_computation.4 | loop fusion | flops 344064 | bytes 430080 | tf_op jit(solution)/shard_map/convert_element_type | solution.py:499
  (23 shorter events, 0.1 us)
Async XLA Ops:
  1.8 7.7 %collective-permute-start = (bf16[3,4,3712]{2,1,0:T(4,128)(2,1)S(1)}, bf16[3,4,3712]{2,1,0:T(4,128)(2,1)S(1)}, u32[]{:S(2)}, u32[]{:S(2)}) collective-permute-start(bf16[3,4,3712]{2,1,0:T(4,128)(2,1)S(1)} %token_rows.1.refs_0_), channel_id=1, source_target_pairs={{0,6},{1,7},{2,4},{3,5},{4,2},{5,3},{6,0},{7,1},{8,9},{9,8},{10,11... | collective-permute-start | bytes 267272 | tf_op jit(solution)/shard_map/ppermute | solution.py:42
  6.9 5.5 %collective-permute-start.1 = (bf16[3,4,3712]{2,1,0:T(4,128)(2,1)S(1)}, bf16[3,4,3712]{2,1,0:T(4,128)(2,1)S(1)}, u32[]{:S(2)}, u32[]{:S(2)}) collective-permute-start(bf16[3,4,3712]{2,1,0:T(4,128)(2,1)S(1)} %token_rows.1.refs_0_), channel_id=1, source_target_pairs={{0,4},{1,5},{2,6},{3,7},{4,0},{5,1},{6,2},{7,3},{8,24},{9,25},{10,... | collective-permute-start | bytes 267272 | tf_op jit(solution)/shard_map/ppermute | solution.py:42
  6.9 5.5 %collective-permute-start.2 = (bf16[3,4,3712]{2,1,0:T(4,128)(2,1)S(1)}, bf16[3,4,3712]{2,1,0:T(4,128)(2,1)S(1)}, u32[]{:S(2)}, u32[]{:S(2)}) collective-permute-start(bf16[3,4,3712]{2,1,0:T(4,128)(2,1)S(1)} %token_rows.1.refs_0_), channel_id=1, source_target_pairs={{0,2},{1,3},{2,0},{3,1},{4,6},{5,7},{6,4},{7,5},{8,25},{9,24},{10,... | collective-permute-start | bytes 267272 | tf_op jit(solution)/shard_map/ppermute | solution.py:42
  12.5 10.5 %collective-permute-start.3 = (bf16[48,3712]{1,0:T(8,128)(2,1)S(1)}, bf16[48,3712]{1,0:T(8,128)(2,1)S(1)}, u32[]{:S(2)}, u32[]{:S(2)}) collective-permute-start(bf16[48,3712]{1,0:T(8,128)(2,1)S(1)} %line_rows.1.refs_0_.refs_1_), channel_id=1, source_target_pairs={{0,1},{1,0},{2,3},{3,2},{4,5},{5,4},{6,7},{7,6},{8,12},{9,13},{10,... | collective-permute-start | bytes 1069064 | tf_op jit(solution)/shard_map/ppermute | solution.py:42
  14.1 8.9 %collective-permute-start.4 = (bf16[48,3712]{1,0:T(8,128)(2,1)S(1)}, bf16[48,3712]{1,0:T(8,128)(2,1)S(1)}, u32[]{:S(2)}, u32[]{:S(2)}) collective-permute-start(bf16[48,3712]{1,0:T(8,128)(2,1)S(1)} %line_rows.1.refs_0_.refs_1_), channel_id=1, source_target_pairs={{0,16},{1,17},{2,18},{3,19},{4,20},{5,21},{6,22},{7,23},{8,10},{9,... | collective-permute-start | bytes 1069064 | tf_op jit(solution)/shard_map/ppermute | solution.py:42
  15.6 9.7 %collective-permute-start.5 = (bf16[48,3712]{1,0:T(8,128)(2,1)S(1)}, bf16[48,3712]{1,0:T(8,128)(2,1)S(1)}, u32[]{:S(2)}, u32[]{:S(2)}) collective-permute-start(bf16[48,3712]{1,0:T(8,128)(2,1)S(1)} %line_rows.1.refs_0_.refs_1_), channel_id=1, source_target_pairs={{0,17},{1,16},{2,19},{3,18},{4,21},{5,20},{6,23},{7,22},{8,14},{9,... | collective-permute-start | bytes 1069064 | tf_op jit(solution)/shard_map/ppermute | solution.py:42
  16.0 12.6 %collective-permute-start.9 = (bf16[48,3712]{1,0:T(8,128)(2,1)S(1)}, bf16[48,3712]{1,0:T(8,128)(2,1)S(1)}, u32[]{:S(2)}, u32[]{:S(2)}) collective-permute-start(bf16[48,3712]{1,0:T(8,128)(2,1)S(1)} %line_rows.1.refs_0_.refs_1_), channel_id=1, source_target_pairs={{0,8},{1,9},{2,10},{3,11},{4,12},{5,13},{6,14},{7,15},{8,0},{9,1},... | collective-permute-start | bytes 1069064 | tf_op jit(solution)/shard_map/ppermute | solution.py:42
  25.2 3.5 %collective-permute-start.6 = (bf16[48,3712]{1,0:T(8,128)(2,1)S(1)}, bf16[48,3712]{1,0:T(8,128)(2,1)S(1)}, u32[]{:S(2)}, u32[]{:S(2)}) collective-permute-start(bf16[48,3712]{1,0:T(8,128)(2,1)S(1)} %get-tuple-element.31.refs_1_), channel_id=1, source_target_pairs={{0,8},{1,9},{2,10},{3,11},{4,12},{5,13},{6,14},{7,15},{8,0},{9,1},... | collective-permute-start | bytes 1069064 | tf_op jit(solution)/shard_map/ppermute | solution.py:42
  26.2 2.4 %collective-permute-start.7 = (bf16[48,3712]{1,0:T(8,128)(2,1)S(1)}, bf16[48,3712]{1,0:T(8,128)(2,1)S(1)}, u32[]{:S(2)}, u32[]{:S(2)}) collective-permute-start(bf16[48,3712]{1,0:T(8,128)(2,1)S(1)} %get-tuple-element.32.refs_2_), channel_id=1, source_target_pairs={{0,8},{1,9},{2,10},{3,11},{4,12},{5,13},{6,14},{7,15},{8,0},{9,1},... | collective-permute-start | bytes 1069064 | tf_op jit(solution)/shard_map/ppermute | solution.py:42
  26.2 2.4 %collective-permute-start.8 = (bf16[48,3712]{1,0:T(8,128)(2,1)S(1)}, bf16[48,3712]{1,0:T(8,128)(2,1)S(1)}, u32[]{:S(2)}, u32[]{:S(2)}) collective-permute-start(bf16[48,3712]{1,0:T(8,128)(2,1)S(1)} %get-tuple-element.33.refs_3_), channel_id=1, source_target_pairs={{0,8},{1,9},{2,10},{3,11},{4,12},{5,13},{6,14},{7,15},{8,0},{9,1},... | collective-permute-start | bytes 1069064 | tf_op jit(solution)/shard_map/ppermute | solution.py:42
  28.7 6.0 %copy-start = (bf16[3,4,576]{2,1,0:T(4,128)(2,1)S(1)}, bf16[3,4,576]{2,1,0:T(4,128)(2,1)}, u32[]{:S(2)}) copy-start(bf16[3,4,576]{2,1,0:T(4,128)(2,1)} %refs_5_.1) | copy-start | bytes 41476
  28.7 6.0 %copy-start.2 = (s32[4]{0:T(128)S(1)}, s32[4]{0:T(128)}, u32[]{:S(2)}) copy-start(s32[4]{0:T(128)} %refs_1_.5) | copy-start | bytes 52
  31.2 1.7 %collective-permute-start.10 = (bf16[48,3584]{1,0:T(8,128)(2,1)S(1)}, bf16[48,3584]{1,0:T(8,128)(2,1)S(1)}, u32[]{:S(2)}, u32[]{:S(2)}) collective-permute-start(bf16[48,3584]{1,0:T(8,128)(2,1)S(1)} %get-tuple-element.36), channel_id=1, source_target_pairs={{0,8},{1,9},{2,10},{3,11},{4,12},{5,13},{6,14},{7,15},{8,0},{9,1},... | collective-permute-start | bytes 1032200 | tf_op jit(solution)/shard_map/ppermute | solution.py:42
  31.4 16.9 %collective-permute-start.19 = (bf16[48,3584]{1,0:T(8,128)(2,1)S(1)}, bf16[48,3584]{1,0:T(8,128)(2,1)S(1)}, u32[]{:S(2)}, u32[]{:S(2)}) collective-permute-start(bf16[48,3584]{1,0:T(8,128)(2,1)S(1)} %get-tuple-element.48), channel_id=1, source_target_pairs={{0,8},{1,9},{2,10},{3,11},{4,12},{5,13},{6,14},{7,15},{8,0},{9,1},... | collective-permute-start | bytes 1032200 | tf_op jit(solution)/shard_map/ppermute | solution.py:42
  31.7 8.7 %collective-permute-start.11 = (bf16[48,3584]{1,0:T(8,128)(2,1)S(1)}, bf16[48,3584]{1,0:T(8,128)(2,1)S(1)}, u32[]{:S(2)}, u32[]{:S(2)}) collective-permute-start(bf16[48,3584]{1,0:T(8,128)(2,1)S(1)} %get-tuple-element.39), channel_id=1, source_target_pairs={{0,8},{1,9},{2,10},{3,11},{4,12},{5,13},{6,14},{7,15},{8,0},{9,1},... | collective-permute-start | bytes 1032200 | tf_op jit(solution)/shard_map/ppermute | solution.py:42
  31.9 8.5 %collective-permute-start.12 = (bf16[48,3584]{1,0:T(8,128)(2,1)S(1)}, bf16[48,3584]{1,0:T(8,128)(2,1)S(1)}, u32[]{:S(2)}, u32[]{:S(2)}) collective-permute-start(bf16[48,3584]{1,0:T(8,128)(2,1)S(1)} %get-tuple-element.40), channel_id=1, source_target_pairs={{0,8},{1,9},{2,10},{3,11},{4,12},{5,13},{6,14},{7,15},{8,0},{9,1},... | collective-permute-start | bytes 1032200 | tf_op jit(solution)/shard_map/ppermute | solution.py:42
  33.0 8.2 %collective-permute-start.13 = (bf16[48,3584]{1,0:T(8,128)(2,1)S(1)}, bf16[48,3584]{1,0:T(8,128)(2,1)S(1)}, u32[]{:S(2)}, u32[]{:S(2)}) collective-permute-start(bf16[48,3584]{1,0:T(8,128)(2,1)S(1)} %add_convert_fusion.3.refs_1_), channel_id=1, source_target_pairs={{0,17},{1,16},{2,19},{3,18},{4,21},{5,20},{6,23},{7,22},{8,10},{9,... | collective-permute-start | bytes 1032200 | tf_op jit(solution)/shard_map/ppermute | solution.py:42
  40.5 15.7 %copy-start.1 = (s32[4,1,2,2]{0,3,2,1:T(2,128)S(1)}, s32[4,1,2,2]{0,3,2,1:T(2,128)}, u32[]{:S(2)}) copy-start(s32[4,1,2,2]{0,3,2,1:T(2,128)} %param.21) | copy-start | bytes 196
  41.3 8.3 %collective-permute-start.17 = (bf16[48,3584]{1,0:T(8,128)(2,1)S(1)}, bf16[48,3584]{1,0:T(8,128)(2,1)S(1)}, u32[]{:S(2)}, u32[]{:S(2)}) collective-permute-start(bf16[48,3584]{1,0:T(8,128)(2,1)S(1)} %add_if_odd.1), channel_id=1, source_target_pairs={{0,1},{1,0},{2,3},{3,2},{4,5},{5,4},{6,7},{7,6},{8,12},{9,13},{10,... | collective-permute-start | bytes 1032200 | tf_op jit(solution)/shard_map/ppermute | solution.py:42
  42.0 7.5 %collective-permute-start.18 = (bf16[48,3584]{1,0:T(8,128)(2,1)S(1)}, bf16[48,3584]{1,0:T(8,128)(2,1)S(1)}, u32[]{:S(2)}, u32[]{:S(2)}) collective-permute-start(bf16[48,3584]{1,0:T(8,128)(2,1)S(1)} %gate.5.refs_0_), channel_id=1, source_target_pairs={{0,16},{1,17},{2,18},{3,19},{4,20},{5,21},{6,22},{7,23},{8,10},{9,... | collective-permute-start | bytes 1032200 | tf_op jit(solution)/shard_map/ppermute | solution.py:42
  45.7 9.4 %collective-permute-start.14 = (bf16[576,128]{1,0:T(8,128)(2,1)S(1)}, bf16[576,128]{1,0:T(8,128)(2,1)S(1)}, u32[]{:S(2)}, u32[]{:S(2)}) collective-permute-start(bf16[576,128]{1,0:T(8,128)(2,1)S(1)} %get-tuple-element.43.refs_0_), channel_id=1, source_target_pairs={{0,8},{1,9},{2,10},{3,11},{4,12},{5,13},{6,14},{7,15},{8,0},{9,1},... | collective-permute-start | bytes 442376 | tf_op jit(solution)/shard_map/ppermute | solution.py:42
  48.1 7.5 %collective-permute-start.15 = (bf16[576,128]{1,0:T(8,128)(2,1)S(1)}, bf16[576,128]{1,0:T(8,128)(2,1)S(1)}, u32[]{:S(2)}, u32[]{:S(2)}) collective-permute-start(bf16[576,128]{1,0:T(8,128)(2,1)S(1)} %get-tuple-element.44), channel_id=1, source_target_pairs={{0,16},{1,17},{2,18},{3,19},{4,20},{5,21},{6,22},{7,23},{8,24},{9,... | collective-permute-start | bytes 442376 | tf_op jit(solution)/shard_map/ppermute | solution.py:42
  48.3 7.9 %collective-permute-start.16 = (bf16[576,128]{1,0:T(8,128)(2,1)S(1)}, bf16[576,128]{1,0:T(8,128)(2,1)S(1)}, u32[]{:S(2)}, u32[]{:S(2)}) collective-permute-start(bf16[576,128]{1,0:T(8,128)(2,1)S(1)} %get-tuple-element.45), channel_id=1, source_target_pairs={{0,24},{1,25},{2,26},{3,27},{4,28},{5,29},{6,30},{7,31},{8,16},{9,... | collective-permute-start | bytes 442376 | tf_op jit(solution)/shard_map/ppermute | solution.py:42
  49.8 7.7 %collective-permute-start.20 = (bf16[3,4,3584]{2,1,0:T(4,128)(2,1)S(1)}, bf16[3,4,3584]{2,1,0:T(4,128)(2,1)S(1)}, u32[]{:S(2)}, u32[]{:S(2)}) collective-permute-start(bf16[3,4,3584]{2,1,0:T(4,128)(2,1)S(1)} %get-tuple-element.50), channel_id=1, source_target_pairs={{0,6},{1,7},{2,4},{3,5},{4,2},{5,3},{6,0},{7,1},{8,9},{9,8},{10,11... | collective-permute-start | bytes 258056 | tf_op jit(solution)/shard_map/ppermute | solution.py:42
  51.7 6.6 %collective-permute-start.21 = (bf16[3,4,3584]{2,1,0:T(4,128)(2,1)S(1)}, bf16[3,4,3584]{2,1,0:T(4,128)(2,1)S(1)}, u32[]{:S(2)}, u32[]{:S(2)}) collective-permute-start(bf16[3,4,3584]{2,1,0:T(4,128)(2,1)S(1)} %get-tuple-element.51), channel_id=1, source_target_pairs={{0,4},{1,5},{2,6},{3,7},{4,0},{5,1},{6,2},{7,3},{8,24},{9,25},{10,... | collective-permute-start | bytes 258056 | tf_op jit(solution)/shard_map/ppermute | solution.py:42
  55.0 4.5 %collective-permute-start.22 = (bf16[3,4,3584]{2,1,0:T(4,128)(2,1)S(1)}, bf16[3,4,3584]{2,1,0:T(4,128)(2,1)S(1)}, u32[]{:S(2)}, u32[]{:S(2)}) collective-permute-start(bf16[3,4,3584]{2,1,0:T(4,128)(2,1)S(1)} %get-tuple-element.52), channel_id=1, source_target_pairs={{0,2},{1,3},{2,0},{3,1},{4,6},{5,7},{6,4},{7,5},{8,25},{9,24},{10,... | collective-permute-start | bytes 258056 | tf_op jit(solution)/shard_map/ppermute | solution.py:42

commit v8 on v7

--- a/solution.py
+++ b/solution.py
@@ -505,7 +505,7 @@
     groups = lax.axis_size("grp")
     steps, trace_count, _ = moe_input.shape
     core, neighbour, skip, opposite = (1, 0), (0, 2), (0, 4), (0, 6)
-    beside, above, diagonal = (0, 1), (2, 0), (2, 1)
+    beside, above, diagonal = (2, 0), (0, 1), (2, 1)
     first_flips = [(opposite, beside), (skip, above), (neighbour, diagonal)]
     odd = (lax.axis_index("grp") % 2).reshape(1)
     rows = token_rows(group, expert_ids, route_gains, moe_input)

time: 60.9 us -> 60.3 us (level)
  starting transfers between devices: 25.4 us -> 24.6 us
    ppermute x23, starting transfers between devices: 25.4 us -> 24.6 us  [across(): return lax.ppermute(values, BOTH, pairs)]
  transfers between devices with their start and end apart: 23 -> 23, of which waited for: 8 -> 9; matrix products, arithmetic and copies ran while one was open for 1% -> 1% of each run, Pallas kernels for 30% -> 31%
where the time goes in v8:
time: 60.3 us; the launch traced here: 60 us
  starting transfers between devices  24.6 us (41%)
  Pallas kernels  22 us (36%)
  waiting for transfers between devices  11.5 us (19%)
  other arithmetic  1.08 us (2%)
  between operations  0.83 us (1%)
    ppermute x23, starting transfers between devices, across(): return lax.ppermute(values, BOTH, pairs)  24.6 us
    ppermute x23, waiting for transfers between devices, across(): return lax.ppermute(values, BOTH, pairs)  11.5 us
    pallas_call x3, Pallas kernels, expert(): pl.pallas_call(ignoring(expert_kernel, 0, len(others)), in_specs=[ANYWHER...  6.4 us
    pallas_call x1, Pallas kernels, attention(): pl.pallas_call(ignoring(partial(attention_kernel, block), 1, len(others))...  5.78 us
    pallas_call x1, Pallas kernels, fetch(): pl.pallas_call(ignoring(fetch_kernel, 0, len(others)), in_specs=[ANYWHERE...  4.82 us
    pallas_call x1, Pallas kernels, outgoing(): pl.pallas_call(ignoring(partial(outgoing_kernel, others), 0, len(behind))...  2.12 us
    pallas_call x1, Pallas kernels, place(): pl.pallas_call(place_kernel, in_specs=[smem, smem] + [ANYWHERE] * (len(re...  1.32 us
  transfers between devices with their start and end apart: 23, of which 9 were waited for; matrix products, arithmetic and copies ran while one was open for 1% of the time, Pallas kernels for 31%

profile of v8, /device:TPU:0, one launch (start us, length us, event | category | flops | bytes accessed | tf_op | source)
XLA Modules:
  0.0 60.0 jit_solution(11273610072923096181)
XLA Ops:
  0.6 1.1 %token_rows.1.refs_0_ = bf16[3,4,3712]{2,1,0:T(4,128)(2,1)S(1)} custom-call(s32[1]{0:T(128)} %bitcast.1.group_ref.refs_3_, s32[3,4,4,8]{3,2,1,0:T(4,128)} %refs_0_.2, f32[3,4,4,8]{3,2,1,0:T(4,128)} %refs_1_.3, bf16[3,4,3584]{2,1,0:T(4,128)(2,1)} %refs_2_.2), custom_call_target="tpu_custom_call" | custom-call | flops 1 | bytes 100000000 | tf_op jit(solution)/shard_map/token_rows/pallas_call | solution.py:190
  1.8 5.1 %collective-permute-start = (bf16[3,4,3712]{2,1,0:T(4,128)(2,1)S(1)}, bf16[3,4,3712]{2,1,0:T(4,128)(2,1)S(1)}, u32[]{:S(2)}, u32[]{:S(2)}) collective-permute-start(bf16[3,4,3712]{2,1,0:T(4,128)(2,1)S(1)} %token_rows.1.refs_0_), channel_id=1, source_target_pairs={{0,6},{1,7},{2,4},{3,5},{4,2},{5,3},{6,0},{7,1},{8,24},{9,25},{10,... | collective-permute-start | bytes 267272 | tf_op jit(solution)/shard_map/ppermute | solution.py:42
  6.9 0.6 %collective-permute-start.2 = (bf16[3,4,3712]{2,1,0:T(4,128)(2,1)S(1)}, bf16[3,4,3712]{2,1,0:T(4,128)(2,1)S(1)}, u32[]{:S(2)}, u32[]{:S(2)}) collective-permute-start(bf16[3,4,3712]{2,1,0:T(4,128)(2,1)S(1)} %token_rows.1.refs_0_), channel_id=1, source_target_pairs={{0,2},{1,3},{2,0},{3,1},{4,6},{5,7},{6,4},{7,5},{8,25},{9,24},{10,... | collective-permute-start | bytes 267272 | tf_op jit(solution)/shard_map/ppermute | solution.py:42
  7.5 2.0 %collective-permute-done.refs_1_ = bf16[3,4,3712]{2,1,0:T(4,128)(2,1)S(1)} collective-permute-done((bf16[3,4,3712]{2,1,0:T(4,128)(2,1)S(1)}, bf16[3,4,3712]{2,1,0:T(4,128)(2,1)S(1)}, u32[]{:S(2)}, u32[]{:S(2)}) %collective-permute-start) | collective-permute-done | bytes 89120 | tf_op jit(solution)/shard_map/ppermute | solution.py:42
  9.5 2.9 %collective-permute-done.1.refs_2_ = bf16[3,4,3712]{2,1,0:T(4,128)(2,1)S(1)} collective-permute-done((bf16[3,4,3712]{2,1,0:T(4,128)(2,1)S(1)}, bf16[3,4,3712]{2,1,0:T(4,128)(2,1)S(1)}, u32[]{:S(2)}, u32[]{:S(2)}) %collective-permute-start.1) | collective-permute-done | bytes 89120 | tf_op jit(solution)/shard_map/ppermute | solution.py:42
  12.4 0.1 line_rows.1.refs_0_.refs_1_
  12.5 1.6 %collective-permute-start.3 = (bf16[48,3712]{1,0:T(8,128)(2,1)S(1)}, bf16[48,3712]{1,0:T(8,128)(2,1)S(1)}, u32[]{:S(2)}, u32[]{:S(2)}) collective-permute-start(bf16[48,3712]{1,0:T(8,128)(2,1)S(1)} %line_rows.1.refs_0_.refs_1_), channel_id=1, source_target_pairs={{0,16},{1,17},{2,18},{3,19},{4,20},{5,21},{6,22},{7,23},{8,12},{9,... | collective-permute-start | bytes 1069064 | tf_op jit(solution)/shard_map/ppermute | solution.py:42
  14.0 2.7 %collective-permute-start.4 = (bf16[48,3712]{1,0:T(8,128)(2,1)S(1)}, bf16[48,3712]{1,0:T(8,128)(2,1)S(1)}, u32[]{:S(2)}, u32[]{:S(2)}) collective-permute-start(bf16[48,3712]{1,0:T(8,128)(2,1)S(1)} %line_rows.1.refs_0_.refs_1_), channel_id=1, source_target_pairs={{0,1},{1,0},{2,3},{3,2},{4,5},{5,4},{6,7},{7,6},{8,10},{9,11},{10,... | collective-permute-start | bytes 1069064 | tf_op jit(solution)/shard_map/ppermute | solution.py:42
  16.7 4.8 %fetch.1 = (bf16[3584,512]{1,0:T(8,128)(2,1)S(1)}, bf16[3584,512]{1,0:T(8,128)(2,1)S(1)}, bf16[512,3584]{1,0:T(8,128)(2,1)S(1)}, s32[8,128]{1,0:T(8,128)}) custom-call(bf16[48,3712]{1,0:T(8,128)(2,1)S(1)} %line_rows.1.refs_0_.refs_1_, bf16[1,3584,512]{2,1,0:T(8,128)(2,1)} %refs_1_.4, bf16[1,3584,512]{2,1,0:T(8,128)(2,1)} %refs_2_.3, ...), custom_call_target="tpu_custom_call" | custom-call | flops 1 | bytes 100000000 | tf_op jit(solution)/shard_map/fetch/pallas_call | solution.py:393
  21.6 2.1 %expert.3.refs_3_ = bf16[48,3584]{1,0:T(8,128)(2,1)S(1)} custom-call(s32[1]{0:T(128)} %bitcast.refs_0_.refs_1_, bf16[48,3712]{1,0:T(8,128)(2,1)S(1)} %line_rows.1.refs_0_.refs_1_, bf16[3584,512]{1,0:T(8,128)(2,1)S(1)} %get-tuple-element.28.refs_2_.refs_4_.refs_6_, bf16[3584,512]{1,0:T(8,128)(2,1)S(1)} %get-tuple-element.29.refs_3_.refs_5_.refs_7_, ...), custom_call_target="tpu_custom_call" | custom-call | flops 1 | bytes 100000000 | tf_op jit(solution)/shard_map/expert/pallas_call | solution.py:481
  23.7 2.2 %collective-permute-done.4.refs_1_ = bf16[48,3712]{1,0:T(8,128)(2,1)S(1)} collective-permute-done((bf16[48,3712]{1,0:T(8,128)(2,1)S(1)}, bf16[48,3712]{1,0:T(8,128)(2,1)S(1)}, u32[]{:S(2)}, u32[]{:S(2)}) %collective-permute-start.4) | collective-permute-done | bytes 356384 | tf_op jit(solution)/shard_map/ppermute | solution.py:42
  25.9 0.3 collective-permute-start.6
  26.2 0.2 collective-permute-start.7
  26.4 0.3 collective-permute-start.8
  26.8 1.9 %expert.4 = (bf16[48,3584]{1,0:T(8,128)(2,1)S(1)}, bf16[48,3584]{1,0:T(8,128)(2,1)S(1)}, bf16[48,3584]{1,0:T(8,128)(2,1)S(1)}) custom-call(s32[1]{0:T(128)} %bitcast.refs_0_.refs_1_, bf16[48,3712]{1,0:T(8,128)(2,1)S(1)} %get-tuple-element.31.refs_1_, bf16[48,3712]{1,0:T(8,128)(2,1)S(1)} %get-tuple-element.32.refs_2_, ...), custom_call_target="tpu_custom_call" | custom-call | flops 1 | bytes 100000000 | tf_op jit(solution)/shard_map/expert/pallas_call | solution.py:481
  28.7 0.0 copy-start
  28.7 0.0 copy-start.2
  28.7 2.4 %expert.5 = (bf16[48,3584]{1,0:T(8,128)(2,1)S(1)}, bf16[48,3584]{1,0:T(8,128)(2,1)S(1)}, bf16[48,3584]{1,0:T(8,128)(2,1)S(1)}, bf16[48,3584]{1,0:T(8,128)(2,1)S(1)}) custom-call(bf16[48,3584]{1,0:T(8,128)(2,1)S(1)} %get-tuple-element.35.refs_0_, s32[1]{0:T(128)} %bitcast.refs_0_.refs_1_, bf16[48,3712]{1,0:T(8,128)(2,1)S(1)} %collective-permute-done.6.refs_2_, ...), custom_call_target="tpu_custom_call" | custom-call | flops 1 | bytes 100000000 | tf_op jit(solution)/shard_map/expert/pallas_call | solution.py:481
  31.2 0.3 collective-permute-start.10
  31.4 0.3 collective-permute-start.19
  31.7 0.2 collective-permute-start.11
  31.9 0.3 collective-permute-start.12
  32.2 0.6 %collective-permute-done.10 = bf16[48,3584]{1,0:T(8,128)(2,1)S(1)} collective-permute-done((bf16[48,3584]{1,0:T(8,128)(2,1)S(1)}, bf16[48,3584]{1,0:T(8,128)(2,1)S(1)}, u32[]{:S(2)}, u32[]{:S(2)}) %collective-permute-start.10) | collective-permute-done | bytes 344096 | tf_op jit(solution)/shard_map/ppermute | solution.py:42
  32.9 0.1 add_convert_fusion.3.refs_1_
  33.0 1.5 %collective-permute-start.13 = (bf16[48,3584]{1,0:T(8,128)(2,1)S(1)}, bf16[48,3584]{1,0:T(8,128)(2,1)S(1)}, u32[]{:S(2)}, u32[]{:S(2)}) collective-permute-start(bf16[48,3584]{1,0:T(8,128)(2,1)S(1)} %add_convert_fusion.3.refs_1_), channel_id=1, source_target_pairs={{0,17},{1,16},{2,19},{3,18},{4,21},{5,20},{6,23},{7,22},{8,10},{9,... | collective-permute-start | bytes 1032200 | tf_op jit(solution)/shard_map/ppermute | solution.py:42
  34.5 5.8 %attention.1 = (bf16[3,4,128,512]{3,2,1,0:T(8,128)(2,1)}, bf16[4,576,128]{2,1,0:T(8,128)(2,1)}, s32[8,128]{1,0:T(8,128)S(1)}) custom-call(s32[4]{0:T(128)S(1)} %copy-done.2, bf16[48,3584]{1,0:T(8,128)(2,1)S(1)} %add_convert_fusion.3.refs_1_, bf16[3,4,576,128]{3,2,1,0:T(8,128)(2,1)} %bitcast.13, bf16[4,576,128]{2,1,0:T(8,128)(2,1)} %bitcast.11, ...), custom_call_target="tpu_custom_call" | custom-call | flops 1 | bytes 100000000 | tf_op jit(solution)/shard_map/attention/pallas_call | solution.py:412
  40.3 0.0 copy-start.1
  40.3 0.1 add_convert_fusion.1.rows_ref
  40.4 0.1 add_convert_fusion.2.refs_0_
  40.4 0.7 %collective-permute-done.13.refs_1_.more_ref.refs_2_ = bf16[48,3584]{1,0:T(8,128)(2,1)S(1)} collective-permute-done((bf16[48,3584]{1,0:T(8,128)(2,1)S(1)}, bf16[48,3584]{1,0:T(8,128)(2,1)S(1)}, u32[]{:S(2)}, u32[]{:S(2)}) %collective-permute-start.13) | collective-permute-done | bytes 344096 | tf_op jit(solution)/shard_map/ppermute | solution.py:42
  41.2 0.1 add_if_odd.1
  41.3 1.4 %collective-permute-start.17 = (bf16[48,3584]{1,0:T(8,128)(2,1)S(1)}, bf16[48,3584]{1,0:T(8,128)(2,1)S(1)}, u32[]{:S(2)}, u32[]{:S(2)}) collective-permute-start(bf16[48,3584]{1,0:T(8,128)(2,1)S(1)} %add_if_odd.1), channel_id=1, source_target_pairs={{0,16},{1,17},{2,18},{3,19},{4,20},{5,21},{6,22},{7,23},{8,12},{9,... | collective-permute-start | bytes 1032200 | tf_op jit(solution)/shard_map/ppermute | solution.py:42
  42.7 0.7 %collective-permute-start.18 = (bf16[48,3584]{1,0:T(8,128)(2,1)S(1)}, bf16[48,3584]{1,0:T(8,128)(2,1)S(1)}, u32[]{:S(2)}, u32[]{:S(2)}) collective-permute-start(bf16[48,3584]{1,0:T(8,128)(2,1)S(1)} %gate.5.refs_0_), channel_id=1, source_target_pairs={{0,1},{1,0},{2,3},{3,2},{4,5},{5,4},{6,7},{7,6},{8,10},{9,11},{10,... | collective-permute-start | bytes 1032200 | tf_op jit(solution)/shard_map/ppermute | solution.py:42
  43.3 2.1 %outgoing.1 = (bf16[576,128]{1,0:T(8,128)(2,1)S(1)}, bf16[576,128]{1,0:T(8,128)(2,1)S(1)}, bf16[576,128]{1,0:T(8,128)(2,1)S(1)}) custom-call(bf16[48,3584]{1,0:T(8,128)(2,1)S(1)} %gate.5.refs_0_, s32[4]{0:T(128)} %refs_1_.5, s32[2,2,4]{2,1,0:T(2,128)} %bitcast.9, s32[1]{0:T(128)} %bitcast.1.group_ref.refs_3_, bf16[4,576,128]{2,1,0:T(8,128)(2,1)} %bitcast.12, ...), custom_call_target="tpu_custom_call" | custom-call | flops 1 | bytes 100000000 | tf_op jit(solution)/shard_map/outgoing/pallas_call | solution.py:231
  45.5 2.6 %collective-permute-start.14 = (bf16[576,128]{1,0:T(8,128)(2,1)S(1)}, bf16[576,128]{1,0:T(8,128)(2,1)S(1)}, u32[]{:S(2)}, u32[]{:S(2)}) collective-permute-start(bf16[576,128]{1,0:T(8,128)(2,1)S(1)} %get-tuple-element.43.refs_0_), channel_id=1, source_target_pairs={{0,8},{1,9},{2,10},{3,11},{4,12},{5,13},{6,14},{7,15},{8,0},{9,1},... | collective-permute-start | bytes 442376 | tf_op jit(solution)/shard_map/ppermute | solution.py:42
  48.1 0.2 collective-permute-start.15
  48.3 1.2 %collective-permute-start.16 = (bf16[576,128]{1,0:T(8,128)(2,1)S(1)}, bf16[576,128]{1,0:T(8,128)(2,1)S(1)}, u32[]{:S(2)}, u32[]{:S(2)}) collective-permute-start(bf16[576,128]{1,0:T(8,128)(2,1)S(1)} %get-tuple-element.45), channel_id=1, source_target_pairs={{0,24},{1,25},{2,26},{3,27},{4,28},{5,29},{6,30},{7,31},{8,16},{9,... | collective-permute-start | bytes 442376 | tf_op jit(solution)/shard_map/ppermute | solution.py:42
  49.5 0.1 add_convert_fusion.refs_5_
  49.6 0.3 collective-permute-done.18.refs_4_
  49.9 0.2 line_sums.1
  50.2 1.4 %collective-permute-start.20 = (bf16[3,4,3584]{2,1,0:T(4,128)(2,1)S(1)}, bf16[3,4,3584]{2,1,0:T(4,128)(2,1)S(1)}, u32[]{:S(2)}, u32[]{:S(2)}) collective-permute-start(bf16[3,4,3584]{2,1,0:T(4,128)(2,1)S(1)} %get-tuple-element.50), channel_id=1, source_target_pairs={{0,6},{1,7},{2,4},{3,5},{4,2},{5,3},{6,0},{7,1},{8,24},{9,25},{10,... | collective-permute-start | bytes 258056 | tf_op jit(solution)/shard_map/ppermute | solution.py:42
  51.6 3.1 %collective-permute-start.21 = (bf16[3,4,3584]{2,1,0:T(4,128)(2,1)S(1)}, bf16[3,4,3584]{2,1,0:T(4,128)(2,1)S(1)}, u32[]{:S(2)}, u32[]{:S(2)}) collective-permute-start(bf16[3,4,3584]{2,1,0:T(4,128)(2,1)S(1)} %get-tuple-element.51), channel_id=1, source_target_pairs={{0,4},{1,5},{2,6},{3,7},{4,0},{5,1},{6,2},{7,3},{8,9},{9,8},{10,11... | collective-permute-start | bytes 258056 | tf_op jit(solution)/shard_map/ppermute | solution.py:42
  54.7 0.5 collective-permute-start.22
  55.2 0.9 %collective-permute-done.16.refs_2_ = bf16[576,128]{1,0:T(8,128)(2,1)S(1)} collective-permute-done((bf16[576,128]{1,0:T(8,128)(2,1)S(1)}, bf16[576,128]{1,0:T(8,128)(2,1)S(1)}, u32[]{:S(2)}, u32[]{:S(2)}) %collective-permute-start.16) | collective-permute-done | bytes 147488 | tf_op jit(solution)/shard_map/ppermute | solution.py:42
  56.2 1.3 %place.1 = bf16[4,576,128]{2,1,0:T(8,128)(2,1)} custom-call(s32[2,2,4]{2,1,0:T(2,128)S(1)} %bitcast.10, s32[1]{0:T(128)} %bitcast.1.group_ref.refs_3_, bf16[576,128]{1,0:T(8,128)(2,1)S(1)} %collective-permute-done.14.refs_0_, bf16[576,128]{1,0:T(8,128)(2,1)S(1)} %collective-permute-done.15.refs_1_, ...), custom_call_target="tpu_custom_call", output_to_operand_aliasing={{}: (5, {})} | custom-call | flops 1 | bytes 100000000 | tf_op jit(solution)/shard_map/place/pallas_call | solution.py:363
  57.5 0.8 %collective-permute-done.21 = bf16[3,4,3584]{2,1,0:T(4,128)(2,1)S(1)} collective-permute-done((bf16[3,4,3584]{2,1,0:T(4,128)(2,1)S(1)}, bf16[3,4,3584]{2,1,0:T(4,128)(2,1)S(1)}, u32[]{:S(2)}, u32[]{:S(2)}) %collective-permute-start.21) | collective-permute-done | bytes 86048 | tf_op jit(solution)/shard_map/ppermute | solution.py:42
  58.3 0.9 %collective-permute-done.22 = bf16[3,4,3584]{2,1,0:T(4,128)(2,1)S(1)} collective-permute-done((bf16[3,4,3584]{2,1,0:T(4,128)(2,1)S(1)}, bf16[3,4,3584]{2,1,0:T(4,128)(2,1)S(1)}, u32[]{:S(2)}, u32[]{:S(2)}) %collective-permute-start.22) | collective-permute-done | bytes 86048 | tf_op jit(solution)/shard_map/ppermute | solution.py:42
  59.3 0.7 %add_convert_fusion.4 = bf16[3,4,3584]{2,1,0:T(4,128)(2,1)} fusion(bf16[3,4,3584]{2,1,0:T(4,128)(2,1)S(1)} %collective-permute-done.22, bf16[3,4,3584]{2,1,0:T(4,128)(2,1)S(1)} %collective-permute-done.21, bf16[3,4,3584]{2,1,0:T(4,128)(2,1)S(1)} %collective-permute-done.20, bf16[3,4,3584]{2,1,0:T(4,128)(2,1)S(1)} %get-tuple-element.49), kind=kLoop, calls=%fused_computation.4 | loop fusion | flops 344064 | bytes 430080 | tf_op jit(solution)/shard_map/convert_element_type | solution.py:499
  (23 shorter events, 0.1 us)
Async XLA Ops:
  1.8 7.7 %collective-permute-start = (bf16[3,4,3712]{2,1,0:T(4,128)(2,1)S(1)}, bf16[3,4,3712]{2,1,0:T(4,128)(2,1)S(1)}, u32[]{:S(2)}, u32[]{:S(2)}) collective-permute-start(bf16[3,4,3712]{2,1,0:T(4,128)(2,1)S(1)} %token_rows.1.refs_0_), channel_id=1, source_target_pairs={{0,6},{1,7},{2,4},{3,5},{4,2},{5,3},{6,0},{7,1},{8,24},{9,25},{10,... | collective-permute-start | bytes 267272 | tf_op jit(solution)/shard_map/ppermute | solution.py:42
  6.9 5.5 %collective-permute-start.1 = (bf16[3,4,3712]{2,1,0:T(4,128)(2,1)S(1)}, bf16[3,4,3712]{2,1,0:T(4,128)(2,1)S(1)}, u32[]{:S(2)}, u32[]{:S(2)}) collective-permute-start(bf16[3,4,3712]{2,1,0:T(4,128)(2,1)S(1)} %token_rows.1.refs_0_), channel_id=1, source_target_pairs={{0,4},{1,5},{2,6},{3,7},{4,0},{5,1},{6,2},{7,3},{8,9},{9,8},{10,11... | collective-permute-start | bytes 267272 | tf_op jit(solution)/shard_map/ppermute | solution.py:42
  6.9 5.5 %collective-permute-start.2 = (bf16[3,4,3712]{2,1,0:T(4,128)(2,1)S(1)}, bf16[3,4,3712]{2,1,0:T(4,128)(2,1)S(1)}, u32[]{:S(2)}, u32[]{:S(2)}) collective-permute-start(bf16[3,4,3712]{2,1,0:T(4,128)(2,1)S(1)} %token_rows.1.refs_0_), channel_id=1, source_target_pairs={{0,2},{1,3},{2,0},{3,1},{4,6},{5,7},{6,4},{7,5},{8,25},{9,24},{10,... | collective-permute-start | bytes 267272 | tf_op jit(solution)/shard_map/ppermute | solution.py:42
  12.5 11.2 %collective-permute-start.3 = (bf16[48,3712]{1,0:T(8,128)(2,1)S(1)}, bf16[48,3712]{1,0:T(8,128)(2,1)S(1)}, u32[]{:S(2)}, u32[]{:S(2)}) collective-permute-start(bf16[48,3712]{1,0:T(8,128)(2,1)S(1)} %line_rows.1.refs_0_.refs_1_), channel_id=1, source_target_pairs={{0,16},{1,17},{2,18},{3,19},{4,20},{5,21},{6,22},{7,23},{8,12},{9,... | collective-permute-start | bytes 1069064 | tf_op jit(solution)/shard_map/ppermute | solution.py:42
  14.0 11.9 %collective-permute-start.4 = (bf16[48,3712]{1,0:T(8,128)(2,1)S(1)}, bf16[48,3712]{1,0:T(8,128)(2,1)S(1)}, u32[]{:S(2)}, u32[]{:S(2)}) collective-permute-start(bf16[48,3712]{1,0:T(8,128)(2,1)S(1)} %line_rows.1.refs_0_.refs_1_), channel_id=1, source_target_pairs={{0,1},{1,0},{2,3},{3,2},{4,5},{5,4},{6,7},{7,6},{8,10},{9,11},{10,... | collective-permute-start | bytes 1069064 | tf_op jit(solution)/shard_map/ppermute | solution.py:42
  16.7 9.2 %collective-permute-start.5 = (bf16[48,3712]{1,0:T(8,128)(2,1)S(1)}, bf16[48,3712]{1,0:T(8,128)(2,1)S(1)}, u32[]{:S(2)}, u32[]{:S(2)}) collective-permute-start(bf16[48,3712]{1,0:T(8,128)(2,1)S(1)} %line_rows.1.refs_0_.refs_1_), channel_id=1, source_target_pairs={{0,17},{1,16},{2,19},{3,18},{4,21},{5,20},{6,23},{7,22},{8,14},{9,... | collective-permute-start | bytes 1069064 | tf_op jit(solution)/shard_map/ppermute | solution.py:42
  16.7 11.9 %collective-permute-start.9 = (bf16[48,3712]{1,0:T(8,128)(2,1)S(1)}, bf16[48,3712]{1,0:T(8,128)(2,1)S(1)}, u32[]{:S(2)}, u32[]{:S(2)}) collective-permute-start(bf16[48,3712]{1,0:T(8,128)(2,1)S(1)} %line_rows.1.refs_0_.refs_1_), channel_id=1, source_target_pairs={{0,8},{1,9},{2,10},{3,11},{4,12},{5,13},{6,14},{7,15},{8,0},{9,1},... | collective-permute-start | bytes 1069064 | tf_op jit(solution)/shard_map/ppermute | solution.py:42
  25.9 2.7 %collective-permute-start.6 = (bf16[48,3712]{1,0:T(8,128)(2,1)S(1)}, bf16[48,3712]{1,0:T(8,128)(2,1)S(1)}, u32[]{:S(2)}, u32[]{:S(2)}) collective-permute-start(bf16[48,3712]{1,0:T(8,128)(2,1)S(1)} %get-tuple-element.31.refs_1_), channel_id=1, source_target_pairs={{0,8},{1,9},{2,10},{3,11},{4,12},{5,13},{6,14},{7,15},{8,0},{9,1},... | collective-permute-start | bytes 1069064 | tf_op jit(solution)/shard_map/ppermute | solution.py:42
  26.2 2.4 %collective-permute-start.7 = (bf16[48,3712]{1,0:T(8,128)(2,1)S(1)}, bf16[48,3712]{1,0:T(8,128)(2,1)S(1)}, u32[]{:S(2)}, u32[]{:S(2)}) collective-permute-start(bf16[48,3712]{1,0:T(8,128)(2,1)S(1)} %get-tuple-element.32.refs_2_), channel_id=1, source_target_pairs={{0,8},{1,9},{2,10},{3,11},{4,12},{5,13},{6,14},{7,15},{8,0},{9,1},... | collective-permute-start | bytes 1069064 | tf_op jit(solution)/shard_map/ppermute | solution.py:42
  26.4 2.3 %collective-permute-start.8 = (bf16[48,3712]{1,0:T(8,128)(2,1)S(1)}, bf16[48,3712]{1,0:T(8,128)(2,1)S(1)}, u32[]{:S(2)}, u32[]{:S(2)}) collective-permute-start(bf16[48,3712]{1,0:T(8,128)(2,1)S(1)} %get-tuple-element.33.refs_3_), channel_id=1, source_target_pairs={{0,8},{1,9},{2,10},{3,11},{4,12},{5,13},{6,14},{7,15},{8,0},{9,1},... | collective-permute-start | bytes 1069064 | tf_op jit(solution)/shard_map/ppermute | solution.py:42
  28.7 5.8 %copy-start = (bf16[3,4,576]{2,1,0:T(4,128)(2,1)S(1)}, bf16[3,4,576]{2,1,0:T(4,128)(2,1)}, u32[]{:S(2)}) copy-start(bf16[3,4,576]{2,1,0:T(4,128)(2,1)} %refs_5_.1) | copy-start | bytes 41476
  28.7 5.8 %copy-start.2 = (s32[4]{0:T(128)S(1)}, s32[4]{0:T(128)}, u32[]{:S(2)}) copy-start(s32[4]{0:T(128)} %refs_1_.5) | copy-start | bytes 52
  31.2 1.7 %collective-permute-start.10 = (bf16[48,3584]{1,0:T(8,128)(2,1)S(1)}, bf16[48,3584]{1,0:T(8,128)(2,1)S(1)}, u32[]{:S(2)}, u32[]{:S(2)}) collective-permute-start(bf16[48,3584]{1,0:T(8,128)(2,1)S(1)} %get-tuple-element.36), channel_id=1, source_target_pairs={{0,8},{1,9},{2,10},{3,11},{4,12},{5,13},{6,14},{7,15},{8,0},{9,1},... | collective-permute-start | bytes 1032200 | tf_op jit(solution)/shard_map/ppermute | solution.py:42
  31.4 16.9 %collective-permute-start.19 = (bf16[48,3584]{1,0:T(8,128)(2,1)S(1)}, bf16[48,3584]{1,0:T(8,128)(2,1)S(1)}, u32[]{:S(2)}, u32[]{:S(2)}) collective-permute-start(bf16[48,3584]{1,0:T(8,128)(2,1)S(1)} %get-tuple-element.48), channel_id=1, source_target_pairs={{0,8},{1,9},{2,10},{3,11},{4,12},{5,13},{6,14},{7,15},{8,0},{9,1},... | collective-permute-start | bytes 1032200 | tf_op jit(solution)/shard_map/ppermute | solution.py:42
  31.7 8.5 %collective-permute-start.11 = (bf16[48,3584]{1,0:T(8,128)(2,1)S(1)}, bf16[48,3584]{1,0:T(8,128)(2,1)S(1)}, u32[]{:S(2)}, u32[]{:S(2)}) collective-permute-start(bf16[48,3584]{1,0:T(8,128)(2,1)S(1)} %get-tuple-element.39), channel_id=1, source_target_pairs={{0,8},{1,9},{2,10},{3,11},{4,12},{5,13},{6,14},{7,15},{8,0},{9,1},... | collective-permute-start | bytes 1032200 | tf_op jit(solution)/shard_map/ppermute | solution.py:42
  31.9 8.3 %collective-permute-start.12 = (bf16[48,3584]{1,0:T(8,128)(2,1)S(1)}, bf16[48,3584]{1,0:T(8,128)(2,1)S(1)}, u32[]{:S(2)}, u32[]{:S(2)}) collective-permute-start(bf16[48,3584]{1,0:T(8,128)(2,1)S(1)} %get-tuple-element.40), channel_id=1, source_target_pairs={{0,8},{1,9},{2,10},{3,11},{4,12},{5,13},{6,14},{7,15},{8,0},{9,1},... | collective-permute-start | bytes 1032200 | tf_op jit(solution)/shard_map/ppermute | solution.py:42
  33.0 8.2 %collective-permute-start.13 = (bf16[48,3584]{1,0:T(8,128)(2,1)S(1)}, bf16[48,3584]{1,0:T(8,128)(2,1)S(1)}, u32[]{:S(2)}, u32[]{:S(2)}) collective-permute-start(bf16[48,3584]{1,0:T(8,128)(2,1)S(1)} %add_convert_fusion.3.refs_1_), channel_id=1, source_target_pairs={{0,17},{1,16},{2,19},{3,18},{4,21},{5,20},{6,23},{7,22},{8,10},{9,... | collective-permute-start | bytes 1032200 | tf_op jit(solution)/shard_map/ppermute | solution.py:42
  40.3 15.9 %copy-start.1 = (s32[4,1,2,2]{0,3,2,1:T(2,128)S(1)}, s32[4,1,2,2]{0,3,2,1:T(2,128)}, u32[]{:S(2)}) copy-start(s32[4,1,2,2]{0,3,2,1:T(2,128)} %param.21) | copy-start | bytes 196
  41.3 8.3 %collective-permute-start.17 = (bf16[48,3584]{1,0:T(8,128)(2,1)S(1)}, bf16[48,3584]{1,0:T(8,128)(2,1)S(1)}, u32[]{:S(2)}, u32[]{:S(2)}) collective-permute-start(bf16[48,3584]{1,0:T(8,128)(2,1)S(1)} %add_if_odd.1), channel_id=1, source_target_pairs={{0,16},{1,17},{2,18},{3,19},{4,20},{5,21},{6,22},{7,23},{8,12},{9,... | collective-permute-start | bytes 1032200 | tf_op jit(solution)/shard_map/ppermute | solution.py:42
  42.7 7.2 %collective-permute-start.18 = (bf16[48,3584]{1,0:T(8,128)(2,1)S(1)}, bf16[48,3584]{1,0:T(8,128)(2,1)S(1)}, u32[]{:S(2)}, u32[]{:S(2)}) collective-permute-start(bf16[48,3584]{1,0:T(8,128)(2,1)S(1)} %gate.5.refs_0_), channel_id=1, source_target_pairs={{0,1},{1,0},{2,3},{3,2},{4,5},{5,4},{6,7},{7,6},{8,10},{9,11},{10,... | collective-permute-start | bytes 1032200 | tf_op jit(solution)/shard_map/ppermute | solution.py:42
  45.5 9.3 %collective-permute-start.14 = (bf16[576,128]{1,0:T(8,128)(2,1)S(1)}, bf16[576,128]{1,0:T(8,128)(2,1)S(1)}, u32[]{:S(2)}, u32[]{:S(2)}) collective-permute-start(bf16[576,128]{1,0:T(8,128)(2,1)S(1)} %get-tuple-element.43.refs_0_), channel_id=1, source_target_pairs={{0,8},{1,9},{2,10},{3,11},{4,12},{5,13},{6,14},{7,15},{8,0},{9,1},... | collective-permute-start | bytes 442376 | tf_op jit(solution)/shard_map/ppermute | solution.py:42
  48.1 7.2 %collective-permute-start.15 = (bf16[576,128]{1,0:T(8,128)(2,1)S(1)}, bf16[576,128]{1,0:T(8,128)(2,1)S(1)}, u32[]{:S(2)}, u32[]{:S(2)}) collective-permute-start(bf16[576,128]{1,0:T(8,128)(2,1)S(1)} %get-tuple-element.44), channel_id=1, source_target_pairs={{0,16},{1,17},{2,18},{3,19},{4,20},{5,21},{6,22},{7,23},{8,24},{9,... | collective-permute-start | bytes 442376 | tf_op jit(solution)/shard_map/ppermute | solution.py:42
  48.3 7.9 %collective-permute-start.16 = (bf16[576,128]{1,0:T(8,128)(2,1)S(1)}, bf16[576,128]{1,0:T(8,128)(2,1)S(1)}, u32[]{:S(2)}, u32[]{:S(2)}) collective-permute-start(bf16[576,128]{1,0:T(8,128)(2,1)S(1)} %get-tuple-element.45), channel_id=1, source_target_pairs={{0,24},{1,25},{2,26},{3,27},{4,28},{5,29},{6,30},{7,31},{8,16},{9,... | collective-permute-start | bytes 442376 | tf_op jit(solution)/shard_map/ppermute | solution.py:42
  50.2 7.3 %collective-permute-start.20 = (bf16[3,4,3584]{2,1,0:T(4,128)(2,1)S(1)}, bf16[3,4,3584]{2,1,0:T(4,128)(2,1)S(1)}, u32[]{:S(2)}, u32[]{:S(2)}) collective-permute-start(bf16[3,4,3584]{2,1,0:T(4,128)(2,1)S(1)} %get-tuple-element.50), channel_id=1, source_target_pairs={{0,6},{1,7},{2,4},{3,5},{4,2},{5,3},{6,0},{7,1},{8,24},{9,25},{10,... | collective-permute-start | bytes 258056 | tf_op jit(solution)/shard_map/ppermute | solution.py:42
  51.6 6.8 %collective-permute-start.21 = (bf16[3,4,3584]{2,1,0:T(4,128)(2,1)S(1)}, bf16[3,4,3584]{2,1,0:T(4,128)(2,1)S(1)}, u32[]{:S(2)}, u32[]{:S(2)}) collective-permute-start(bf16[3,4,3584]{2,1,0:T(4,128)(2,1)S(1)} %get-tuple-element.51), channel_id=1, source_target_pairs={{0,4},{1,5},{2,6},{3,7},{4,0},{5,1},{6,2},{7,3},{8,9},{9,8},{10,11... | collective-permute-start | bytes 258056 | tf_op jit(solution)/shard_map/ppermute | solution.py:42
  54.7 4.5 %collective-permute-start.22 = (bf16[3,4,3584]{2,1,0:T(4,128)(2,1)S(1)}, bf16[3,4,3584]{2,1,0:T(4,128)(2,1)S(1)}, u32[]{:S(2)}, u32[]{:S(2)}) collective-permute-start(bf16[3,4,3584]{2,1,0:T(4,128)(2,1)S(1)} %get-tuple-element.52), channel_id=1, source_target_pairs={{0,2},{1,3},{2,0},{3,1},{4,6},{5,7},{6,4},{7,5},{8,25},{9,24},{10,... | collective-permute-start | bytes 258056 | tf_op jit(solution)/shard_map/ppermute | solution.py:42
